TPU v7x, 128 devices: a whole 4x4x4 slice. The times are simulated.
128 devices in a mesh: row: 32 (over z_lo, x, y), col: 4 (over z_hi, core).
Axes of the slice: x: 4, y: 4, z: 4 (z_hi: 2, z_lo: 2; z = z_hi * 2 + z_lo), core: 2. Of those that a mesh axis runs over, the one named last changes fastest.
Arguments:
- amplitudes: bfloat16 [1024, 28672], P(('row', 'col')), may hold values from -6 to 6
- amplitude_mask: int32 [1024, 224], P(('row', 'col')), may hold values 0 or 1
- integrals: bfloat16 [28672, 28672], P('row', 'col'), may hold values from -0.03125 to 0.03125
- integral_mask: int32 [224, 224], P('row', 'col'), may hold values from 0 to 1, as said below
- tile_order: int32 [224], replicated, may hold values from 0 to 223, each once
Outputs:
- ladder: bfloat16 [1024, 28672], P(('row', 'col'))
Inputs may be any that keep to these rules, and one draw needn't show every extreme that they name: `amplitude_mask`: 1 keeps a tile of amplitudes, 0 drops it. `integral_mask`: 1 keeps a tile of integrals, 0 drops it. `tile_order`: each tile of 0 to 223 appears once.
All inputs are finite; a program needn't handle non-finite values. No bound on the sum of `amplitude_mask` on one device may be relied on, other than what follows from the above.
Results may differ from a plain program's by a relative error of at most 0.0012.
Values may be sent and summed in bfloat16 or wider, within the bound.
No kernel may reach another device: no remote copies, remote signals or barrier semaphores. Data moves between devices by JAX's collectives and lax.ppermute only.
A program may use at most 128 MiB of HBM per device.

v0:
```python
import jax
import jax.numpy as jnp
from jax import lax
from jax.sharding import PartitionSpec as P


def mask_block(block_values, flag_tiles):
    row_count, col_count = block_values.shape
    row_tiles, col_tiles = flag_tiles.shape
    shaped = block_values.reshape(
        row_tiles, row_count // row_tiles, col_tiles, col_count // col_tiles
    )
    return (shaped * flag_tiles.astype(jnp.bfloat16)[:, None, :, None]).reshape(
        row_count, col_count
    )


def per_device(amplitudes, amplitude_mask, integrals, integral_mask, tile_order):
    pair_count, full_width = amplitudes.shape
    tile_count = amplitude_mask.shape[1]
    shaped = (
        amplitudes.reshape(pair_count, tile_count, full_width // tile_count)
        * amplitude_mask.astype(jnp.bfloat16)[:, :, None]
    )
    ordered = jnp.take(shaped, tile_order, axis=1).reshape(pair_count, full_width)
    grouped = lax.all_gather(ordered, "col", axis=0, tiled=True)
    placed = lax.all_to_all(grouped, "row", split_axis=1, concat_axis=0, tiled=True)
    weights = mask_block(integrals, integral_mask)
    partial_value = jnp.dot(placed, weights, preferred_element_type=jnp.float32)
    summed = lax.psum_scatter(partial_value, "row", scatter_dimension=0, tiled=True)
    return lax.all_to_all(
        summed.astype(jnp.bfloat16), "col", split_axis=0, concat_axis=1, tiled=True
    )


def solution(mesh):
    in_specs = (
        P(("row", "col"), None),
        P(("row", "col"), None),
        P("row", "col"),
        P("row", "col"),
        P(),
    )
    out_specs = P(("row", "col"), None)
    return jax.shard_map(
        per_device, mesh=mesh, in_specs=in_specs, out_specs=out_specs, check_vma=False
    )
```

profile of v0, /device:TPU:1, one launch (start us, length us, event | category | flops | bytes accessed | tf_op | source)
XLA Modules:
  0.0 452.4 jit_solution(5331006858073416076)
XLA Ops:
  6.5 0.0 all-gather.2.cloned.1.call-start
  6.5 0.7 compare_and_fusion
  7.2 0.7 compare_select_fusion
  7.9 0.7 convert_element_type.9
  8.6 0.1 broadcast_bitcast_fusion
  8.7 0.1 copy.10
  8.9 1.3 bitcast_multiply_fusion.2
  10.2 0.8 gather_fusion
  11.0 0.9 bitcast_select_fusion
  11.9 0.0 all-gather.2.cloned.1.call-update
  11.9 29.1 %all-gather.2.cloned.1.call-done = bf16[32,28672]{1,0:T(8,128)(2,1)} async-done(((bf16[8,28672]{1,0:T(8,128)(2,1)}), bf16[32,28672]{1,0:T(8,128)(2,1)}) %all-gather.2.cloned.1.call-update) | async-done | bytes 1835024 | tf_op jit(solution)/shard_map/all_gather | solution.py:26
  41.0 2.9 copy.19
  43.9 6.9 %all-to-all-start = ((bf16[32,32,896]{2,0,1:T(8,128)(2,1)}), bf16[32,32,896]{2,0,1:T(8,128)(2,1)S(1)}, u32[]{:S(2)}, u32[]{:S(2)}) async-start(bf16[32,32,896]{2,0,1:T(8,128)(2,1)} %bitcast.25), calls=%async_computation | async-start | bytes 3670016 | tf_op jit(solution)/shard_map/all_to_all | solution.py:27
  50.8 0.0 reduce-scatter.2.cloned.1.call-start
  50.8 0.7 convert_element_type.10
  51.5 24.2 %all-to-all-done = bf16[32,32,896]{2,0,1:T(8,128)(2,1)S(1)} async-done(((bf16[32,32,896]{2,0,1:T(8,128)(2,1)}), bf16[32,32,896]{2,0,1:T(8,128)(2,1)S(1)}, u32[]{:S(2)}, u32[]{:S(2)}) %all-to-all-start) | async-done | bytes 1835040 | tf_op jit(solution)/shard_map/all_to_all | solution.py:27
  75.7 6.3 %mul.21 = bf16[7,128,56,128]{3,2,1,0:T(8,128)(2,1)} broadcast(bf16[7,56]{1,0:T(8,128)(2,1)S(1)} %convert_element_type.10), dimensions={0,2} | broadcast | bytes 12845840 | tf_op jit(solution)/shard_map/mul | solution.py:13
  82.0 27.9 %fusion = f32[1024,7168]{1,0:T(8,128)} fusion(bf16[1024,896]{1,0:T(8,128)(2,1)S(1)} %bitcast.27, bf16[896,7168]{1,0:T(8,128)(2,1)} %param.7, bf16[112,8,56,128]{3,2,1,0:T(8,128)(2,1)} %bitcast.26), kind=kOutput, calls=%fused_computation.2 | convolution fusion | flops 13159759872 | bytes 56885248 | tf_op jit(solution)/shard_map/dot_general | solution.py:29
  109.9 0.0 reduce-scatter.2.cloned.1.call-update
  109.9 320.3 %reduce-scatter.2.cloned.1.call-done = f32[32,7168]{1,0:T(8,128)} async-done(((f32[1024,7168]{1,0:T(8,128)}), f32[32,7168]{1,0:T(8,128)}) %reduce-scatter.2.cloned.1.call-update) | async-done | bytes 917520 | tf_op jit(solution)/shard_map/reduce_scatter | solution.py:30
  430.2 1.2 convert_bitcast_fusion
  431.4 13.4 %all_to_all.38 = bf16[4,8,7168]{2,1,0:T(8,128)(2,1)S(1)} all-to-all(bf16[4,8,7168]{2,1,0:T(8,128)(2,1)S(1)} %convert_bitcast_fusion), channel_id=1, replica_groups=mesh['row'=32,'col'=4] {'col'}, dimensions={0} | all-to-all | bytes 917504 | tf_op jit(solution)/shard_map/all_to_all | solution.py:31
  444.8 0.8 copy.21
  (1 shorter events, 0.0 us)
Async XLA Ops:
  6.5 34.4 %all-gather.2.cloned.1.call-start = ((), (), s32[]{:S(2)}) async-start(), calls=%async_computation.3 | async-start | bytes 2293760 | tf_op jit(solution)/shard_map/all_gather | solution.py:26
  43.9 31.8 %all-to-all-start = ((bf16[32,32,896]{2,0,1:T(8,128)(2,1)}), bf16[32,32,896]{2,0,1:T(8,128)(2,1)S(1)}, u32[]{:S(2)}, u32[]{:S(2)}) async-start(bf16[32,32,896]{2,0,1:T(8,128)(2,1)} %bitcast.25), calls=%async_computation | async-start | bytes 3670016 | tf_op jit(solution)/shard_map/all_to_all | solution.py:27
  50.8 379.4 %reduce-scatter.2.cloned.1.call-start = ((), (), s32[]{:S(2)}) async-start(), calls=%async_computation.4 | async-start | bytes 30277632 | tf_op jit(solution)/shard_map/reduce_scatter | solution.py:30
Sparse Core Ops, SparseCore 0:
  12.0 28.9 all-gather.1
  110.0 320.0 reduce-scatter.1
where the time goes:
time: 453 us; the launch traced here: 452 us
  waiting for transfers between devices  374 us (83%)
  matrix products  27.9 us (6%)
  blocking collectives  13.4 us (3%)
  between operations  13.4 us (3%)
  local copies, waits for them, and re-layouts  11 us (2%)
  starting transfers between devices  6.95 us (2%)
  other arithmetic  6.21 us (1%)
    reduce_scatter x1, waiting for transfers between devices, per_device(): lax.psum_scatter(partial_value, 'row', scatter_dimension=0, tiled=True)  320 us
    all_gather x1, waiting for transfers between devices, per_device(): grouped = lax.all_gather(ordered, 'col', axis=0, tiled=True)  29.1 us
    dot_general x1, matrix products, per_device(): partial_value = jnp.dot(placed, weights, preferred_element_type=jnp.float32)  27.9 us
    all_to_all x1, waiting for transfers between devices, per_device(): lax.all_to_all(grouped, 'row', split_axis=1, concat_axis=0, tiled=True)  24.2 us
    all_to_all x1, blocking collectives, per_device(): lax.all_to_all(summed.astype(jnp.bfloat16), 'col', split_axis=0, concat_a...  13.4 us
  transfers between devices with their start and end apart: 3, of which 3 were waited for; matrix products, arithmetic and copies ran while one was open for 0% of the time, Pallas kernels for 0%

commit v1 on v0

v1 whole, which is shorter than its diff:
```python
import functools

import jax
import jax.numpy as jnp
from jax import lax
from jax.experimental import pallas as pl
from jax.experimental.pallas import tpu as pltpu
from jax.sharding import PartitionSpec as P

N_CHUNK = 2
TILE = 256
LEVELS = 32600.0
STEPS = 32.0
VMEM_LIMIT = 48 * 1024 * 1024


def shift(dz, dx, dy):
    pairs = []
    for index in range(32):
        z, x, y = index // 16, (index // 4) % 4, index % 4
        pairs.append((index, ((z + dz) % 2) * 16 + ((x + dx) % 4) * 4 + (y + dy) % 4))
    return pairs


FORWARD = (shift(0, 1, 0), shift(0, 0, 1))
BACKWARD = (shift(0, -1, 0), shift(0, 0, -1))
ACROSS = shift(1, 0, 0)


def send(value, pairs):
    return lax.ppermute(value, "row", pairs)


def left_rows(a_ref, kind, first):
    first_stride, second_stride = (128, 32) if kind == 0 else (32, 128)
    blocks = []
    for z in range(2):
        for second in range(4):
            start = pl.multiple_of(z * 512 + second * second_stride + first * first_stride, 32)
            blocks.append(a_ref[pl.ds(start, 32), :])
    return jnp.concatenate(blocks, axis=0)


def masked(b_ref, m_ref):
    parts = [
        b_ref[k * 128:(k + 1) * 128, :] * m_ref[k:k + 1, :].astype(jnp.bfloat16) for k in range(b_ref.shape[0] // 128)
    ]
    return jnp.concatenate(parts, axis=0)


def dot(left, right):
    return jnp.dot(left, right, preferred_element_type=jnp.float32)


def encode(value, step, out_ref, codes_ref):
    largest = jnp.maximum(jnp.max(jnp.abs(value), axis=1, keepdims=True), 1e-30)
    code = jnp.ceil(jnp.log2(largest) * STEPS)
    factor = jnp.exp2(code * (-1.0 / STEPS)) * LEVELS
    at = pl.ds(pl.multiple_of(step * TILE, TILE), TILE)
    out_ref[:, at] = jnp.round(value * factor).astype(jnp.int32).astype(jnp.int16)
    lane = lax.broadcasted_iota(jnp.int32, codes_ref.shape, 1)
    codes = jnp.where(lane == step, code, codes_ref[...])
    codes_ref[...] = codes
    width = out_ref.shape[1] - 128

    @pl.when(step == pl.num_programs(0) - 1)
    def _():
        out_ref[:, width:] = codes.astype(jnp.int32).astype(jnp.int16)


def decode(data_ref, code_ref, step):
    codes = code_ref[...].astype(jnp.int32).astype(jnp.float32)
    lane = lax.broadcasted_iota(jnp.int32, codes.shape, 1)
    code = jnp.sum(jnp.where(lane == step, codes, 0.0), axis=1, keepdims=True)
    factor = jnp.exp2(code * (1.0 / STEPS)) * (1.0 / LEVELS)
    return data_ref[...].astype(jnp.int32).astype(jnp.float32) * factor


def opposite_kernel(pos, a, b0, b1, m0, m1, p0, q0, p1, q1, *codes):
    step = pl.program_id(0)

    for kind, b, m, p, q in ((0, b0, m0, p0, q0), (1, b1, m1, p1, q1)):
        rows = left_rows(a, kind, (pos[1 + kind] + 2) % 4)
        sums = dot(rows, masked(b, m))
        encode(sums[:128], step, p, codes[2 * kind])
        encode(sums[128:], step, q, codes[2 * kind + 1])


def neighbour_kernel(pos, a, b0, b1, m0, m1, *refs):
    step = pl.program_id(0)
    taken, outs, codes = refs[:8], refs[8:12], refs[12:]
    for kind, b, m in ((0, b0, m0), (1, b1, m1)):
        right = masked(b, m)
        for way in range(2):
            first = (pos[1 + kind] + (1 if way == 0 else 3)) % 4
            sums = dot(left_rows(a, kind, first), right)
            got = decode(taken[4 * kind + 2 * way], taken[4 * kind + 2 * way + 1], step)
            if way == 0:
                sums = jnp.concatenate([sums[:128] + got, sums[128:]], axis=0)
            else:
                sums = jnp.concatenate([sums[:128], sums[128:] + got], axis=0)
            encode(sums, step, outs[2 * kind + way], codes[2 * kind + way])


def own_kernel(pos, a, b0, b1, m0, m1, *refs):
    step = pl.program_id(0)
    taken, outs, codes = refs[:8], refs[8:14], refs[14:]
    for kind, b, m in ((0, b0, m0), (1, b1, m1)):
        sums = dot(left_rows(a, kind, pos[1 + kind]), masked(b, m))
        for way in range(2):
            sums = sums + decode(taken[4 * kind + 2 * way], taken[4 * kind + 2 * way + 1], step)
        p, q, kept = outs[3 * kind:3 * kind + 3]
        kept[...] = sums
        second = (pos[2 - kind] + 2) % 4
        for z, out in ((0, p), (1, q)):
            encode(kept[pl.ds(pl.multiple_of(z * 128 + second * 32, 32), 32), :], step, out, codes[2 * kind + z])


def second_neighbour_kernel(pos, *refs):
    step = pl.program_id(0)
    taken, outs, codes = refs[:10], refs[10:14], refs[14:]
    for kind in range(2):
        kept = taken[5 * kind]
        for way in range(2):
            second = (pos[2 - kind] + (1 if way == 0 else 3)) % 4
            got = decode(taken[5 * kind + 1 + 2 * way], taken[5 * kind + 2 + 2 * way], step)
            parts = [kept[pl.ds(pl.multiple_of(z * 128 + second * 32, 32), 32), :] for z in range(2)]
            parts[way] = parts[way] + got
            encode(jnp.concatenate(parts, axis=0), step, outs[2 * kind + way], codes[2 * kind + way])


def second_own_kernel(pos, *refs):
    step = pl.program_id(0)
    taken, outs, codes, scratch = refs[:10], refs[10:14], refs[14:16], refs[16]
    for kind in range(2):
        kept = taken[5 * kind]
        second = pos[2 - kind]
        parts = [kept[pl.ds(pl.multiple_of(z * 128 + second * 32, 32), 32), :] for z in range(2)]
        sums = jnp.concatenate(parts, axis=0)
        for way in range(2):
            sums = sums + decode(taken[5 * kind + 1 + 2 * way], taken[5 * kind + 2 + 2 * way], step)
        scratch[...] = sums
        z = pos[0]
        encode(scratch[pl.ds(pl.multiple_of((1 - z) * 32, 32), 32), :], step, outs[2 * kind], codes[kind])
        outs[2 * kind + 1][...] = scratch[pl.ds(pl.multiple_of(z * 32, 32), 32), :]


def last_kernel(*refs):
    step = pl.program_id(0)
    taken, outs = refs[:6], refs[6:]
    for kind in range(2):
        sums = taken[3 * kind][...] + decode(taken[3 * kind + 1], taken[3 * kind + 2], step)
        outs[kind][...] = sums.astype(jnp.bfloat16)


def whole(shape):
    return pl.BlockSpec(shape, lambda j: (0, 0))


def pieces(rows, start=0):
    return pl.BlockSpec((rows, TILE), lambda j: (0, j + start))


def coded(rows, width):
    return [pieces(rows), pl.BlockSpec((rows, 128), lambda j: (0, width // 128))]


def twice(values):
    return [v for value in values for v in (value, value)]


def call(kernel, args, in_specs, outs, out_specs, scratch, width, name):
    return pl.pallas_call(
        kernel,
        grid=(width // TILE,),
        in_specs=in_specs,
        out_specs=out_specs,
        out_shape=outs,
        scratch_shapes=scratch,
        compiler_params=pltpu.CompilerParams(vmem_limit_bytes=VMEM_LIMIT),
        cost_estimate=pl.CostEstimate(flops=1000000, bytes_accessed=1000000, transcendentals=0),
        name=name,
    )(*args)


SMEM = pl.BlockSpec(memory_space=pltpu.SMEM)


def per_device(amplitudes, amplitude_mask, integrals, integral_mask, tile_order):
    pair_count, full_width = amplitudes.shape
    tile_count = amplitude_mask.shape[1]
    depth, columns = integrals.shape
    width = columns // (2 * N_CHUNK)
    tiles = width // TILE
    row = lax.axis_index("row")
    pos = jnp.stack([row // 16, (row // 4) % 4, row % 4]).astype(jnp.int32)
    shaped = (
        amplitudes.reshape(pair_count, tile_count, full_width // tile_count)
        * amplitude_mask.astype(jnp.bfloat16)[:, :, None]
    )
    ordered = jnp.take(shaped, tile_order, axis=1).reshape(pair_count, full_width)
    placed = lax.all_to_all(ordered, "row", split_axis=1, concat_axis=0, tiled=True)
    col = lax.axis_index("col")
    beside = lax.ppermute(placed, "col", [(0, 1), (1, 0), (2, 3), (3, 2)])
    over = lax.ppermute(placed, "col", [(0, 2), (1, 3), (2, 0), (3, 1)])
    both = lax.ppermute(over, "col", [(0, 1), (1, 0), (2, 3), (3, 2)])
    core, z_hi = col % 2, col // 2
    even, odd = jnp.where(core == 0, placed, beside), jnp.where(core == 0, beside, placed)
    far_even, far_odd = jnp.where(core == 0, over, both), jnp.where(core == 0, both, over)
    four = [
        jnp.where(z_hi == 0, even, far_even),
        jnp.where(z_hi == 0, odd, far_odd),
        jnp.where(z_hi == 0, far_even, even),
        jnp.where(z_hi == 0, far_odd, odd),
    ]
    left = jnp.stack([v.reshape(32, 8, depth) for v in four], axis=1).reshape(1024, depth)
    flags = jnp.repeat(integral_mask.astype(jnp.float32), 128, axis=1)

    def sent(rows):
        return jax.ShapeDtypeStruct((rows, width + 128), jnp.int16)

    def codes(rows, count):
        return [pltpu.VMEM((rows, 128), jnp.float32)] * count

    finals = []
    stage = []

    def product_args(j):
        args = [pos, left, integrals, integrals, flags, flags]
        starts = [2 * j * tiles, (2 * j + 1) * tiles]
        specs = [SMEM, whole((1024, depth))]
        specs += [pieces(depth, s) for s in starts] + [pieces(integral_mask.shape[0], s) for s in starts]
        return args, specs

    def begin(j):
        args, specs = product_args(j)
        p0, q0, p1, q1 = call(
            opposite_kernel, args, specs, [sent(128)] * 4, [whole((128, width + 128))] * 4, codes(128, 4), width,
            "opposite",
        )
        return [send(p0, FORWARD[0]), send(q0, BACKWARD[0]), send(p1, FORWARD[1]), send(q1, BACKWARD[1])]

    def second(j, got):
        args, specs = product_args(j)
        outs = call(
            neighbour_kernel, args + twice(got), specs + coded(128, width) * 4, [sent(256)] * 4,
            [whole((256, width + 128))] * 4, codes(256, 4), width, "neighbour",
        )
        return [send(outs[2 * k + w], (FORWARD, BACKWARD)[w][k]) for k in range(2) for w in range(2)]

    def third(j, got):
        args, specs = product_args(j)
        kept = jax.ShapeDtypeStruct((256, width), jnp.float32)
        p0, q0, k0, p1, q1, k1 = call(
            own_kernel, args + twice(got), specs + coded(256, width) * 4, [sent(32), sent(32), kept] * 2,
            [whole((32, width + 128))] * 2 + [pieces(256)] + [whole((32, width + 128))] * 2 + [pieces(256)],
            codes(32, 4), width, "own",
        )
        return [k0, k1], [send(p0, FORWARD[1]), send(q0, BACKWARD[1]), send(p1, FORWARD[0]), send(q1, BACKWARD[0])]

    def fourth(kept, got):
        args = [pos, kept[0]] + twice(got[:2]) + [kept[1]] + twice(got[2:])
        specs = [SMEM] + ([pieces(256)] + coded(32, width) * 2) * 2
        outs = call(
            second_neighbour_kernel, args, specs, [sent(64)] * 4, [whole((64, width + 128))] * 4, codes(64, 4), width,
            "second_neighbour",
        )
        return [send(outs[2 * k + w], (FORWARD, BACKWARD)[w][1 - k]) for k in range(2) for w in range(2)]

    def fifth(kept, got):
        args = [pos, kept[0]] + twice(got[:2]) + [kept[1]] + twice(got[2:])
        specs = [SMEM] + ([pieces(256)] + coded(64, width) * 2) * 2
        rest = jax.ShapeDtypeStruct((32, width), jnp.float32)
        p0, k0, p1, k1 = call(
            second_own_kernel, args, specs, [sent(32), rest] * 2, [whole((32, width + 128)), pieces(32)] * 2,
            codes(32, 2) + [pltpu.VMEM((64, TILE), jnp.float32)], width, "second_own",
        )
        return [k0, k1], [send(p0, ACROSS), send(p1, ACROSS)]

    def sixth(kept, got):
        args = [kept[0], got[0], got[0], kept[1], got[1], got[1]]
        specs = ([pieces(32)] + coded(32, width)) * 2
        return call(
            last_kernel, args, specs, [jax.ShapeDtypeStruct((32, width), jnp.bfloat16)] * 2, [pieces(32)] * 2, [],
            width, "last",
        )

    ones = [begin(j) for j in range(N_CHUNK)]
    twos = [second(j, ones[j]) for j in range(N_CHUNK)]
    for j in range(N_CHUNK):
        kept, got = third(j, twos[j])
        got = fourth(kept, got)
        rest, got = fifth(kept, got)
        finals += sixth(rest, got)
    summed = jnp.concatenate(finals, axis=1)
    return lax.all_to_all(summed, "col", split_axis=0, concat_axis=1, tiled=True)


def solution(mesh):
    in_specs = (
        P(("row", "col"), None),
        P(("row", "col"), None),
        P("row", "col"),
        P("row", "col"),
        P(),
    )
    out_specs = P(("row", "col"), None)
    return jax.shard_map(
        per_device, mesh=mesh, in_specs=in_specs, out_specs=out_specs, check_vma=False
    )
```

time: 453 us -> 252 us (0.56)
  waiting for transfers between devices: 374 us -> 47 us
  Pallas kernels: 0 us -> 109 us
  starting transfers between devices: 6.95 us -> 46.7 us
  blocking collectives: 13.4 us -> 43 us
  matrix products: 27.9 us -> 0 us
  between operations: 13.4 us -> 0.35 us
  local copies, waits for them, and re-layouts: 11 us -> 2.09 us
    reduce_scatter x1 -> x0, waiting for transfers between devices: 320 us -> none  [per_device(): lax.psum_scatter(partial_value, 'row', scatter_dimension=0, tiled=True)]
    pallas_call x0 -> x12, Pallas kernels: none -> 109 us  [call(): pl.pallas_call(kernel, grid=(width // TILE,), in_specs=in_specs, out_spec...]
    ppermute x0 -> x39, waiting for transfers between devices: none -> 47 us  [the longest x36 40.5 us: send(): return lax.ppermute(value, 'row', pairs)]
    ppermute x0 -> x39, starting transfers between devices: none -> 46.7 us  [the longest x36 37.3 us: send(): return lax.ppermute(value, 'row', pairs)]
    all_to_all x1 -> x2, blocking collectives: 13.4 us -> 43 us  [the longest x1 24.6 us: per_device(): lax.all_to_all(summed, 'col', split_axis=0, concat_axis=1, tiled=True)]
    all_gather x1 -> x0, waiting for transfers between devices: 29.1 us -> none  [per_device(): grouped = lax.all_gather(ordered, 'col', axis=0, tiled=True)]
    dot_general x1 -> x0, matrix products: 27.9 us -> none  [per_device(): partial_value = jnp.dot(placed, weights, preferred_element_type=jnp.float32)]
    all_to_all x1 -> x0, waiting for transfers between devices: 24.2 us -> none  [per_device(): lax.all_to_all(grouped, 'row', split_axis=1, concat_axis=0, tiled=True)]
  transfers between devices with their start and end apart: 3 -> 39, of which waited for: 3 -> 8; matrix products, arithmetic and copies ran while one was open for 0% -> 0% of each run, Pallas kernels for 0% -> 38%
where the time goes in v1:
time: 252 us
  Pallas kernels  109 us (43%)
  waiting for transfers between devices  47 us (19%)
  starting transfers between devices  46.7 us (19%)
  blocking collectives  43 us (17%)
  other arithmetic  4.18 us (2%)
    pallas_call x12, Pallas kernels, call(): pl.pallas_call(kernel, grid=(width // TILE,), in_specs=in_specs, out_spec...  109 us
    ppermute x36, waiting for transfers between devices, send(): return lax.ppermute(value, 'row', pairs)  40.5 us
    ppermute x36, starting transfers between devices, send(): return lax.ppermute(value, 'row', pairs)  37.3 us
    all_to_all x1, blocking collectives, per_device(): lax.all_to_all(summed, 'col', split_axis=0, concat_axis=1, tiled=True)  24.6 us
    all_to_all x1, blocking collectives, per_device(): lax.all_to_all(ordered, 'row', split_axis=1, concat_axis=0, tiled=True)  18.4 us
    ppermute x1, waiting for transfers between devices, per_device(): over = lax.ppermute(placed, 'col', [(0, 2), (1, 3), (2, 0), (3, 1)])  5.35 us
  transfers between devices with their start and end apart: 39, of which 8 were waited for; matrix products, arithmetic and copies ran while one was open for 0% of the time, Pallas kernels for 38%

profile of v1, /device:TPU:1, one launch (start us, length us, event | category | flops | bytes accessed | tf_op | source)
XLA Modules:
  0.0 252.0 jit_solution(10244317115508103441)
XLA Ops:
  4.8 18.4 %all_to_all.35 = bf16[8,32,896]{2,0,1:T(8,128)(2,1)S(1)} all-to-all(bf16[8,32,896]{2,0,1:T(8,128)(2,1)S(1)} %broadcast_select_fusion), channel_id=1, replica_groups=mesh['row'=32,'col'=4] {'row'}, dimensions={1} | all-to-all | bytes 917504 | tf_op jit(solution)/shard_map/all_to_all | solution.py:202
  23.2 3.3 %collective-permute-start.1 = (bf16[256,896]{1,0:T(8,128)(2,1)S(1)}, bf16[256,896]{1,0:T(8,128)(2,1)S(1)}, u32[]{:S(2)}, u32[]{:S(2)}) collective-permute-start(bf16[256,896]{1,0:T(8,128)(2,1)S(1)} %bitcast.57), channel_id=1, source_target_pairs={{0,2},{1,3},{2,0},{3,1},{4,6},{5,7},{6,4},{7,5},{8,10},{9,11},{10,... | collective-permute-start | bytes 1376264 | tf_op jit(solution)/shard_map/ppermute | solution.py:205
  26.5 2.9 %collective-permute-start = (bf16[256,896]{1,0:T(8,128)(2,1)S(1)}, bf16[256,896]{1,0:T(8,128)(2,1)S(1)}, u32[]{:S(2)}, u32[]{:S(2)}) collective-permute-start(bf16[256,896]{1,0:T(8,128)(2,1)S(1)} %bitcast.58), channel_id=1, source_target_pairs={{0,1},{1,0},{2,3},{3,2},{4,5},{5,4},{6,7},{7,6},{8,9},{9,8},{10,11... | collective-permute-start | bytes 1376264 | tf_op jit(solution)/shard_map/ppermute | solution.py:204
  29.3 5.4 %collective-permute-done.1 = bf16[256,896]{1,0:T(8,128)(2,1)S(1)} collective-permute-done((bf16[256,896]{1,0:T(8,128)(2,1)S(1)}, bf16[256,896]{1,0:T(8,128)(2,1)S(1)}, u32[]{:S(2)}, u32[]{:S(2)}) %collective-permute-start.1) | collective-permute-done | bytes 458784 | tf_op jit(solution)/shard_map/ppermute | solution.py:205
  34.7 3.2 %collective-permute-start.2 = (bf16[256,896]{1,0:T(8,128)(2,1)S(1)}, bf16[256,896]{1,0:T(8,128)(2,1)S(1)}, u32[]{:S(2)}, u32[]{:S(2)}) collective-permute-start(bf16[256,896]{1,0:T(8,128)(2,1)S(1)} %collective-permute-done.1), channel_id=1, source_target_pairs={{0,1},{1,0},{2,3},{3,2},{4,5},{5,4},{6,7},{7,6},{8,9},{9,8},{10,11... | collective-permute-start | bytes 1376264 | tf_op jit(solution)/shard_map/ppermute | solution.py:206
  39.9 10.7 %opposite.3 = (s16[128,1920]{1,0:T(8,128)(2,1)S(1)}, s16[128,1920]{1,0:T(8,128)(2,1)S(1)}, s16[128,1920]{1,0:T(8,128)(2,1)S(1)}, s16[128,1920]{1,0:T(8,128)(2,1)S(1)}) custom-call(s32[3]{0:T(128)S(1)} %pad_add_fusion.pos, bf16[1024,896]{1,0:T(8,128)(2,1)S(1)} %bitcast.38, bf16[896,7168]{1,0:T(8,128)(2,1)} %b1.11, bf16[896,7168]{1,0:T(8,128)(2,1)} %b1.11, ...), custom_call_target="tpu_custom_call" | custom-call | flops 1000000 | bytes 1000000 | tf_op jit(solution)/shard_map/opposite/pallas_call | solution.py:173
  51.2 2.1 collective-permute-start.22
  53.3 1.5 collective-permute-start.23
  56.0 10.0 %opposite.2 = (s16[128,1920]{1,0:T(8,128)(2,1)S(1)}, s16[128,1920]{1,0:T(8,128)(2,1)S(1)}, s16[128,1920]{1,0:T(8,128)(2,1)S(1)}, s16[128,1920]{1,0:T(8,128)(2,1)S(1)}) custom-call(s32[3]{0:T(128)S(1)} %pad_add_fusion.pos, bf16[1024,896]{1,0:T(8,128)(2,1)S(1)} %bitcast.39, bf16[896,7168]{1,0:T(8,128)(2,1)} %b1.11, bf16[896,7168]{1,0:T(8,128)(2,1)} %b1.11, ...), custom_call_target="tpu_custom_call" | custom-call | flops 1000000 | bytes 1000000 | tf_op jit(solution)/shard_map/opposite/pallas_call | solution.py:173
  66.1 2.7 %collective-permute-start.4 = (s16[128,1920]{1,0:T(8,128)(2,1)S(1)}, s16[128,1920]{1,0:T(8,128)(2,1)S(1)}, u32[]{:S(2)}, u32[]{:S(2)}) collective-permute-start(s16[128,1920]{1,0:T(8,128)(2,1)S(1)} %get-tuple-element.54), channel_id=1, source_target_pairs={{0,48},{4,52},{8,56},{12,60},{16,0},{20,4},{24,8},{28,12},{32,16},... | collective-permute-start | bytes 1474568 | tf_op jit(solution)/shard_map/ppermute | solution.py:31
  68.8 17.7 %neighbour.3 = (s16[256,1920]{1,0:T(8,128)(2,1)S(1)}, s16[256,1920]{1,0:T(8,128)(2,1)S(1)}, s16[256,1920]{1,0:T(8,128)(2,1)S(1)}, s16[256,1920]{1,0:T(8,128)(2,1)S(1)}) custom-call(s32[3]{0:T(128)S(1)} %pad_add_fusion.pos, bf16[1024,896]{1,0:T(8,128)(2,1)} %bitcast.40, bf16[896,7168]{1,0:T(8,128)(2,1)} %b1.11, bf16[896,7168]{1,0:T(8,128)(2,1)} %b1.11, ...), custom_call_target="tpu_custom_call" | custom-call | flops 1000000 | bytes 1000000 | tf_op jit(solution)/shard_map/neighbour/pallas_call | solution.py:173
  86.6 2.7 %collective-permute-start.26 = (s16[256,1920]{1,0:T(8,128)(2,1)S(1)}, s16[256,1920]{1,0:T(8,128)(2,1)S(1)}, u32[]{:S(2)}, u32[]{:S(2)}) collective-permute-start(s16[256,1920]{1,0:T(8,128)(2,1)S(1)} %get-tuple-element.82), channel_id=1, source_target_pairs={{0,48},{4,52},{8,56},{12,60},{16,0},{20,4},{24,8},{28,12},{32,16},... | collective-permute-start | bytes 2949128 | tf_op jit(solution)/shard_map/ppermute | solution.py:31
  89.5 2.6 %collective-permute-start.6 = (s16[128,1920]{1,0:T(8,128)(2,1)S(1)}, s16[128,1920]{1,0:T(8,128)(2,1)S(1)}, u32[]{:S(2)}, u32[]{:S(2)}) collective-permute-start(s16[128,1920]{1,0:T(8,128)(2,1)S(1)} %get-tuple-element.56), channel_id=1, source_target_pairs={{0,12},{4,0},{8,4},{12,8},{16,28},{20,16},{24,20},{28,24},{32,44},... | collective-permute-start | bytes 1474568 | tf_op jit(solution)/shard_map/ppermute | solution.py:31
  92.1 29.5 %collective-permute-done.5.refs_4_.refs_5_ = s16[128,1920]{1,0:T(8,128)(2,1)S(1)} collective-permute-done((s16[128,1920]{1,0:T(8,128)(2,1)S(1)}, s16[128,1920]{1,0:T(8,128)(2,1)S(1)}, u32[]{:S(2)}, u32[]{:S(2)}) %collective-permute-start.5) | collective-permute-done | bytes 491552 | tf_op jit(solution)/shard_map/ppermute | solution.py:31
  121.6 17.6 %neighbour.2 = (s16[256,1920]{1,0:T(8,128)(2,1)S(1)}, s16[256,1920]{1,0:T(8,128)(2,1)S(1)}, s16[256,1920]{1,0:T(8,128)(2,1)S(1)}, s16[256,1920]{1,0:T(8,128)(2,1)S(1)}) custom-call(s32[3]{0:T(128)S(1)} %pad_add_fusion.pos, bf16[1024,896]{1,0:T(8,128)(2,1)} %bitcast.41, bf16[896,7168]{1,0:T(8,128)(2,1)} %b1.11, bf16[896,7168]{1,0:T(8,128)(2,1)} %b1.11, ...), custom_call_target="tpu_custom_call" | custom-call | flops 1000000 | bytes 1000000 | tf_op jit(solution)/shard_map/neighbour/pallas_call | solution.py:173
  139.3 2.7 %collective-permute-start.8 = (s16[256,1920]{1,0:T(8,128)(2,1)S(1)}, s16[256,1920]{1,0:T(8,128)(2,1)S(1)}, u32[]{:S(2)}, u32[]{:S(2)}) collective-permute-start(s16[256,1920]{1,0:T(8,128)(2,1)S(1)} %get-tuple-element.58), channel_id=1, source_target_pairs={{0,48},{4,52},{8,56},{12,60},{16,0},{20,4},{24,8},{28,12},{32,16},... | collective-permute-start | bytes 2949128 | tf_op jit(solution)/shard_map/ppermute | solution.py:31
  142.0 1.4 collective-permute-start.9
  144.6 12.9 %own.3 = (s16[32,1920]{1,0:T(8,128)(2,1)S(1)}, s16[32,1920]{1,0:T(8,128)(2,1)S(1)}, f32[256,1792]{1,0:T(8,128)}, s16[32,1920]{1,0:T(8,128)(2,1)S(1)}, s16[32,1920]{1,0:T(8,128)(2,1)S(1)}, /*index=5*/f32[256,1792]{1,0:T(8,128)}) custom-call(s32[3]{0:T(128)S(1)} %pad_add_fusion.pos, bf16[1024,896]{1,0:T(8,128)(2,1)} %bitcast.42, bf16[896,7168]{1,0:T(8,128)(2,1)} %b1.11, ...), custom_call_target="tpu_custom_call" | custom-call | flops 1000000 | bytes 1000000 | tf_op jit(solution)/shard_map/own/pallas_call | solution.py:173
  157.8 2.4 collective-permute-done.7.refs_0_.refs_1_
  160.2 2.1 collective-permute-done.9.refs_4_.refs_5_
  162.9 13.0 %own.2 = (s16[32,1920]{1,0:T(8,128)(2,1)S(1)}, s16[32,1920]{1,0:T(8,128)(2,1)S(1)}, f32[256,1792]{1,0:T(8,128)}, s16[32,1920]{1,0:T(8,128)(2,1)S(1)}, s16[32,1920]{1,0:T(8,128)(2,1)S(1)}, /*index=5*/f32[256,1792]{1,0:T(8,128)}) custom-call(s32[3]{0:T(128)S(1)} %pad_add_fusion.pos, bf16[1024,896]{1,0:T(8,128)(2,1)} %bitcast.43, bf16[896,7168]{1,0:T(8,128)(2,1)} %b1.11, ...), custom_call_target="tpu_custom_call" | custom-call | flops 1000000 | bytes 1000000 | tf_op jit(solution)/shard_map/own/pallas_call | solution.py:173
  177.2 1.5 collective-permute-start.12
  178.7 7.2 %second_neighbour.3 = (s16[64,1920]{1,0:T(8,128)(2,1)S(1)}, s16[64,1920]{1,0:T(8,128)(2,1)S(1)}, s16[64,1920]{1,0:T(8,128)(2,1)S(1)}, s16[64,1920]{1,0:T(8,128)(2,1)S(1)}) custom-call(s32[3]{0:T(128)S(1)} %pad_add_fusion.pos, f32[256,1792]{1,0:T(8,128)S(1)} %copy-done.1, s16[32,1920]{1,0:T(8,128)(2,1)S(1)} %collective-permute-done.29.refs_1_.refs_2_, ...), custom_call_target="tpu_custom_call" | custom-call | flops 1000000 | bytes 1000000 | tf_op jit(solution)/shard_map/second_neighbour/pallas_call | solution.py:173
  186.0 2.7 %collective-permute-start.34 = (s16[64,1920]{1,0:T(8,128)(2,1)S(1)}, s16[64,1920]{1,0:T(8,128)(2,1)S(1)}, u32[]{:S(2)}, u32[]{:S(2)}) collective-permute-start(s16[64,1920]{1,0:T(8,128)(2,1)S(1)} %get-tuple-element.92), channel_id=1, source_target_pairs={{0,12},{4,0},{8,4},{12,8},{16,28},{20,16},{24,20},{28,24},{32,44},... | collective-permute-start | bytes 737288 | tf_op jit(solution)/shard_map/ppermute | solution.py:31
  189.3 2.6 %collective-permute-start.14 = (s16[32,1920]{1,0:T(8,128)(2,1)S(1)}, s16[32,1920]{1,0:T(8,128)(2,1)S(1)}, u32[]{:S(2)}, u32[]{:S(2)}) collective-permute-start(s16[32,1920]{1,0:T(8,128)(2,1)S(1)} %get-tuple-element.66), channel_id=1, source_target_pairs={{0,48},{4,52},{8,56},{12,60},{16,0},{20,4},{24,8},{28,12},{32,16},... | collective-permute-start | bytes 368648 | tf_op jit(solution)/shard_map/ppermute | solution.py:31
  191.9 4.3 %collective-permute-done.13.refs_6_.refs_7_ = s16[32,1920]{1,0:T(8,128)(2,1)S(1)} collective-permute-done((s16[32,1920]{1,0:T(8,128)(2,1)S(1)}, s16[32,1920]{1,0:T(8,128)(2,1)S(1)}, u32[]{:S(2)}, u32[]{:S(2)}) %collective-permute-start.13) | collective-permute-done | bytes 122912 | tf_op jit(solution)/shard_map/ppermute | solution.py:31
  196.2 7.2 %second_neighbour.2 = (s16[64,1920]{1,0:T(8,128)(2,1)S(1)}, s16[64,1920]{1,0:T(8,128)(2,1)S(1)}, s16[64,1920]{1,0:T(8,128)(2,1)S(1)}, s16[64,1920]{1,0:T(8,128)(2,1)S(1)}) custom-call(s32[3]{0:T(128)S(1)} %pad_add_fusion.pos, f32[256,1792]{1,0:T(8,128)S(1)} %copy-done.3, s16[32,1920]{1,0:T(8,128)(2,1)S(1)} %collective-permute-done.11.refs_1_.refs_2_, ...), custom_call_target="tpu_custom_call" | custom-call | flops 1000000 | bytes 1000000 | tf_op jit(solution)/shard_map/second_neighbour/pallas_call | solution.py:173
  203.5 2.7 %collective-permute-start.16 = (s16[64,1920]{1,0:T(8,128)(2,1)S(1)}, s16[64,1920]{1,0:T(8,128)(2,1)S(1)}, u32[]{:S(2)}, u32[]{:S(2)}) collective-permute-start(s16[64,1920]{1,0:T(8,128)(2,1)S(1)} %get-tuple-element.68), channel_id=1, source_target_pairs={{0,12},{4,0},{8,4},{12,8},{16,28},{20,16},{24,20},{28,24},{32,44},... | collective-permute-start | bytes 737288 | tf_op jit(solution)/shard_map/ppermute | solution.py:31
  206.2 1.5 collective-permute-start.17
  208.9 4.8 %second_own.3 = (s16[32,1920]{1,0:T(8,128)(2,1)S(1)}, f32[32,1792]{1,0:T(8,128)S(1)}, s16[32,1920]{1,0:T(8,128)(2,1)S(1)}, f32[32,1792]{1,0:T(8,128)S(1)}) custom-call(s32[3]{0:T(128)S(1)} %pad_add_fusion.pos, f32[256,1792]{1,0:T(8,128)S(1)} %copy-done.1, s16[64,1920]{1,0:T(8,128)(2,1)S(1)} %collective-permute-done.33.refs_1_.refs_2_, ...), custom_call_target="tpu_custom_call" | custom-call | flops 1000000 | bytes 1000000 | tf_op jit(solution)/shard_map/second_own/pallas_call | solution.py:173
  215.3 4.8 %second_own.2 = (s16[32,1920]{1,0:T(8,128)(2,1)S(1)}, f32[32,1792]{1,0:T(8,128)S(1)}, s16[32,1920]{1,0:T(8,128)(2,1)S(1)}, f32[32,1792]{1,0:T(8,128)S(1)}) custom-call(s32[3]{0:T(128)S(1)} %pad_add_fusion.pos, f32[256,1792]{1,0:T(8,128)S(1)} %copy-done.3, s16[64,1920]{1,0:T(8,128)(2,1)S(1)} %collective-permute-done.15.refs_1_.refs_2_, ...), custom_call_target="tpu_custom_call" | custom-call | flops 1000000 | bytes 1000000 | tf_op jit(solution)/shard_map/second_own/pallas_call | solution.py:173
  226.6 24.6 %all_to_all.36 = bf16[4,8,7168]{2,1,0:T(8,128)(2,1)S(1)} all-to-all(bf16[4,8,7168]{2,1,0:T(8,128)(2,1)S(1)} %maximum_bitcast_fusion), channel_id=1, replica_groups=mesh['row'=32,'col'=4] {'col'}, dimensions={0} | all-to-all | bytes 917504 | tf_op jit(solution)/shard_map/all_to_all | solution.py:296
  (91 shorter events, 23.2 us)
Async XLA Ops:
  23.2 11.5 %collective-permute-start.1 = (bf16[256,896]{1,0:T(8,128)(2,1)S(1)}, bf16[256,896]{1,0:T(8,128)(2,1)S(1)}, u32[]{:S(2)}, u32[]{:S(2)}) collective-permute-start(bf16[256,896]{1,0:T(8,128)(2,1)S(1)} %bitcast.57), channel_id=1, source_target_pairs={{0,2},{1,3},{2,0},{3,1},{4,6},{5,7},{6,4},{7,5},{8,10},{9,11},{10,... | collective-permute-start | bytes 1376264 | tf_op jit(solution)/shard_map/ppermute | solution.py:205
  26.5 11.8 %collective-permute-start = (bf16[256,896]{1,0:T(8,128)(2,1)S(1)}, bf16[256,896]{1,0:T(8,128)(2,1)S(1)}, u32[]{:S(2)}, u32[]{:S(2)}) collective-permute-start(bf16[256,896]{1,0:T(8,128)(2,1)S(1)} %bitcast.58), channel_id=1, source_target_pairs={{0,1},{1,0},{2,3},{3,2},{4,5},{5,4},{6,7},{7,6},{8,9},{9,8},{10,11... | collective-permute-start | bytes 1376264 | tf_op jit(solution)/shard_map/ppermute | solution.py:204
  50.6 15.5 %collective-permute-start.21 = (s16[128,1920]{1,0:T(8,128)(2,1)S(1)}, s16[128,1920]{1,0:T(8,128)(2,1)S(1)}, u32[]{:S(2)}, u32[]{:S(2)}) collective-permute-start(s16[128,1920]{1,0:T(8,128)(2,1)S(1)} %get-tuple-element.77), channel_id=1, source_target_pairs={{0,16},{4,20},{8,24},{12,28},{16,32},{20,36},{24,40},{28,44},{32,4... | collective-permute-start | bytes 1474568 | tf_op jit(solution)/shard_map/ppermute | solution.py:31
  51.2 17.6 %collective-permute-start.22 = (s16[128,1920]{1,0:T(8,128)(2,1)S(1)}, s16[128,1920]{1,0:T(8,128)(2,1)S(1)}, u32[]{:S(2)}, u32[]{:S(2)}) collective-permute-start(s16[128,1920]{1,0:T(8,128)(2,1)S(1)} %get-tuple-element.78), channel_id=1, source_target_pairs={{0,48},{4,52},{8,56},{12,60},{16,0},{20,4},{24,8},{28,12},{32,16},... | collective-permute-start | bytes 1474568 | tf_op jit(solution)/shard_map/ppermute | solution.py:31
  53.3 15.5 %collective-permute-start.23 = (s16[128,1920]{1,0:T(8,128)(2,1)S(1)}, s16[128,1920]{1,0:T(8,128)(2,1)S(1)}, u32[]{:S(2)}, u32[]{:S(2)}) collective-permute-start(s16[128,1920]{1,0:T(8,128)(2,1)S(1)} %get-tuple-element.79), channel_id=1, source_target_pairs={{0,4},{4,8},{8,12},{12,0},{16,20},{20,24},{24,28},{28,16},{32,36},... | collective-permute-start | bytes 1474568 | tf_op jit(solution)/shard_map/ppermute | solution.py:31
  54.8 14.0 %collective-permute-start.24 = (s16[128,1920]{1,0:T(8,128)(2,1)S(1)}, s16[128,1920]{1,0:T(8,128)(2,1)S(1)}, u32[]{:S(2)}, u32[]{:S(2)}) collective-permute-start(s16[128,1920]{1,0:T(8,128)(2,1)S(1)} %get-tuple-element.80), channel_id=1, source_target_pairs={{0,12},{4,0},{8,4},{12,8},{16,28},{20,16},{24,20},{28,24},{32,44},... | collective-permute-start | bytes 1474568 | tf_op jit(solution)/shard_map/ppermute | solution.py:31
  66.0 23.4 %collective-permute-start.3 = (s16[128,1920]{1,0:T(8,128)(2,1)S(1)}, s16[128,1920]{1,0:T(8,128)(2,1)S(1)}, u32[]{:S(2)}, u32[]{:S(2)}) collective-permute-start(s16[128,1920]{1,0:T(8,128)(2,1)S(1)} %get-tuple-element.53), channel_id=1, source_target_pairs={{0,16},{4,20},{8,24},{12,28},{16,32},{20,36},{24,40},{28,44},{32,4... | collective-permute-start | bytes 1474568 | tf_op jit(solution)/shard_map/ppermute | solution.py:31
  66.1 23.4 %collective-permute-start.4 = (s16[128,1920]{1,0:T(8,128)(2,1)S(1)}, s16[128,1920]{1,0:T(8,128)(2,1)S(1)}, u32[]{:S(2)}, u32[]{:S(2)}) collective-permute-start(s16[128,1920]{1,0:T(8,128)(2,1)S(1)} %get-tuple-element.54), channel_id=1, source_target_pairs={{0,48},{4,52},{8,56},{12,60},{16,0},{20,4},{24,8},{28,12},{32,16},... | collective-permute-start | bytes 1474568 | tf_op jit(solution)/shard_map/ppermute | solution.py:31
  86.5 52.8 %collective-permute-start.25 = (s16[256,1920]{1,0:T(8,128)(2,1)S(1)}, s16[256,1920]{1,0:T(8,128)(2,1)S(1)}, u32[]{:S(2)}, u32[]{:S(2)}) collective-permute-start(s16[256,1920]{1,0:T(8,128)(2,1)S(1)} %get-tuple-element.81), channel_id=1, source_target_pairs={{0,16},{4,20},{8,24},{12,28},{16,32},{20,36},{24,40},{28,44},{32,4... | collective-permute-start | bytes 2949128 | tf_op jit(solution)/shard_map/ppermute | solution.py:31
  86.6 55.4 %collective-permute-start.26 = (s16[256,1920]{1,0:T(8,128)(2,1)S(1)}, s16[256,1920]{1,0:T(8,128)(2,1)S(1)}, u32[]{:S(2)}, u32[]{:S(2)}) collective-permute-start(s16[256,1920]{1,0:T(8,128)(2,1)S(1)} %get-tuple-element.82), channel_id=1, source_target_pairs={{0,48},{4,52},{8,56},{12,60},{16,0},{20,4},{24,8},{28,12},{32,16},... | collective-permute-start | bytes 2949128 | tf_op jit(solution)/shard_map/ppermute | solution.py:31
  89.2 54.2 %collective-permute-start.27 = (s16[256,1920]{1,0:T(8,128)(2,1)S(1)}, s16[256,1920]{1,0:T(8,128)(2,1)S(1)}, u32[]{:S(2)}, u32[]{:S(2)}) collective-permute-start(s16[256,1920]{1,0:T(8,128)(2,1)S(1)} %get-tuple-element.83), channel_id=1, source_target_pairs={{0,4},{4,8},{8,12},{12,0},{16,20},{20,24},{24,28},{28,16},{32,36},... | collective-permute-start | bytes 2949128 | tf_op jit(solution)/shard_map/ppermute | solution.py:31
  89.4 32.2 %collective-permute-start.5 = (s16[128,1920]{1,0:T(8,128)(2,1)S(1)}, s16[128,1920]{1,0:T(8,128)(2,1)S(1)}, u32[]{:S(2)}, u32[]{:S(2)}) collective-permute-start(s16[128,1920]{1,0:T(8,128)(2,1)S(1)} %get-tuple-element.55), channel_id=1, source_target_pairs={{0,4},{4,8},{8,12},{12,0},{16,20},{20,24},{24,28},{28,16},{32,36},... | collective-permute-start | bytes 1474568 | tf_op jit(solution)/shard_map/ppermute | solution.py:31
  89.5 32.1 %collective-permute-start.6 = (s16[128,1920]{1,0:T(8,128)(2,1)S(1)}, s16[128,1920]{1,0:T(8,128)(2,1)S(1)}, u32[]{:S(2)}, u32[]{:S(2)}) collective-permute-start(s16[128,1920]{1,0:T(8,128)(2,1)S(1)} %get-tuple-element.56), channel_id=1, source_target_pairs={{0,12},{4,0},{8,4},{12,8},{16,28},{20,16},{24,20},{28,24},{32,44},... | collective-permute-start | bytes 1474568 | tf_op jit(solution)/shard_map/ppermute | solution.py:31
  121.6 23.0 %collective-permute-start.28 = (s16[256,1920]{1,0:T(8,128)(2,1)S(1)}, s16[256,1920]{1,0:T(8,128)(2,1)S(1)}, u32[]{:S(2)}, u32[]{:S(2)}) collective-permute-start(s16[256,1920]{1,0:T(8,128)(2,1)S(1)} %get-tuple-element.84), channel_id=1, source_target_pairs={{0,12},{4,0},{8,4},{12,8},{16,28},{20,16},{24,20},{28,24},{32,44},... | collective-permute-start | bytes 2949128 | tf_op jit(solution)/shard_map/ppermute | solution.py:31
  139.2 21.0 %collective-permute-start.7 = (s16[256,1920]{1,0:T(8,128)(2,1)S(1)}, s16[256,1920]{1,0:T(8,128)(2,1)S(1)}, u32[]{:S(2)}, u32[]{:S(2)}) collective-permute-start(s16[256,1920]{1,0:T(8,128)(2,1)S(1)} %get-tuple-element.57), channel_id=1, source_target_pairs={{0,16},{4,20},{8,24},{12,28},{16,32},{20,36},{24,40},{28,44},{32,4... | collective-permute-start | bytes 2949128 | tf_op jit(solution)/shard_map/ppermute | solution.py:31
  139.3 20.9 %collective-permute-start.8 = (s16[256,1920]{1,0:T(8,128)(2,1)S(1)}, s16[256,1920]{1,0:T(8,128)(2,1)S(1)}, u32[]{:S(2)}, u32[]{:S(2)}) collective-permute-start(s16[256,1920]{1,0:T(8,128)(2,1)S(1)} %get-tuple-element.58), channel_id=1, source_target_pairs={{0,48},{4,52},{8,56},{12,60},{16,0},{20,4},{24,8},{28,12},{32,16},... | collective-permute-start | bytes 2949128 | tf_op jit(solution)/shard_map/ppermute | solution.py:31
  142.0 20.4 %collective-permute-start.9 = (s16[256,1920]{1,0:T(8,128)(2,1)S(1)}, s16[256,1920]{1,0:T(8,128)(2,1)S(1)}, u32[]{:S(2)}, u32[]{:S(2)}) collective-permute-start(s16[256,1920]{1,0:T(8,128)(2,1)S(1)} %get-tuple-element.59), channel_id=1, source_target_pairs={{0,4},{4,8},{8,12},{12,0},{16,20},{20,24},{24,28},{28,16},{32,36},... | collective-permute-start | bytes 2949128 | tf_op jit(solution)/shard_map/ppermute | solution.py:31
  143.4 19.6 %collective-permute-start.10 = (s16[256,1920]{1,0:T(8,128)(2,1)S(1)}, s16[256,1920]{1,0:T(8,128)(2,1)S(1)}, u32[]{:S(2)}, u32[]{:S(2)}) collective-permute-start(s16[256,1920]{1,0:T(8,128)(2,1)S(1)} %get-tuple-element.60), channel_id=1, source_target_pairs={{0,12},{4,0},{8,4},{12,8},{16,28},{20,16},{24,20},{28,24},{32,44},... | collective-permute-start | bytes 2949128 | tf_op jit(solution)/shard_map/ppermute | solution.py:31
  157.6 19.6 %collective-permute-start.29 = (s16[32,1920]{1,0:T(8,128)(2,1)S(1)}, s16[32,1920]{1,0:T(8,128)(2,1)S(1)}, u32[]{:S(2)}, u32[]{:S(2)}) collective-permute-start(s16[32,1920]{1,0:T(8,128)(2,1)S(1)} %get-tuple-element.86), channel_id=1, source_target_pairs={{0,4},{4,8},{8,12},{12,0},{16,20},{20,24},{24,28},{28,16},{32,36},... | collective-permute-start | bytes 368648 | tf_op jit(solution)/shard_map/ppermute | solution.py:31
  160.2 18.5 %collective-permute-start.30 = (s16[32,1920]{1,0:T(8,128)(2,1)S(1)}, s16[32,1920]{1,0:T(8,128)(2,1)S(1)}, u32[]{:S(2)}, u32[]{:S(2)}) collective-permute-start(s16[32,1920]{1,0:T(8,128)(2,1)S(1)} %get-tuple-element.87), channel_id=1, source_target_pairs={{0,12},{4,0},{8,4},{12,8},{16,28},{20,16},{24,20},{28,24},{32,44},... | collective-permute-start | bytes 368648 | tf_op jit(solution)/shard_map/ppermute | solution.py:31
  160.2 18.4 %collective-permute-start.31 = (s16[32,1920]{1,0:T(8,128)(2,1)S(1)}, s16[32,1920]{1,0:T(8,128)(2,1)S(1)}, u32[]{:S(2)}, u32[]{:S(2)}) collective-permute-start(s16[32,1920]{1,0:T(8,128)(2,1)S(1)} %get-tuple-element.89), channel_id=1, source_target_pairs={{0,16},{4,20},{8,24},{12,28},{16,32},{20,36},{24,40},{28,44},{32,4... | collective-permute-start | bytes 368648 | tf_op jit(solution)/shard_map/ppermute | solution.py:31
  162.3 16.3 %collective-permute-start.32 = (s16[32,1920]{1,0:T(8,128)(2,1)S(1)}, s16[32,1920]{1,0:T(8,128)(2,1)S(1)}, u32[]{:S(2)}, u32[]{:S(2)}) collective-permute-start(s16[32,1920]{1,0:T(8,128)(2,1)S(1)} %get-tuple-element.90), channel_id=1, source_target_pairs={{0,48},{4,52},{8,56},{12,60},{16,0},{20,4},{24,8},{28,12},{32,16},... | collective-permute-start | bytes 368648 | tf_op jit(solution)/shard_map/ppermute | solution.py:31
  176.0 13.3 %collective-permute-start.11 = (s16[32,1920]{1,0:T(8,128)(2,1)S(1)}, s16[32,1920]{1,0:T(8,128)(2,1)S(1)}, u32[]{:S(2)}, u32[]{:S(2)}) collective-permute-start(s16[32,1920]{1,0:T(8,128)(2,1)S(1)} %get-tuple-element.62), channel_id=1, source_target_pairs={{0,4},{4,8},{8,12},{12,0},{16,20},{20,24},{24,28},{28,16},{32,36},... | collective-permute-start | bytes 368648 | tf_op jit(solution)/shard_map/ppermute | solution.py:31
  177.2 12.1 %collective-permute-start.12 = (s16[32,1920]{1,0:T(8,128)(2,1)S(1)}, s16[32,1920]{1,0:T(8,128)(2,1)S(1)}, u32[]{:S(2)}, u32[]{:S(2)}) collective-permute-start(s16[32,1920]{1,0:T(8,128)(2,1)S(1)} %get-tuple-element.63), channel_id=1, source_target_pairs={{0,12},{4,0},{8,4},{12,8},{16,28},{20,16},{24,20},{28,24},{32,44},... | collective-permute-start | bytes 368648 | tf_op jit(solution)/shard_map/ppermute | solution.py:31
  185.9 17.6 %collective-permute-start.33 = (s16[64,1920]{1,0:T(8,128)(2,1)S(1)}, s16[64,1920]{1,0:T(8,128)(2,1)S(1)}, u32[]{:S(2)}, u32[]{:S(2)}) collective-permute-start(s16[64,1920]{1,0:T(8,128)(2,1)S(1)} %get-tuple-element.91), channel_id=1, source_target_pairs={{0,4},{4,8},{8,12},{12,0},{16,20},{20,24},{24,28},{28,16},{32,36},... | collective-permute-start | bytes 737288 | tf_op jit(solution)/shard_map/ppermute | solution.py:31
  186.0 20.2 %collective-permute-start.34 = (s16[64,1920]{1,0:T(8,128)(2,1)S(1)}, s16[64,1920]{1,0:T(8,128)(2,1)S(1)}, u32[]{:S(2)}, u32[]{:S(2)}) collective-permute-start(s16[64,1920]{1,0:T(8,128)(2,1)S(1)} %get-tuple-element.92), channel_id=1, source_target_pairs={{0,12},{4,0},{8,4},{12,8},{16,28},{20,16},{24,20},{28,24},{32,44},... | collective-permute-start | bytes 737288 | tf_op jit(solution)/shard_map/ppermute | solution.py:31
  188.6 19.0 %collective-permute-start.35 = (s16[64,1920]{1,0:T(8,128)(2,1)S(1)}, s16[64,1920]{1,0:T(8,128)(2,1)S(1)}, u32[]{:S(2)}, u32[]{:S(2)}) collective-permute-start(s16[64,1920]{1,0:T(8,128)(2,1)S(1)} %get-tuple-element.93), channel_id=1, source_target_pairs={{0,16},{4,20},{8,24},{12,28},{16,32},{20,36},{24,40},{28,44},{32,4... | collective-permute-start | bytes 737288 | tf_op jit(solution)/shard_map/ppermute | solution.py:31
  196.2 12.7 %collective-permute-start.36 = (s16[64,1920]{1,0:T(8,128)(2,1)S(1)}, s16[64,1920]{1,0:T(8,128)(2,1)S(1)}, u32[]{:S(2)}, u32[]{:S(2)}) collective-permute-start(s16[64,1920]{1,0:T(8,128)(2,1)S(1)} %get-tuple-element.94), channel_id=1, source_target_pairs={{0,48},{4,52},{8,56},{12,60},{16,0},{20,4},{24,8},{28,12},{32,16},... | collective-permute-start | bytes 737288 | tf_op jit(solution)/shard_map/ppermute | solution.py:31
  203.4 11.2 %collective-permute-start.15 = (s16[64,1920]{1,0:T(8,128)(2,1)S(1)}, s16[64,1920]{1,0:T(8,128)(2,1)S(1)}, u32[]{:S(2)}, u32[]{:S(2)}) collective-permute-start(s16[64,1920]{1,0:T(8,128)(2,1)S(1)} %get-tuple-element.67), channel_id=1, source_target_pairs={{0,4},{4,8},{8,12},{12,0},{16,20},{20,24},{24,28},{28,16},{32,36},... | collective-permute-start | bytes 737288 | tf_op jit(solution)/shard_map/ppermute | solution.py:31
  203.5 11.7 %collective-permute-start.16 = (s16[64,1920]{1,0:T(8,128)(2,1)S(1)}, s16[64,1920]{1,0:T(8,128)(2,1)S(1)}, u32[]{:S(2)}, u32[]{:S(2)}) collective-permute-start(s16[64,1920]{1,0:T(8,128)(2,1)S(1)} %get-tuple-element.68), channel_id=1, source_target_pairs={{0,12},{4,0},{8,4},{12,8},{16,28},{20,16},{24,20},{28,24},{32,44},... | collective-permute-start | bytes 737288 | tf_op jit(solution)/shard_map/ppermute | solution.py:31
  206.2 9.1 %collective-permute-start.17 = (s16[64,1920]{1,0:T(8,128)(2,1)S(1)}, s16[64,1920]{1,0:T(8,128)(2,1)S(1)}, u32[]{:S(2)}, u32[]{:S(2)}) collective-permute-start(s16[64,1920]{1,0:T(8,128)(2,1)S(1)} %get-tuple-element.69), channel_id=1, source_target_pairs={{0,16},{4,20},{8,24},{12,28},{16,32},{20,36},{24,40},{28,44},{32,4... | collective-permute-start | bytes 737288 | tf_op jit(solution)/shard_map/ppermute | solution.py:31
  213.7 8.0 %collective-permute-start.37 = (s16[32,1920]{1,0:T(8,128)(2,1)S(1)}, s16[32,1920]{1,0:T(8,128)(2,1)S(1)}, u32[]{:S(2)}, u32[]{:S(2)}) collective-permute-start(s16[32,1920]{1,0:T(8,128)(2,1)S(1)} %get-tuple-element.96), channel_id=1, source_target_pairs={{0,64},{4,68},{8,72},{12,76},{16,80},{20,84},{24,88},{28,92},{32,9... | collective-permute-start | bytes 368648 | tf_op jit(solution)/shard_map/ppermute | solution.py:31
  (13 other events, 160.7 us)

commit v2 on v0

v2 whole, which is shorter than its diff:
```python
import functools

import jax
import jax.numpy as jnp
from jax import lax
from jax.experimental import pallas as pl
from jax.experimental.pallas import tpu as pltpu
from jax.sharding import PartitionSpec as P

LEVELS = 32600.0
STEPS = 32.0
ROUNDER = 12582912.0
CODE_ROWS = 16
VMEM_LIMIT = 48 * 1024 * 1024


def shift(dz, dx, dy):
    pairs = []
    for index in range(32):
        z, x, y = index // 16, (index // 4) % 4, index % 4
        pairs.append((index, ((z + dz) % 2) * 16 + ((x + dx) % 4) * 4 + (y + dy) % 4))
    return pairs


FORWARD = (shift(0, 1, 0), shift(0, 0, 1))
BACKWARD = (shift(0, -1, 0), shift(0, 0, -1))
ACROSS = shift(1, 0, 0)


def send(value, pairs):
    return lax.ppermute(value, "row", pairs)


def send_col(value, step):
    return lax.ppermute(value, "col", [(c, c ^ step) for c in range(4)])


def encode(value, out_ref):
    rows, width = value.shape
    largest = jnp.max(jnp.max(jnp.abs(value.reshape(rows // 8, 8, width)), axis=0), axis=0, keepdims=True)
    code = jnp.ceil(jnp.log2(jnp.maximum(largest, 1e-30)) * STEPS)
    factor = jnp.exp2(code * (-1.0 / STEPS)) * LEVELS
    rounded = (value * factor + ROUNDER) - ROUNDER
    out_ref[:rows, :] = rounded.astype(jnp.int32).astype(jnp.int16)
    out_ref[rows:, :] = jnp.broadcast_to(code, (CODE_ROWS, width)).astype(jnp.int32).astype(jnp.int16)


def decode(in_ref):
    rows = in_ref.shape[0] - CODE_ROWS
    code = in_ref[rows:, :].astype(jnp.int32).astype(jnp.float32)[:1]
    factor = jnp.exp2(code * (1.0 / STEPS)) * (1.0 / LEVELS)
    return in_ref[:rows, :].astype(jnp.int32).astype(jnp.float32) * factor


def copy_rows(a_ref, left_ref, at, kind, first, z):
    first_stride, second_stride = (128, 32) if kind == 0 else (32, 128)
    for second in range(4):
        start = pl.multiple_of(z * 512 + second * second_stride + first * first_stride, 32)
        left_ref[at + second * 32:at + second * 32 + 32, :] = a_ref[pl.ds(start, 32), :]


def product(left_ref, b_ref, m_ref):
    parts = [b_ref[k * 128:(k + 1) * 128, :] * m_ref[k:k + 1, :] for k in range(b_ref.shape[0] // 128)]
    return jnp.dot(left_ref[...], jnp.concatenate(parts, axis=0), preferred_element_type=jnp.float32)


def arrange_kernel(order, values, flags, out, kept):
    tiles = flags.shape[1]
    for t in range(tiles):
        at = slice(t * 128, (t + 1) * 128)
        kept[:, at] = values[:, at] * flags[:, t:t + 1].astype(jnp.float32).astype(jnp.bfloat16)
    for k in range(tiles):
        out[:, k * 128:(k + 1) * 128] = kept[:, pl.ds(pl.multiple_of(order[k] * 128, 128), 128)]


def opposite_kernel(kind, pos, a, b, m, p, q, left):
    @pl.when(pl.program_id(0) == 0)
    def _():
        first = (pos[1 + kind] + 2) % 4
        copy_rows(a, left, 0, kind, first, 0)
        copy_rows(a, left, 128, kind, first, 1)

    sums = product(left, b, m)
    encode(sums[:128], p)
    encode(sums[128:], q)


def rest_kernel(kind, pos, a, b, m, ip, iq, later, own, left):
    @pl.when(pl.program_id(0) == 0)
    def _():
        here = pos[1 + kind]
        ahead, behind = (here + 1) % 4, (here + 3) % 4
        for at, (first, z) in enumerate(((ahead, 0), (behind, 1), (ahead, 1), (behind, 0), (here, 0), (here, 1))):
            copy_rows(a, left, at * 128, kind, first, z)

    sums = product(left, b, m)
    later[...] = sums[:256]
    encode(sums[256:384], ip)
    encode(sums[384:512], iq)
    own[...] = sums[512:]


def pass_on_kernel(later, p, q, dp, dq):
    encode(later[:128, :] + decode(p), dp)
    encode(later[128:, :] + decode(q), dq)


def gather_kernel(kind, pos, own, dp, ip, dq, iq, p, q, kept):
    kept[:128, :] = own[:128, :] + decode(dp) + decode(iq)
    kept[128:, :] = own[128:, :] + decode(ip) + decode(dq)
    second = (pos[2 - kind] + 2) % 4
    for z, out in ((0, p), (1, q)):
        encode(kept[pl.ds(pl.multiple_of(z * 128 + second * 32, 32), 32), :], out)


def second_pass_kernel(kind, pos, kept, p, q, np, nq):
    for way, got, out in ((0, p, np), (1, q, nq)):
        second = (pos[2 - kind] + (1 if way == 0 else 3)) % 4
        parts = [kept[pl.ds(pl.multiple_of(z * 128 + second * 32, 32), 32), :] for z in range(2)]
        parts[way] = parts[way] + decode(got)
        encode(jnp.concatenate(parts, axis=0), out)


def second_gather_kernel(kind, pos, kept, p, q, out, rest, scratch):
    second = pos[2 - kind]
    parts = [kept[pl.ds(pl.multiple_of(z * 128 + second * 32, 32), 32), :] for z in range(2)]
    scratch[...] = jnp.concatenate(parts, axis=0) + decode(p) + decode(q)
    z = pos[0]
    encode(scratch[pl.ds(pl.multiple_of((1 - z) * 32, 32), 32), :], out)
    rest[...] = scratch[pl.ds(pl.multiple_of(z * 32, 32), 32), :]


def last_kernel(rest0, got0, rest1, got1, out0, out1):
    out0[...] = (rest0[...] + decode(got0)).astype(jnp.bfloat16)
    out1[...] = (rest1[...] + decode(got1)).astype(jnp.bfloat16)


SMEM = pl.BlockSpec(memory_space=pltpu.SMEM)


def call(kernel, args, ins, outs, tile, width, scratch=()):
    def spec(s):
        if isinstance(s, pl.BlockSpec):
            return s
        rows, start = s if isinstance(s, tuple) else (s, 0)
        return pl.BlockSpec((rows, tile), lambda j: (0, j + start))

    name = kernel.func.__name__ if isinstance(kernel, functools.partial) else kernel.__name__
    return pl.pallas_call(
        kernel,
        grid=(width // tile,),
        in_specs=[spec(s) for s in ins],
        out_specs=[spec(s.shape[0]) for s in outs],
        out_shape=outs,
        scratch_shapes=list(scratch),
        compiler_params=pltpu.CompilerParams(vmem_limit_bytes=VMEM_LIMIT),
        cost_estimate=pl.CostEstimate(flops=1000000, bytes_accessed=1000000, transcendentals=0),
        name=name,
    )(*args)


def per_device(amplitudes, amplitude_mask, integrals, integral_mask, tile_order):
    pair_count, full_width = amplitudes.shape
    depth, columns = integrals.shape
    width = columns // 2
    row, col = lax.axis_index("row"), lax.axis_index("col")
    pos = jnp.stack([row // 16, (row // 4) % 4, row % 4]).astype(jnp.int32)

    ordered = pl.pallas_call(
        arrange_kernel,
        in_specs=[SMEM, pl.BlockSpec(memory_space=pltpu.VMEM), pl.BlockSpec(memory_space=pltpu.VMEM)],
        out_specs=pl.BlockSpec(memory_space=pltpu.VMEM),
        out_shape=jax.ShapeDtypeStruct((pair_count, full_width), jnp.bfloat16),
        scratch_shapes=[pltpu.VMEM((pair_count, full_width), jnp.bfloat16)],
        name="arrange",
    )(tile_order, amplitudes, amplitude_mask)
    placed = lax.all_to_all(ordered, "row", split_axis=1, concat_axis=0, tiled=True)
    over = send_col(placed, 2)
    beside = send_col(placed, 1)
    both = send_col(over, 1)
    core, z_hi = col % 2, col // 2
    even, odd = jnp.where(core == 0, placed, beside), jnp.where(core == 0, beside, placed)
    far_even, far_odd = jnp.where(core == 0, over, both), jnp.where(core == 0, both, over)
    four = [
        jnp.where(z_hi == 0, even, far_even),
        jnp.where(z_hi == 0, odd, far_odd),
        jnp.where(z_hi == 0, far_even, even),
        jnp.where(z_hi == 0, far_odd, odd),
    ]
    left = jnp.stack([v.reshape(32, 8, depth) for v in four], axis=1).reshape(1024, depth)
    flags = jnp.repeat(integral_mask.astype(jnp.bfloat16), 128, axis=1)

    def sent(rows):
        return jax.ShapeDtypeStruct((rows + CODE_ROWS, width), jnp.int16)

    def floats(rows):
        return jax.ShapeDtypeStruct((rows, width), jnp.float32)

    coded = [128 + CODE_ROWS, 32 + CODE_ROWS, 64 + CODE_ROWS]
    whole_left = pl.BlockSpec((1024, depth), lambda j: (0, 0))
    flag_rows = integral_mask.shape[0]

    def left_scratch(rows):
        return [pltpu.VMEM((rows, depth), jnp.bfloat16)]

    def exchange(kind, p, q):
        return send(p, FORWARD[kind]), send(q, BACKWARD[kind])

    def operands(kind, tile):
        start = kind * (width // tile)
        return [pos, left, integrals, flags], [SMEM, whole_left, (depth, start), (flag_rows, start)]

    got, state = [None, None], [None, None]
    for kind in range(2):
        args, ins = operands(kind, 1792)
        p, q = call(
            functools.partial(opposite_kernel, kind), args, ins, [sent(128)] * 2, 1792, width, left_scratch(256)
        )
        got[kind] = exchange(kind, p, q)
    for kind in range(2):
        args, ins = operands(kind, 896)
        ip, iq, later, own = call(
            functools.partial(rest_kernel, kind), args, ins, [sent(128)] * 2 + [floats(256)] * 2, 896, width,
            left_scratch(768),
        )
        state[kind] = (exchange(kind, ip, iq), later, own)
    kept = [None, None]
    for kind in range(2):
        free, later, own = state[kind]
        dp, dq = call(pass_on_kernel, [later, *got[kind]], [256, coded[0], coded[0]], [sent(128)] * 2, 896, width)
        state[kind] = (free, exchange(kind, dp, dq), own)
    for kind in range(2):
        free, bound, own = state[kind]
        p, q, kept[kind] = call(
            functools.partial(gather_kernel, kind), [pos, own, bound[0], free[0], bound[1], free[1]],
            [SMEM, 256] + [coded[0]] * 4, [sent(32)] * 2 + [floats(256)], 896, width,
        )
        got[kind] = exchange(1 - kind, p, q)
    for kind in range(2):
        p, q = call(
            functools.partial(second_pass_kernel, kind), [pos, kept[kind], *got[kind]],
            [SMEM, 256, coded[1], coded[1]], [sent(64)] * 2, 1792, width,
        )
        got[kind] = exchange(1 - kind, p, q)
    rest = [None, None]
    for kind in range(2):
        p, rest[kind] = call(
            functools.partial(second_gather_kernel, kind), [pos, kept[kind], *got[kind]],
            [SMEM, 256, coded[2], coded[2]], [sent(32), floats(32)], 1792, width,
            [pltpu.VMEM((64, 1792), jnp.float32)],
        )
        got[kind] = send(p, ACROSS)
    halves = call(
        last_kernel, [rest[0], got[0], rest[1], got[1]], [32, coded[1], 32, coded[1]],
        [jax.ShapeDtypeStruct((32, width), jnp.bfloat16)] * 2, 1792, width,
    )
    summed = jnp.concatenate(halves, axis=1).reshape(4, 8, columns)
    pieces = [lax.dynamic_index_in_dim(summed, col, 0, keepdims=False)]
    for step in (1, 2, 3):
        pieces.append(send_col(lax.dynamic_index_in_dim(summed, col ^ step, 0, keepdims=False), step))
    pair = [jnp.where(core == 0, pieces[k], pieces[k ^ 1]) for k in range(4)]
    blocks = [jnp.where(z_hi == 0, pair[k], pair[k ^ 2]) for k in range(4)]
    return jnp.concatenate(blocks, axis=1)


def solution(mesh):
    in_specs = (
        P(("row", "col"), None),
        P(("row", "col"), None),
        P("row", "col"),
        P("row", "col"),
        P(),
    )
    out_specs = P(("row", "col"), None)
    return jax.shard_map(
        per_device, mesh=mesh, in_specs=in_specs, out_specs=out_specs, check_vma=False
    )
```

time: 453 us -> 193 us (0.43)
  waiting for transfers between devices: 374 us -> 63.8 us
  Pallas kernels: 0 us -> 60.3 us
  starting transfers between devices: 6.95 us -> 45.5 us
  matrix products: 27.9 us -> 0 us
  between operations: 13.4 us -> 0.18 us
  local copies, waits for them, and re-layouts: 11 us -> 2.22 us
  blocking collectives: 13.4 us -> 18.6 us
  other arithmetic: 6.21 us -> 1.46 us
    reduce_scatter x1 -> x0, waiting for transfers between devices: 320 us -> none  [per_device(): lax.psum_scatter(partial_value, 'row', scatter_dimension=0, tiled=True)]
    ppermute x0 -> x28, waiting for transfers between devices: none -> 63.8 us  [the longest x22 50.9 us: send(): return lax.ppermute(value, 'row', pairs)]
    pallas_call x0 -> x14, Pallas kernels: none -> 60.3 us  [the longest x13 57.7 us: call(): pl.pallas_call(kernel, grid=(width // tile,), in_specs=[spec(s) for s in...]
    ppermute x0 -> x28, starting transfers between devices: none -> 45.5 us  [the longest x22 25.5 us: send(): return lax.ppermute(value, 'row', pairs)]
    all_gather x1 -> x0, waiting for transfers between devices: 29.1 us -> none  [per_device(): grouped = lax.all_gather(ordered, 'col', axis=0, tiled=True)]
    dot_general x1 -> x0, matrix products: 27.9 us -> none  [per_device(): partial_value = jnp.dot(placed, weights, preferred_element_type=jnp.float32)]
    all_to_all x1 -> x0, waiting for transfers between devices: 24.2 us -> none  [per_device(): lax.all_to_all(grouped, 'row', split_axis=1, concat_axis=0, tiled=True)]
    all_to_all x1 -> x0, starting transfers between devices: 6.9 us -> none  [per_device(): lax.all_to_all(grouped, 'row', split_axis=1, concat_axis=0, tiled=True)]
  transfers between devices with their start and end apart: 3 -> 28, of which waited for: 3 -> 14; matrix products, arithmetic and copies ran while one was open for 0% -> 0% of each run, Pallas kernels for 0% -> 27%
where the time goes in v2:
time: 193 us; the launch traced here: 192 us
  waiting for transfers between devices  63.8 us (33%)
  Pallas kernels  60.3 us (31%)
  starting transfers between devices  45.5 us (24%)
  blocking collectives  18.6 us (10%)
  local copies, waits for them, and re-layouts  2.22 us (1%)
    pallas_call x13, Pallas kernels, call(): pl.pallas_call(kernel, grid=(width // tile,), in_specs=[spec(s) for s in...  57.7 us
    ppermute x22, waiting for transfers between devices, send(): return lax.ppermute(value, 'row', pairs)  50.9 us
    ppermute x22, starting transfers between devices, send(): return lax.ppermute(value, 'row', pairs)  25.5 us
    ppermute x6, starting transfers between devices, send_col(): return lax.ppermute(value, 'col', [(c, c ^ step) for c in range(4)])  20 us
    all_to_all x1, blocking collectives, per_device(): lax.all_to_all(ordered, 'row', split_axis=1, concat_axis=0, tiled=True)  18.6 us
    ppermute x6, waiting for transfers between devices, send_col(): return lax.ppermute(value, 'col', [(c, c ^ step) for c in range(4)])  12.9 us
  transfers between devices with their start and end apart: 28, of which 14 were waited for; matrix products, arithmetic and copies ran while one was open for 0% of the time, Pallas kernels for 27%

profile of v2, /device:TPU:1, one launch (start us, length us, event | category | flops | bytes accessed | tf_op | source)
XLA Modules:
  0.0 192.0 jit_solution(6138526832319816181)
XLA Ops:
  0.0 2.5 %arrange.1 = bf16[8,28672]{1,0:T(8,128)(2,1)} custom-call(s32[224]{0:T(256)} %order.1, bf16[8,28672]{1,0:T(8,128)(2,1)} %values.1, s32[8,224]{1,0:T(8,128)} %flags.1), custom_call_target="tpu_custom_call" | custom-call | tf_op jit(solution)/shard_map/arrange/pallas_call | solution.py:169
  2.5 18.6 %all_to_all.19 = bf16[8,32,896]{2,0,1:T(8,128)(2,1)S(1)} all-to-all(bf16[8,32,896]{2,0,1:T(8,128)(2,1)} %bitcast.52), channel_id=1, replica_groups=mesh['row'=32,'col'=4] {'row'}, dimensions={1} | all-to-all | bytes 917504 | tf_op jit(solution)/shard_map/all_to_all | solution.py:177
  21.1 3.3 %collective-permute-start.1 = (bf16[256,896]{1,0:T(8,128)(2,1)S(1)}, bf16[256,896]{1,0:T(8,128)(2,1)S(1)}, u32[]{:S(2)}, u32[]{:S(2)}) collective-permute-start(bf16[256,896]{1,0:T(8,128)(2,1)S(1)} %bitcast.53), channel_id=1, source_target_pairs={{0,2},{1,3},{2,0},{3,1},{4,6},{5,7},{6,4},{7,5},{8,10},{9,11},{10,... | collective-permute-start | bytes 1376264 | tf_op jit(solution)/shard_map/ppermute | solution.py:35
  24.4 2.9 %collective-permute-start = (bf16[256,896]{1,0:T(8,128)(2,1)S(1)}, bf16[256,896]{1,0:T(8,128)(2,1)S(1)}, u32[]{:S(2)}, u32[]{:S(2)}) collective-permute-start(bf16[256,896]{1,0:T(8,128)(2,1)S(1)} %bitcast.54), channel_id=1, source_target_pairs={{0,1},{1,0},{2,3},{3,2},{4,5},{5,4},{6,7},{7,6},{8,9},{9,8},{10,11... | collective-permute-start | bytes 1376264 | tf_op jit(solution)/shard_map/ppermute | solution.py:35
  27.3 5.4 %collective-permute-done.1 = bf16[256,896]{1,0:T(8,128)(2,1)S(1)} collective-permute-done((bf16[256,896]{1,0:T(8,128)(2,1)S(1)}, bf16[256,896]{1,0:T(8,128)(2,1)S(1)}, u32[]{:S(2)}, u32[]{:S(2)}) %collective-permute-start.1) | collective-permute-done | bytes 458784 | tf_op jit(solution)/shard_map/ppermute | solution.py:35
  32.6 3.2 %collective-permute-start.2 = (bf16[256,896]{1,0:T(8,128)(2,1)S(1)}, bf16[256,896]{1,0:T(8,128)(2,1)S(1)}, u32[]{:S(2)}, u32[]{:S(2)}) collective-permute-start(bf16[256,896]{1,0:T(8,128)(2,1)S(1)} %collective-permute-done.1), channel_id=1, source_target_pairs={{0,1},{1,0},{2,3},{3,2},{4,5},{5,4},{6,7},{7,6},{8,9},{9,8},{10,11... | collective-permute-start | bytes 1376264 | tf_op jit(solution)/shard_map/ppermute | solution.py:35
  37.9 5.1 %opposite_kernel.3 = (s16[144,3584]{1,0:T(8,128)(2,1)S(1)}, s16[144,3584]{1,0:T(8,128)(2,1)S(1)}) custom-call(s32[3]{0:T(128)S(1)} %pad_add_fusion.pos, bf16[1024,896]{1,0:T(8,128)(2,1)S(1)} %bitcast.44, bf16[896,7168]{1,0:T(8,128)(2,1)} %b.7, bf16[7,7168]{1,0:T(8,128)(2,1)S(1)} %bitcast.48), custom_call_target="tpu_custom_call" | custom-call | flops 1000000 | bytes 1000000 | tf_op jit(solution)/shard_map/opposite_kernel/pallas_call | solution.py:149
  45.7 5.8 %opposite_kernel.2 = (s16[144,3584]{1,0:T(8,128)(2,1)S(1)}, s16[144,3584]{1,0:T(8,128)(2,1)}) custom-call(s32[3]{0:T(128)S(1)} %pad_add_fusion.pos, bf16[1024,896]{1,0:T(8,128)(2,1)S(1)} %bitcast.45, bf16[896,7168]{1,0:T(8,128)(2,1)} %b.7, bf16[7,7168]{1,0:T(8,128)(2,1)S(1)} %bitcast.49), custom_call_target="tpu_custom_call" | custom-call | flops 1000000 | bytes 1000000 | tf_op jit(solution)/shard_map/opposite_kernel/pallas_call | solution.py:149
  52.1 2.1 %collective-permute-start.4 = (s16[144,3584]{1,0:T(8,128)(2,1)}, s16[144,3584]{1,0:T(8,128)(2,1)S(1)}, u32[]{:S(2)}, u32[]{:S(2)}) collective-permute-start(s16[144,3584]{1,0:T(8,128)(2,1)} %get-tuple-element.40), channel_id=1, source_target_pairs={{0,48},{4,52},{8,56},{12,60},{16,0},{20,4},{24,8},{28,12},{32,16},... | collective-permute-start | bytes 3096584 | tf_op jit(solution)/shard_map/ppermute | solution.py:31
  54.3 10.6 %rest_kernel.3 = (s16[144,3584]{1,0:T(8,128)(2,1)S(1)}, s16[144,3584]{1,0:T(8,128)(2,1)S(1)}, f32[256,3584]{1,0:T(8,128)}, f32[256,3584]{1,0:T(8,128)}) custom-call(s32[3]{0:T(128)S(1)} %pad_add_fusion.pos, bf16[1024,896]{1,0:T(8,128)(2,1)S(1)} %bitcast.46, bf16[896,7168]{1,0:T(8,128)(2,1)} %b.7, bf16[7,7168]{1,0:T(8,128)(2,1)S(1)} %bitcast.50), custom_call_target="tpu_custom_call" | custom-call | flops 1000000 | bytes 1000000 | tf_op jit(solution)/shard_map/rest_kernel/pallas_call | solution.py:149
  65.1 3.2 %collective-permute-done.14.p = s16[144,3584]{1,0:T(8,128)(2,1)S(1)} collective-permute-done((s16[144,3584]{1,0:T(8,128)(2,1)S(1)}, s16[144,3584]{1,0:T(8,128)(2,1)S(1)}, u32[]{:S(2)}, u32[]{:S(2)}) %collective-permute-start.14) | collective-permute-done | bytes 1032224 | tf_op jit(solution)/shard_map/ppermute | solution.py:31
  68.3 4.4 %pass_on_kernel.3 = (s16[144,3584]{1,0:T(8,128)(2,1)}, s16[144,3584]{1,0:T(8,128)(2,1)S(1)}) custom-call(f32[256,3584]{1,0:T(8,128)} %get-tuple-element.53.later, s16[144,3584]{1,0:T(8,128)(2,1)S(1)} %collective-permute-done.14.p, s16[144,3584]{1,0:T(8,128)(2,1)S(1)} %collective-permute-done.15.q), custom_call_target="tpu_custom_call" | custom-call | flops 1000000 | bytes 1000000 | tf_op jit(solution)/shard_map/pass_on_kernel/pallas_call | solution.py:149
  74.2 10.6 %rest_kernel.2 = (s16[144,3584]{1,0:T(8,128)(2,1)S(1)}, s16[144,3584]{1,0:T(8,128)(2,1)S(1)}, f32[256,3584]{1,0:T(8,128)}, f32[256,3584]{1,0:T(8,128)}) custom-call(s32[3]{0:T(128)S(1)} %pad_add_fusion.pos, bf16[1024,896]{1,0:T(8,128)(2,1)S(1)} %bitcast.47, bf16[896,7168]{1,0:T(8,128)(2,1)} %b.7, bf16[7,7168]{1,0:T(8,128)(2,1)S(1)} %bitcast.51), custom_call_target="tpu_custom_call" | custom-call | flops 1000000 | bytes 1000000 | tf_op jit(solution)/shard_map/rest_kernel/pallas_call | solution.py:149
  86.6 3.7 %pass_on_kernel.2 = (s16[144,3584]{1,0:T(8,128)(2,1)S(1)}, s16[144,3584]{1,0:T(8,128)(2,1)S(1)}) custom-call(f32[256,3584]{1,0:T(8,128)} %get-tuple-element.38.later, s16[144,3584]{1,0:T(8,128)(2,1)S(1)} %collective-permute-done.3.p, s16[144,3584]{1,0:T(8,128)(2,1)S(1)} %collective-permute-done.4.q), custom_call_target="tpu_custom_call" | custom-call | flops 1000000 | bytes 1000000 | tf_op jit(solution)/shard_map/pass_on_kernel/pallas_call | solution.py:149
  92.4 2.1 %collective-permute-start.8 = (s16[144,3584]{1,0:T(8,128)(2,1)S(1)}, s16[144,3584]{1,0:T(8,128)(2,1)S(1)}, u32[]{:S(2)}, u32[]{:S(2)}) collective-permute-start(s16[144,3584]{1,0:T(8,128)(2,1)S(1)} %get-tuple-element.44), channel_id=1, source_target_pairs={{0,48},{4,52},{8,56},{12,60},{16,0},{20,4},{24,8},{28,12},{32,16},... | collective-permute-start | bytes 3096584 | tf_op jit(solution)/shard_map/ppermute | solution.py:31
  94.5 17.2 %collective-permute-done.16.dp = s16[144,3584]{1,0:T(8,128)(2,1)S(1)} collective-permute-done((s16[144,3584]{1,0:T(8,128)(2,1)}, s16[144,3584]{1,0:T(8,128)(2,1)S(1)}, u32[]{:S(2)}, u32[]{:S(2)}) %collective-permute-start.16) | collective-permute-done | bytes 1032224 | tf_op jit(solution)/shard_map/ppermute | solution.py:31
  111.6 3.0 %collective-permute-start.7 = (s16[144,3584]{1,0:T(8,128)(2,1)}, s16[144,3584]{1,0:T(8,128)(2,1)S(1)}, u32[]{:S(2)}, u32[]{:S(2)}) collective-permute-start(s16[144,3584]{1,0:T(8,128)(2,1)} %copy-done.2), channel_id=1, source_target_pairs={{0,48},{4,52},{8,56},{12,60},{16,0},{20,4},{24,8},{28,12},{32,16},... | collective-permute-start | bytes 3096584 | tf_op jit(solution)/shard_map/ppermute | solution.py:31
  114.6 5.4 %gather_kernel.3 = (s16[48,3584]{1,0:T(8,128)(2,1)S(1)}, s16[48,3584]{1,0:T(8,128)(2,1)S(1)}, f32[256,3584]{1,0:T(8,128)}) custom-call(s32[3]{0:T(128)S(1)} %pad_add_fusion.pos, f32[256,3584]{1,0:T(8,128)} %get-tuple-element.52.own, s16[144,3584]{1,0:T(8,128)(2,1)S(1)} %collective-permute-done.16.dp, s16[144,3584]{1,0:T(8,128)(2,1)S(1)} %collective-permute-done.17.ip, ...), custom_call_target="tpu_custom_call" | custom-call | flops 1000000 | bytes 1000000 | tf_op jit(solution)/shard_map/gather_kernel/pallas_call | solution.py:149
  120.1 2.7 %collective-permute-start.21 = (s16[48,3584]{1,0:T(8,128)(2,1)S(1)}, s16[48,3584]{1,0:T(8,128)(2,1)S(1)}, u32[]{:S(2)}, u32[]{:S(2)}) collective-permute-start(s16[48,3584]{1,0:T(8,128)(2,1)S(1)} %get-tuple-element.62), channel_id=1, source_target_pairs={{0,48},{4,52},{8,56},{12,60},{16,0},{20,4},{24,8},{28,12},{32,16},... | collective-permute-start | bytes 1032200 | tf_op jit(solution)/shard_map/ppermute | solution.py:31
  122.7 7.7 %collective-permute-done.5.dp = s16[144,3584]{1,0:T(8,128)(2,1)S(1)} collective-permute-done((s16[144,3584]{1,0:T(8,128)(2,1)}, s16[144,3584]{1,0:T(8,128)(2,1)S(1)}, u32[]{:S(2)}, u32[]{:S(2)}) %collective-permute-start.5) | collective-permute-done | bytes 1032224 | tf_op jit(solution)/shard_map/ppermute | solution.py:31
  130.5 7.2 %collective-permute-done.7.dq = s16[144,3584]{1,0:T(8,128)(2,1)S(1)} collective-permute-done((s16[144,3584]{1,0:T(8,128)(2,1)}, s16[144,3584]{1,0:T(8,128)(2,1)S(1)}, u32[]{:S(2)}, u32[]{:S(2)}) %collective-permute-start.7) | collective-permute-done | bytes 1032224 | tf_op jit(solution)/shard_map/ppermute | solution.py:31
  137.6 5.6 %gather_kernel.2 = (s16[48,3584]{1,0:T(8,128)(2,1)S(1)}, s16[48,3584]{1,0:T(8,128)(2,1)S(1)}, f32[256,3584]{1,0:T(8,128)}) custom-call(s32[3]{0:T(128)S(1)} %pad_add_fusion.pos, f32[256,3584]{1,0:T(8,128)} %get-tuple-element.37.own, s16[144,3584]{1,0:T(8,128)(2,1)S(1)} %collective-permute-done.5.dp, s16[144,3584]{1,0:T(8,128)(2,1)S(1)} %collective-permute-done.6.ip, ...), custom_call_target="tpu_custom_call" | custom-call | flops 1000000 | bytes 1000000 | tf_op jit(solution)/shard_map/gather_kernel/pallas_call | solution.py:149
  147.2 2.8 %collective-permute-start.23 = (s16[80,3584]{1,0:T(8,128)(2,1)S(1)}, s16[80,3584]{1,0:T(8,128)(2,1)S(1)}, u32[]{:S(2)}, u32[]{:S(2)}) collective-permute-start(s16[80,3584]{1,0:T(8,128)(2,1)S(1)} %get-tuple-element.64), channel_id=1, source_target_pairs={{0,48},{4,52},{8,56},{12,60},{16,0},{20,4},{24,8},{28,12},{32,16},... | collective-permute-start | bytes 1720328 | tf_op jit(solution)/shard_map/ppermute | solution.py:31
  150.5 1.5 second_pass_kernel.2
  152.4 2.4 %collective-permute-start.12 = (s16[80,3584]{1,0:T(8,128)(2,1)S(1)}, s16[80,3584]{1,0:T(8,128)(2,1)S(1)}, u32[]{:S(2)}, u32[]{:S(2)}) collective-permute-start(s16[80,3584]{1,0:T(8,128)(2,1)S(1)} %get-tuple-element.49), channel_id=1, source_target_pairs={{0,12},{4,0},{8,4},{12,8},{16,28},{20,16},{24,20},{28,24},{32,44},... | collective-permute-start | bytes 1720328 | tf_op jit(solution)/shard_map/ppermute | solution.py:31
  154.8 3.7 %collective-permute-done.22.p = s16[80,3584]{1,0:T(8,128)(2,1)S(1)} collective-permute-done((s16[80,3584]{1,0:T(8,128)(2,1)S(1)}, s16[80,3584]{1,0:T(8,128)(2,1)S(1)}, u32[]{:S(2)}, u32[]{:S(2)}) %collective-permute-start.22) | collective-permute-done | bytes 573472 | tf_op jit(solution)/shard_map/ppermute | solution.py:31
  160.1 3.4 %collective-permute-done.11.p = s16[80,3584]{1,0:T(8,128)(2,1)S(1)} collective-permute-done((s16[80,3584]{1,0:T(8,128)(2,1)S(1)}, s16[80,3584]{1,0:T(8,128)(2,1)S(1)}, u32[]{:S(2)}, u32[]{:S(2)}) %collective-permute-start.11) | collective-permute-done | bytes 573472 | tf_op jit(solution)/shard_map/ppermute | solution.py:31
  166.5 7.2 %collective-permute-done.13.got0 = s16[48,3584]{1,0:T(8,128)(2,1)S(1)} collective-permute-done((s16[48,3584]{1,0:T(8,128)(2,1)S(1)}, s16[48,3584]{1,0:T(8,128)(2,1)S(1)}, u32[]{:S(2)}, u32[]{:S(2)}) %collective-permute-start.13) | collective-permute-done | bytes 344096 | tf_op jit(solution)/shard_map/ppermute | solution.py:31
  174.2 7.3 %collective-permute-start.25 = (bf16[8,7168]{1,0:T(8,128)(2,1)S(1)}, bf16[8,7168]{1,0:T(8,128)(2,1)S(1)}, u32[]{:S(2)}, u32[]{:S(2)}) collective-permute-start(bf16[8,7168]{1,0:T(8,128)(2,1)S(1)} %get-tuple-element.77), channel_id=1, source_target_pairs={{0,1},{1,0},{2,3},{3,2},{4,5},{5,4},{6,7},{7,6},{8,9},{9,8},{10,11... | collective-permute-start | bytes 344072 | tf_op jit(solution)/shard_map/ppermute | solution.py:35
  181.5 3.0 %collective-permute-start.26 = (bf16[8,7168]{1,0:T(8,128)(2,1)S(1)}, bf16[8,7168]{1,0:T(8,128)(2,1)S(1)}, u32[]{:S(2)}, u32[]{:S(2)}) collective-permute-start(bf16[8,7168]{1,0:T(8,128)(2,1)S(1)} %get-tuple-element.79), channel_id=1, source_target_pairs={{0,2},{1,3},{2,0},{3,1},{4,6},{5,7},{6,4},{7,5},{8,10},{9,11},{10,... | collective-permute-start | bytes 344072 | tf_op jit(solution)/shard_map/ppermute | solution.py:35
  184.7 3.0 %collective-permute-done.26 = bf16[8,7168]{1,0:T(8,128)(2,1)S(1)} collective-permute-done((bf16[8,7168]{1,0:T(8,128)(2,1)S(1)}, bf16[8,7168]{1,0:T(8,128)(2,1)S(1)}, u32[]{:S(2)}, u32[]{:S(2)}) %collective-permute-start.26) | collective-permute-done | bytes 114720 | tf_op jit(solution)/shard_map/ppermute | solution.py:35
  187.7 3.4 %collective-permute-done.27 = bf16[8,7168]{1,0:T(8,128)(2,1)S(1)} collective-permute-done((bf16[8,7168]{1,0:T(8,128)(2,1)S(1)}, bf16[8,7168]{1,0:T(8,128)(2,1)S(1)}, u32[]{:S(2)}, u32[]{:S(2)}) %collective-permute-start.27) | collective-permute-done | bytes 114720 | tf_op jit(solution)/shard_map/ppermute | solution.py:35
  (59 shorter events, 21.6 us)
Async XLA Ops:
  0.0 35.9 %copy-start.4 = (s32[7,56]{1,0:T(8,128)S(1)}, s32[7,56]{1,0:T(8,128)}, u32[]{:S(2)}) copy-start(s32[7,56]{1,0:T(8,128)} %param.8) | copy-start | bytes 4708
  21.1 11.5 %collective-permute-start.1 = (bf16[256,896]{1,0:T(8,128)(2,1)S(1)}, bf16[256,896]{1,0:T(8,128)(2,1)S(1)}, u32[]{:S(2)}, u32[]{:S(2)}) collective-permute-start(bf16[256,896]{1,0:T(8,128)(2,1)S(1)} %bitcast.53), channel_id=1, source_target_pairs={{0,2},{1,3},{2,0},{3,1},{4,6},{5,7},{6,4},{7,5},{8,10},{9,11},{10,... | collective-permute-start | bytes 1376264 | tf_op jit(solution)/shard_map/ppermute | solution.py:35
  24.4 11.7 %collective-permute-start = (bf16[256,896]{1,0:T(8,128)(2,1)S(1)}, bf16[256,896]{1,0:T(8,128)(2,1)S(1)}, u32[]{:S(2)}, u32[]{:S(2)}) collective-permute-start(bf16[256,896]{1,0:T(8,128)(2,1)S(1)} %bitcast.54), channel_id=1, source_target_pairs={{0,1},{1,0},{2,3},{3,2},{4,5},{5,4},{6,7},{7,6},{8,9},{9,8},{10,11... | collective-permute-start | bytes 1376264 | tf_op jit(solution)/shard_map/ppermute | solution.py:35
  32.6 4.7 %collective-permute-start.2 = (bf16[256,896]{1,0:T(8,128)(2,1)S(1)}, bf16[256,896]{1,0:T(8,128)(2,1)S(1)}, u32[]{:S(2)}, u32[]{:S(2)}) collective-permute-start(bf16[256,896]{1,0:T(8,128)(2,1)S(1)} %collective-permute-done.1), channel_id=1, source_target_pairs={{0,1},{1,0},{2,3},{3,2},{4,5},{5,4},{6,7},{7,6},{8,9},{9,8},{10,11... | collective-permute-start | bytes 1376264 | tf_op jit(solution)/shard_map/ppermute | solution.py:35
  43.0 25.3 %collective-permute-start.14 = (s16[144,3584]{1,0:T(8,128)(2,1)S(1)}, s16[144,3584]{1,0:T(8,128)(2,1)S(1)}, u32[]{:S(2)}, u32[]{:S(2)}) collective-permute-start(s16[144,3584]{1,0:T(8,128)(2,1)S(1)} %get-tuple-element.54), channel_id=1, source_target_pairs={{0,4},{4,8},{8,12},{12,0},{16,20},{20,24},{24,28},{28,16},{32,36},... | collective-permute-start | bytes 3096584 | tf_op jit(solution)/shard_map/ppermute | solution.py:31
  44.5 23.8 %collective-permute-start.15 = (s16[144,3584]{1,0:T(8,128)(2,1)S(1)}, s16[144,3584]{1,0:T(8,128)(2,1)S(1)}, u32[]{:S(2)}, u32[]{:S(2)}) collective-permute-start(s16[144,3584]{1,0:T(8,128)(2,1)S(1)} %get-tuple-element.55), channel_id=1, source_target_pairs={{0,12},{4,0},{8,4},{12,8},{16,28},{20,16},{24,20},{28,24},{32,44},... | collective-permute-start | bytes 3096584 | tf_op jit(solution)/shard_map/ppermute | solution.py:31
  51.6 33.2 %collective-permute-start.3 = (s16[144,3584]{1,0:T(8,128)(2,1)S(1)}, s16[144,3584]{1,0:T(8,128)(2,1)S(1)}, u32[]{:S(2)}, u32[]{:S(2)}) collective-permute-start(s16[144,3584]{1,0:T(8,128)(2,1)S(1)} %get-tuple-element.39), channel_id=1, source_target_pairs={{0,16},{4,20},{8,24},{12,28},{16,32},{20,36},{24,40},{28,44},{32,4... | collective-permute-start | bytes 3096584 | tf_op jit(solution)/shard_map/ppermute | solution.py:31
  52.1 33.2 %collective-permute-start.4 = (s16[144,3584]{1,0:T(8,128)(2,1)}, s16[144,3584]{1,0:T(8,128)(2,1)S(1)}, u32[]{:S(2)}, u32[]{:S(2)}) collective-permute-start(s16[144,3584]{1,0:T(8,128)(2,1)} %get-tuple-element.40), channel_id=1, source_target_pairs={{0,48},{4,52},{8,56},{12,60},{16,0},{20,4},{24,8},{28,12},{32,16},... | collective-permute-start | bytes 3096584 | tf_op jit(solution)/shard_map/ppermute | solution.py:31
  64.9 27.5 %collective-permute-start.17 = (s16[144,3584]{1,0:T(8,128)(2,1)S(1)}, s16[144,3584]{1,0:T(8,128)(2,1)S(1)}, u32[]{:S(2)}, u32[]{:S(2)}) collective-permute-start(s16[144,3584]{1,0:T(8,128)(2,1)S(1)} %get-tuple-element.57), channel_id=1, source_target_pairs={{0,4},{4,8},{8,12},{12,0},{16,20},{20,24},{24,28},{28,16},{32,36},... | collective-permute-start | bytes 3096584 | tf_op jit(solution)/shard_map/ppermute | solution.py:31
  68.3 26.2 %collective-permute-start.19 = (s16[144,3584]{1,0:T(8,128)(2,1)S(1)}, s16[144,3584]{1,0:T(8,128)(2,1)S(1)}, u32[]{:S(2)}, u32[]{:S(2)}) collective-permute-start(s16[144,3584]{1,0:T(8,128)(2,1)S(1)} %get-tuple-element.59), channel_id=1, source_target_pairs={{0,12},{4,0},{8,4},{12,8},{16,28},{20,16},{24,20},{28,24},{32,44},... | collective-permute-start | bytes 3096584 | tf_op jit(solution)/shard_map/ppermute | solution.py:31
  72.8 38.9 %collective-permute-start.16 = (s16[144,3584]{1,0:T(8,128)(2,1)}, s16[144,3584]{1,0:T(8,128)(2,1)S(1)}, u32[]{:S(2)}, u32[]{:S(2)}) collective-permute-start(s16[144,3584]{1,0:T(8,128)(2,1)} %get-tuple-element.56), channel_id=1, source_target_pairs={{0,4},{4,8},{8,12},{12,0},{16,20},{20,24},{24,28},{28,16},{32,36},... | collective-permute-start | bytes 3096584 | tf_op jit(solution)/shard_map/ppermute | solution.py:31
  84.8 35.2 %collective-permute-start.6 = (s16[144,3584]{1,0:T(8,128)(2,1)S(1)}, s16[144,3584]{1,0:T(8,128)(2,1)S(1)}, u32[]{:S(2)}, u32[]{:S(2)}) collective-permute-start(s16[144,3584]{1,0:T(8,128)(2,1)S(1)} %get-tuple-element.42), channel_id=1, source_target_pairs={{0,16},{4,20},{8,24},{12,28},{16,32},{20,36},{24,40},{28,44},{32,4... | collective-permute-start | bytes 3096584 | tf_op jit(solution)/shard_map/ppermute | solution.py:31
  85.4 29.2 %collective-permute-start.18 = (s16[144,3584]{1,0:T(8,128)(2,1)S(1)}, s16[144,3584]{1,0:T(8,128)(2,1)S(1)}, u32[]{:S(2)}, u32[]{:S(2)}) collective-permute-start(s16[144,3584]{1,0:T(8,128)(2,1)S(1)} %get-tuple-element.58), channel_id=1, source_target_pairs={{0,12},{4,0},{8,4},{12,8},{16,28},{20,16},{24,20},{28,24},{32,44},... | collective-permute-start | bytes 3096584 | tf_op jit(solution)/shard_map/ppermute | solution.py:31
  91.3 1.0 copy-start.3
  92.4 30.4 %collective-permute-start.8 = (s16[144,3584]{1,0:T(8,128)(2,1)S(1)}, s16[144,3584]{1,0:T(8,128)(2,1)S(1)}, u32[]{:S(2)}, u32[]{:S(2)}) collective-permute-start(s16[144,3584]{1,0:T(8,128)(2,1)S(1)} %get-tuple-element.44), channel_id=1, source_target_pairs={{0,48},{4,52},{8,56},{12,60},{16,0},{20,4},{24,8},{28,12},{32,16},... | collective-permute-start | bytes 3096584 | tf_op jit(solution)/shard_map/ppermute | solution.py:31
  94.5 36.0 %collective-permute-start.5 = (s16[144,3584]{1,0:T(8,128)(2,1)}, s16[144,3584]{1,0:T(8,128)(2,1)S(1)}, u32[]{:S(2)}, u32[]{:S(2)}) collective-permute-start(s16[144,3584]{1,0:T(8,128)(2,1)} %copy-done.3), channel_id=1, source_target_pairs={{0,16},{4,20},{8,24},{12,28},{16,32},{20,36},{24,40},{28,44},{32,4... | collective-permute-start | bytes 3096584 | tf_op jit(solution)/shard_map/ppermute | solution.py:31
  111.6 26.0 %collective-permute-start.7 = (s16[144,3584]{1,0:T(8,128)(2,1)}, s16[144,3584]{1,0:T(8,128)(2,1)S(1)}, u32[]{:S(2)}, u32[]{:S(2)}) collective-permute-start(s16[144,3584]{1,0:T(8,128)(2,1)} %copy-done.2), channel_id=1, source_target_pairs={{0,48},{4,52},{8,56},{12,60},{16,0},{20,4},{24,8},{28,12},{32,16},... | collective-permute-start | bytes 3096584 | tf_op jit(solution)/shard_map/ppermute | solution.py:31
  120.1 24.6 %collective-permute-start.20 = (s16[48,3584]{1,0:T(8,128)(2,1)S(1)}, s16[48,3584]{1,0:T(8,128)(2,1)S(1)}, u32[]{:S(2)}, u32[]{:S(2)}) collective-permute-start(s16[48,3584]{1,0:T(8,128)(2,1)S(1)} %get-tuple-element.61), channel_id=1, source_target_pairs={{0,16},{4,20},{8,24},{12,28},{16,32},{20,36},{24,40},{28,44},{32,4... | collective-permute-start | bytes 1032200 | tf_op jit(solution)/shard_map/ppermute | solution.py:31
  120.1 24.8 %collective-permute-start.21 = (s16[48,3584]{1,0:T(8,128)(2,1)S(1)}, s16[48,3584]{1,0:T(8,128)(2,1)S(1)}, u32[]{:S(2)}, u32[]{:S(2)}) collective-permute-start(s16[48,3584]{1,0:T(8,128)(2,1)S(1)} %get-tuple-element.62), channel_id=1, source_target_pairs={{0,48},{4,52},{8,56},{12,60},{16,0},{20,4},{24,8},{28,12},{32,16},... | collective-permute-start | bytes 1032200 | tf_op jit(solution)/shard_map/ppermute | solution.py:31
  137.6 7.3 %copy-start = (f32[256,3584]{1,0:T(8,128)S(1)}, f32[256,3584]{1,0:T(8,128)}, u32[]{:S(2)}) copy-start(f32[256,3584]{1,0:T(8,128)} %get-tuple-element.60.kept) | copy-start | bytes 11010052
  143.2 6.8 %collective-permute-start.10 = (s16[48,3584]{1,0:T(8,128)(2,1)S(1)}, s16[48,3584]{1,0:T(8,128)(2,1)S(1)}, u32[]{:S(2)}, u32[]{:S(2)}) collective-permute-start(s16[48,3584]{1,0:T(8,128)(2,1)S(1)} %get-tuple-element.47), channel_id=1, source_target_pairs={{0,12},{4,0},{8,4},{12,8},{16,28},{20,16},{24,20},{28,24},{32,44},... | collective-permute-start | bytes 1032200 | tf_op jit(solution)/shard_map/ppermute | solution.py:31
  143.2 7.3 %collective-permute-start.9 = (s16[48,3584]{1,0:T(8,128)(2,1)S(1)}, s16[48,3584]{1,0:T(8,128)(2,1)S(1)}, u32[]{:S(2)}, u32[]{:S(2)}) collective-permute-start(s16[48,3584]{1,0:T(8,128)(2,1)S(1)} %get-tuple-element.46), channel_id=1, source_target_pairs={{0,4},{4,8},{8,12},{12,0},{16,20},{20,24},{24,28},{28,16},{32,36},... | collective-permute-start | bytes 1032200 | tf_op jit(solution)/shard_map/ppermute | solution.py:31
  144.9 5.6 %copy-start.1 = (f32[256,3584]{1,0:T(8,128)S(1)}, f32[256,3584]{1,0:T(8,128)}, u32[]{:S(2)}) copy-start(f32[256,3584]{1,0:T(8,128)} %get-tuple-element.45.kept) | copy-start | bytes 11010052
  146.4 12.1 %collective-permute-start.22 = (s16[80,3584]{1,0:T(8,128)(2,1)S(1)}, s16[80,3584]{1,0:T(8,128)(2,1)S(1)}, u32[]{:S(2)}, u32[]{:S(2)}) collective-permute-start(s16[80,3584]{1,0:T(8,128)(2,1)S(1)} %get-tuple-element.63), channel_id=1, source_target_pairs={{0,16},{4,20},{8,24},{12,28},{16,32},{20,36},{24,40},{28,44},{32,4... | collective-permute-start | bytes 1720328 | tf_op jit(solution)/shard_map/ppermute | solution.py:31
  147.2 11.4 %collective-permute-start.23 = (s16[80,3584]{1,0:T(8,128)(2,1)S(1)}, s16[80,3584]{1,0:T(8,128)(2,1)S(1)}, u32[]{:S(2)}, u32[]{:S(2)}) collective-permute-start(s16[80,3584]{1,0:T(8,128)(2,1)S(1)} %get-tuple-element.64), channel_id=1, source_target_pairs={{0,48},{4,52},{8,56},{12,60},{16,0},{20,4},{24,8},{28,12},{32,16},... | collective-permute-start | bytes 1720328 | tf_op jit(solution)/shard_map/ppermute | solution.py:31
  152.1 11.5 %collective-permute-start.11 = (s16[80,3584]{1,0:T(8,128)(2,1)S(1)}, s16[80,3584]{1,0:T(8,128)(2,1)S(1)}, u32[]{:S(2)}, u32[]{:S(2)}) collective-permute-start(s16[80,3584]{1,0:T(8,128)(2,1)S(1)} %get-tuple-element.48), channel_id=1, source_target_pairs={{0,4},{4,8},{8,12},{12,0},{16,20},{20,24},{24,28},{28,16},{32,36},... | collective-permute-start | bytes 1720328 | tf_op jit(solution)/shard_map/ppermute | solution.py:31
  152.4 11.1 %collective-permute-start.12 = (s16[80,3584]{1,0:T(8,128)(2,1)S(1)}, s16[80,3584]{1,0:T(8,128)(2,1)S(1)}, u32[]{:S(2)}, u32[]{:S(2)}) collective-permute-start(s16[80,3584]{1,0:T(8,128)(2,1)S(1)} %get-tuple-element.49), channel_id=1, source_target_pairs={{0,12},{4,0},{8,4},{12,8},{16,28},{20,16},{24,20},{28,24},{32,44},... | collective-permute-start | bytes 1720328 | tf_op jit(solution)/shard_map/ppermute | solution.py:31
  160.0 6.5 %collective-permute-start.24 = (s16[48,3584]{1,0:T(8,128)(2,1)S(1)}, s16[48,3584]{1,0:T(8,128)(2,1)S(1)}, u32[]{:S(2)}, u32[]{:S(2)}) collective-permute-start(s16[48,3584]{1,0:T(8,128)(2,1)S(1)} %get-tuple-element.66), channel_id=1, source_target_pairs={{0,64},{4,68},{8,72},{12,76},{16,80},{20,84},{24,88},{28,92},{32,9... | collective-permute-start | bytes 1032200 | tf_op jit(solution)/shard_map/ppermute | solution.py:31
  165.0 8.7 %collective-permute-start.13 = (s16[48,3584]{1,0:T(8,128)(2,1)S(1)}, s16[48,3584]{1,0:T(8,128)(2,1)S(1)}, u32[]{:S(2)}, u32[]{:S(2)}) collective-permute-start(s16[48,3584]{1,0:T(8,128)(2,1)S(1)} %get-tuple-element.51), channel_id=1, source_target_pairs={{0,64},{4,68},{8,72},{12,76},{16,80},{20,84},{24,88},{28,92},{32,9... | collective-permute-start | bytes 1032200 | tf_op jit(solution)/shard_map/ppermute | solution.py:31
  174.2 10.6 %collective-permute-start.25 = (bf16[8,7168]{1,0:T(8,128)(2,1)S(1)}, bf16[8,7168]{1,0:T(8,128)(2,1)S(1)}, u32[]{:S(2)}, u32[]{:S(2)}) collective-permute-start(bf16[8,7168]{1,0:T(8,128)(2,1)S(1)} %get-tuple-element.77), channel_id=1, source_target_pairs={{0,1},{1,0},{2,3},{3,2},{4,5},{5,4},{6,7},{7,6},{8,9},{9,8},{10,11... | collective-permute-start | bytes 344072 | tf_op jit(solution)/shard_map/ppermute | solution.py:35
  181.5 6.2 %collective-permute-start.26 = (bf16[8,7168]{1,0:T(8,128)(2,1)S(1)}, bf16[8,7168]{1,0:T(8,128)(2,1)S(1)}, u32[]{:S(2)}, u32[]{:S(2)}) collective-permute-start(bf16[8,7168]{1,0:T(8,128)(2,1)S(1)} %get-tuple-element.79), channel_id=1, source_target_pairs={{0,2},{1,3},{2,0},{3,1},{4,6},{5,7},{6,4},{7,5},{8,10},{9,11},{10,... | collective-permute-start | bytes 344072 | tf_op jit(solution)/shard_map/ppermute | solution.py:35
  184.5 6.6 %collective-permute-start.27 = (bf16[8,7168]{1,0:T(8,128)(2,1)S(1)}, bf16[8,7168]{1,0:T(8,128)(2,1)S(1)}, u32[]{:S(2)}, u32[]{:S(2)}) collective-permute-start(bf16[8,7168]{1,0:T(8,128)(2,1)S(1)} %get-tuple-element.78), channel_id=1, source_target_pairs={{0,3},{1,2},{2,1},{3,0},{4,7},{5,6},{6,5},{7,4},{8,11},{9,10},{10,... | collective-permute-start | bytes 344072 | tf_op jit(solution)/shard_map/ppermute | solution.py:35
  (1 other events, 1.0 us)

commit v3 on v0

v3 whole, which is shorter than its diff:
```python
import functools

import jax
import jax.numpy as jnp
from jax import lax
from jax.experimental import pallas as pl
from jax.experimental.pallas import tpu as pltpu
from jax.sharding import PartitionSpec as P

LEVELS = 32600.0
STEPS = 32.0
ROUNDER = 12582912.0
CODES = (32, 128)
VMEM_LIMIT = 24 * 1024 * 1024
TILE = 896


def shift(dz, dx, dy):
    pairs = []
    for index in range(32):
        z, x, y = index // 16, (index // 4) % 4, index % 4
        pairs.append((index, ((z + dz) % 2) * 16 + ((x + dx) % 4) * 4 + (y + dy) % 4))
    return pairs


FORWARD = (shift(0, 1, 0), shift(0, 0, 1))
BACKWARD = (shift(0, -1, 0), shift(0, 0, -1))
ACROSS = shift(1, 0, 0)
DIAGONAL = [(r * 4 + c, s * 4 + (c ^ 2)) for r, s in ACROSS for c in range(4)]


def send(value, pairs):
    return lax.ppermute(value, "row", pairs)


def send_col(value, step):
    return lax.ppermute(value, "col", [(c, c ^ step) for c in range(4)])


def quantised(value):
    rows, tile = value.shape
    largest = jnp.max(jnp.max(jnp.abs(value.reshape(rows // 8, 8, tile)), axis=0), axis=0, keepdims=True)
    code = jnp.ceil(jnp.log2(jnp.maximum(largest, 1e-30)) * STEPS)
    factor = jnp.exp2(code * (-1.0 / STEPS)) * LEVELS
    rounded = (value * factor + ROUNDER) - ROUNDER
    return rounded.astype(jnp.int32).astype(jnp.int16), code


def finish(out_ref, code_ref):
    rows, width = out_ref.shape[0], out_ref.shape[1] - 128
    out_ref[:32, width:] = code_ref[...].astype(jnp.int32).astype(jnp.int16)
    if rows > 32:
        out_ref[32:, width:] = jnp.zeros((rows - 32, 128), jnp.int16)


def encode(value, out_ref, code_ref):
    step, tile = pl.program_id(0), value.shape[1]
    out_ref[:, pl.ds(pl.multiple_of(step * tile, 128), tile)], code = quantised(value)

    @pl.when(step == 0)
    def _():
        code_ref[...] = jnp.zeros(CODES, jnp.float32)

    for i in range(tile // 128):
        code_ref[pl.ds(step * (tile // 128) + i, 1), :] = code[:, i * 128:(i + 1) * 128]

    @pl.when(step == pl.num_programs(0) - 1)
    def _():
        finish(out_ref, code_ref)


def encode_at(value, t, out_ref, code_ref):
    count = TILE // 128
    out_ref[:, columns_of(t)], code = quantised(value)
    for i in range(count):
        code_ref[pl.ds(t * count + i, 1), :] = code[:, i * 128:(i + 1) * 128]


def columns_of(t):
    return pl.ds(pl.multiple_of(t * TILE, 128), TILE)


def each_tile(width):
    return pl.loop(0, width // TILE)


def factors(code_ref, factor_ref, tile):
    step, count = pl.program_id(0), tile // 128

    @pl.when(step == 0)
    def _():
        factor_ref[...] = jnp.exp2(code_ref[...].astype(jnp.int32).astype(jnp.float32) * (1.0 / STEPS)) * (1.0 / LEVELS)

    return jnp.concatenate([factor_ref[pl.ds(step * count + i, 1), :] for i in range(count)], axis=1)


def wide(data_ref):
    return data_ref[...].astype(jnp.int32).astype(jnp.float32)


def decode(data_ref, code_ref, factor_ref):
    return wide(data_ref) * factors(code_ref, factor_ref, data_ref.shape[1])


def copy_rows(parts, left_ref, at, kind, first, z):
    first_stride, second_stride = (4, 1) if kind == 0 else (1, 4)
    for second in range(4):
        start = pl.multiple_of((z * 16 + second * second_stride + first * first_stride) * 16, 16)
        for part in parts:
            left_ref[at:at + 16, :] = part[pl.ds(start, 16), :]
            at += 16


def arrange_kernel(order, values, flags, out, kept):
    tiles = flags.shape[1]
    for t in range(tiles):
        at = slice(t * 128, (t + 1) * 128)
        kept[:, at] = values[:, at] * flags[:, t:t + 1].astype(jnp.float32).astype(jnp.bfloat16)
    for k in range(tiles):
        out[:, k * 128:(k + 1) * 128] = kept[:, pl.ds(pl.multiple_of(order[k] * 128, 128), 128)]


def clear(*code_refs):
    for code_ref in code_refs:
        code_ref[...] = jnp.zeros(CODES, jnp.float32)


def dot(left, right):
    return jnp.dot(left, right, preferred_element_type=jnp.float32)


def opposite_rows(pos, a, left):
    for kind in range(2):
        first = (pos[1 + kind] + 2) % 4
        copy_rows((a,), left.at[kind], 0, kind, first, 0)
        copy_rows((a,), left.at[kind], 64, kind, first, 1)


def begin_kernel(pos, a, b0, b1, m0, m1, p0, q0, p1, q1, w0, w1, left, *code_refs):
    @pl.when(pl.program_id(0) == 0)
    def _():
        opposite_rows(pos, a, left)

    for kind, b, m, p, q, w in ((0, b0, m0, p0, q0, w0), (1, b1, m1, p1, q1, w1)):
        for k in range(b.shape[0] // 128):
            w[k * 128:(k + 1) * 128, :] = b[k * 128:(k + 1) * 128, :] * m[k:k + 1, :]
        sums = dot(left[kind], w[...])
        encode(sums[:64], p, code_refs[2 * kind])
        encode(sums[64:], q, code_refs[2 * kind + 1])


def opposite_kernel(pos, w0, w1, a, p0, q0, p1, q1, left, *code_refs):
    clear(*code_refs)
    opposite_rows(pos, a, left)
    for kind, w, p, q in ((0, w0, p0, q0), (1, w1, p1, q1)):
        @each_tile(w.shape[1])
        def _(t):
            sums = dot(left[kind], w[:, columns_of(t)])
            encode_at(sums[:64], t, p, code_refs[2 * kind])
            encode_at(sums[64:], t, q, code_refs[2 * kind + 1])

        finish(p, code_refs[2 * kind])
        finish(q, code_refs[2 * kind + 1])


def free_kernel(pos, w0, w1, near, far, p0, q0, p1, q1, left, *code_refs):
    clear(*code_refs)
    for kind, w, p, q in ((0, w0, p0, q0), (1, w1, p1, q1)):
        copy_rows((near, far), left, 0, kind, (pos[1 + kind] + 1) % 4, 1)
        copy_rows((near, far), left, 128, kind, (pos[1 + kind] + 3) % 4, 0)

        @each_tile(w.shape[1])
        def _(t):
            sums = dot(left[...], w[:, columns_of(t)])
            encode_at(sums[:128], t, p, code_refs[2 * kind])
            encode_at(sums[128:], t, q, code_refs[2 * kind + 1])

        finish(p, code_refs[2 * kind])
        finish(q, code_refs[2 * kind + 1])


def own_kernel(pos, w0, w1, near, far, own0, own1, left):
    for kind, w, own in ((0, w0, own0), (1, w1, own1)):
        for z in range(2):
            copy_rows((near, far), left, z * 128, kind, pos[1 + kind], z)

        @each_tile(w.shape[1])
        def _(t):
            own[:, columns_of(t)] = dot(left[...], w[:, columns_of(t)])


def read_factors(ref, factor_ref):
    codes = ref[:32, ref.shape[1] - 128:].astype(jnp.int32).astype(jnp.float32)
    factor_ref[...] = jnp.exp2(codes * (1.0 / STEPS)) * (1.0 / LEVELS)


def decode_at(ref, factor_ref, t):
    count = TILE // 128
    scale = jnp.concatenate([factor_ref[pl.ds(t * count + i, 1), :] for i in range(count)], axis=1)
    return ref[:, columns_of(t)].astype(jnp.int32).astype(jnp.float32) * scale


def pass_on_kernel(pos, w0, w1, near, far, *refs):
    outs, left, factor_refs, code_refs = refs[8:12], refs[12], refs[13:21], refs[21:]
    clear(*code_refs)
    for kind, w in ((0, w0), (1, w1)):
        got, scale = refs[4 * kind:4 * kind + 4], factor_refs[4 * kind:4 * kind + 4]
        copy_rows((near, far), left, 0, kind, (pos[1 + kind] + 1) % 4, 0)
        copy_rows((near, far), left, 128, kind, (pos[1 + kind] + 3) % 4, 1)
        for ref, factor in zip(got, scale):
            read_factors(ref, factor)

        @each_tile(w.shape[1])
        def _(t):
            sums = dot(left[...], w[:, columns_of(t)])
            for way in range(2):
                n, f = (decode_at(got[2 * part + way], scale[2 * part + way], t) for part in range(2))
                mixed = []
                for second in range(4):
                    mixed += [n[second * 16:second * 16 + 16], f[second * 16:second * 16 + 16]]
                value = sums[way * 128:way * 128 + 128] + jnp.concatenate(mixed, axis=0)
                encode_at(value, t, outs[2 * kind + way], code_refs[2 * kind + way])

        for way in range(2):
            finish(outs[2 * kind + way], code_refs[2 * kind + way])


def stage_one(refs, code_refs, scratch):
    own0, own1, dp, iq, ip, dq = refs
    tile = own0.shape[1]
    fdp, fiq, fip, fdq = (factors(c, f, tile) for c, f in zip(code_refs, scratch))
    return [own0[...] + wide(dp) * fdp + wide(iq) * fiq, own1[...] + wide(ip) * fip + wide(dq) * fdq]


def second_opposite_kernel(pos, *refs):
    for kind in range(2):
        some, outs, scratch = refs[10 * kind:10 * kind + 10], refs[20 + 2 * kind:22 + 2 * kind], refs[24 + 6 * kind:]
        sums = stage_one(some[:6], some[6:10], scratch[:4])
        encode(sums[0], outs[0], scratch[4])
        encode(sums[1], outs[1], scratch[5])


def keep_kernel(pos, *refs):
    for kind in range(2):
        own, dp, dpc, iq, iqc, ip, ipc, dq, dqc = refs[9 * kind:9 * kind + 9]
        out, scratch = refs[18 + kind], refs[20 + 4 * kind:24 + 4 * kind]
        out[:128, :] = own[:128, :] + decode(dp, dpc, scratch[0]) + decode(iq, iqc, scratch[1])
        out[128:, :] = own[128:, :] + decode(ip, ipc, scratch[2]) + decode(dq, dqc, scratch[3])


def block(kept, z, second, t):
    return kept[pl.ds(pl.multiple_of(z * 128 + second * 32, 32), 32), columns_of(t)]


def second_neighbour_kernel(pos, *refs):
    outs, factor_refs, code_refs = refs[6:10], refs[10:14], refs[14:]
    clear(*code_refs)
    for kind in range(2):
        kept, got = refs[3 * kind], refs[3 * kind + 1:3 * kind + 3]
        for way in range(2):
            read_factors(got[way], factor_refs[2 * kind + way])

        @each_tile(kept.shape[1])
        def _(t):
            for way in range(2):
                second = (pos[2 - kind] + (1 if way == 0 else 3)) % 4
                parts = [block(kept, z, second, t) for z in range(2)]
                parts[way] = parts[way] + decode_at(got[way], factor_refs[2 * kind + way], t)
                encode_at(jnp.concatenate(parts, axis=0), t, outs[2 * kind + way], code_refs[2 * kind + way])

        for way in range(2):
            finish(outs[2 * kind + way], code_refs[2 * kind + way])


def spread_kernel(pos, *refs):
    outs, sums, factor_refs, code_refs = refs[6:10], refs[10], refs[11:15], refs[15:]
    clear(*code_refs)
    z = pos[0]
    for kind in range(2):
        for way in range(2):
            read_factors(refs[3 * kind + 1 + way], factor_refs[2 * kind + way])

    def rows(h, far):
        at = [pl.multiple_of(kind * 64 + h * 32 + far * 16, 16) for kind in range(2)]
        return jnp.concatenate([sums[pl.ds(a, 16), :] for a in at], axis=0)

    @each_tile(refs[0].shape[1])
    def _(t):
        for kind in range(2):
            kept, got = refs[3 * kind], refs[3 * kind + 1:3 * kind + 3]
            value = jnp.concatenate([block(kept, h, pos[2 - kind], t) for h in range(2)], axis=0)
            for way in range(2):
                value = value + decode_at(got[way], factor_refs[2 * kind + way], t)
            sums[kind * 64:kind * 64 + 64, :] = value
        for at, (h, far) in enumerate(((1 - z, 0), (z, 1), (1 - z, 1))):
            encode_at(rows(h, far), t, outs[at], code_refs[at])
        outs[3][:, columns_of(t)] = rows(z, 0)

    for at in range(3):
        finish(outs[at], code_refs[at])


def last_kernel(pos, rest, a, b, c, near0, near1, far0, far1, f0, f1, f2):
    for ref, factor in ((a, f0), (b, f1), (c, f2)):
        read_factors(ref, factor)

    @each_tile(rest.shape[1])
    def _(t):
        at = columns_of(t)
        near = (rest[:, at] + decode_at(a, f0, t)).astype(jnp.bfloat16)
        far = (decode_at(b, f1, t) + decode_at(c, f2, t)).astype(jnp.bfloat16)
        near0[:, at], near1[:, at] = near[:16], near[16:]
        far0[:, at], far1[:, at] = far[:16], far[16:]


COST = pl.CostEstimate(flops=1000, bytes_accessed=1000, transcendentals=0)


class Calls:
    def __init__(self, pos, width, first):
        self.pos, self.width, self.last = pos, width, first

    def in_vmem(self, kernel, values, outs, scratch=(), after=()):
        after = [self.last, *after]
        skipped = len(after)
        name = kernel.func.__name__ if isinstance(kernel, functools.partial) else kernel.__name__
        vmem = pl.BlockSpec(memory_space=pltpu.VMEM)
        results = pl.pallas_call(
            lambda *refs: kernel(refs[skipped], *refs[skipped + 1:]),
            in_specs=[pl.BlockSpec(memory_space=pl.ANY)] * skipped + [pl.BlockSpec(memory_space=pltpu.SMEM)]
            + [vmem] * len(values),
            out_specs=[vmem] * len(outs),
            out_shape=outs,
            scratch_shapes=list(scratch),
            compiler_params=pltpu.CompilerParams(vmem_limit_bytes=VMEM_LIMIT),
            cost_estimate=COST,
            name=name,
        )(*after, self.pos, *values)
        self.last = results[0]
        return results

    def columns(self, value, rows, start=0):
        return [(value, lambda tile: pl.BlockSpec((rows, tile), lambda j, pos: (0, j + start * self.width // tile)))]

    def whole(self, value):
        return [(value, lambda tile: pl.BlockSpec(value.shape, lambda j, pos: (0, 0)))]

    def codes(self, value):
        return [(value, lambda tile: pl.BlockSpec(CODES, lambda j, pos: (0, self.width // 128)))]

    def coded(self, value, rows):
        return self.columns(value, rows) + self.codes(value)

    def some_rows(self, value, which):
        return [(value, lambda tile: pl.BlockSpec((32, tile), lambda j, pos: (which(pos), j)))]

    def __call__(self, kernel, operands, outs, tile, scratch=(), after=()):
        after = [self.last, *after]
        out_specs = []
        for o in outs:
            if o.dtype == jnp.int16:
                out_specs.append(pl.BlockSpec(o.shape, lambda j, pos: (0, 0)))
            else:
                out_specs.append(pl.BlockSpec((o.shape[0], tile), lambda j, pos: (0, j)))
        skipped = len(after)
        name = kernel.func.__name__ if isinstance(kernel, functools.partial) else kernel.__name__
        results = pl.pallas_call(
            lambda pos, *refs: kernel(pos, *refs[skipped:]),
            grid_spec=pltpu.PrefetchScalarGridSpec(
                num_scalar_prefetch=1,
                grid=(self.width // tile,),
                in_specs=[pl.BlockSpec(memory_space=pl.ANY)] * skipped + [spec(tile) for _, spec in operands],
                out_specs=out_specs,
                scratch_shapes=list(scratch),
            ),
            out_shape=outs,
            compiler_params=pltpu.CompilerParams(vmem_limit_bytes=VMEM_LIMIT),
            cost_estimate=COST,
            name=name,
        )(self.pos, *after, *[value for value, _ in operands])
        self.last = results[0]
        return results


def scales(count):
    return [pltpu.VMEM(CODES, jnp.float32)] * count


def per_device(amplitudes, amplitude_mask, integrals, integral_mask, tile_order):
    pair_count, full_width = amplitudes.shape
    depth, columns = integrals.shape
    width = columns // 2
    row, col = lax.axis_index("row"), lax.axis_index("col")
    core, z_hi = col % 2, col // 2
    pos = jnp.stack([row // 16, (row // 4) % 4, row % 4]).astype(jnp.int32)
    flags = jnp.repeat(integral_mask.astype(jnp.bfloat16), 128, axis=1)

    ordered = pl.pallas_call(
        arrange_kernel,
        in_specs=[pl.BlockSpec(memory_space=pltpu.SMEM)] + [pl.BlockSpec(memory_space=pltpu.VMEM)] * 2,
        out_specs=pl.BlockSpec(memory_space=pltpu.VMEM),
        out_shape=jax.ShapeDtypeStruct((pair_count, full_width), jnp.bfloat16),
        scratch_shapes=[pltpu.VMEM((pair_count, full_width), jnp.bfloat16)],
        name="arrange",
    )(tile_order, amplitudes, amplitude_mask)
    placed = lax.all_to_all(ordered, "row", split_axis=1, concat_axis=0, tiled=True)

    def both_cores(mine, other):
        even, odd = jnp.where(core == 0, mine, other), jnp.where(core == 0, other, mine)
        return jnp.stack([even.reshape(32, 8, depth), odd.reshape(32, 8, depth)], axis=1).reshape(512, depth)

    over = send_col(placed, 2)
    near = both_cores(placed, send_col(placed, 1))

    def sent(rows):
        return jax.ShapeDtypeStruct((rows, width + 128), jnp.int16)

    def floats(rows):
        return jax.ShapeDtypeStruct((rows, width), jnp.float32)

    call = Calls(pos, width, placed)

    def kept(rows):
        return pltpu.VMEM((rows, width), jnp.float32)

    def left_rows(*rows):
        return [pltpu.VMEM((*rows, depth), jnp.bfloat16)]

    def exchange_both(outs, ahead=(), turned=0):
        if ahead:
            *outs, _ = lax.optimization_barrier((*outs, *ahead))[:5]
        return [send(outs[2 * k + w], (FORWARD, BACKWARD)[w][k ^ turned]) for k in range(2) for w in range(2)]

    flag_rows = integral_mask.shape[0]
    results = call(
        begin_kernel,
        call.whole(near) + call.columns(integrals, depth, 0) + call.columns(integrals, depth, 1)
        + call.columns(flags, flag_rows, 0) + call.columns(flags, flag_rows, 1),
        [sent(64)] * 4 + [pltpu.VMEM((depth, width), jnp.bfloat16)] * 2, TILE, left_rows(2, 128) + scales(4),
    )
    n, weights = exchange_both(results[:4]), list(results[4:])
    over, _ = lax.optimization_barrier((over, call.last))
    far = both_cores(over, send_col(over, 1))
    f = exchange_both(call.in_vmem(opposite_kernel, weights + [far], [sent(64)] * 4, left_rows(2, 128) + scales(4)), n)
    i = exchange_both(
        call.in_vmem(free_kernel, weights + [near, far], [sent(128)] * 4, left_rows(256) + scales(4), n), f
    )
    operands = [v for k in range(2) for v in (*n[2 * k:2 * k + 2], *f[2 * k:2 * k + 2])]
    d = exchange_both(
        call.in_vmem(pass_on_kernel, weights + [near, far] + operands, [sent(128)] * 4, left_rows(256) + scales(12)), i
    )
    own = call.in_vmem(own_kernel, weights + [near, far], [kept(256)] * 2, left_rows(256), i)

    def arrived(kind):
        (ip, iq), (dp, dq) = i[2 * kind:2 * kind + 2], d[2 * kind:2 * kind + 2]
        return dp, iq, ip, dq

    operands = []
    for kind in range(2):
        def opposite(pos, kind=kind):
            return (pos[2 - kind] + 2) % 4

        for z in range(2):
            operands += call.some_rows(own[kind], lambda pos, z=z, at=opposite: z * 4 + at(pos))
        for v in arrived(kind):
            operands += call.some_rows(v, opposite)
        for v in arrived(kind):
            operands += call.codes(v)
    got = exchange_both(call(second_opposite_kernel, operands, [sent(32)] * 4, 1792, scales(12)), turned=1)
    operands = []
    for kind in range(2):
        operands += call.columns(own[kind], 256) + [o for v in arrived(kind) for o in call.coded(v, 128)]
    sums = call(keep_kernel, operands, [kept(256)] * 2, 896, scales(8))
    got = exchange_both(
        call.in_vmem(second_neighbour_kernel, [sums[0], *got[:2], sums[1], *got[2:]], [sent(64)] * 4, scales(8)),
        turned=1,
    )
    a, b, c, rest = call.in_vmem(
        spread_kernel, [sums[0], *got[:2], sums[1], *got[2:]], [sent(32)] * 3 + [floats(32)],
        [pltpu.VMEM((128, TILE), jnp.float32)] + scales(7),
    )
    a, b, c = send(a, ACROSS), send_col(b, 2), lax.ppermute(c, ("row", "col"), DIAGONAL)
    outs = call.in_vmem(
        last_kernel, [rest, a, b, c], [jax.ShapeDtypeStruct((16, width), jnp.bfloat16)] * 4, scales(3)
    )
    summed = jnp.concatenate(outs, axis=1).reshape(2, 8, 2 * columns)
    mine = lax.dynamic_index_in_dim(summed, core, 0, keepdims=False)
    other = send_col(lax.dynamic_index_in_dim(summed, 1 - core, 0, keepdims=False), 1)
    even, odd = jnp.where(core == 0, mine, other), jnp.where(core == 0, other, mine)
    near_pair = [even[:, :columns], odd[:, :columns]]
    far_pair = [even[:, columns:], odd[:, columns:]]
    first = [jnp.where(z_hi == 0, u, v) for u, v in zip(near_pair, far_pair)]
    last = [jnp.where(z_hi == 0, v, u) for u, v in zip(near_pair, far_pair)]
    return jnp.concatenate(first + last, axis=1)


def solution(mesh):
    in_specs = (
        P(("row", "col"), None),
        P(("row", "col"), None),
        P("row", "col"),
        P("row", "col"),
        P(),
    )
    out_specs = P(("row", "col"), None)
    return jax.shard_map(
        per_device, mesh=mesh, in_specs=in_specs, out_specs=out_specs, check_vma=False
    )
```

time: 453 us -> 170 us (0.38)
  waiting for transfers between devices: 374 us -> 38.6 us
  Pallas kernels: 0 us -> 50.9 us
  starting transfers between devices: 6.95 us -> 52.2 us
  matrix products: 27.9 us -> 0 us
  between operations: 13.4 us -> 0.26 us
  blocking collectives: 13.4 us -> 18.6 us
    reduce_scatter x1 -> x0, waiting for transfers between devices: 320 us -> none  [per_device(): lax.psum_scatter(partial_value, 'row', scatter_dimension=0, tiled=True)]
    ppermute x0 -> x31, starting transfers between devices: none -> 52.2 us  [the longest x25 32.4 us: send(): return lax.ppermute(value, 'row', pairs)]
    pallas_call x0 -> x11, Pallas kernels: none -> 50.9 us  [the longest x7 30.2 us: in_vmem(): pl.pallas_call(lambda *refs: kernel(refs[skipped], *refs[skipped + 1:]),...]
    ppermute x0 -> x31, waiting for transfers between devices: none -> 38.6 us  [the longest x25 31 us: send(): return lax.ppermute(value, 'row', pairs)]
    all_gather x1 -> x0, waiting for transfers between devices: 29.1 us -> none  [per_device(): grouped = lax.all_gather(ordered, 'col', axis=0, tiled=True)]
    dot_general x1 -> x0, matrix products: 27.9 us -> none  [per_device(): partial_value = jnp.dot(placed, weights, preferred_element_type=jnp.float32)]
    all_to_all x1 -> x0, waiting for transfers between devices: 24.2 us -> none  [per_device(): lax.all_to_all(grouped, 'row', split_axis=1, concat_axis=0, tiled=True)]
    all_to_all x1 -> x0, starting transfers between devices: 6.9 us -> none  [per_device(): lax.all_to_all(grouped, 'row', split_axis=1, concat_axis=0, tiled=True)]
  transfers between devices with their start and end apart: 3 -> 31, of which waited for: 3 -> 13; matrix products, arithmetic and copies ran while one was open for 0% -> 1% of each run, Pallas kernels for 0% -> 24%
where the time goes in v3:
time: 170 us
  starting transfers between devices  52.2 us (31%)
  Pallas kernels  50.9 us (30%)
  waiting for transfers between devices  38.6 us (23%)
  blocking collectives  18.6 us (11%)
  local copies, waits for them, and re-layouts  7.64 us (4%)
  other arithmetic  2.05 us (1%)
    ppermute x25, starting transfers between devices, send(): return lax.ppermute(value, 'row', pairs)  32.4 us
    ppermute x25, waiting for transfers between devices, send(): return lax.ppermute(value, 'row', pairs)  31 us
    pallas_call x7, Pallas kernels, in_vmem(): pl.pallas_call(lambda *refs: kernel(refs[skipped], *refs[skipped + 1:]),...  30.2 us
    ppermute x5, starting transfers between devices, send_col(): return lax.ppermute(value, 'col', [(c, c ^ step) for c in range(4)])  19.1 us
    all_to_all x1, blocking collectives, per_device(): lax.all_to_all(ordered, 'row', split_axis=1, concat_axis=0, tiled=True)  18.6 us
    pallas_call x3, Pallas kernels, __call__(): pl.pallas_call(lambda pos, *refs: kernel(pos, *refs[skipped:]), grid_spec...  18.2 us
    unnamed x8, local copies, waits for them, and re-layouts  7.61 us
    ppermute x5, waiting for transfers between devices, send_col(): return lax.ppermute(value, 'col', [(c, c ^ step) for c in range(4)])  5.15 us
  transfers between devices with their start and end apart: 31, of which 13 were waited for; matrix products, arithmetic and copies ran while one was open for 1% of the time, Pallas kernels for 24%

profile of v3, /device:TPU:1, one launch (start us, length us, event | category | flops | bytes accessed | tf_op | source)
XLA Modules:
  0.0 170.2 jit_solution(17622468972038607578)
XLA Ops:
  0.0 2.5 %arrange.1 = bf16[8,28672]{1,0:T(8,128)(2,1)} custom-call(s32[224]{0:T(256)} %order.1, bf16[8,28672]{1,0:T(8,128)(2,1)} %values.1, s32[8,224]{1,0:T(8,128)} %flags.1), custom_call_target="tpu_custom_call" | custom-call | tf_op jit(solution)/shard_map/arrange/pallas_call | solution.py:398
  2.5 18.6 %all_to_all.19 = bf16[8,32,896]{2,0,1:T(8,128)(2,1)S(1)} all-to-all(bf16[8,32,896]{2,0,1:T(8,128)(2,1)} %bitcast.52), channel_id=1, replica_groups=mesh['row'=32,'col'=4] {'row'}, dimensions={1} | all-to-all | bytes 917504 | tf_op jit(solution)/shard_map/all_to_all | solution.py:406
  21.1 2.6 %collective-permute-start = (bf16[256,896]{1,0:T(8,128)(2,1)S(1)}, bf16[256,896]{1,0:T(8,128)(2,1)S(1)}, u32[]{:S(2)}, u32[]{:S(2)}) collective-permute-start(bf16[256,896]{1,0:T(8,128)(2,1)S(1)} %bitcast.47), channel_id=1, source_target_pairs={{0,1},{1,0},{2,3},{3,2},{4,5},{5,4},{6,7},{7,6},{8,9},{9,8},{10,11... | collective-permute-start | bytes 1376264 | tf_op jit(solution)/shard_map/ppermute | solution.py:37
  24.5 3.4 %collective-permute-start.1 = (bf16[256,896]{1,0:T(8,128)(2,1)S(1)}, bf16[256,896]{1,0:T(8,128)(2,1)S(1)}, u32[]{:S(2)}, u32[]{:S(2)}) collective-permute-start(bf16[256,896]{1,0:T(8,128)(2,1)S(1)} %bitcast.48), channel_id=1, source_target_pairs={{0,2},{1,3},{2,0},{3,1},{4,6},{5,7},{6,4},{7,5},{8,10},{9,11},{10,... | collective-permute-start | bytes 1376264 | tf_op jit(solution)/shard_map/ppermute | solution.py:37
  28.2 4.6 %copy-done.2 = bf16[896,7168]{1,0:T(8,128)(2,1)S(1)} copy-done((bf16[896,7168]{1,0:T(8,128)(2,1)S(1)}, bf16[896,7168]{1,0:T(8,128)(2,1)}, u32[]{:S(2)}) %copy-start.2) | copy-done | bytes 12845080
  32.9 7.6 %begin_kernel.1 = (s16[64,3712]{1,0:T(8,128)(2,1)S(1)}, s16[64,3712]{1,0:T(8,128)(2,1)S(1)}, s16[64,3712]{1,0:T(8,128)(2,1)S(1)}, s16[64,3712]{1,0:T(8,128)(2,1)...) custom-call(s32[3]{0:T(128)S(1)} %pad_add_fusion.pos.refs_1_.refs_5_, bf16[256,896]{1,0:T(8,128)(2,1)S(1)} %bitcast.49, ...), custom_call_target="tpu_custom_call" | custom-call | flops 1000 | bytes 1000 | tf_op jit(solution)/shard_map/begin_kernel/pallas_call | solution.py:367
  43.7 2.5 %collective-permute-start.6 = (s16[64,3712]{1,0:T(8,128)(2,1)S(1)}, s16[64,3712]{1,0:T(8,128)(2,1)S(1)}, u32[]{:S(2)}, u32[]{:S(2)}) collective-permute-start(s16[64,3712]{1,0:T(8,128)(2,1)S(1)} %get-tuple-element.63), channel_id=1, source_target_pairs={{0,12},{4,0},{8,4},{12,8},{16,28},{20,16},{24,20},{28,24},{32,44},... | collective-permute-start | bytes 1425416 | tf_op jit(solution)/shard_map/ppermute | solution.py:33
  46.4 4.8 %opposite_kernel.1 = (s16[64,3712]{1,0:T(8,128)(2,1)S(1)}, s16[64,3712]{1,0:T(8,128)(2,1)S(1)}, s16[64,3712]{1,0:T(8,128)(2,1)S(1)}, s16[64,3712]{1,0:T(8,128)(2,1)S(1)}) custom-call(s16[64,3712]{1,0:T(8,128)(2,1)S(1)} %get-tuple-element.56.refs_0_, s32[3]{0:T(128)S(1)} %pad_add_fusion.pos.refs_1_.refs_5_, ...), custom_call_target="tpu_custom_call" | custom-call | flops 1000 | bytes 1000 | tf_op jit(solution)/shard_map/opposite_kernel/pallas_call | solution.py:328
  51.2 3.1 %collective-permute-done.3.refs_1_.refs_6_ = s16[64,3712]{1,0:T(8,128)(2,1)S(1)} collective-permute-done((s16[64,3712]{1,0:T(8,128)(2,1)S(1)}, s16[64,3712]{1,0:T(8,128)(2,1)S(1)}, u32[]{:S(2)}, u32[]{:S(2)}) %collective-permute-start.3) | collective-permute-done | bytes 475168 | tf_op jit(solution)/shard_map/ppermute | solution.py:33
  56.4 2.7 %collective-permute-start.8 = (s16[64,3712]{1,0:T(8,128)(2,1)S(1)}, s16[64,3712]{1,0:T(8,128)(2,1)S(1)}, u32[]{:S(2)}, u32[]{:S(2)}) collective-permute-start(s16[64,3712]{1,0:T(8,128)(2,1)S(1)} %get-tuple-element.69), channel_id=1, source_target_pairs={{0,48},{4,52},{8,56},{12,60},{16,0},{20,4},{24,8},{28,12},{32,16},... | collective-permute-start | bytes 1425416 | tf_op jit(solution)/shard_map/ppermute | solution.py:33
  59.0 2.7 %collective-permute-start.10 = (s16[64,3712]{1,0:T(8,128)(2,1)S(1)}, s16[64,3712]{1,0:T(8,128)(2,1)S(1)}, u32[]{:S(2)}, u32[]{:S(2)}) collective-permute-start(s16[64,3712]{1,0:T(8,128)(2,1)S(1)} %get-tuple-element.71), channel_id=1, source_target_pairs={{0,12},{4,0},{8,4},{12,8},{16,28},{20,16},{24,20},{28,24},{32,44},... | collective-permute-start | bytes 1425416 | tf_op jit(solution)/shard_map/ppermute | solution.py:33
  61.7 7.3 %free_kernel.1 = (s16[128,3712]{1,0:T(8,128)(2,1)S(1)}, s16[128,3712]{1,0:T(8,128)(2,1)S(1)}, s16[128,3712]{1,0:T(8,128)(2,1)S(1)}, s16[128,3712]{1,0:T(8,128)(2,1)S(1)}) custom-call(s16[64,3712]{1,0:T(8,128)(2,1)S(1)} %get-tuple-element.68.refs_0_, s16[64,3712]{1,0:T(8,128)(2,1)S(1)} %collective-permute-done.3.refs_1_.refs_6_, ...), custom_call_target="tpu_custom_call" | custom-call | flops 1000 | bytes 1000 | tf_op jit(solution)/shard_map/free_kernel/pallas_call | solution.py:328
  70.4 2.7 %collective-permute-start.12 = (s16[128,3712]{1,0:T(8,128)(2,1)S(1)}, s16[128,3712]{1,0:T(8,128)(2,1)S(1)}, u32[]{:S(2)}, u32[]{:S(2)}) collective-permute-start(s16[128,3712]{1,0:T(8,128)(2,1)S(1)} %get-tuple-element.77), channel_id=1, source_target_pairs={{0,48},{4,52},{8,56},{12,60},{16,0},{20,4},{24,8},{28,12},{32,16},... | collective-permute-start | bytes 2850824 | tf_op jit(solution)/shard_map/ppermute | solution.py:33
  73.3 2.4 %collective-permute-start.14 = (s16[128,3712]{1,0:T(8,128)(2,1)S(1)}, s16[128,3712]{1,0:T(8,128)(2,1)S(1)}, u32[]{:S(2)}, u32[]{:S(2)}) collective-permute-start(s16[128,3712]{1,0:T(8,128)(2,1)S(1)} %get-tuple-element.79), channel_id=1, source_target_pairs={{0,12},{4,0},{8,4},{12,8},{16,28},{20,16},{24,20},{28,24},{32,44},... | collective-permute-start | bytes 2850824 | tf_op jit(solution)/shard_map/ppermute | solution.py:33
  75.7 2.8 %copy-done.1 = bf16[896,3584]{1,0:T(8,128)(2,1)S(1)} copy-done((bf16[896,3584]{1,0:T(8,128)(2,1)S(1)}, bf16[896,3584]{1,0:T(8,128)(2,1)}, u32[]{:S(2)}) %copy-start.1) | copy-done | bytes 6422552
  78.5 7.5 %pass_on_kernel.1 = (s16[128,3712]{1,0:T(8,128)(2,1)S(1)}, s16[128,3712]{1,0:T(8,128)(2,1)S(1)}, s16[128,3712]{1,0:T(8,128)(2,1)S(1)}, s16[128,3712]{1,0:T(8,128)(2,1)S(1)}) custom-call(s16[128,3712]{1,0:T(8,128)(2,1)S(1)} %get-tuple-element.76.refs_0_, s32[3]{0:T(128)S(1)} %pad_add_fusion.pos.refs_1_.refs_5_, ...), custom_call_target="tpu_custom_call" | custom-call | flops 1000 | bytes 1000 | tf_op jit(solution)/shard_map/pass_on_kernel/pallas_call | solution.py:328
  86.0 4.9 %collective-permute-done.11.refs_1_.refs_5_.refs_9_.refs_6_.refs_7_ = s16[128,3712]{1,0:T(8,128)(2,1)S(1)} collective-permute-done((s16[128,3712]{1,0:T(8,128)(2,1)S(1)}, s16[128,3712]{1,0:T(8,128)(2,1)S(1)}, u32[]{:S(2)}, u32[]{:S(2)}) %collective-permute-start.11) | collective-permute-done | bytes 950304 | tf_op jit(solution)/shard_map/ppermute | solution.py:33
  93.1 2.7 %collective-permute-start.16 = (s16[128,3712]{1,0:T(8,128)(2,1)S(1)}, s16[128,3712]{1,0:T(8,128)(2,1)S(1)}, u32[]{:S(2)}, u32[]{:S(2)}) collective-permute-start(s16[128,3712]{1,0:T(8,128)(2,1)S(1)} %get-tuple-element.85), channel_id=1, source_target_pairs={{0,48},{4,52},{8,56},{12,60},{16,0},{20,4},{24,8},{28,12},{32,16},... | collective-permute-start | bytes 2850824 | tf_op jit(solution)/shard_map/ppermute | solution.py:33
  95.8 2.6 %collective-permute-start.18 = (s16[128,3712]{1,0:T(8,128)(2,1)S(1)}, s16[128,3712]{1,0:T(8,128)(2,1)S(1)}, u32[]{:S(2)}, u32[]{:S(2)}) collective-permute-start(s16[128,3712]{1,0:T(8,128)(2,1)S(1)} %get-tuple-element.88), channel_id=1, source_target_pairs={{0,12},{4,0},{8,4},{12,8},{16,28},{20,16},{24,20},{28,24},{32,44},... | collective-permute-start | bytes 2850824 | tf_op jit(solution)/shard_map/ppermute | solution.py:33
  98.4 6.1 %own_kernel.1 = (f32[256,3584]{1,0:T(8,128)S(1)}, f32[256,3584]{1,0:T(8,128)S(1)}) custom-call(s16[128,3712]{1,0:T(8,128)(2,1)S(1)} %get-tuple-element.84.refs_0_, s16[128,3712]{1,0:T(8,128)(2,1)S(1)} %collective-permute-done.11.refs_1_.refs_5_.refs_9_.refs_6_.refs_7_, s16[128,3712]{1,0:T(8,128)(2,1)S(1)} %collective-permute-done.12.refs_2_.refs_4_.refs_8_.refs_5_, ...), custom_call_target="tpu_custom_call" | custom-call | flops 1000 | bytes 1000 | tf_op jit(solution)/shard_map/own_kernel/pallas_call | solution.py:328
  104.6 7.6 %collective-permute-done.15.refs_3_.refs_7_.refs_2_ = s16[128,3712]{1,0:T(8,128)(2,1)S(1)} collective-permute-done((s16[128,3712]{1,0:T(8,128)(2,1)S(1)}, s16[128,3712]{1,0:T(8,128)(2,1)S(1)}, u32[]{:S(2)}, u32[]{:S(2)}) %collective-permute-start.15) | collective-permute-done | bytes 950304 | tf_op jit(solution)/shard_map/ppermute | solution.py:33
  114.3 3.7 %second_opposite_kernel.1 = (s16[32,3712]{1,0:T(8,128)(2,1)S(1)}, s16[32,3712]{1,0:T(8,128)(2,1)S(1)}, s16[32,3712]{1,0:T(8,128)(2,1)S(1)}, s16[32,3712]{1,0:T(8,128)(2,1)S(1)}) custom-call(s32[3]{0:T(128)S(1)} %pad_add_fusion.pos.refs_1_.refs_5_, f32[256,3584]{1,0:T(8,128)S(1)} %get-tuple-element.80.refs_0_.refs_1_.refs_2_, ...), custom_call_target="tpu_custom_call" | custom-call | flops 1000 | bytes 1000 | tf_op jit(solution)/shard_map/second_opposite_kernel/pallas_call | solution.py:367
  118.1 2.6 %collective-permute-start.20 = (s16[32,3712]{1,0:T(8,128)(2,1)S(1)}, s16[32,3712]{1,0:T(8,128)(2,1)S(1)}, u32[]{:S(2)}, u32[]{:S(2)}) collective-permute-start(s16[32,3712]{1,0:T(8,128)(2,1)S(1)} %get-tuple-element.91), channel_id=1, source_target_pairs={{0,12},{4,0},{8,4},{12,8},{16,28},{20,16},{24,20},{28,24},{32,44},... | collective-permute-start | bytes 712712 | tf_op jit(solution)/shard_map/ppermute | solution.py:33
  120.8 2.7 %collective-permute-start.22 = (s16[32,3712]{1,0:T(8,128)(2,1)S(1)}, s16[32,3712]{1,0:T(8,128)(2,1)S(1)}, u32[]{:S(2)}, u32[]{:S(2)}) collective-permute-start(s16[32,3712]{1,0:T(8,128)(2,1)S(1)} %get-tuple-element.94), channel_id=1, source_target_pairs={{0,48},{4,52},{8,56},{12,60},{16,0},{20,4},{24,8},{28,12},{32,16},... | collective-permute-start | bytes 712712 | tf_op jit(solution)/shard_map/ppermute | solution.py:33
  123.4 6.9 %keep_kernel.1 = (f32[256,3584]{1,0:T(8,128)S(1)}, f32[256,3584]{1,0:T(8,128)S(1)}) custom-call(s32[3]{0:T(128)S(1)} %pad_add_fusion.pos.refs_1_.refs_5_, s16[32,3712]{1,0:T(8,128)(2,1)S(1)} %get-tuple-element.89.refs_0_, f32[256,3584]{1,0:T(8,128)S(1)} %get-tuple-element.80.refs_0_.refs_1_.refs_2_, ...), custom_call_target="tpu_custom_call" | custom-call | flops 1000 | bytes 1000 | tf_op jit(solution)/shard_map/keep_kernel/pallas_call | solution.py:367
  132.4 2.7 %collective-permute-start.24 = (s16[64,3712]{1,0:T(8,128)(2,1)S(1)}, s16[64,3712]{1,0:T(8,128)(2,1)S(1)}, u32[]{:S(2)}, u32[]{:S(2)}) collective-permute-start(s16[64,3712]{1,0:T(8,128)(2,1)S(1)} %get-tuple-element.96), channel_id=1, source_target_pairs={{0,12},{4,0},{8,4},{12,8},{16,28},{20,16},{24,20},{28,24},{32,44},... | collective-permute-start | bytes 1425416 | tf_op jit(solution)/shard_map/ppermute | solution.py:33
  135.1 2.7 %collective-permute-start.26 = (s16[64,3712]{1,0:T(8,128)(2,1)S(1)}, s16[64,3712]{1,0:T(8,128)(2,1)S(1)}, u32[]{:S(2)}, u32[]{:S(2)}) collective-permute-start(s16[64,3712]{1,0:T(8,128)(2,1)S(1)} %get-tuple-element.98), channel_id=1, source_target_pairs={{0,48},{4,52},{8,56},{12,60},{16,0},{20,4},{24,8},{28,12},{32,16},... | collective-permute-start | bytes 1425416 | tf_op jit(solution)/shard_map/ppermute | solution.py:33
  137.8 3.4 %collective-permute-done.23.refs_3_ = s16[64,3712]{1,0:T(8,128)(2,1)S(1)} collective-permute-done((s16[64,3712]{1,0:T(8,128)(2,1)S(1)}, s16[64,3712]{1,0:T(8,128)(2,1)S(1)}, u32[]{:S(2)}, u32[]{:S(2)}) %collective-permute-start.23) | collective-permute-done | bytes 475168 | tf_op jit(solution)/shard_map/ppermute | solution.py:33
  141.1 3.0 %collective-permute-done.25.refs_6_ = s16[64,3712]{1,0:T(8,128)(2,1)S(1)} collective-permute-done((s16[64,3712]{1,0:T(8,128)(2,1)S(1)}, s16[64,3712]{1,0:T(8,128)(2,1)S(1)}, u32[]{:S(2)}, u32[]{:S(2)}) %collective-permute-start.25) | collective-permute-done | bytes 475168 | tf_op jit(solution)/shard_map/ppermute | solution.py:33
  146.0 3.1 %collective-permute-start.28 = (s16[32,3712]{1,0:T(8,128)(2,1)S(1)}, s16[32,3712]{1,0:T(8,128)(2,1)S(1)}, u32[]{:S(2)}, u32[]{:S(2)}) collective-permute-start(s16[32,3712]{1,0:T(8,128)(2,1)S(1)} %get-tuple-element.101), channel_id=1, source_target_pairs={{0,2},{1,3},{2,0},{3,1},{4,6},{5,7},{6,4},{7,5},{8,10},{9,11},{10,... | collective-permute-start | bytes 712712 | tf_op jit(solution)/shard_map/ppermute | solution.py:37
  151.2 4.0 %collective-permute-done.28.refs_4_ = s16[32,3712]{1,0:T(8,128)(2,1)S(1)} collective-permute-done((s16[32,3712]{1,0:T(8,128)(2,1)S(1)}, s16[32,3712]{1,0:T(8,128)(2,1)S(1)}, u32[]{:S(2)}, u32[]{:S(2)}) %collective-permute-start.28) | collective-permute-done | bytes 237600 | tf_op jit(solution)/shard_map/ppermute | solution.py:37
  158.5 9.6 %collective-permute-start.30 = (bf16[8,14336]{1,0:T(8,128)(2,1)S(1)}, bf16[8,14336]{1,0:T(8,128)(2,1)S(1)}, u32[]{:S(2)}, u32[]{:S(2)}) collective-permute-start(bf16[8,14336]{1,0:T(8,128)(2,1)S(1)} %dynamic-slice_bitcast_fusion), channel_id=1, source_target_pairs={{0,1},{1,0},{2,3},{3,2},{4,5},{5,4},{6,7},{7,6},{8,9},{9,8},{10,11... | collective-permute-start | bytes 688136 | tf_op jit(solution)/shard_map/ppermute | solution.py:37
  (61 shorter events, 23.8 us)
Async XLA Ops:
  21.1 6.9 %collective-permute-start = (bf16[256,896]{1,0:T(8,128)(2,1)S(1)}, bf16[256,896]{1,0:T(8,128)(2,1)S(1)}, u32[]{:S(2)}, u32[]{:S(2)}) collective-permute-start(bf16[256,896]{1,0:T(8,128)(2,1)S(1)} %bitcast.47), channel_id=1, source_target_pairs={{0,1},{1,0},{2,3},{3,2},{4,5},{5,4},{6,7},{7,6},{8,9},{9,8},{10,11... | collective-permute-start | bytes 1376264 | tf_op jit(solution)/shard_map/ppermute | solution.py:37
  24.5 16.0 %collective-permute-start.1 = (bf16[256,896]{1,0:T(8,128)(2,1)S(1)}, bf16[256,896]{1,0:T(8,128)(2,1)S(1)}, u32[]{:S(2)}, u32[]{:S(2)}) collective-permute-start(bf16[256,896]{1,0:T(8,128)(2,1)S(1)} %bitcast.48), channel_id=1, source_target_pairs={{0,2},{1,3},{2,0},{3,1},{4,6},{5,7},{6,4},{7,5},{8,10},{9,11},{10,... | collective-permute-start | bytes 1376264 | tf_op jit(solution)/shard_map/ppermute | solution.py:37
  40.5 21.2 %copy-start = (bf16[896,3584]{1,0:T(8,128)(2,1)}, bf16[896,3584]{1,0:T(8,128)(2,1)S(1)}, u32[]{:S(2)}) copy-start(bf16[896,3584]{1,0:T(8,128)(2,1)S(1)} %get-tuple-element.58.refs_3_.refs_7_) | copy-start | bytes 19267588
  40.5 5.7 %collective-permute-start.2 = (bf16[256,896]{1,0:T(8,128)(2,1)S(1)}, bf16[256,896]{1,0:T(8,128)(2,1)S(1)}, u32[]{:S(2)}, u32[]{:S(2)}) collective-permute-start(bf16[256,896]{1,0:T(8,128)(2,1)S(1)} %collective-permute-done.1), channel_id=1, source_target_pairs={{0,1},{1,0},{2,3},{3,2},{4,5},{5,4},{6,7},{7,6},{8,9},{9,8},{10,11... | collective-permute-start | bytes 1376264 | tf_op jit(solution)/shard_map/ppermute | solution.py:37
  40.9 13.5 %collective-permute-start.3 = (s16[64,3712]{1,0:T(8,128)(2,1)S(1)}, s16[64,3712]{1,0:T(8,128)(2,1)S(1)}, u32[]{:S(2)}, u32[]{:S(2)}) collective-permute-start(s16[64,3712]{1,0:T(8,128)(2,1)S(1)} %get-tuple-element.56.refs_0_), channel_id=1, source_target_pairs={{0,16},{4,20},{8,24},{12,28},{16,32},{20,36},{24,40},{28,44},{32,4... | collective-permute-start | bytes 1425416 | tf_op jit(solution)/shard_map/ppermute | solution.py:33
  41.2 13.1 %collective-permute-start.4 = (s16[64,3712]{1,0:T(8,128)(2,1)S(1)}, s16[64,3712]{1,0:T(8,128)(2,1)S(1)}, u32[]{:S(2)}, u32[]{:S(2)}) collective-permute-start(s16[64,3712]{1,0:T(8,128)(2,1)S(1)} %get-tuple-element.61), channel_id=1, source_target_pairs={{0,48},{4,52},{8,56},{12,60},{16,0},{20,4},{24,8},{28,12},{32,16},... | collective-permute-start | bytes 1425416 | tf_op jit(solution)/shard_map/ppermute | solution.py:33
  43.5 12.8 %collective-permute-start.5 = (s16[64,3712]{1,0:T(8,128)(2,1)S(1)}, s16[64,3712]{1,0:T(8,128)(2,1)S(1)}, u32[]{:S(2)}, u32[]{:S(2)}) collective-permute-start(s16[64,3712]{1,0:T(8,128)(2,1)S(1)} %get-tuple-element.62), channel_id=1, source_target_pairs={{0,4},{4,8},{8,12},{12,0},{16,20},{20,24},{24,28},{28,16},{32,36},... | collective-permute-start | bytes 1425416 | tf_op jit(solution)/shard_map/ppermute | solution.py:33
  43.7 12.6 %collective-permute-start.6 = (s16[64,3712]{1,0:T(8,128)(2,1)S(1)}, s16[64,3712]{1,0:T(8,128)(2,1)S(1)}, u32[]{:S(2)}, u32[]{:S(2)}) collective-permute-start(s16[64,3712]{1,0:T(8,128)(2,1)S(1)} %get-tuple-element.63), channel_id=1, source_target_pairs={{0,12},{4,0},{8,4},{12,8},{16,28},{20,16},{24,20},{28,24},{32,44},... | collective-permute-start | bytes 1425416 | tf_op jit(solution)/shard_map/ppermute | solution.py:33
  56.3 12.7 %collective-permute-start.7 = (s16[64,3712]{1,0:T(8,128)(2,1)S(1)}, s16[64,3712]{1,0:T(8,128)(2,1)S(1)}, u32[]{:S(2)}, u32[]{:S(2)}) collective-permute-start(s16[64,3712]{1,0:T(8,128)(2,1)S(1)} %get-tuple-element.68.refs_0_), channel_id=1, source_target_pairs={{0,16},{4,20},{8,24},{12,28},{16,32},{20,36},{24,40},{28,44},{32,4... | collective-permute-start | bytes 1425416 | tf_op jit(solution)/shard_map/ppermute | solution.py:33
  56.4 12.7 %collective-permute-start.8 = (s16[64,3712]{1,0:T(8,128)(2,1)S(1)}, s16[64,3712]{1,0:T(8,128)(2,1)S(1)}, u32[]{:S(2)}, u32[]{:S(2)}) collective-permute-start(s16[64,3712]{1,0:T(8,128)(2,1)S(1)} %get-tuple-element.69), channel_id=1, source_target_pairs={{0,48},{4,52},{8,56},{12,60},{16,0},{20,4},{24,8},{28,12},{32,16},... | collective-permute-start | bytes 1425416 | tf_op jit(solution)/shard_map/ppermute | solution.py:33
  59.0 11.3 %collective-permute-start.9 = (s16[64,3712]{1,0:T(8,128)(2,1)S(1)}, s16[64,3712]{1,0:T(8,128)(2,1)S(1)}, u32[]{:S(2)}, u32[]{:S(2)}) collective-permute-start(s16[64,3712]{1,0:T(8,128)(2,1)S(1)} %get-tuple-element.70), channel_id=1, source_target_pairs={{0,4},{4,8},{8,12},{12,0},{16,20},{20,24},{24,28},{28,16},{32,36},... | collective-permute-start | bytes 1425416 | tf_op jit(solution)/shard_map/ppermute | solution.py:33
  59.0 11.3 %collective-permute-start.10 = (s16[64,3712]{1,0:T(8,128)(2,1)S(1)}, s16[64,3712]{1,0:T(8,128)(2,1)S(1)}, u32[]{:S(2)}, u32[]{:S(2)}) collective-permute-start(s16[64,3712]{1,0:T(8,128)(2,1)S(1)} %get-tuple-element.71), channel_id=1, source_target_pairs={{0,12},{4,0},{8,4},{12,8},{16,28},{20,16},{24,20},{28,24},{32,44},... | collective-permute-start | bytes 1425416 | tf_op jit(solution)/shard_map/ppermute | solution.py:33
  70.4 20.6 %collective-permute-start.11 = (s16[128,3712]{1,0:T(8,128)(2,1)S(1)}, s16[128,3712]{1,0:T(8,128)(2,1)S(1)}, u32[]{:S(2)}, u32[]{:S(2)}) collective-permute-start(s16[128,3712]{1,0:T(8,128)(2,1)S(1)} %get-tuple-element.76.refs_0_), channel_id=1, source_target_pairs={{0,16},{4,20},{8,24},{12,28},{16,32},{20,36},{24,40},{28,44},{32,4... | collective-permute-start | bytes 2850824 | tf_op jit(solution)/shard_map/ppermute | solution.py:33
  70.4 20.6 %collective-permute-start.12 = (s16[128,3712]{1,0:T(8,128)(2,1)S(1)}, s16[128,3712]{1,0:T(8,128)(2,1)S(1)}, u32[]{:S(2)}, u32[]{:S(2)}) collective-permute-start(s16[128,3712]{1,0:T(8,128)(2,1)S(1)} %get-tuple-element.77), channel_id=1, source_target_pairs={{0,48},{4,52},{8,56},{12,60},{16,0},{20,4},{24,8},{28,12},{32,16},... | collective-permute-start | bytes 2850824 | tf_op jit(solution)/shard_map/ppermute | solution.py:33
  73.0 20.0 %collective-permute-start.13 = (s16[128,3712]{1,0:T(8,128)(2,1)S(1)}, s16[128,3712]{1,0:T(8,128)(2,1)S(1)}, u32[]{:S(2)}, u32[]{:S(2)}) collective-permute-start(s16[128,3712]{1,0:T(8,128)(2,1)S(1)} %get-tuple-element.78), channel_id=1, source_target_pairs={{0,4},{4,8},{8,12},{12,0},{16,20},{20,24},{24,28},{28,16},{32,36},... | collective-permute-start | bytes 2850824 | tf_op jit(solution)/shard_map/ppermute | solution.py:33
  73.3 19.8 %collective-permute-start.14 = (s16[128,3712]{1,0:T(8,128)(2,1)S(1)}, s16[128,3712]{1,0:T(8,128)(2,1)S(1)}, u32[]{:S(2)}, u32[]{:S(2)}) collective-permute-start(s16[128,3712]{1,0:T(8,128)(2,1)S(1)} %get-tuple-element.79), channel_id=1, source_target_pairs={{0,12},{4,0},{8,4},{12,8},{16,28},{20,16},{24,20},{28,24},{32,44},... | collective-permute-start | bytes 2850824 | tf_op jit(solution)/shard_map/ppermute | solution.py:33
  93.1 19.1 %collective-permute-start.15 = (s16[128,3712]{1,0:T(8,128)(2,1)S(1)}, s16[128,3712]{1,0:T(8,128)(2,1)S(1)}, u32[]{:S(2)}, u32[]{:S(2)}) collective-permute-start(s16[128,3712]{1,0:T(8,128)(2,1)S(1)} %get-tuple-element.84.refs_0_), channel_id=1, source_target_pairs={{0,16},{4,20},{8,24},{12,28},{16,32},{20,36},{24,40},{28,44},{32,4... | collective-permute-start | bytes 2850824 | tf_op jit(solution)/shard_map/ppermute | solution.py:33
  93.1 19.1 %collective-permute-start.16 = (s16[128,3712]{1,0:T(8,128)(2,1)S(1)}, s16[128,3712]{1,0:T(8,128)(2,1)S(1)}, u32[]{:S(2)}, u32[]{:S(2)}) collective-permute-start(s16[128,3712]{1,0:T(8,128)(2,1)S(1)} %get-tuple-element.85), channel_id=1, source_target_pairs={{0,48},{4,52},{8,56},{12,60},{16,0},{20,4},{24,8},{28,12},{32,16},... | collective-permute-start | bytes 2850824 | tf_op jit(solution)/shard_map/ppermute | solution.py:33
  95.8 18.6 %collective-permute-start.17 = (s16[128,3712]{1,0:T(8,128)(2,1)S(1)}, s16[128,3712]{1,0:T(8,128)(2,1)S(1)}, u32[]{:S(2)}, u32[]{:S(2)}) collective-permute-start(s16[128,3712]{1,0:T(8,128)(2,1)S(1)} %get-tuple-element.87), channel_id=1, source_target_pairs={{0,4},{4,8},{8,12},{12,0},{16,20},{20,24},{24,28},{28,16},{32,36},... | collective-permute-start | bytes 2850824 | tf_op jit(solution)/shard_map/ppermute | solution.py:33
  95.8 18.5 %collective-permute-start.18 = (s16[128,3712]{1,0:T(8,128)(2,1)S(1)}, s16[128,3712]{1,0:T(8,128)(2,1)S(1)}, u32[]{:S(2)}, u32[]{:S(2)}) collective-permute-start(s16[128,3712]{1,0:T(8,128)(2,1)S(1)} %get-tuple-element.88), channel_id=1, source_target_pairs={{0,12},{4,0},{8,4},{12,8},{16,28},{20,16},{24,20},{28,24},{32,44},... | collective-permute-start | bytes 2850824 | tf_op jit(solution)/shard_map/ppermute | solution.py:33
  118.0 12.4 %collective-permute-start.19 = (s16[32,3712]{1,0:T(8,128)(2,1)S(1)}, s16[32,3712]{1,0:T(8,128)(2,1)S(1)}, u32[]{:S(2)}, u32[]{:S(2)}) collective-permute-start(s16[32,3712]{1,0:T(8,128)(2,1)S(1)} %get-tuple-element.89.refs_0_), channel_id=1, source_target_pairs={{0,4},{4,8},{8,12},{12,0},{16,20},{20,24},{24,28},{28,16},{32,36},... | collective-permute-start | bytes 712712 | tf_op jit(solution)/shard_map/ppermute | solution.py:33
  118.1 12.3 %collective-permute-start.20 = (s16[32,3712]{1,0:T(8,128)(2,1)S(1)}, s16[32,3712]{1,0:T(8,128)(2,1)S(1)}, u32[]{:S(2)}, u32[]{:S(2)}) collective-permute-start(s16[32,3712]{1,0:T(8,128)(2,1)S(1)} %get-tuple-element.91), channel_id=1, source_target_pairs={{0,12},{4,0},{8,4},{12,8},{16,28},{20,16},{24,20},{28,24},{32,44},... | collective-permute-start | bytes 712712 | tf_op jit(solution)/shard_map/ppermute | solution.py:33
  120.7 9.7 %collective-permute-start.21 = (s16[32,3712]{1,0:T(8,128)(2,1)S(1)}, s16[32,3712]{1,0:T(8,128)(2,1)S(1)}, u32[]{:S(2)}, u32[]{:S(2)}) collective-permute-start(s16[32,3712]{1,0:T(8,128)(2,1)S(1)} %get-tuple-element.93), channel_id=1, source_target_pairs={{0,16},{4,20},{8,24},{12,28},{16,32},{20,36},{24,40},{28,44},{32,4... | collective-permute-start | bytes 712712 | tf_op jit(solution)/shard_map/ppermute | solution.py:33
  120.8 9.7 %collective-permute-start.22 = (s16[32,3712]{1,0:T(8,128)(2,1)S(1)}, s16[32,3712]{1,0:T(8,128)(2,1)S(1)}, u32[]{:S(2)}, u32[]{:S(2)}) collective-permute-start(s16[32,3712]{1,0:T(8,128)(2,1)S(1)} %get-tuple-element.94), channel_id=1, source_target_pairs={{0,48},{4,52},{8,56},{12,60},{16,0},{20,4},{24,8},{28,12},{32,16},... | collective-permute-start | bytes 712712 | tf_op jit(solution)/shard_map/ppermute | solution.py:33
  132.3 8.8 %collective-permute-start.23 = (s16[64,3712]{1,0:T(8,128)(2,1)S(1)}, s16[64,3712]{1,0:T(8,128)(2,1)S(1)}, u32[]{:S(2)}, u32[]{:S(2)}) collective-permute-start(s16[64,3712]{1,0:T(8,128)(2,1)S(1)} %get-tuple-element.95.refs_0_), channel_id=1, source_target_pairs={{0,4},{4,8},{8,12},{12,0},{16,20},{20,24},{24,28},{28,16},{32,36},... | collective-permute-start | bytes 1425416 | tf_op jit(solution)/shard_map/ppermute | solution.py:33
  132.4 8.7 %collective-permute-start.24 = (s16[64,3712]{1,0:T(8,128)(2,1)S(1)}, s16[64,3712]{1,0:T(8,128)(2,1)S(1)}, u32[]{:S(2)}, u32[]{:S(2)}) collective-permute-start(s16[64,3712]{1,0:T(8,128)(2,1)S(1)} %get-tuple-element.96), channel_id=1, source_target_pairs={{0,12},{4,0},{8,4},{12,8},{16,28},{20,16},{24,20},{28,24},{32,44},... | collective-permute-start | bytes 1425416 | tf_op jit(solution)/shard_map/ppermute | solution.py:33
  135.1 9.0 %collective-permute-start.25 = (s16[64,3712]{1,0:T(8,128)(2,1)S(1)}, s16[64,3712]{1,0:T(8,128)(2,1)S(1)}, u32[]{:S(2)}, u32[]{:S(2)}) collective-permute-start(s16[64,3712]{1,0:T(8,128)(2,1)S(1)} %get-tuple-element.97), channel_id=1, source_target_pairs={{0,16},{4,20},{8,24},{12,28},{16,32},{20,36},{24,40},{28,44},{32,4... | collective-permute-start | bytes 1425416 | tf_op jit(solution)/shard_map/ppermute | solution.py:33
  135.1 9.0 %collective-permute-start.26 = (s16[64,3712]{1,0:T(8,128)(2,1)S(1)}, s16[64,3712]{1,0:T(8,128)(2,1)S(1)}, u32[]{:S(2)}, u32[]{:S(2)}) collective-permute-start(s16[64,3712]{1,0:T(8,128)(2,1)S(1)} %get-tuple-element.98), channel_id=1, source_target_pairs={{0,48},{4,52},{8,56},{12,60},{16,0},{20,4},{24,8},{28,12},{32,16},... | collective-permute-start | bytes 1425416 | tf_op jit(solution)/shard_map/ppermute | solution.py:33
  145.9 5.3 %collective-permute-start.27 = (s16[32,3712]{1,0:T(8,128)(2,1)S(1)}, s16[32,3712]{1,0:T(8,128)(2,1)S(1)}, u32[]{:S(2)}, u32[]{:S(2)}) collective-permute-start(s16[32,3712]{1,0:T(8,128)(2,1)S(1)} %get-tuple-element.99.refs_0_), channel_id=1, source_target_pairs={{0,64},{4,68},{8,72},{12,76},{16,80},{20,84},{24,88},{28,92},{32,9... | collective-permute-start | bytes 712712 | tf_op jit(solution)/shard_map/ppermute | solution.py:33
  146.0 9.3 %collective-permute-start.28 = (s16[32,3712]{1,0:T(8,128)(2,1)S(1)}, s16[32,3712]{1,0:T(8,128)(2,1)S(1)}, u32[]{:S(2)}, u32[]{:S(2)}) collective-permute-start(s16[32,3712]{1,0:T(8,128)(2,1)S(1)} %get-tuple-element.101), channel_id=1, source_target_pairs={{0,2},{1,3},{2,0},{3,1},{4,6},{5,7},{6,4},{7,5},{8,10},{9,11},{10,... | collective-permute-start | bytes 712712 | tf_op jit(solution)/shard_map/ppermute | solution.py:37
  149.1 8.6 %collective-permute-start.29 = (s16[32,3712]{1,0:T(8,128)(2,1)S(1)}, s16[32,3712]{1,0:T(8,128)(2,1)S(1)}, u32[]{:S(2)}, u32[]{:S(2)}) collective-permute-start(s16[32,3712]{1,0:T(8,128)(2,1)S(1)} %get-tuple-element.102), channel_id=1, source_target_pairs={{0,66},{1,67},{2,64},{3,65},{4,70},{5,71},{6,68},{7,69},{8,74},{9,... | collective-permute-start | bytes 712712 | tf_op jit(solution)/shard_map/ppermute | solution.py:482
  158.5 10.7 %collective-permute-start.30 = (bf16[8,14336]{1,0:T(8,128)(2,1)S(1)}, bf16[8,14336]{1,0:T(8,128)(2,1)S(1)}, u32[]{:S(2)}, u32[]{:S(2)}) collective-permute-start(bf16[8,14336]{1,0:T(8,128)(2,1)S(1)} %dynamic-slice_bitcast_fusion), channel_id=1, source_target_pairs={{0,1},{1,0},{2,3},{3,2},{4,5},{5,4},{6,7},{7,6},{8,9},{9,8},{10,11... | collective-permute-start | bytes 688136 | tf_op jit(solution)/shard_map/ppermute | solution.py:37
  (2 other events, 7.5 us)

commit v4 on v0

v4 whole, which is shorter than its diff:
```python
import functools

import jax
import jax.numpy as jnp
from jax import lax
from jax.experimental import pallas as pl
from jax.experimental.pallas import tpu as pltpu
from jax.sharding import PartitionSpec as P

LEVELS = 32600.0
STEPS = 32.0
ROUNDER = 12582912.0
CODES = (32, 128)
VMEM_LIMIT = 12 * 1024 * 1024
BEGIN_LIMIT = 36 * 1024 * 1024
TILE = 896


def shift(dz, dx, dy):
    pairs = []
    for index in range(32):
        z, x, y = index // 16, (index // 4) % 4, index % 4
        pairs.append((index, ((z + dz) % 2) * 16 + ((x + dx) % 4) * 4 + (y + dy) % 4))
    return pairs


FORWARD = (shift(0, 1, 0), shift(0, 0, 1))
BACKWARD = (shift(0, -1, 0), shift(0, 0, -1))
ACROSS = shift(1, 0, 0)
DIAGONAL = [(r * 4 + c, s * 4 + (c ^ 2)) for r, s in ACROSS for c in range(4)]


def send(value, pairs):
    return lax.ppermute(value, "row", pairs)


def send_col(value, step):
    return lax.ppermute(value, "col", [(c, c ^ step) for c in range(4)])


def quantised(value):
    rows, tile = value.shape
    largest = jnp.max(jnp.max(jnp.abs(value.reshape(rows // 8, 8, tile)), axis=0), axis=0, keepdims=True)
    code = jnp.ceil(jnp.log2(jnp.maximum(largest, 1e-30)) * STEPS)
    factor = jnp.exp2(code * (-1.0 / STEPS)) * LEVELS
    rounded = (value * factor + ROUNDER) - ROUNDER
    return rounded.astype(jnp.int32).astype(jnp.int16), code


def finish(out_ref, code_ref):
    rows = out_ref.shape[0]
    codes = code_ref[...].astype(jnp.int32).astype(jnp.int16)
    if rows == 16:
        width = out_ref.shape[1] - 256
        out_ref[:, width:width + 128] = codes[:16]
        out_ref[:, width + 128:] = codes[16:]
        return
    width = out_ref.shape[1] - 128
    out_ref[:32, width:] = codes
    if rows > 32:
        out_ref[32:, width:] = jnp.zeros((rows - 32, 128), jnp.int16)


def encode(value, t, out_ref, code_ref):
    count = TILE // 128
    out_ref[:, columns_of(t)], code = quantised(value)
    for i in range(count):
        code_ref[pl.ds(t * count + i, 1), :] = code[:, i * 128:(i + 1) * 128]


def columns_of(t):
    return pl.ds(pl.multiple_of(t * TILE, 128), TILE)


def each_tile(width, unroll=1):
    return pl.loop(0, width // TILE, unroll=unroll)


def copy_rows(parts, left_ref, at, kind, first, z):
    first_stride, second_stride = (4, 1) if kind == 0 else (1, 4)
    for second in range(4):
        start = pl.multiple_of((z * 16 + second * second_stride + first * first_stride) * 16, 16)
        for part in parts:
            left_ref[at:at + 16, :] = part[pl.ds(start, 16), :]
            at += 16


def arrange_kernel(order, values, flags, tile_flags, out, flags_out, kept):
    for l in range(tile_flags.shape[1]):
        wide = jnp.broadcast_to(tile_flags[:, l:l + 1].astype(jnp.float32), (tile_flags.shape[0], 128))
        flags_out[:, l * 128:(l + 1) * 128] = wide.astype(jnp.bfloat16)
    tiles = flags.shape[1]
    for t in range(tiles):
        at = slice(t * 128, (t + 1) * 128)
        kept[:, at] = values[:, at] * flags[:, t:t + 1].astype(jnp.float32).astype(jnp.bfloat16)
    for k in range(tiles):
        out[:, k * 128:(k + 1) * 128] = kept[:, pl.ds(pl.multiple_of(order[k] * 128, 128), 128)]


def clear(*code_refs):
    for code_ref in code_refs:
        code_ref[...] = jnp.zeros(CODES, jnp.float32)


def dot(left, right):
    return jnp.dot(left, right, preferred_element_type=jnp.float32)


def opposite_rows(pos, kind, a, left, at_p, at_q):
    first = (pos[1 + kind] + 2) % 4
    copy_rows((a,), left, at_p, kind, first, 0)
    copy_rows((a,), left, at_q, kind, first, 1)


def free_rows(pos, kind, a, left, at_p, at_q):
    copy_rows((a,), left, at_p, kind, (pos[1 + kind] + 1) % 4, 1)
    copy_rows((a,), left, at_q, kind, (pos[1 + kind] + 3) % 4, 0)


def begin_kernel(pos, b, m, a, p0, q0, p1, q1, w0, w1, left, sems, *code_refs):
    tiles = w0.shape[1] // TILE

    def copy(kind, t):
        w = (w0, w1)[kind]
        at = pl.ds(kind * tiles * TILE + t * TILE, TILE)
        return pltpu.make_async_copy(b.at[:, at], w.at[:, pl.ds(t * TILE, TILE)], sems.at[kind * tiles + t])

    for t in range(tiles):
        for kind in range(2):
            copy(kind, t).start()
    clear(*code_refs)
    for kind in range(2):
        opposite_rows(pos, kind, a, left.at[kind], 0, 128)
        free_rows(pos, kind, a, left.at[kind], 64, 192)
    for t in range(tiles):
        for kind, w, p, q in ((0, w0, p0, q0), (1, w1, p1, q1)):
            copy(kind, t).wait()
            at = slice(t * TILE, (t + 1) * TILE)
            flags = m[:, (kind * tiles + t) * TILE:(kind * tiles + t + 1) * TILE]
            for k in range(w.shape[0] // 128):
                rows = slice(k * 128, (k + 1) * 128)
                w[rows, at] = w[rows, at] * flags[k:k + 1, :]
            sums = dot(left[kind], w[:, at])
            encode(sums[:128], t, p, code_refs[2 * kind])
            encode(sums[128:], t, q, code_refs[2 * kind + 1])
    for ref, code_ref in zip((p0, q0, p1, q1), code_refs):
        finish(ref, code_ref)


def far_kernel(rows, pos, w0, w1, a, p0, q0, p1, q1, left, *code_refs):
    clear(*code_refs)
    for kind, w, p, q in ((0, w0, p0, q0), (1, w1, p1, q1)):
        rows(pos, kind, a, left, 0, 64)

        @each_tile(w.shape[1], 2)
        def _(t):
            sums = dot(left[...], w[:, columns_of(t)])
            encode(sums[:64], t, p, code_refs[2 * kind])
            encode(sums[64:], t, q, code_refs[2 * kind + 1])

        finish(p, code_refs[2 * kind])
        finish(q, code_refs[2 * kind + 1])


def own_kernel(pos, w0, w1, near, far, own0, own1, left):
    for kind, w, own in ((0, w0, own0), (1, w1, own1)):
        for z in range(2):
            copy_rows((near, far), left, z * 128, kind, pos[1 + kind], z)

        @each_tile(w.shape[1], 2)
        def _(t):
            own[:, columns_of(t)] = dot(left[...], w[:, columns_of(t)])


def read_factors(ref, factor_ref):
    if ref.shape[0] == 16:
        width = ref.shape[1] - 256
        codes = jnp.concatenate([ref[:, width:width + 128], ref[:, width + 128:]], axis=0)
    else:
        codes = ref[:32, ref.shape[1] - 128:]
    factor_ref[...] = jnp.exp2(codes.astype(jnp.int32).astype(jnp.float32) * (1.0 / STEPS)) * (1.0 / LEVELS)


def decode(ref, factor_ref, t, rows=slice(None)):
    count = TILE // 128
    scale = jnp.concatenate([factor_ref[pl.ds(t * count + i, 1), :] for i in range(count)], axis=1)
    return ref[rows, columns_of(t)].astype(jnp.int32).astype(jnp.float32) * scale


def pass_on_kernel(pos, w0, w1, near, far, *refs):
    outs, left, factor_refs, code_refs = refs[8:12], refs[12], refs[13:21], refs[21:]
    clear(*code_refs)
    for kind, w in ((0, w0), (1, w1)):
        got, scale = refs[4 * kind:4 * kind + 4], factor_refs[4 * kind:4 * kind + 4]
        copy_rows((near, far), left, 0, kind, (pos[1 + kind] + 1) % 4, 0)
        copy_rows((near, far), left, 128, kind, (pos[1 + kind] + 3) % 4, 1)
        for ref, factor in zip(got, scale):
            read_factors(ref, factor)

        @each_tile(w.shape[1], 2)
        def _(t):
            sums = dot(left[...], w[:, columns_of(t)])
            for way in range(2):
                n, f = (decode(got[2 * part + way], scale[2 * part + way], t, slice(0, 64)) for part in range(2))
                mixed = []
                for second in range(4):
                    mixed += [n[second * 16:second * 16 + 16], f[second * 16:second * 16 + 16]]
                value = sums[way * 128:way * 128 + 128] + jnp.concatenate(mixed, axis=0)
                encode(value, t, outs[2 * kind + way], code_refs[2 * kind + way])

        for way in range(2):
            finish(outs[2 * kind + way], code_refs[2 * kind + way])


def stage_one(refs, factor_refs, second, t):
    own, dp, dq, np, nq, ip, iq = refs
    fdp, fdq, fnp, fnq, fip, fiq = factor_refs
    here, above = (pl.ds(pl.multiple_of(z * 128 + second * 32, 32), 32) for z in range(2))
    near, far = (pl.ds(pl.multiple_of(start + second * 16, 16), 16) for start in (64, 0))

    def free(n, fn, f, ff):
        return jnp.concatenate([decode(n, fn, t, near), decode(f, ff, t, far)], axis=0)

    return [
        own[here, columns_of(t)] + decode(dp, fdp, t, here) + free(nq, fnq, iq, fiq),
        own[above, columns_of(t)] + decode(dq, fdq, t, here) + free(np, fnp, ip, fip),
    ]


def second_opposite_kernel(kind, pos, *refs):
    some, outs, factor_refs, code_refs = refs[:7], refs[7:9], refs[9:15], refs[15:]
    clear(*code_refs)
    for ref, factor in zip(some[1:], factor_refs):
        read_factors(ref, factor)

    @each_tile(some[0].shape[1], 2)
    def _(t):
        sums = stage_one(some, factor_refs, (pos[2 - kind] + 2) % 4, t)
        for z in range(2):
            encode(sums[z], t, outs[z], code_refs[z])

    for z in range(2):
        finish(outs[z], code_refs[z])


def second_neighbour_kernel(kind, pos, *refs):
    some, got, outs, factor_refs, code_refs = refs[:7], refs[7:9], refs[9:11], refs[11:19], refs[19:]
    clear(*code_refs)
    for ref, factor in zip(refs[1:9], factor_refs):
        read_factors(ref, factor)

    @each_tile(some[0].shape[1], 2)
    def _(t):
        for way in range(2):
            sums = stage_one(some, factor_refs[:6], (pos[2 - kind] + (1 if way == 0 else 3)) % 4, t)
            sums[way] = sums[way] + decode(got[way], factor_refs[6 + way], t)
            encode(jnp.concatenate(sums, axis=0), t, outs[way], code_refs[way])

    for way in range(2):
        finish(outs[way], code_refs[way])


def spread_kernel(kind, pos, *refs):
    some, got, outs, sums, factor_refs, code_refs = refs[:7], refs[7:9], refs[9:13], refs[13], refs[14:22], refs[22:]
    clear(*code_refs)
    z = pos[0]
    for ref, factor in zip(refs[1:9], factor_refs):
        read_factors(ref, factor)

    def rows(h, far):
        return sums[pl.ds(pl.multiple_of(h * 32 + far * 16, 16), 16), :]

    @each_tile(some[0].shape[1], 2)
    def _(t):
        value = jnp.concatenate(stage_one(some, factor_refs[:6], pos[2 - kind], t), axis=0)
        sums[...] = value + decode(got[0], factor_refs[6], t) + decode(got[1], factor_refs[7], t)
        for at, (h, far) in enumerate(((1 - z, 0), (z, 1), (1 - z, 1))):
            encode(rows(h, far), t, outs[at], code_refs[at])
        outs[3][:, columns_of(t)] = rows(z, 0)

    for at in range(3):
        finish(outs[at], code_refs[at])


def last_kernel(pos, rest, a, b, c, near, far, f0, f1, f2):
    for ref, factor in ((a, f0), (b, f1), (c, f2)):
        read_factors(ref, factor)

    @each_tile(rest.shape[1], 2)
    def _(t):
        at = columns_of(t)
        near[:, at] = (rest[:, at] + decode(a, f0, t)).astype(jnp.bfloat16)
        far[:, at] = (decode(b, f1, t) + decode(c, f2, t)).astype(jnp.bfloat16)


COST = pl.CostEstimate(flops=1000, bytes_accessed=1000, transcendentals=0)


class Calls:
    def __init__(self, pos, first):
        self.pos, self.last = pos, first

    def __call__(self, kernel, values, outs, scratch=(), after=(), in_hbm=(), limit=VMEM_LIMIT):
        after = [self.last, *after]
        skipped = len(after)
        name = kernel.func.__name__ if isinstance(kernel, functools.partial) else kernel.__name__
        vmem = pl.BlockSpec(memory_space=pltpu.VMEM)
        results = pl.pallas_call(
            lambda *refs: kernel(refs[skipped], *refs[skipped + 1:]),
            in_specs=[pl.BlockSpec(memory_space=pl.ANY)] * skipped
            + [pl.BlockSpec(memory_space=pltpu.SMEM)]
            + [pl.BlockSpec(memory_space=pltpu.HBM)] * len(in_hbm) + [vmem] * len(values),
            out_specs=[vmem] * len(outs),
            out_shape=outs,
            scratch_shapes=list(scratch),
            compiler_params=pltpu.CompilerParams(vmem_limit_bytes=limit),
            cost_estimate=COST,
            name=name,
        )(*after, self.pos, *in_hbm, *values)
        self.last = results[0]
        return results


def scales(count):
    return [pltpu.VMEM(CODES, jnp.float32)] * count


def per_device(amplitudes, amplitude_mask, integrals, integral_mask, tile_order):
    pair_count, full_width = amplitudes.shape
    depth, columns = integrals.shape
    width = columns // 2
    row, col = lax.axis_index("row"), lax.axis_index("col")
    core, z_hi = col % 2, col // 2
    pos = jnp.stack([row // 16, (row // 4) % 4, row % 4]).astype(jnp.int32)

    ordered, flags = pl.pallas_call(
        arrange_kernel,
        in_specs=[pl.BlockSpec(memory_space=pltpu.SMEM)] + [pl.BlockSpec(memory_space=pltpu.VMEM)] * 3,
        out_specs=[pl.BlockSpec(memory_space=pltpu.VMEM)] * 2,
        out_shape=[
            jax.ShapeDtypeStruct((pair_count, full_width), jnp.bfloat16),
            pltpu.VMEM((integral_mask.shape[0], columns), jnp.bfloat16),
        ],
        scratch_shapes=[pltpu.VMEM((pair_count, full_width), jnp.bfloat16)],
        name="arrange",
    )(tile_order, amplitudes, amplitude_mask, integral_mask)
    ordered, pos = lax.optimization_barrier((ordered, pos))
    placed = lax.all_to_all(ordered, "row", split_axis=1, concat_axis=0, tiled=True)

    def both_cores(mine, other):
        even, odd = jnp.where(core == 0, mine, other), jnp.where(core == 0, other, mine)
        return jnp.stack([even.reshape(32, 8, depth), odd.reshape(32, 8, depth)], axis=1).reshape(512, depth)

    over = send_col(placed, 2)
    near = both_cores(placed, send_col(placed, 1))

    def sent(rows):
        return jax.ShapeDtypeStruct((rows, width + max(128, 4096 // rows)), jnp.int16)

    def floats(rows):
        return jax.ShapeDtypeStruct((rows, width), jnp.float32)

    call = Calls(pos, placed)

    def kept(rows):
        return pltpu.VMEM((rows, width), jnp.float32)

    def left_rows(*rows):
        return [pltpu.VMEM((*rows, depth), jnp.bfloat16)]

    def exchange_both(outs, ahead=()):
        sends = []
        for k in range(2):
            p, q = outs[2 * k:2 * k + 2]
            if ahead:
                p, q, *_ = lax.optimization_barrier((p, q, *ahead[2 * k:2 * k + 2]))
            sends += [send(p, FORWARD[k]), send(q, BACKWARD[k])]
        return sends

    results = call(
        begin_kernel, [flags, near], [sent(128)] * 4 + [pltpu.VMEM((depth, width), jnp.bfloat16)] * 2,
        left_rows(2, 256) + [pltpu.SemaphoreType.DMA((columns // TILE,))] + scales(4), in_hbm=[integrals],
        limit=BEGIN_LIMIT,
    )
    n, weights = exchange_both(results[:4]), list(results[4:])
    over, _ = lax.optimization_barrier((over, call.last))
    far = both_cores(over, send_col(over, 1))

    def far_part(rows, after):
        return call(
            functools.partial(far_kernel, rows), weights + [far], [sent(64)] * 4, left_rows(128) + scales(4), after
        )

    f = exchange_both(far_part(opposite_rows, ()), n)
    i = exchange_both(far_part(free_rows, n), f)
    operands = [v for k in range(2) for v in (*n[2 * k:2 * k + 2], *f[2 * k:2 * k + 2])]
    d = exchange_both(
        call(pass_on_kernel, weights + [near, far] + operands, [sent(128)] * 4, left_rows(256) + scales(12)), i
    )
    own = call(own_kernel, weights + [near, far], [kept(256)] * 2, left_rows(256), i)

    def stage_one_of(kind):
        return [own[kind]] + [v for part in (d, n, i) for v in part[2 * kind:2 * kind + 2]]

    got = [None, None]
    for k in range(2):
        p, q = call(functools.partial(second_opposite_kernel, k), stage_one_of(k), [sent(32)] * 2, scales(8))
        got[k] = send(p, FORWARD[1 - k]), send(q, BACKWARD[1 - k])
    for k in range(2):
        p, q = call(
            functools.partial(second_neighbour_kernel, k), stage_one_of(k) + [*got[k]], [sent(64)] * 2, scales(10)
        )
        got[k] = send(p, FORWARD[1 - k]), send(q, BACKWARD[1 - k])
    for k in range(2):
        a, b, c, rest = call(
            functools.partial(spread_kernel, k), stage_one_of(k) + [*got[k]], [sent(16)] * 3 + [floats(16)],
            [pltpu.VMEM((64, TILE), jnp.float32)] + scales(11),
        )
        got[k] = rest, send(a, ACROSS), send_col(b, 2), lax.ppermute(c, ("row", "col"), DIAGONAL)
    outs = []
    for k in range(2):
        outs.append(call(last_kernel, [*got[k]], [jax.ShapeDtypeStruct((16, width), jnp.bfloat16)] * 2, scales(3)))
    outs = [outs[k][part] for part in range(2) for k in range(2)]
    summed = jnp.concatenate(outs, axis=1).reshape(2, 8, 2 * columns)
    mine = lax.dynamic_index_in_dim(summed, core, 0, keepdims=False)
    other = send_col(lax.dynamic_index_in_dim(summed, 1 - core, 0, keepdims=False), 1)
    even, odd = jnp.where(core == 0, mine, other), jnp.where(core == 0, other, mine)
    near_pair = [even[:, :columns], odd[:, :columns]]
    far_pair = [even[:, columns:], odd[:, columns:]]
    first = [jnp.where(z_hi == 0, u, v) for u, v in zip(near_pair, far_pair)]
    last = [jnp.where(z_hi == 0, v, u) for u, v in zip(near_pair, far_pair)]
    return jnp.concatenate(first + last, axis=1)


def solution(mesh):
    in_specs = (
        P(("row", "col"), None),
        P(("row", "col"), None),
        P("row", "col"),
        P("row", "col"),
        P(),
    )
    out_specs = P(("row", "col"), None)
    return jax.shard_map(
        per_device, mesh=mesh, in_specs=in_specs, out_specs=out_specs, check_vma=False
    )
```

time: 453 us -> 152 us (0.34)
  waiting for transfers between devices: 374 us -> 38.3 us
  starting transfers between devices: 6.95 us -> 51 us
  Pallas kernels: 0 us -> 42.4 us
  matrix products: 27.9 us -> 0 us
  between operations: 13.4 us -> 0.23 us
  local copies, waits for them, and re-layouts: 11 us -> 0.02 us
  blocking collectives: 13.4 us -> 18.6 us
  other arithmetic: 6.21 us -> 1.36 us
    reduce_scatter x1 -> x0, waiting for transfers between devices: 320 us -> none  [per_device(): lax.psum_scatter(partial_value, 'row', scatter_dimension=0, tiled=True)]
    ppermute x0 -> x34, starting transfers between devices: none -> 51 us  [the longest x26 32.7 us: send(): return lax.ppermute(value, 'row', pairs)]
    pallas_call x0 -> x14, Pallas kernels: none -> 42.4 us  [the longest x13 39.7 us: __call__(): pl.pallas_call(lambda *refs: kernel(refs[skipped], *refs[skipped + 1:]),...]
    ppermute x0 -> x34, waiting for transfers between devices: none -> 38.3 us  [the longest x26 31.3 us: send(): return lax.ppermute(value, 'row', pairs)]
    all_gather x1 -> x0, waiting for transfers between devices: 29.1 us -> none  [per_device(): grouped = lax.all_gather(ordered, 'col', axis=0, tiled=True)]
    dot_general x1 -> x0, matrix products: 27.9 us -> none  [per_device(): partial_value = jnp.dot(placed, weights, preferred_element_type=jnp.float32)]
    all_to_all x1 -> x0, waiting for transfers between devices: 24.2 us -> none  [per_device(): lax.all_to_all(grouped, 'row', split_axis=1, concat_axis=0, tiled=True)]
    all_to_all x1 -> x0, starting transfers between devices: 6.9 us -> none  [per_device(): lax.all_to_all(grouped, 'row', split_axis=1, concat_axis=0, tiled=True)]
  transfers between devices with their start and end apart: 3 -> 34, of which waited for: 3 -> 10; matrix products, arithmetic and copies ran while one was open for 0% -> 0% of each run, Pallas kernels for 0% -> 26%
where the time goes in v4:
time: 152 us
  starting transfers between devices  51 us (34%)
  Pallas kernels  42.4 us (28%)
  waiting for transfers between devices  38.3 us (25%)
  blocking collectives  18.6 us (12%)
    pallas_call x13, Pallas kernels, __call__(): pl.pallas_call(lambda *refs: kernel(refs[skipped], *refs[skipped + 1:]),...  39.7 us
    ppermute x26, starting transfers between devices, send(): return lax.ppermute(value, 'row', pairs)  32.7 us
    ppermute x26, waiting for transfers between devices, send(): return lax.ppermute(value, 'row', pairs)  31.3 us
    all_to_all x1, blocking collectives, per_device(): lax.all_to_all(ordered, 'row', split_axis=1, concat_axis=0, tiled=True)  18.6 us
    ppermute x6, starting transfers between devices, send_col(): return lax.ppermute(value, 'col', [(c, c ^ step) for c in range(4)])  14.9 us
    ppermute x6, waiting for transfers between devices, send_col(): return lax.ppermute(value, 'col', [(c, c ^ step) for c in range(4)])  4.48 us
    ppermute x2, starting transfers between devices, per_device(): lax.ppermute(c, ('row', 'col'), DIAGONAL)  3.43 us
  transfers between devices with their start and end apart: 34, of which 10 were waited for; matrix products, arithmetic and copies ran while one was open for 0% of the time, Pallas kernels for 26%

profile of v4, /device:TPU:1, one launch (start us, length us, event | category | flops | bytes accessed | tf_op | source)
XLA Modules:
  0.0 151.9 jit_solution(10452100064078673340)
XLA Ops:
  0.1 2.6 %arrange.1 = (bf16[8,28672]{1,0:T(8,128)(2,1)}, bf16[7,7168]{1,0:T(8,128)(2,1)S(1)}) custom-call(s32[224]{0:T(256)} %order.1, bf16[8,28672]{1,0:T(8,128)(2,1)} %values.1, s32[8,224]{1,0:T(8,128)} %flags.1, s32[7,56]{1,0:T(8,128)} %tile_flags.1), custom_call_target="tpu_custom_call" | custom-call | tf_op jit(solution)/shard_map/arrange/pallas_call | solution.py:336
  2.7 18.6 %all_to_all.19 = bf16[8,32,896]{2,0,1:T(8,128)(2,1)S(1)} all-to-all(bf16[8,32,896]{2,0,1:T(8,128)(2,1)} %bitcast.44), channel_id=1, replica_groups=mesh['row'=32,'col'=4] {'row'}, dimensions={1} | all-to-all | bytes 917504 | tf_op jit(solution)/shard_map/all_to_all | solution.py:348
  21.3 2.6 %collective-permute-start = (bf16[256,896]{1,0:T(8,128)(2,1)S(1)}, bf16[256,896]{1,0:T(8,128)(2,1)S(1)}, u32[]{:S(2)}, u32[]{:S(2)}) collective-permute-start(bf16[256,896]{1,0:T(8,128)(2,1)S(1)} %bitcast.41), channel_id=1, source_target_pairs={{0,1},{1,0},{2,3},{3,2},{4,5},{5,4},{6,7},{7,6},{8,9},{9,8},{10,11... | collective-permute-start | bytes 1376264 | tf_op jit(solution)/shard_map/ppermute | solution.py:38
  23.9 3.3 %collective-permute-start.1 = (bf16[256,896]{1,0:T(8,128)(2,1)S(1)}, bf16[256,896]{1,0:T(8,128)(2,1)S(1)}, u32[]{:S(2)}, u32[]{:S(2)}) collective-permute-start(bf16[256,896]{1,0:T(8,128)(2,1)S(1)} %bitcast.42), channel_id=1, source_target_pairs={{0,2},{1,3},{2,0},{3,1},{4,6},{5,7},{6,4},{7,5},{8,10},{9,11},{10,... | collective-permute-start | bytes 1376264 | tf_op jit(solution)/shard_map/ppermute | solution.py:38
  27.4 9.6 %begin_kernel.1 = (s16[128,3712]{1,0:T(8,128)(2,1)S(1)}, s16[128,3712]{1,0:T(8,128)(2,1)S(1)}, s16[128,3712]{1,0:T(8,128)(2,1)S(1)}, s16[128,3712]{1,0:T(8,128)(...) custom-call(bf16[256,896]{1,0:T(8,128)(2,1)S(1)} %bitcast.43, s32[3]{0:T(128)S(1)} %pad_add_fusion.refs_1_.refs_5_, ...), custom_call_target="tpu_custom_call" | custom-call | flops 1000 | bytes 1000 | tf_op jit(solution)/shard_map/begin_kernel/pallas_call | solution.py:308
  37.4 2.3 %collective-permute-start.4 = (s16[128,3712]{1,0:T(8,128)(2,1)S(1)}, s16[128,3712]{1,0:T(8,128)(2,1)S(1)}, u32[]{:S(2)}, u32[]{:S(2)}) collective-permute-start(s16[128,3712]{1,0:T(8,128)(2,1)S(1)} %get-tuple-element.71), channel_id=1, source_target_pairs={{0,48},{4,52},{8,56},{12,60},{16,0},{20,4},{24,8},{28,12},{32,16},... | collective-permute-start | bytes 2850824 | tf_op jit(solution)/shard_map/ppermute | solution.py:34
  40.8 2.5 %collective-permute-start.6 = (s16[128,3712]{1,0:T(8,128)(2,1)S(1)}, s16[128,3712]{1,0:T(8,128)(2,1)S(1)}, u32[]{:S(2)}, u32[]{:S(2)}) collective-permute-start(s16[128,3712]{1,0:T(8,128)(2,1)S(1)} %get-tuple-element.73), channel_id=1, source_target_pairs={{0,12},{4,0},{8,4},{12,8},{16,28},{20,16},{24,20},{28,24},{32,44},... | collective-permute-start | bytes 2850824 | tf_op jit(solution)/shard_map/ppermute | solution.py:34
  43.4 3.9 %far_kernel.2 = (s16[64,3712]{1,0:T(8,128)(2,1)S(1)}, s16[64,3712]{1,0:T(8,128)(2,1)S(1)}, s16[64,3712]{1,0:T(8,128)(2,1)S(1)}, s16[64,3712]{1,0:T(8,128)(2,1)S(1)}) custom-call(s16[128,3712]{1,0:T(8,128)(2,1)S(1)} %get-tuple-element.66.refs_0_, s32[3]{0:T(128)S(1)} %pad_add_fusion.refs_1_.refs_5_, bf16[896,3584]{1,0:T(8,128)(2,1)S(1)} %get-tuple-element.67.refs_2_.refs_6_, ...), custom_call_target="tpu_custom_call" | custom-call | flops 1000 | bytes 1000 | tf_op jit(solution)/shard_map/far_kernel/pallas_call | solution.py:308
  47.3 13.3 %collective-permute-done.3.refs_1_.refs_6_.refs_5_ = s16[128,3712]{1,0:T(8,128)(2,1)S(1)} collective-permute-done((s16[128,3712]{1,0:T(8,128)(2,1)S(1)}, s16[128,3712]{1,0:T(8,128)(2,1)S(1)}, u32[]{:S(2)}, u32[]{:S(2)}) %collective-permute-start.3) | collective-permute-done | bytes 950304 | tf_op jit(solution)/shard_map/ppermute | solution.py:34
  60.6 2.7 %collective-permute-start.8 = (s16[64,3712]{1,0:T(8,128)(2,1)S(1)}, s16[64,3712]{1,0:T(8,128)(2,1)S(1)}, u32[]{:S(2)}, u32[]{:S(2)}) collective-permute-start(s16[64,3712]{1,0:T(8,128)(2,1)S(1)} %get-tuple-element.77), channel_id=1, source_target_pairs={{0,48},{4,52},{8,56},{12,60},{16,0},{20,4},{24,8},{28,12},{32,16},... | collective-permute-start | bytes 1425416 | tf_op jit(solution)/shard_map/ppermute | solution.py:34
  64.5 2.7 %collective-permute-start.10 = (s16[64,3712]{1,0:T(8,128)(2,1)S(1)}, s16[64,3712]{1,0:T(8,128)(2,1)S(1)}, u32[]{:S(2)}, u32[]{:S(2)}) collective-permute-start(s16[64,3712]{1,0:T(8,128)(2,1)S(1)} %get-tuple-element.81), channel_id=1, source_target_pairs={{0,12},{4,0},{8,4},{12,8},{16,28},{20,16},{24,20},{28,24},{32,44},... | collective-permute-start | bytes 1425416 | tf_op jit(solution)/shard_map/ppermute | solution.py:34
  67.1 3.9 %far_kernel.3 = (s16[64,3712]{1,0:T(8,128)(2,1)S(1)}, s16[64,3712]{1,0:T(8,128)(2,1)S(1)}, s16[64,3712]{1,0:T(8,128)(2,1)S(1)}, s16[64,3712]{1,0:T(8,128)(2,1)S(1)}) custom-call(s16[64,3712]{1,0:T(8,128)(2,1)S(1)} %get-tuple-element.76.refs_0_, s16[128,3712]{1,0:T(8,128)(2,1)S(1)} %collective-permute-done.3.refs_1_.refs_6_.refs_5_, ...), custom_call_target="tpu_custom_call" | custom-call | flops 1000 | bytes 1000 | tf_op jit(solution)/shard_map/far_kernel/pallas_call | solution.py:308
  71.1 2.0 %collective-permute-done.7.refs_8_ = s16[64,3712]{1,0:T(8,128)(2,1)S(1)} collective-permute-done((s16[64,3712]{1,0:T(8,128)(2,1)S(1)}, s16[64,3712]{1,0:T(8,128)(2,1)S(1)}, u32[]{:S(2)}, u32[]{:S(2)}) %collective-permute-start.7) | collective-permute-done | bytes 475168 | tf_op jit(solution)/shard_map/ppermute | solution.py:34
  73.3 2.5 %collective-permute-start.12 = (s16[64,3712]{1,0:T(8,128)(2,1)S(1)}, s16[64,3712]{1,0:T(8,128)(2,1)S(1)}, u32[]{:S(2)}, u32[]{:S(2)}) collective-permute-start(s16[64,3712]{1,0:T(8,128)(2,1)S(1)} %get-tuple-element.85), channel_id=1, source_target_pairs={{0,48},{4,52},{8,56},{12,60},{16,0},{20,4},{24,8},{28,12},{32,16},... | collective-permute-start | bytes 1425416 | tf_op jit(solution)/shard_map/ppermute | solution.py:34
  77.5 2.5 %collective-permute-start.14 = (s16[64,3712]{1,0:T(8,128)(2,1)S(1)}, s16[64,3712]{1,0:T(8,128)(2,1)S(1)}, u32[]{:S(2)}, u32[]{:S(2)}) collective-permute-start(s16[64,3712]{1,0:T(8,128)(2,1)S(1)} %get-tuple-element.89), channel_id=1, source_target_pairs={{0,12},{4,0},{8,4},{12,8},{16,28},{20,16},{24,20},{28,24},{32,44},... | collective-permute-start | bytes 1425416 | tf_op jit(solution)/shard_map/ppermute | solution.py:34
  80.0 6.7 %pass_on_kernel.1 = (s16[128,3712]{1,0:T(8,128)(2,1)S(1)}, s16[128,3712]{1,0:T(8,128)(2,1)S(1)}, s16[128,3712]{1,0:T(8,128)(2,1)S(1)}, s16[128,3712]{1,0:T(8,128)(2,1)S(1)}) custom-call(s16[64,3712]{1,0:T(8,128)(2,1)S(1)} %get-tuple-element.84.refs_0_, s32[3]{0:T(128)S(1)} %pad_add_fusion.refs_1_.refs_5_, ...), custom_call_target="tpu_custom_call" | custom-call | flops 1000 | bytes 1000 | tf_op jit(solution)/shard_map/pass_on_kernel/pallas_call | solution.py:308
  86.8 2.7 %collective-permute-start.16 = (s16[128,3712]{1,0:T(8,128)(2,1)S(1)}, s16[128,3712]{1,0:T(8,128)(2,1)S(1)}, u32[]{:S(2)}, u32[]{:S(2)}) collective-permute-start(s16[128,3712]{1,0:T(8,128)(2,1)S(1)} %get-tuple-element.93), channel_id=1, source_target_pairs={{0,48},{4,52},{8,56},{12,60},{16,0},{20,4},{24,8},{28,12},{32,16},... | collective-permute-start | bytes 2850824 | tf_op jit(solution)/shard_map/ppermute | solution.py:34
  89.5 2.7 %collective-permute-start.18 = (s16[128,3712]{1,0:T(8,128)(2,1)S(1)}, s16[128,3712]{1,0:T(8,128)(2,1)S(1)}, u32[]{:S(2)}, u32[]{:S(2)}) collective-permute-start(s16[128,3712]{1,0:T(8,128)(2,1)S(1)} %get-tuple-element.99), channel_id=1, source_target_pairs={{0,12},{4,0},{8,4},{12,8},{16,28},{20,16},{24,20},{28,24},{32,44},... | collective-permute-start | bytes 2850824 | tf_op jit(solution)/shard_map/ppermute | solution.py:34
  92.2 5.5 %own_kernel.1 = (f32[256,3584]{1,0:T(8,128)S(1)}, f32[256,3584]{1,0:T(8,128)S(1)}) custom-call(s16[128,3712]{1,0:T(8,128)(2,1)S(1)} %get-tuple-element.92.refs_0_, s16[64,3712]{1,0:T(8,128)(2,1)S(1)} %collective-permute-done.11.refs_1_.refs_7_, s16[64,3712]{1,0:T(8,128)(2,1)S(1)} %collective-permute-done.12.refs_2_.refs_8_, ...), custom_call_target="tpu_custom_call" | custom-call | flops 1000 | bytes 1000 | tf_op jit(solution)/shard_map/own_kernel/pallas_call | solution.py:308
  97.7 10.6 %collective-permute-done.15.refs_3_ = s16[128,3712]{1,0:T(8,128)(2,1)S(1)} collective-permute-done((s16[128,3712]{1,0:T(8,128)(2,1)S(1)}, s16[128,3712]{1,0:T(8,128)(2,1)S(1)}, u32[]{:S(2)}, u32[]{:S(2)}) %collective-permute-start.15) | collective-permute-done | bytes 950304 | tf_op jit(solution)/shard_map/ppermute | solution.py:34
  109.5 2.7 %collective-permute-start.20 = (s16[32,3712]{1,0:T(8,128)(2,1)S(1)}, s16[32,3712]{1,0:T(8,128)(2,1)S(1)}, u32[]{:S(2)}, u32[]{:S(2)}) collective-permute-start(s16[32,3712]{1,0:T(8,128)(2,1)S(1)} %get-tuple-element.101), channel_id=1, source_target_pairs={{0,12},{4,0},{8,4},{12,8},{16,28},{20,16},{24,20},{28,24},{32,44},... | collective-permute-start | bytes 712712 | tf_op jit(solution)/shard_map/ppermute | solution.py:34
  113.5 2.7 %collective-permute-start.22 = (s16[32,3712]{1,0:T(8,128)(2,1)S(1)}, s16[32,3712]{1,0:T(8,128)(2,1)S(1)}, u32[]{:S(2)}, u32[]{:S(2)}) collective-permute-start(s16[32,3712]{1,0:T(8,128)(2,1)S(1)} %get-tuple-element.103), channel_id=1, source_target_pairs={{0,48},{4,52},{8,56},{12,60},{16,0},{20,4},{24,8},{28,12},{32,16},... | collective-permute-start | bytes 712712 | tf_op jit(solution)/shard_map/ppermute | solution.py:34
  116.1 1.8 %second_neighbour_kernel.2 = (s16[64,3712]{1,0:T(8,128)(2,1)S(1)}, s16[64,3712]{1,0:T(8,128)(2,1)S(1)}) custom-call(s16[32,3712]{1,0:T(8,128)(2,1)S(1)} %get-tuple-element.100.refs_0_, s32[3]{0:T(128)S(1)} %pad_add_fusion.refs_1_.refs_5_, f32[256,3584]{1,0:T(8,128)S(1)} %get-tuple-element.90.refs_0_.refs_2_, ...), custom_call_target="tpu_custom_call" | custom-call | flops 1000 | bytes 1000 | tf_op jit(solution)/shard_map/second_neighbour_kernel/pallas_call | solution.py:308
  118.4 2.2 %collective-permute-start.24 = (s16[64,3712]{1,0:T(8,128)(2,1)S(1)}, s16[64,3712]{1,0:T(8,128)(2,1)S(1)}, u32[]{:S(2)}, u32[]{:S(2)}) collective-permute-start(s16[64,3712]{1,0:T(8,128)(2,1)S(1)} %get-tuple-element.105), channel_id=1, source_target_pairs={{0,12},{4,0},{8,4},{12,8},{16,28},{20,16},{24,20},{28,24},{32,44},... | collective-permute-start | bytes 1425416 | tf_op jit(solution)/shard_map/ppermute | solution.py:34
  120.6 1.8 %second_neighbour_kernel.3 = (s16[64,3712]{1,0:T(8,128)(2,1)S(1)}, s16[64,3712]{1,0:T(8,128)(2,1)S(1)}) custom-call(s16[64,3712]{1,0:T(8,128)(2,1)S(1)} %get-tuple-element.102.refs_0_, s32[3]{0:T(128)S(1)} %pad_add_fusion.refs_1_.refs_5_, f32[256,3584]{1,0:T(8,128)S(1)} %get-tuple-element.95.refs_2_, s16[128,3712]{1,0:T(8,128)(2,1)S(1)} %collective-permute-done.17.refs_3_, ...), custom_call_target="tpu_custom_call" | custom-call | flops 1000 | bytes 1000 | tf_op jit(solution)/shard_map/second_neighbour_kernel/pallas_call | solution.py:308
  122.5 2.7 %collective-permute-start.26 = (s16[64,3712]{1,0:T(8,128)(2,1)S(1)}, s16[64,3712]{1,0:T(8,128)(2,1)S(1)}, u32[]{:S(2)}, u32[]{:S(2)}) collective-permute-start(s16[64,3712]{1,0:T(8,128)(2,1)S(1)} %get-tuple-element.107), channel_id=1, source_target_pairs={{0,48},{4,52},{8,56},{12,60},{16,0},{20,4},{24,8},{28,12},{32,16},... | collective-permute-start | bytes 1425416 | tf_op jit(solution)/shard_map/ppermute | solution.py:34
  125.2 2.1 %collective-permute-done.23.refs_9_ = s16[64,3712]{1,0:T(8,128)(2,1)S(1)} collective-permute-done((s16[64,3712]{1,0:T(8,128)(2,1)S(1)}, s16[64,3712]{1,0:T(8,128)(2,1)S(1)}, u32[]{:S(2)}, u32[]{:S(2)}) %collective-permute-start.23) | collective-permute-done | bytes 475168 | tf_op jit(solution)/shard_map/ppermute | solution.py:34
  128.8 2.1 %collective-permute-start.28 = (s16[16,3840]{1,0:T(8,128)(2,1)S(1)}, s16[16,3840]{1,0:T(8,128)(2,1)S(1)}, u32[]{:S(2)}, u32[]{:S(2)}) collective-permute-start(s16[16,3840]{1,0:T(8,128)(2,1)S(1)} %get-tuple-element.110), channel_id=1, source_target_pairs={{0,2},{1,3},{2,0},{3,1},{4,6},{5,7},{6,4},{7,5},{8,10},{9,11},{10,... | collective-permute-start | bytes 368648 | tf_op jit(solution)/shard_map/ppermute | solution.py:38
  134.3 2.1 %collective-permute-start.31 = (s16[16,3840]{1,0:T(8,128)(2,1)S(1)}, s16[16,3840]{1,0:T(8,128)(2,1)S(1)}, u32[]{:S(2)}, u32[]{:S(2)}) collective-permute-start(s16[16,3840]{1,0:T(8,128)(2,1)S(1)} %get-tuple-element.114), channel_id=1, source_target_pairs={{0,2},{1,3},{2,0},{3,1},{4,6},{5,7},{6,4},{7,5},{8,10},{9,11},{10,... | collective-permute-start | bytes 368648 | tf_op jit(solution)/shard_map/ppermute | solution.py:38
  139.4 3.4 %collective-permute-done.31.refs_4_ = s16[16,3840]{1,0:T(8,128)(2,1)S(1)} collective-permute-done((s16[16,3840]{1,0:T(8,128)(2,1)S(1)}, s16[16,3840]{1,0:T(8,128)(2,1)S(1)}, u32[]{:S(2)}, u32[]{:S(2)}) %collective-permute-start.31) | collective-permute-done | bytes 122912 | tf_op jit(solution)/shard_map/ppermute | solution.py:38
  142.7 2.5 %collective-permute-done.32.refs_5_ = s16[16,3840]{1,0:T(8,128)(2,1)S(1)} collective-permute-done((s16[16,3840]{1,0:T(8,128)(2,1)S(1)}, s16[16,3840]{1,0:T(8,128)(2,1)S(1)}, u32[]{:S(2)}, u32[]{:S(2)}) %collective-permute-start.32) | collective-permute-done | bytes 122912 | tf_op jit(solution)/shard_map/ppermute | solution.py:419
  146.0 3.9 %collective-permute-start.33 = (bf16[8,14336]{1,0:T(8,128)(2,1)S(1)}, bf16[8,14336]{1,0:T(8,128)(2,1)S(1)}, u32[]{:S(2)}, u32[]{:S(2)}) collective-permute-start(bf16[8,14336]{1,0:T(8,128)(2,1)S(1)} %dynamic-slice_bitcast_fusion), channel_id=1, source_target_pairs={{0,1},{1,0},{2,3},{3,2},{4,5},{5,4},{6,7},{7,6},{8,9},{9,8},{10,11... | collective-permute-start | bytes 688136 | tf_op jit(solution)/shard_map/ppermute | solution.py:38
  (61 shorter events, 18.8 us)
Async XLA Ops:
  21.3 5.9 %collective-permute-start = (bf16[256,896]{1,0:T(8,128)(2,1)S(1)}, bf16[256,896]{1,0:T(8,128)(2,1)S(1)}, u32[]{:S(2)}, u32[]{:S(2)}) collective-permute-start(bf16[256,896]{1,0:T(8,128)(2,1)S(1)} %bitcast.41), channel_id=1, source_target_pairs={{0,1},{1,0},{2,3},{3,2},{4,5},{5,4},{6,7},{7,6},{8,9},{9,8},{10,11... | collective-permute-start | bytes 1376264 | tf_op jit(solution)/shard_map/ppermute | solution.py:38
  23.9 15.8 %collective-permute-start.1 = (bf16[256,896]{1,0:T(8,128)(2,1)S(1)}, bf16[256,896]{1,0:T(8,128)(2,1)S(1)}, u32[]{:S(2)}, u32[]{:S(2)}) collective-permute-start(bf16[256,896]{1,0:T(8,128)(2,1)S(1)} %bitcast.42), channel_id=1, source_target_pairs={{0,2},{1,3},{2,0},{3,1},{4,6},{5,7},{6,4},{7,5},{8,10},{9,11},{10,... | collective-permute-start | bytes 1376264 | tf_op jit(solution)/shard_map/ppermute | solution.py:38
  37.0 23.6 %collective-permute-start.3 = (s16[128,3712]{1,0:T(8,128)(2,1)S(1)}, s16[128,3712]{1,0:T(8,128)(2,1)S(1)}, u32[]{:S(2)}, u32[]{:S(2)}) collective-permute-start(s16[128,3712]{1,0:T(8,128)(2,1)S(1)} %get-tuple-element.66.refs_0_), channel_id=1, source_target_pairs={{0,16},{4,20},{8,24},{12,28},{16,32},{20,36},{24,40},{28,44},{32,4... | collective-permute-start | bytes 2850824 | tf_op jit(solution)/shard_map/ppermute | solution.py:34
  37.4 23.2 %collective-permute-start.4 = (s16[128,3712]{1,0:T(8,128)(2,1)S(1)}, s16[128,3712]{1,0:T(8,128)(2,1)S(1)}, u32[]{:S(2)}, u32[]{:S(2)}) collective-permute-start(s16[128,3712]{1,0:T(8,128)(2,1)S(1)} %get-tuple-element.71), channel_id=1, source_target_pairs={{0,48},{4,52},{8,56},{12,60},{16,0},{20,4},{24,8},{28,12},{32,16},... | collective-permute-start | bytes 2850824 | tf_op jit(solution)/shard_map/ppermute | solution.py:34
  40.6 23.9 %collective-permute-start.5 = (s16[128,3712]{1,0:T(8,128)(2,1)S(1)}, s16[128,3712]{1,0:T(8,128)(2,1)S(1)}, u32[]{:S(2)}, u32[]{:S(2)}) collective-permute-start(s16[128,3712]{1,0:T(8,128)(2,1)S(1)} %get-tuple-element.72), channel_id=1, source_target_pairs={{0,4},{4,8},{8,12},{12,0},{16,20},{20,24},{24,28},{28,16},{32,36},... | collective-permute-start | bytes 2850824 | tf_op jit(solution)/shard_map/ppermute | solution.py:34
  40.8 23.7 %collective-permute-start.6 = (s16[128,3712]{1,0:T(8,128)(2,1)S(1)}, s16[128,3712]{1,0:T(8,128)(2,1)S(1)}, u32[]{:S(2)}, u32[]{:S(2)}) collective-permute-start(s16[128,3712]{1,0:T(8,128)(2,1)S(1)} %get-tuple-element.73), channel_id=1, source_target_pairs={{0,12},{4,0},{8,4},{12,8},{16,28},{20,16},{24,20},{28,24},{32,44},... | collective-permute-start | bytes 2850824 | tf_op jit(solution)/shard_map/ppermute | solution.py:34
  60.6 12.5 %collective-permute-start.7 = (s16[64,3712]{1,0:T(8,128)(2,1)S(1)}, s16[64,3712]{1,0:T(8,128)(2,1)S(1)}, u32[]{:S(2)}, u32[]{:S(2)}) collective-permute-start(s16[64,3712]{1,0:T(8,128)(2,1)S(1)} %get-tuple-element.76.refs_0_), channel_id=1, source_target_pairs={{0,16},{4,20},{8,24},{12,28},{16,32},{20,36},{24,40},{28,44},{32,4... | collective-permute-start | bytes 1425416 | tf_op jit(solution)/shard_map/ppermute | solution.py:34
  60.6 12.5 %collective-permute-start.8 = (s16[64,3712]{1,0:T(8,128)(2,1)S(1)}, s16[64,3712]{1,0:T(8,128)(2,1)S(1)}, u32[]{:S(2)}, u32[]{:S(2)}) collective-permute-start(s16[64,3712]{1,0:T(8,128)(2,1)S(1)} %get-tuple-element.77), channel_id=1, source_target_pairs={{0,48},{4,52},{8,56},{12,60},{16,0},{20,4},{24,8},{28,12},{32,16},... | collective-permute-start | bytes 1425416 | tf_op jit(solution)/shard_map/ppermute | solution.py:34
  64.5 12.8 %collective-permute-start.9 = (s16[64,3712]{1,0:T(8,128)(2,1)S(1)}, s16[64,3712]{1,0:T(8,128)(2,1)S(1)}, u32[]{:S(2)}, u32[]{:S(2)}) collective-permute-start(s16[64,3712]{1,0:T(8,128)(2,1)S(1)} %get-tuple-element.80), channel_id=1, source_target_pairs={{0,4},{4,8},{8,12},{12,0},{16,20},{20,24},{24,28},{28,16},{32,36},... | collective-permute-start | bytes 1425416 | tf_op jit(solution)/shard_map/ppermute | solution.py:34
  64.5 12.8 %collective-permute-start.10 = (s16[64,3712]{1,0:T(8,128)(2,1)S(1)}, s16[64,3712]{1,0:T(8,128)(2,1)S(1)}, u32[]{:S(2)}, u32[]{:S(2)}) collective-permute-start(s16[64,3712]{1,0:T(8,128)(2,1)S(1)} %get-tuple-element.81), channel_id=1, source_target_pairs={{0,12},{4,0},{8,4},{12,8},{16,28},{20,16},{24,20},{28,24},{32,44},... | collective-permute-start | bytes 1425416 | tf_op jit(solution)/shard_map/ppermute | solution.py:34
  73.1 13.6 %collective-permute-start.11 = (s16[64,3712]{1,0:T(8,128)(2,1)S(1)}, s16[64,3712]{1,0:T(8,128)(2,1)S(1)}, u32[]{:S(2)}, u32[]{:S(2)}) collective-permute-start(s16[64,3712]{1,0:T(8,128)(2,1)S(1)} %get-tuple-element.84.refs_0_), channel_id=1, source_target_pairs={{0,16},{4,20},{8,24},{12,28},{16,32},{20,36},{24,40},{28,44},{32,4... | collective-permute-start | bytes 1425416 | tf_op jit(solution)/shard_map/ppermute | solution.py:34
  73.3 13.4 %collective-permute-start.12 = (s16[64,3712]{1,0:T(8,128)(2,1)S(1)}, s16[64,3712]{1,0:T(8,128)(2,1)S(1)}, u32[]{:S(2)}, u32[]{:S(2)}) collective-permute-start(s16[64,3712]{1,0:T(8,128)(2,1)S(1)} %get-tuple-element.85), channel_id=1, source_target_pairs={{0,48},{4,52},{8,56},{12,60},{16,0},{20,4},{24,8},{28,12},{32,16},... | collective-permute-start | bytes 1425416 | tf_op jit(solution)/shard_map/ppermute | solution.py:34
  77.3 12.2 %collective-permute-start.13 = (s16[64,3712]{1,0:T(8,128)(2,1)S(1)}, s16[64,3712]{1,0:T(8,128)(2,1)S(1)}, u32[]{:S(2)}, u32[]{:S(2)}) collective-permute-start(s16[64,3712]{1,0:T(8,128)(2,1)S(1)} %get-tuple-element.88), channel_id=1, source_target_pairs={{0,4},{4,8},{8,12},{12,0},{16,20},{20,24},{24,28},{28,16},{32,36},... | collective-permute-start | bytes 1425416 | tf_op jit(solution)/shard_map/ppermute | solution.py:34
  77.5 12.0 %collective-permute-start.14 = (s16[64,3712]{1,0:T(8,128)(2,1)S(1)}, s16[64,3712]{1,0:T(8,128)(2,1)S(1)}, u32[]{:S(2)}, u32[]{:S(2)}) collective-permute-start(s16[64,3712]{1,0:T(8,128)(2,1)S(1)} %get-tuple-element.89), channel_id=1, source_target_pairs={{0,12},{4,0},{8,4},{12,8},{16,28},{20,16},{24,20},{28,24},{32,44},... | collective-permute-start | bytes 1425416 | tf_op jit(solution)/shard_map/ppermute | solution.py:34
  86.7 21.6 %collective-permute-start.15 = (s16[128,3712]{1,0:T(8,128)(2,1)S(1)}, s16[128,3712]{1,0:T(8,128)(2,1)S(1)}, u32[]{:S(2)}, u32[]{:S(2)}) collective-permute-start(s16[128,3712]{1,0:T(8,128)(2,1)S(1)} %get-tuple-element.92.refs_0_), channel_id=1, source_target_pairs={{0,16},{4,20},{8,24},{12,28},{16,32},{20,36},{24,40},{28,44},{32,4... | collective-permute-start | bytes 2850824 | tf_op jit(solution)/shard_map/ppermute | solution.py:34
  86.8 21.5 %collective-permute-start.16 = (s16[128,3712]{1,0:T(8,128)(2,1)S(1)}, s16[128,3712]{1,0:T(8,128)(2,1)S(1)}, u32[]{:S(2)}, u32[]{:S(2)}) collective-permute-start(s16[128,3712]{1,0:T(8,128)(2,1)S(1)} %get-tuple-element.93), channel_id=1, source_target_pairs={{0,48},{4,52},{8,56},{12,60},{16,0},{20,4},{24,8},{28,12},{32,16},... | collective-permute-start | bytes 2850824 | tf_op jit(solution)/shard_map/ppermute | solution.py:34
  89.5 22.7 %collective-permute-start.17 = (s16[128,3712]{1,0:T(8,128)(2,1)S(1)}, s16[128,3712]{1,0:T(8,128)(2,1)S(1)}, u32[]{:S(2)}, u32[]{:S(2)}) collective-permute-start(s16[128,3712]{1,0:T(8,128)(2,1)S(1)} %get-tuple-element.98), channel_id=1, source_target_pairs={{0,4},{4,8},{8,12},{12,0},{16,20},{20,24},{24,28},{28,16},{32,36},... | collective-permute-start | bytes 2850824 | tf_op jit(solution)/shard_map/ppermute | solution.py:34
  89.5 22.7 %collective-permute-start.18 = (s16[128,3712]{1,0:T(8,128)(2,1)S(1)}, s16[128,3712]{1,0:T(8,128)(2,1)S(1)}, u32[]{:S(2)}, u32[]{:S(2)}) collective-permute-start(s16[128,3712]{1,0:T(8,128)(2,1)S(1)} %get-tuple-element.99), channel_id=1, source_target_pairs={{0,12},{4,0},{8,4},{12,8},{16,28},{20,16},{24,20},{28,24},{32,44},... | collective-permute-start | bytes 2850824 | tf_op jit(solution)/shard_map/ppermute | solution.py:34
  109.5 6.7 %collective-permute-start.19 = (s16[32,3712]{1,0:T(8,128)(2,1)S(1)}, s16[32,3712]{1,0:T(8,128)(2,1)S(1)}, u32[]{:S(2)}, u32[]{:S(2)}) collective-permute-start(s16[32,3712]{1,0:T(8,128)(2,1)S(1)} %get-tuple-element.94.refs_0_), channel_id=1, source_target_pairs={{0,4},{4,8},{8,12},{12,0},{16,20},{20,24},{24,28},{28,16},{32,36},... | collective-permute-start | bytes 712712 | tf_op jit(solution)/shard_map/ppermute | solution.py:34
  109.5 6.6 %collective-permute-start.20 = (s16[32,3712]{1,0:T(8,128)(2,1)S(1)}, s16[32,3712]{1,0:T(8,128)(2,1)S(1)}, u32[]{:S(2)}, u32[]{:S(2)}) collective-permute-start(s16[32,3712]{1,0:T(8,128)(2,1)S(1)} %get-tuple-element.101), channel_id=1, source_target_pairs={{0,12},{4,0},{8,4},{12,8},{16,28},{20,16},{24,20},{28,24},{32,44},... | collective-permute-start | bytes 712712 | tf_op jit(solution)/shard_map/ppermute | solution.py:34
  113.4 7.3 %collective-permute-start.21 = (s16[32,3712]{1,0:T(8,128)(2,1)S(1)}, s16[32,3712]{1,0:T(8,128)(2,1)S(1)}, u32[]{:S(2)}, u32[]{:S(2)}) collective-permute-start(s16[32,3712]{1,0:T(8,128)(2,1)S(1)} %get-tuple-element.100.refs_0_), channel_id=1, source_target_pairs={{0,16},{4,20},{8,24},{12,28},{16,32},{20,36},{24,40},{28,44},{32,4... | collective-permute-start | bytes 712712 | tf_op jit(solution)/shard_map/ppermute | solution.py:34
  113.5 7.2 %collective-permute-start.22 = (s16[32,3712]{1,0:T(8,128)(2,1)S(1)}, s16[32,3712]{1,0:T(8,128)(2,1)S(1)}, u32[]{:S(2)}, u32[]{:S(2)}) collective-permute-start(s16[32,3712]{1,0:T(8,128)(2,1)S(1)} %get-tuple-element.103), channel_id=1, source_target_pairs={{0,48},{4,52},{8,56},{12,60},{16,0},{20,4},{24,8},{28,12},{32,16},... | collective-permute-start | bytes 712712 | tf_op jit(solution)/shard_map/ppermute | solution.py:34
  117.9 9.4 %collective-permute-start.23 = (s16[64,3712]{1,0:T(8,128)(2,1)S(1)}, s16[64,3712]{1,0:T(8,128)(2,1)S(1)}, u32[]{:S(2)}, u32[]{:S(2)}) collective-permute-start(s16[64,3712]{1,0:T(8,128)(2,1)S(1)} %get-tuple-element.102.refs_0_), channel_id=1, source_target_pairs={{0,4},{4,8},{8,12},{12,0},{16,20},{20,24},{24,28},{28,16},{32,36},... | collective-permute-start | bytes 1425416 | tf_op jit(solution)/shard_map/ppermute | solution.py:34
  118.4 8.8 %collective-permute-start.24 = (s16[64,3712]{1,0:T(8,128)(2,1)S(1)}, s16[64,3712]{1,0:T(8,128)(2,1)S(1)}, u32[]{:S(2)}, u32[]{:S(2)}) collective-permute-start(s16[64,3712]{1,0:T(8,128)(2,1)S(1)} %get-tuple-element.105), channel_id=1, source_target_pairs={{0,12},{4,0},{8,4},{12,8},{16,28},{20,16},{24,20},{28,24},{32,44},... | collective-permute-start | bytes 1425416 | tf_op jit(solution)/shard_map/ppermute | solution.py:34
  122.4 10.3 %collective-permute-start.25 = (s16[64,3712]{1,0:T(8,128)(2,1)S(1)}, s16[64,3712]{1,0:T(8,128)(2,1)S(1)}, u32[]{:S(2)}, u32[]{:S(2)}) collective-permute-start(s16[64,3712]{1,0:T(8,128)(2,1)S(1)} %get-tuple-element.104.refs_0_), channel_id=1, source_target_pairs={{0,16},{4,20},{8,24},{12,28},{16,32},{20,36},{24,40},{28,44},{32,4... | collective-permute-start | bytes 1425416 | tf_op jit(solution)/shard_map/ppermute | solution.py:34
  122.5 10.2 %collective-permute-start.26 = (s16[64,3712]{1,0:T(8,128)(2,1)S(1)}, s16[64,3712]{1,0:T(8,128)(2,1)S(1)}, u32[]{:S(2)}, u32[]{:S(2)}) collective-permute-start(s16[64,3712]{1,0:T(8,128)(2,1)S(1)} %get-tuple-element.107), channel_id=1, source_target_pairs={{0,48},{4,52},{8,56},{12,60},{16,0},{20,4},{24,8},{28,12},{32,16},... | collective-permute-start | bytes 1425416 | tf_op jit(solution)/shard_map/ppermute | solution.py:34
  128.7 7.7 %collective-permute-start.27 = (s16[16,3840]{1,0:T(8,128)(2,1)S(1)}, s16[16,3840]{1,0:T(8,128)(2,1)S(1)}, u32[]{:S(2)}, u32[]{:S(2)}) collective-permute-start(s16[16,3840]{1,0:T(8,128)(2,1)S(1)} %get-tuple-element.106.refs_0_), channel_id=1, source_target_pairs={{0,64},{4,68},{8,72},{12,76},{16,80},{20,84},{24,88},{28,92},{32,9... | collective-permute-start | bytes 368648 | tf_op jit(solution)/shard_map/ppermute | solution.py:34
  128.8 9.3 %collective-permute-start.28 = (s16[16,3840]{1,0:T(8,128)(2,1)S(1)}, s16[16,3840]{1,0:T(8,128)(2,1)S(1)}, u32[]{:S(2)}, u32[]{:S(2)}) collective-permute-start(s16[16,3840]{1,0:T(8,128)(2,1)S(1)} %get-tuple-element.110), channel_id=1, source_target_pairs={{0,2},{1,3},{2,0},{3,1},{4,6},{5,7},{6,4},{7,5},{8,10},{9,11},{10,... | collective-permute-start | bytes 368648 | tf_op jit(solution)/shard_map/ppermute | solution.py:38
  131.0 7.2 %collective-permute-start.29 = (s16[16,3840]{1,0:T(8,128)(2,1)S(1)}, s16[16,3840]{1,0:T(8,128)(2,1)S(1)}, u32[]{:S(2)}, u32[]{:S(2)}) collective-permute-start(s16[16,3840]{1,0:T(8,128)(2,1)S(1)} %get-tuple-element.111), channel_id=1, source_target_pairs={{0,66},{1,67},{2,64},{3,65},{4,70},{5,71},{6,68},{7,69},{8,74},{9,... | collective-permute-start | bytes 368648 | tf_op jit(solution)/shard_map/ppermute | solution.py:419
  134.2 5.2 %collective-permute-start.30 = (s16[16,3840]{1,0:T(8,128)(2,1)S(1)}, s16[16,3840]{1,0:T(8,128)(2,1)S(1)}, u32[]{:S(2)}, u32[]{:S(2)}) collective-permute-start(s16[16,3840]{1,0:T(8,128)(2,1)S(1)} %get-tuple-element.108.refs_0_), channel_id=1, source_target_pairs={{0,64},{4,68},{8,72},{12,76},{16,80},{20,84},{24,88},{28,92},{32,9... | collective-permute-start | bytes 368648 | tf_op jit(solution)/shard_map/ppermute | solution.py:34
  134.3 8.5 %collective-permute-start.31 = (s16[16,3840]{1,0:T(8,128)(2,1)S(1)}, s16[16,3840]{1,0:T(8,128)(2,1)S(1)}, u32[]{:S(2)}, u32[]{:S(2)}) collective-permute-start(s16[16,3840]{1,0:T(8,128)(2,1)S(1)} %get-tuple-element.114), channel_id=1, source_target_pairs={{0,2},{1,3},{2,0},{3,1},{4,6},{5,7},{6,4},{7,5},{8,10},{9,11},{10,... | collective-permute-start | bytes 368648 | tf_op jit(solution)/shard_map/ppermute | solution.py:38
  136.4 8.9 %collective-permute-start.32 = (s16[16,3840]{1,0:T(8,128)(2,1)S(1)}, s16[16,3840]{1,0:T(8,128)(2,1)S(1)}, u32[]{:S(2)}, u32[]{:S(2)}) collective-permute-start(s16[16,3840]{1,0:T(8,128)(2,1)S(1)} %get-tuple-element.115), channel_id=1, source_target_pairs={{0,66},{1,67},{2,64},{3,65},{4,70},{5,71},{6,68},{7,69},{8,74},{9,... | collective-permute-start | bytes 368648 | tf_op jit(solution)/shard_map/ppermute | solution.py:419
  (2 other events, 8.6 us)

commit v5 on v4

--- a/solution.py
+++ b/solution.py
@@ -162,14 +162,28 @@
         finish(q, code_refs[2 * kind + 1])
 
 
-def own_kernel(pos, w0, w1, near, far, own0, own1, left):
-    for kind, w, own in ((0, w0, own0), (1, w1, own1)):
+def own_kernel(pos, w0, w1, near, far, *refs):
+    got, outs, left, factor_refs = refs[:8], refs[8:10], refs[10], refs[11:]
+    for ref, factor in zip(got, factor_refs):
+        read_factors(ref, factor)
+    for kind, w, own in ((0, w0, outs[0]), (1, w1, outs[1])):
         for z in range(2):
             copy_rows((near, far), left, z * 128, kind, pos[1 + kind], z)
 
         @each_tile(w.shape[1], 2)
         def _(t):
-            own[:, columns_of(t)] = dot(left[...], w[:, columns_of(t)])
+            sums = dot(left[...], w[:, columns_of(t)])
+            for z in range(2):
+                parts = [
+                    decode(got[4 * kind + at + 1 - z], factor_refs[4 * kind + at + 1 - z], t, slice(start, start + 64))
+                    for at, start in ((0, 64), (2, 0))
+                ]
+                value = sums[z * 128:z * 128 + 128] + mixed(*parts)
+                own[z * 128:z * 128 + 128, columns_of(t)] = value
+
+
+def mixed(near, far):
+    return jnp.concatenate([part[at:at + 16] for at in range(0, 64, 16) for part in (near, far)], axis=0)
 
 
 def read_factors(ref, factor_ref):
@@ -202,10 +216,7 @@
             sums = dot(left[...], w[:, columns_of(t)])
             for way in range(2):
                 n, f = (decode(got[2 * part + way], scale[2 * part + way], t, slice(0, 64)) for part in range(2))
-                mixed = []
-                for second in range(4):
-                    mixed += [n[second * 16:second * 16 + 16], f[second * 16:second * 16 + 16]]
-                value = sums[way * 128:way * 128 + 128] + jnp.concatenate(mixed, axis=0)
+                value = sums[way * 128:way * 128 + 128] + mixed(n, f)
                 encode(value, t, outs[2 * kind + way], code_refs[2 * kind + way])
 
         for way in range(2):
@@ -213,22 +224,16 @@
 
 
 def stage_one(refs, factor_refs, second, t):
-    own, dp, dq, np, nq, ip, iq = refs
-    fdp, fdq, fnp, fnq, fip, fiq = factor_refs
-    here, above = (pl.ds(pl.multiple_of(z * 128 + second * 32, 32), 32) for z in range(2))
-    near, far = (pl.ds(pl.multiple_of(start + second * 16, 16), 16) for start in (64, 0))
-
-    def free(n, fn, f, ff):
-        return jnp.concatenate([decode(n, fn, t, near), decode(f, ff, t, far)], axis=0)
-
+    own, *got = refs
+    here = pl.ds(pl.multiple_of(second * 32, 32), 32)
     return [
-        own[here, columns_of(t)] + decode(dp, fdp, t, here) + free(nq, fnq, iq, fiq),
-        own[above, columns_of(t)] + decode(dq, fdq, t, here) + free(np, fnp, ip, fip),
+        own[pl.ds(pl.multiple_of(z * 128 + second * 32, 32), 32), columns_of(t)] + decode(got[z], factor_refs[z], t, here)
+        for z in range(2)
     ]
 
 
 def second_opposite_kernel(kind, pos, *refs):
-    some, outs, factor_refs, code_refs = refs[:7], refs[7:9], refs[9:15], refs[15:]
+    some, outs, factor_refs, code_refs = refs[:3], refs[3:5], refs[5:7], refs[7:]
     clear(*code_refs)
     for ref, factor in zip(some[1:], factor_refs):
         read_factors(ref, factor)
@@ -244,16 +249,16 @@
 
 
 def second_neighbour_kernel(kind, pos, *refs):
-    some, got, outs, factor_refs, code_refs = refs[:7], refs[7:9], refs[9:11], refs[11:19], refs[19:]
-    clear(*code_refs)
-    for ref, factor in zip(refs[1:9], factor_refs):
+    some, got, outs, factor_refs, code_refs = refs[:3], refs[3:5], refs[5:7], refs[7:11], refs[11:]
+    clear(*code_refs)
+    for ref, factor in zip(refs[1:5], factor_refs):
         read_factors(ref, factor)
 
     @each_tile(some[0].shape[1], 2)
     def _(t):
         for way in range(2):
-            sums = stage_one(some, factor_refs[:6], (pos[2 - kind] + (1 if way == 0 else 3)) % 4, t)
-            sums[way] = sums[way] + decode(got[way], factor_refs[6 + way], t)
+            sums = stage_one(some, factor_refs[:2], (pos[2 - kind] + (1 if way == 0 else 3)) % 4, t)
+            sums[way] = sums[way] + decode(got[way], factor_refs[2 + way], t)
             encode(jnp.concatenate(sums, axis=0), t, outs[way], code_refs[way])
 
     for way in range(2):
@@ -261,10 +266,10 @@
 
 
 def spread_kernel(kind, pos, *refs):
-    some, got, outs, sums, factor_refs, code_refs = refs[:7], refs[7:9], refs[9:13], refs[13], refs[14:22], refs[22:]
+    some, got, outs, sums, factor_refs, code_refs = refs[:3], refs[3:5], refs[5:9], refs[9], refs[10:14], refs[14:]
     clear(*code_refs)
     z = pos[0]
-    for ref, factor in zip(refs[1:9], factor_refs):
+    for ref, factor in zip(refs[1:5], factor_refs):
         read_factors(ref, factor)
 
     def rows(h, far):
@@ -272,8 +277,8 @@
 
     @each_tile(some[0].shape[1], 2)
     def _(t):
-        value = jnp.concatenate(stage_one(some, factor_refs[:6], pos[2 - kind], t), axis=0)
-        sums[...] = value + decode(got[0], factor_refs[6], t) + decode(got[1], factor_refs[7], t)
+        value = jnp.concatenate(stage_one(some, factor_refs[:2], pos[2 - kind], t), axis=0)
+        sums[...] = value + decode(got[0], factor_refs[2], t) + decode(got[1], factor_refs[3], t)
         for at, (h, far) in enumerate(((1 - z, 0), (z, 1), (1 - z, 1))):
             encode(rows(h, far), t, outs[at], code_refs[at])
         outs[3][:, columns_of(t)] = rows(z, 0)
@@ -296,9 +301,14 @@
 COST = pl.CostEstimate(flops=1000, bytes_accessed=1000, transcendentals=0)
 
 
+def position():
+    row = lax.axis_index("row")
+    return row // 16, (row // 4) % 4, row % 4
+
+
 class Calls:
-    def __init__(self, pos, first):
-        self.pos, self.last = pos, first
+    def __init__(self, first):
+        self.last = first
 
     def __call__(self, kernel, values, outs, scratch=(), after=(), in_hbm=(), limit=VMEM_LIMIT):
         after = [self.last, *after]
@@ -306,9 +316,8 @@
         name = kernel.func.__name__ if isinstance(kernel, functools.partial) else kernel.__name__
         vmem = pl.BlockSpec(memory_space=pltpu.VMEM)
         results = pl.pallas_call(
-            lambda *refs: kernel(refs[skipped], *refs[skipped + 1:]),
+            lambda *refs: kernel(position(), *refs[skipped:]),
             in_specs=[pl.BlockSpec(memory_space=pl.ANY)] * skipped
-            + [pl.BlockSpec(memory_space=pltpu.SMEM)]
             + [pl.BlockSpec(memory_space=pltpu.HBM)] * len(in_hbm) + [vmem] * len(values),
             out_specs=[vmem] * len(outs),
             out_shape=outs,
@@ -316,7 +325,7 @@
             compiler_params=pltpu.CompilerParams(vmem_limit_bytes=limit),
             cost_estimate=COST,
             name=name,
-        )(*after, self.pos, *in_hbm, *values)
+        )(*after, *in_hbm, *values)
         self.last = results[0]
         return results
 
@@ -329,9 +338,8 @@
     pair_count, full_width = amplitudes.shape
     depth, columns = integrals.shape
     width = columns // 2
-    row, col = lax.axis_index("row"), lax.axis_index("col")
+    col = lax.axis_index("col")
     core, z_hi = col % 2, col // 2
-    pos = jnp.stack([row // 16, (row // 4) % 4, row % 4]).astype(jnp.int32)
 
     ordered, flags = pl.pallas_call(
         arrange_kernel,
@@ -344,7 +352,6 @@
         scratch_shapes=[pltpu.VMEM((pair_count, full_width), jnp.bfloat16)],
         name="arrange",
     )(tile_order, amplitudes, amplitude_mask, integral_mask)
-    ordered, pos = lax.optimization_barrier((ordered, pos))
     placed = lax.all_to_all(ordered, "row", split_axis=1, concat_axis=0, tiled=True)
 
     def both_cores(mine, other):
@@ -360,7 +367,7 @@
     def floats(rows):
         return jax.ShapeDtypeStruct((rows, width), jnp.float32)
 
-    call = Calls(pos, placed)
+    call = Calls(placed)
 
     def kept(rows):
         return pltpu.VMEM((rows, width), jnp.float32)
@@ -397,26 +404,28 @@
     d = exchange_both(
         call(pass_on_kernel, weights + [near, far] + operands, [sent(128)] * 4, left_rows(256) + scales(12)), i
     )
-    own = call(own_kernel, weights + [near, far], [kept(256)] * 2, left_rows(256), i)
+    operands = [v for k in range(2) for v in (*n[2 * k:2 * k + 2], *i[2 * k:2 * k + 2])]
+    own = call(own_kernel, weights + [near, far] + operands, [kept(256)] * 2, left_rows(256) + scales(8))
 
     def stage_one_of(kind):
-        return [own[kind]] + [v for part in (d, n, i) for v in part[2 * kind:2 * kind + 2]]
+        return [own[kind], *d[2 * kind:2 * kind + 2]]
 
     got = [None, None]
     for k in range(2):
-        p, q = call(functools.partial(second_opposite_kernel, k), stage_one_of(k), [sent(32)] * 2, scales(8))
+        p, q = call(functools.partial(second_opposite_kernel, k), stage_one_of(k), [sent(32)] * 2, scales(4))
         got[k] = send(p, FORWARD[1 - k]), send(q, BACKWARD[1 - k])
     for k in range(2):
         p, q = call(
-            functools.partial(second_neighbour_kernel, k), stage_one_of(k) + [*got[k]], [sent(64)] * 2, scales(10)
+            functools.partial(second_neighbour_kernel, k), stage_one_of(k) + [*got[k]], [sent(64)] * 2, scales(6)
         )
         got[k] = send(p, FORWARD[1 - k]), send(q, BACKWARD[1 - k])
     for k in range(2):
         a, b, c, rest = call(
             functools.partial(spread_kernel, k), stage_one_of(k) + [*got[k]], [sent(16)] * 3 + [floats(16)],
-            [pltpu.VMEM((64, TILE), jnp.float32)] + scales(11),
+            [pltpu.VMEM((64, TILE), jnp.float32)] + scales(7),
         )
-        got[k] = rest, send(a, ACROSS), send_col(b, 2), lax.ppermute(c, ("row", "col"), DIAGONAL)
+        b, c = send_col(b, 2), lax.ppermute(c, ("row", "col"), DIAGONAL)
+        got[k] = rest, send(a, ACROSS), b, c
     outs = []
     for k in range(2):
         outs.append(call(last_kernel, [*got[k]], [jax.ShapeDtypeStruct((16, width), jnp.bfloat16)] * 2, scales(3)))

time: 152 us -> 149 us (0.980)
  Pallas kernels: 42.4 us -> 34.2 us
  waiting for transfers between devices: 38.3 us -> 45.9 us
  starting transfers between devices: 51 us -> 48.9 us
    pallas_call x13, Pallas kernels: 39.7 us -> 31.5 us  [__call__(): pl.pallas_call(lambda *refs: kernel(position(), *refs[skipped:]), in_spec...]
    ppermute x26, waiting for transfers between devices: 31.3 us -> 37.7 us  [send(): return lax.ppermute(value, 'row', pairs)]
    ppermute x6, starting transfers between devices: 14.9 us -> 13.3 us  [send_col(): return lax.ppermute(value, 'col', [(c, c ^ step) for c in range(4)])]
    ppermute x2, waiting for transfers between devices: 2.54 us -> 4.14 us  [per_device(): b, c = (send_col(b, 2), lax.ppermute(c, ('row', 'col'), DIAGONAL))]
  transfers between devices with their start and end apart: 34 -> 34, of which waited for: 10 -> 12; matrix products, arithmetic and copies ran while one was open for 0% -> 0% of each run, Pallas kernels for 26% -> 21%
where the time goes in v5:
time: 149 us
  starting transfers between devices  48.9 us (33%)
  waiting for transfers between devices  45.9 us (31%)
  Pallas kernels  34.2 us (23%)
  blocking collectives  18.6 us (12%)
    ppermute x26, waiting for transfers between devices, send(): return lax.ppermute(value, 'row', pairs)  37.7 us
    ppermute x26, starting transfers between devices, send(): return lax.ppermute(value, 'row', pairs)  32.7 us
    pallas_call x13, Pallas kernels, __call__(): pl.pallas_call(lambda *refs: kernel(position(), *refs[skipped:]), in_spec...  31.5 us
    all_to_all x1, blocking collectives, per_device(): lax.all_to_all(ordered, 'row', split_axis=1, concat_axis=0, tiled=True)  18.6 us
    ppermute x6, starting transfers between devices, send_col(): return lax.ppermute(value, 'col', [(c, c ^ step) for c in range(4)])  13.3 us
    ppermute x2, waiting for transfers between devices, per_device(): b, c = (send_col(b, 2), lax.ppermute(c, ('row', 'col'), DIAGONAL))  4.14 us
    ppermute x6, waiting for transfers between devices, send_col(): return lax.ppermute(value, 'col', [(c, c ^ step) for c in range(4)])  4.03 us
  transfers between devices with their start and end apart: 34, of which 12 were waited for; matrix products, arithmetic and copies ran while one was open for 0% of the time, Pallas kernels for 21%

profile of v5, /device:TPU:1, one launch (start us, length us, event | category | flops | bytes accessed | tf_op | source)
XLA Modules:
  0.0 149.1 jit_solution(12666266771791355235)
XLA Ops:
  0.0 2.6 %arrange.1 = (bf16[8,28672]{1,0:T(8,128)(2,1)}, bf16[7,7168]{1,0:T(8,128)(2,1)S(1)}) custom-call(s32[224]{0:T(256)} %order.1, bf16[8,28672]{1,0:T(8,128)(2,1)} %values.1, s32[8,224]{1,0:T(8,128)} %flags.1, s32[7,56]{1,0:T(8,128)} %tile_flags.1), custom_call_target="tpu_custom_call" | custom-call | tf_op jit(solution)/shard_map/arrange/pallas_call | solution.py:344
  2.6 18.6 %all_to_all.19 = bf16[8,32,896]{2,0,1:T(8,128)(2,1)S(1)} all-to-all(bf16[8,32,896]{2,0,1:T(8,128)(2,1)} %bitcast.41), channel_id=1, replica_groups=mesh['row'=32,'col'=4] {'row'}, dimensions={1} | all-to-all | bytes 917504 | tf_op jit(solution)/shard_map/all_to_all | solution.py:355
  21.2 2.6 %collective-permute-start = (bf16[256,896]{1,0:T(8,128)(2,1)S(1)}, bf16[256,896]{1,0:T(8,128)(2,1)S(1)}, u32[]{:S(2)}, u32[]{:S(2)}) collective-permute-start(bf16[256,896]{1,0:T(8,128)(2,1)S(1)} %bitcast.38), channel_id=1, source_target_pairs={{0,1},{1,0},{2,3},{3,2},{4,5},{5,4},{6,7},{7,6},{8,9},{9,8},{10,11... | collective-permute-start | bytes 1376264 | tf_op jit(solution)/shard_map/ppermute | solution.py:38
  23.8 3.3 %collective-permute-start.1 = (bf16[256,896]{1,0:T(8,128)(2,1)S(1)}, bf16[256,896]{1,0:T(8,128)(2,1)S(1)}, u32[]{:S(2)}, u32[]{:S(2)}) collective-permute-start(bf16[256,896]{1,0:T(8,128)(2,1)S(1)} %bitcast.39), channel_id=1, source_target_pairs={{0,2},{1,3},{2,0},{3,1},{4,6},{5,7},{6,4},{7,5},{8,10},{9,11},{10,... | collective-permute-start | bytes 1376264 | tf_op jit(solution)/shard_map/ppermute | solution.py:38
  27.3 8.9 %begin_kernel.1 = (s16[128,3712]{1,0:T(8,128)(2,1)S(1)}, s16[128,3712]{1,0:T(8,128)(2,1)S(1)}, s16[128,3712]{1,0:T(8,128)(2,1)S(1)}, s16[128,3712]{1,0:T(8,128)(...) custom-call(bf16[256,896]{1,0:T(8,128)(2,1)S(1)} %bitcast.40, bf16[896,7168]{1,0:T(8,128)(2,1)} %refs_1_.1, ...), custom_call_target="tpu_custom_call" | custom-call | flops 1000 | bytes 1000 | tf_op jit(solution)/shard_map/begin_kernel/pallas_call | solution.py:318
  36.6 2.3 %collective-permute-start.4 = (s16[128,3712]{1,0:T(8,128)(2,1)S(1)}, s16[128,3712]{1,0:T(8,128)(2,1)S(1)}, u32[]{:S(2)}, u32[]{:S(2)}) collective-permute-start(s16[128,3712]{1,0:T(8,128)(2,1)S(1)} %get-tuple-element.67), channel_id=1, source_target_pairs={{0,48},{4,52},{8,56},{12,60},{16,0},{20,4},{24,8},{28,12},{32,16},... | collective-permute-start | bytes 2850824 | tf_op jit(solution)/shard_map/ppermute | solution.py:34
  40.0 2.5 %collective-permute-start.6 = (s16[128,3712]{1,0:T(8,128)(2,1)S(1)}, s16[128,3712]{1,0:T(8,128)(2,1)S(1)}, u32[]{:S(2)}, u32[]{:S(2)}) collective-permute-start(s16[128,3712]{1,0:T(8,128)(2,1)S(1)} %get-tuple-element.69), channel_id=1, source_target_pairs={{0,12},{4,0},{8,4},{12,8},{16,28},{20,16},{24,20},{28,24},{32,44},... | collective-permute-start | bytes 2850824 | tf_op jit(solution)/shard_map/ppermute | solution.py:34
  42.7 3.4 %far_kernel.2 = (s16[64,3712]{1,0:T(8,128)(2,1)S(1)}, s16[64,3712]{1,0:T(8,128)(2,1)S(1)}, s16[64,3712]{1,0:T(8,128)(2,1)S(1)}, s16[64,3712]{1,0:T(8,128)(2,1)S(1)}) custom-call(s16[128,3712]{1,0:T(8,128)(2,1)S(1)} %get-tuple-element.62.refs_0_, bf16[896,3584]{1,0:T(8,128)(2,1)S(1)} %get-tuple-element.63.refs_1_.refs_5_, ...), custom_call_target="tpu_custom_call" | custom-call | flops 1000 | bytes 1000 | tf_op jit(solution)/shard_map/far_kernel/pallas_call | solution.py:318
  46.1 13.8 %collective-permute-done.3.refs_1_.refs_5_ = s16[128,3712]{1,0:T(8,128)(2,1)S(1)} collective-permute-done((s16[128,3712]{1,0:T(8,128)(2,1)S(1)}, s16[128,3712]{1,0:T(8,128)(2,1)S(1)}, u32[]{:S(2)}, u32[]{:S(2)}) %collective-permute-start.3) | collective-permute-done | bytes 950304 | tf_op jit(solution)/shard_map/ppermute | solution.py:34
  59.9 2.7 %collective-permute-start.8 = (s16[64,3712]{1,0:T(8,128)(2,1)S(1)}, s16[64,3712]{1,0:T(8,128)(2,1)S(1)}, u32[]{:S(2)}, u32[]{:S(2)}) collective-permute-start(s16[64,3712]{1,0:T(8,128)(2,1)S(1)} %get-tuple-element.73), channel_id=1, source_target_pairs={{0,48},{4,52},{8,56},{12,60},{16,0},{20,4},{24,8},{28,12},{32,16},... | collective-permute-start | bytes 1425416 | tf_op jit(solution)/shard_map/ppermute | solution.py:34
  63.7 2.7 %collective-permute-start.10 = (s16[64,3712]{1,0:T(8,128)(2,1)S(1)}, s16[64,3712]{1,0:T(8,128)(2,1)S(1)}, u32[]{:S(2)}, u32[]{:S(2)}) collective-permute-start(s16[64,3712]{1,0:T(8,128)(2,1)S(1)} %get-tuple-element.77), channel_id=1, source_target_pairs={{0,12},{4,0},{8,4},{12,8},{16,28},{20,16},{24,20},{28,24},{32,44},... | collective-permute-start | bytes 1425416 | tf_op jit(solution)/shard_map/ppermute | solution.py:34
  66.4 3.3 %far_kernel.3 = (s16[64,3712]{1,0:T(8,128)(2,1)S(1)}, s16[64,3712]{1,0:T(8,128)(2,1)S(1)}, s16[64,3712]{1,0:T(8,128)(2,1)S(1)}, s16[64,3712]{1,0:T(8,128)(2,1)S(1)}) custom-call(s16[64,3712]{1,0:T(8,128)(2,1)S(1)} %get-tuple-element.72.refs_0_, s16[128,3712]{1,0:T(8,128)(2,1)S(1)} %collective-permute-done.3.refs_1_.refs_5_, ...), custom_call_target="tpu_custom_call" | custom-call | flops 1000 | bytes 1000 | tf_op jit(solution)/shard_map/far_kernel/pallas_call | solution.py:318
  69.7 2.6 %collective-permute-done.7.refs_7_ = s16[64,3712]{1,0:T(8,128)(2,1)S(1)} collective-permute-done((s16[64,3712]{1,0:T(8,128)(2,1)S(1)}, s16[64,3712]{1,0:T(8,128)(2,1)S(1)}, u32[]{:S(2)}, u32[]{:S(2)}) %collective-permute-start.7) | collective-permute-done | bytes 475168 | tf_op jit(solution)/shard_map/ppermute | solution.py:34
  72.6 2.5 %collective-permute-start.12 = (s16[64,3712]{1,0:T(8,128)(2,1)S(1)}, s16[64,3712]{1,0:T(8,128)(2,1)S(1)}, u32[]{:S(2)}, u32[]{:S(2)}) collective-permute-start(s16[64,3712]{1,0:T(8,128)(2,1)S(1)} %get-tuple-element.81), channel_id=1, source_target_pairs={{0,48},{4,52},{8,56},{12,60},{16,0},{20,4},{24,8},{28,12},{32,16},... | collective-permute-start | bytes 1425416 | tf_op jit(solution)/shard_map/ppermute | solution.py:34
  75.0 1.5 %collective-permute-done.9.refs_11_ = s16[64,3712]{1,0:T(8,128)(2,1)S(1)} collective-permute-done((s16[64,3712]{1,0:T(8,128)(2,1)S(1)}, s16[64,3712]{1,0:T(8,128)(2,1)S(1)}, u32[]{:S(2)}, u32[]{:S(2)}) %collective-permute-start.9) | collective-permute-done | bytes 475168 | tf_op jit(solution)/shard_map/ppermute | solution.py:34
  76.7 2.5 %collective-permute-start.14 = (s16[64,3712]{1,0:T(8,128)(2,1)S(1)}, s16[64,3712]{1,0:T(8,128)(2,1)S(1)}, u32[]{:S(2)}, u32[]{:S(2)}) collective-permute-start(s16[64,3712]{1,0:T(8,128)(2,1)S(1)} %get-tuple-element.85), channel_id=1, source_target_pairs={{0,12},{4,0},{8,4},{12,8},{16,28},{20,16},{24,20},{28,24},{32,44},... | collective-permute-start | bytes 1425416 | tf_op jit(solution)/shard_map/ppermute | solution.py:34
  79.2 6.2 %pass_on_kernel.1 = (s16[128,3712]{1,0:T(8,128)(2,1)S(1)}, s16[128,3712]{1,0:T(8,128)(2,1)S(1)}, s16[128,3712]{1,0:T(8,128)(2,1)S(1)}, s16[128,3712]{1,0:T(8,128)(2,1)S(1)}) custom-call(s16[64,3712]{1,0:T(8,128)(2,1)S(1)} %get-tuple-element.80.refs_0_, bf16[896,3584]{1,0:T(8,128)(2,1)S(1)} %get-tuple-element.63.refs_1_.refs_5_, ...), custom_call_target="tpu_custom_call" | custom-call | flops 1000 | bytes 1000 | tf_op jit(solution)/shard_map/pass_on_kernel/pallas_call | solution.py:318
  85.5 2.7 %collective-permute-start.16 = (s16[128,3712]{1,0:T(8,128)(2,1)S(1)}, s16[128,3712]{1,0:T(8,128)(2,1)S(1)}, u32[]{:S(2)}, u32[]{:S(2)}) collective-permute-start(s16[128,3712]{1,0:T(8,128)(2,1)S(1)} %get-tuple-element.89), channel_id=1, source_target_pairs={{0,48},{4,52},{8,56},{12,60},{16,0},{20,4},{24,8},{28,12},{32,16},... | collective-permute-start | bytes 2850824 | tf_op jit(solution)/shard_map/ppermute | solution.py:34
  88.4 2.7 %collective-permute-start.18 = (s16[128,3712]{1,0:T(8,128)(2,1)S(1)}, s16[128,3712]{1,0:T(8,128)(2,1)S(1)}, u32[]{:S(2)}, u32[]{:S(2)}) collective-permute-start(s16[128,3712]{1,0:T(8,128)(2,1)S(1)} %get-tuple-element.95), channel_id=1, source_target_pairs={{0,12},{4,0},{8,4},{12,8},{16,28},{20,16},{24,20},{28,24},{32,44},... | collective-permute-start | bytes 2850824 | tf_op jit(solution)/shard_map/ppermute | solution.py:34
  91.1 5.1 %own_kernel.1 = (f32[256,3584]{1,0:T(8,128)S(1)}, f32[256,3584]{1,0:T(8,128)S(1)}) custom-call(s16[128,3712]{1,0:T(8,128)(2,1)S(1)} %get-tuple-element.88.refs_0_, bf16[896,3584]{1,0:T(8,128)(2,1)S(1)} %get-tuple-element.63.refs_1_.refs_5_, bf16[896,3584]{1,0:T(8,128)(2,1)S(1)} %get-tuple-element.64.refs_2_.refs_6_, bf16[512,896]{1,0:T(8,128)(2,1)S(1)} %bitcast.37, ...), custom_call_target="tpu_custom_call" | custom-call | flops 1000 | bytes 1000 | tf_op jit(solution)/shard_map/own_kernel/pallas_call | solution.py:318
  96.2 10.8 %collective-permute-done.15.refs_2_ = s16[128,3712]{1,0:T(8,128)(2,1)S(1)} collective-permute-done((s16[128,3712]{1,0:T(8,128)(2,1)S(1)}, s16[128,3712]{1,0:T(8,128)(2,1)S(1)}, u32[]{:S(2)}, u32[]{:S(2)}) %collective-permute-start.15) | collective-permute-done | bytes 950304 | tf_op jit(solution)/shard_map/ppermute | solution.py:34
  107.6 2.7 %collective-permute-start.20 = (s16[32,3712]{1,0:T(8,128)(2,1)S(1)}, s16[32,3712]{1,0:T(8,128)(2,1)S(1)}, u32[]{:S(2)}, u32[]{:S(2)}) collective-permute-start(s16[32,3712]{1,0:T(8,128)(2,1)S(1)} %get-tuple-element.97), channel_id=1, source_target_pairs={{0,12},{4,0},{8,4},{12,8},{16,28},{20,16},{24,20},{28,24},{32,44},... | collective-permute-start | bytes 712712 | tf_op jit(solution)/shard_map/ppermute | solution.py:34
  110.8 2.7 %collective-permute-start.22 = (s16[32,3712]{1,0:T(8,128)(2,1)S(1)}, s16[32,3712]{1,0:T(8,128)(2,1)S(1)}, u32[]{:S(2)}, u32[]{:S(2)}) collective-permute-start(s16[32,3712]{1,0:T(8,128)(2,1)S(1)} %get-tuple-element.99), channel_id=1, source_target_pairs={{0,48},{4,52},{8,56},{12,60},{16,0},{20,4},{24,8},{28,12},{32,16},... | collective-permute-start | bytes 712712 | tf_op jit(solution)/shard_map/ppermute | solution.py:34
  113.5 1.9 %collective-permute-done.19.refs_4_ = s16[32,3712]{1,0:T(8,128)(2,1)S(1)} collective-permute-done((s16[32,3712]{1,0:T(8,128)(2,1)S(1)}, s16[32,3712]{1,0:T(8,128)(2,1)S(1)}, u32[]{:S(2)}, u32[]{:S(2)}) %collective-permute-start.19) | collective-permute-done | bytes 237600 | tf_op jit(solution)/shard_map/ppermute | solution.py:34
  116.7 2.3 %collective-permute-start.24 = (s16[64,3712]{1,0:T(8,128)(2,1)S(1)}, s16[64,3712]{1,0:T(8,128)(2,1)S(1)}, u32[]{:S(2)}, u32[]{:S(2)}) collective-permute-start(s16[64,3712]{1,0:T(8,128)(2,1)S(1)} %get-tuple-element.101), channel_id=1, source_target_pairs={{0,12},{4,0},{8,4},{12,8},{16,28},{20,16},{24,20},{28,24},{32,44},... | collective-permute-start | bytes 1425416 | tf_op jit(solution)/shard_map/ppermute | solution.py:34
  120.1 2.7 %collective-permute-start.26 = (s16[64,3712]{1,0:T(8,128)(2,1)S(1)}, s16[64,3712]{1,0:T(8,128)(2,1)S(1)}, u32[]{:S(2)}, u32[]{:S(2)}) collective-permute-start(s16[64,3712]{1,0:T(8,128)(2,1)S(1)} %get-tuple-element.103), channel_id=1, source_target_pairs={{0,48},{4,52},{8,56},{12,60},{16,0},{20,4},{24,8},{28,12},{32,16},... | collective-permute-start | bytes 1425416 | tf_op jit(solution)/shard_map/ppermute | solution.py:34
  122.7 4.4 %collective-permute-done.23.refs_4_ = s16[64,3712]{1,0:T(8,128)(2,1)S(1)} collective-permute-done((s16[64,3712]{1,0:T(8,128)(2,1)S(1)}, s16[64,3712]{1,0:T(8,128)(2,1)S(1)}, u32[]{:S(2)}, u32[]{:S(2)}) %collective-permute-start.23) | collective-permute-done | bytes 475168 | tf_op jit(solution)/shard_map/ppermute | solution.py:34
  128.0 2.4 %collective-permute-start.28 = (s16[16,3840]{1,0:T(8,128)(2,1)S(1)}, s16[16,3840]{1,0:T(8,128)(2,1)S(1)}, u32[]{:S(2)}, u32[]{:S(2)}) collective-permute-start(s16[16,3840]{1,0:T(8,128)(2,1)S(1)} %get-tuple-element.106), channel_id=1, source_target_pairs={{0,2},{1,3},{2,0},{3,1},{4,6},{5,7},{6,4},{7,5},{8,10},{9,11},{10,... | collective-permute-start | bytes 368648 | tf_op jit(solution)/shard_map/ppermute | solution.py:38
  132.8 2.4 %collective-permute-start.31 = (s16[16,3840]{1,0:T(8,128)(2,1)S(1)}, s16[16,3840]{1,0:T(8,128)(2,1)S(1)}, u32[]{:S(2)}, u32[]{:S(2)}) collective-permute-start(s16[16,3840]{1,0:T(8,128)(2,1)S(1)} %get-tuple-element.110), channel_id=1, source_target_pairs={{0,2},{1,3},{2,0},{3,1},{4,6},{5,7},{6,4},{7,5},{8,10},{9,11},{10,... | collective-permute-start | bytes 368648 | tf_op jit(solution)/shard_map/ppermute | solution.py:38
  138.0 2.9 %collective-permute-done.31.refs_3_ = s16[16,3840]{1,0:T(8,128)(2,1)S(1)} collective-permute-done((s16[16,3840]{1,0:T(8,128)(2,1)S(1)}, s16[16,3840]{1,0:T(8,128)(2,1)S(1)}, u32[]{:S(2)}, u32[]{:S(2)}) %collective-permute-start.31) | collective-permute-done | bytes 122912 | tf_op jit(solution)/shard_map/ppermute | solution.py:38
  140.9 4.1 %collective-permute-done.32.refs_4_ = s16[16,3840]{1,0:T(8,128)(2,1)S(1)} collective-permute-done((s16[16,3840]{1,0:T(8,128)(2,1)S(1)}, s16[16,3840]{1,0:T(8,128)(2,1)S(1)}, u32[]{:S(2)}, u32[]{:S(2)}) %collective-permute-start.32) | collective-permute-done | bytes 122912 | tf_op jit(solution)/shard_map/ppermute | solution.py:427
  145.3 1.8 %collective-permute-start.33 = (bf16[8,14336]{1,0:T(8,128)(2,1)S(1)}, bf16[8,14336]{1,0:T(8,128)(2,1)S(1)}, u32[]{:S(2)}, u32[]{:S(2)}) collective-permute-start(bf16[8,14336]{1,0:T(8,128)(2,1)S(1)} %dynamic-slice_bitcast_fusion), channel_id=1, source_target_pairs={{0,1},{1,0},{2,3},{3,2},{4,5},{5,4},{6,7},{7,6},{8,9},{9,8},{10,11... | collective-permute-start | bytes 688136 | tf_op jit(solution)/shard_map/ppermute | solution.py:38
  (60 shorter events, 15.6 us)
Async XLA Ops:
  21.2 5.9 %collective-permute-start = (bf16[256,896]{1,0:T(8,128)(2,1)S(1)}, bf16[256,896]{1,0:T(8,128)(2,1)S(1)}, u32[]{:S(2)}, u32[]{:S(2)}) collective-permute-start(bf16[256,896]{1,0:T(8,128)(2,1)S(1)} %bitcast.38), channel_id=1, source_target_pairs={{0,1},{1,0},{2,3},{3,2},{4,5},{5,4},{6,7},{7,6},{8,9},{9,8},{10,11... | collective-permute-start | bytes 1376264 | tf_op jit(solution)/shard_map/ppermute | solution.py:38
  23.8 15.1 %collective-permute-start.1 = (bf16[256,896]{1,0:T(8,128)(2,1)S(1)}, bf16[256,896]{1,0:T(8,128)(2,1)S(1)}, u32[]{:S(2)}, u32[]{:S(2)}) collective-permute-start(bf16[256,896]{1,0:T(8,128)(2,1)S(1)} %bitcast.39), channel_id=1, source_target_pairs={{0,2},{1,3},{2,0},{3,1},{4,6},{5,7},{6,4},{7,5},{8,10},{9,11},{10,... | collective-permute-start | bytes 1376264 | tf_op jit(solution)/shard_map/ppermute | solution.py:38
  36.2 23.6 %collective-permute-start.3 = (s16[128,3712]{1,0:T(8,128)(2,1)S(1)}, s16[128,3712]{1,0:T(8,128)(2,1)S(1)}, u32[]{:S(2)}, u32[]{:S(2)}) collective-permute-start(s16[128,3712]{1,0:T(8,128)(2,1)S(1)} %get-tuple-element.62.refs_0_), channel_id=1, source_target_pairs={{0,16},{4,20},{8,24},{12,28},{16,32},{20,36},{24,40},{28,44},{32,4... | collective-permute-start | bytes 2850824 | tf_op jit(solution)/shard_map/ppermute | solution.py:34
  36.6 23.2 %collective-permute-start.4 = (s16[128,3712]{1,0:T(8,128)(2,1)S(1)}, s16[128,3712]{1,0:T(8,128)(2,1)S(1)}, u32[]{:S(2)}, u32[]{:S(2)}) collective-permute-start(s16[128,3712]{1,0:T(8,128)(2,1)S(1)} %get-tuple-element.67), channel_id=1, source_target_pairs={{0,48},{4,52},{8,56},{12,60},{16,0},{20,4},{24,8},{28,12},{32,16},... | collective-permute-start | bytes 2850824 | tf_op jit(solution)/shard_map/ppermute | solution.py:34
  39.8 23.9 %collective-permute-start.5 = (s16[128,3712]{1,0:T(8,128)(2,1)S(1)}, s16[128,3712]{1,0:T(8,128)(2,1)S(1)}, u32[]{:S(2)}, u32[]{:S(2)}) collective-permute-start(s16[128,3712]{1,0:T(8,128)(2,1)S(1)} %get-tuple-element.68), channel_id=1, source_target_pairs={{0,4},{4,8},{8,12},{12,0},{16,20},{20,24},{24,28},{28,16},{32,36},... | collective-permute-start | bytes 2850824 | tf_op jit(solution)/shard_map/ppermute | solution.py:34
  40.0 23.7 %collective-permute-start.6 = (s16[128,3712]{1,0:T(8,128)(2,1)S(1)}, s16[128,3712]{1,0:T(8,128)(2,1)S(1)}, u32[]{:S(2)}, u32[]{:S(2)}) collective-permute-start(s16[128,3712]{1,0:T(8,128)(2,1)S(1)} %get-tuple-element.69), channel_id=1, source_target_pairs={{0,12},{4,0},{8,4},{12,8},{16,28},{20,16},{24,20},{28,24},{32,44},... | collective-permute-start | bytes 2850824 | tf_op jit(solution)/shard_map/ppermute | solution.py:34
  59.9 12.5 %collective-permute-start.7 = (s16[64,3712]{1,0:T(8,128)(2,1)S(1)}, s16[64,3712]{1,0:T(8,128)(2,1)S(1)}, u32[]{:S(2)}, u32[]{:S(2)}) collective-permute-start(s16[64,3712]{1,0:T(8,128)(2,1)S(1)} %get-tuple-element.72.refs_0_), channel_id=1, source_target_pairs={{0,16},{4,20},{8,24},{12,28},{16,32},{20,36},{24,40},{28,44},{32,4... | collective-permute-start | bytes 1425416 | tf_op jit(solution)/shard_map/ppermute | solution.py:34
  59.9 12.5 %collective-permute-start.8 = (s16[64,3712]{1,0:T(8,128)(2,1)S(1)}, s16[64,3712]{1,0:T(8,128)(2,1)S(1)}, u32[]{:S(2)}, u32[]{:S(2)}) collective-permute-start(s16[64,3712]{1,0:T(8,128)(2,1)S(1)} %get-tuple-element.73), channel_id=1, source_target_pairs={{0,48},{4,52},{8,56},{12,60},{16,0},{20,4},{24,8},{28,12},{32,16},... | collective-permute-start | bytes 1425416 | tf_op jit(solution)/shard_map/ppermute | solution.py:34
  63.7 12.8 %collective-permute-start.9 = (s16[64,3712]{1,0:T(8,128)(2,1)S(1)}, s16[64,3712]{1,0:T(8,128)(2,1)S(1)}, u32[]{:S(2)}, u32[]{:S(2)}) collective-permute-start(s16[64,3712]{1,0:T(8,128)(2,1)S(1)} %get-tuple-element.76), channel_id=1, source_target_pairs={{0,4},{4,8},{8,12},{12,0},{16,20},{20,24},{24,28},{28,16},{32,36},... | collective-permute-start | bytes 1425416 | tf_op jit(solution)/shard_map/ppermute | solution.py:34
  63.7 12.8 %collective-permute-start.10 = (s16[64,3712]{1,0:T(8,128)(2,1)S(1)}, s16[64,3712]{1,0:T(8,128)(2,1)S(1)}, u32[]{:S(2)}, u32[]{:S(2)}) collective-permute-start(s16[64,3712]{1,0:T(8,128)(2,1)S(1)} %get-tuple-element.77), channel_id=1, source_target_pairs={{0,12},{4,0},{8,4},{12,8},{16,28},{20,16},{24,20},{28,24},{32,44},... | collective-permute-start | bytes 1425416 | tf_op jit(solution)/shard_map/ppermute | solution.py:34
  72.3 13.1 %collective-permute-start.11 = (s16[64,3712]{1,0:T(8,128)(2,1)S(1)}, s16[64,3712]{1,0:T(8,128)(2,1)S(1)}, u32[]{:S(2)}, u32[]{:S(2)}) collective-permute-start(s16[64,3712]{1,0:T(8,128)(2,1)S(1)} %get-tuple-element.80.refs_0_), channel_id=1, source_target_pairs={{0,16},{4,20},{8,24},{12,28},{16,32},{20,36},{24,40},{28,44},{32,4... | collective-permute-start | bytes 1425416 | tf_op jit(solution)/shard_map/ppermute | solution.py:34
  72.6 12.8 %collective-permute-start.12 = (s16[64,3712]{1,0:T(8,128)(2,1)S(1)}, s16[64,3712]{1,0:T(8,128)(2,1)S(1)}, u32[]{:S(2)}, u32[]{:S(2)}) collective-permute-start(s16[64,3712]{1,0:T(8,128)(2,1)S(1)} %get-tuple-element.81), channel_id=1, source_target_pairs={{0,48},{4,52},{8,56},{12,60},{16,0},{20,4},{24,8},{28,12},{32,16},... | collective-permute-start | bytes 1425416 | tf_op jit(solution)/shard_map/ppermute | solution.py:34
  76.5 11.9 %collective-permute-start.13 = (s16[64,3712]{1,0:T(8,128)(2,1)S(1)}, s16[64,3712]{1,0:T(8,128)(2,1)S(1)}, u32[]{:S(2)}, u32[]{:S(2)}) collective-permute-start(s16[64,3712]{1,0:T(8,128)(2,1)S(1)} %get-tuple-element.84), channel_id=1, source_target_pairs={{0,4},{4,8},{8,12},{12,0},{16,20},{20,24},{24,28},{28,16},{32,36},... | collective-permute-start | bytes 1425416 | tf_op jit(solution)/shard_map/ppermute | solution.py:34
  76.7 11.7 %collective-permute-start.14 = (s16[64,3712]{1,0:T(8,128)(2,1)S(1)}, s16[64,3712]{1,0:T(8,128)(2,1)S(1)}, u32[]{:S(2)}, u32[]{:S(2)}) collective-permute-start(s16[64,3712]{1,0:T(8,128)(2,1)S(1)} %get-tuple-element.85), channel_id=1, source_target_pairs={{0,12},{4,0},{8,4},{12,8},{16,28},{20,16},{24,20},{28,24},{32,44},... | collective-permute-start | bytes 1425416 | tf_op jit(solution)/shard_map/ppermute | solution.py:34
  85.4 21.6 %collective-permute-start.15 = (s16[128,3712]{1,0:T(8,128)(2,1)S(1)}, s16[128,3712]{1,0:T(8,128)(2,1)S(1)}, u32[]{:S(2)}, u32[]{:S(2)}) collective-permute-start(s16[128,3712]{1,0:T(8,128)(2,1)S(1)} %get-tuple-element.88.refs_0_), channel_id=1, source_target_pairs={{0,16},{4,20},{8,24},{12,28},{16,32},{20,36},{24,40},{28,44},{32,4... | collective-permute-start | bytes 2850824 | tf_op jit(solution)/shard_map/ppermute | solution.py:34
  85.5 21.5 %collective-permute-start.16 = (s16[128,3712]{1,0:T(8,128)(2,1)S(1)}, s16[128,3712]{1,0:T(8,128)(2,1)S(1)}, u32[]{:S(2)}, u32[]{:S(2)}) collective-permute-start(s16[128,3712]{1,0:T(8,128)(2,1)S(1)} %get-tuple-element.89), channel_id=1, source_target_pairs={{0,48},{4,52},{8,56},{12,60},{16,0},{20,4},{24,8},{28,12},{32,16},... | collective-permute-start | bytes 2850824 | tf_op jit(solution)/shard_map/ppermute | solution.py:34
  88.4 21.8 %collective-permute-start.17 = (s16[128,3712]{1,0:T(8,128)(2,1)S(1)}, s16[128,3712]{1,0:T(8,128)(2,1)S(1)}, u32[]{:S(2)}, u32[]{:S(2)}) collective-permute-start(s16[128,3712]{1,0:T(8,128)(2,1)S(1)} %get-tuple-element.94), channel_id=1, source_target_pairs={{0,4},{4,8},{8,12},{12,0},{16,20},{20,24},{24,28},{28,16},{32,36},... | collective-permute-start | bytes 2850824 | tf_op jit(solution)/shard_map/ppermute | solution.py:34
  88.4 21.8 %collective-permute-start.18 = (s16[128,3712]{1,0:T(8,128)(2,1)S(1)}, s16[128,3712]{1,0:T(8,128)(2,1)S(1)}, u32[]{:S(2)}, u32[]{:S(2)}) collective-permute-start(s16[128,3712]{1,0:T(8,128)(2,1)S(1)} %get-tuple-element.95), channel_id=1, source_target_pairs={{0,12},{4,0},{8,4},{12,8},{16,28},{20,16},{24,20},{28,24},{32,44},... | collective-permute-start | bytes 2850824 | tf_op jit(solution)/shard_map/ppermute | solution.py:34
  107.5 7.9 %collective-permute-start.19 = (s16[32,3712]{1,0:T(8,128)(2,1)S(1)}, s16[32,3712]{1,0:T(8,128)(2,1)S(1)}, u32[]{:S(2)}, u32[]{:S(2)}) collective-permute-start(s16[32,3712]{1,0:T(8,128)(2,1)S(1)} %get-tuple-element.90.refs_0_), channel_id=1, source_target_pairs={{0,4},{4,8},{8,12},{12,0},{16,20},{20,24},{24,28},{28,16},{32,36},... | collective-permute-start | bytes 712712 | tf_op jit(solution)/shard_map/ppermute | solution.py:34
  107.6 7.8 %collective-permute-start.20 = (s16[32,3712]{1,0:T(8,128)(2,1)S(1)}, s16[32,3712]{1,0:T(8,128)(2,1)S(1)}, u32[]{:S(2)}, u32[]{:S(2)}) collective-permute-start(s16[32,3712]{1,0:T(8,128)(2,1)S(1)} %get-tuple-element.97), channel_id=1, source_target_pairs={{0,12},{4,0},{8,4},{12,8},{16,28},{20,16},{24,20},{28,24},{32,44},... | collective-permute-start | bytes 712712 | tf_op jit(solution)/shard_map/ppermute | solution.py:34
  110.7 8.3 %collective-permute-start.21 = (s16[32,3712]{1,0:T(8,128)(2,1)S(1)}, s16[32,3712]{1,0:T(8,128)(2,1)S(1)}, u32[]{:S(2)}, u32[]{:S(2)}) collective-permute-start(s16[32,3712]{1,0:T(8,128)(2,1)S(1)} %get-tuple-element.96.refs_0_), channel_id=1, source_target_pairs={{0,16},{4,20},{8,24},{12,28},{16,32},{20,36},{24,40},{28,44},{32,4... | collective-permute-start | bytes 712712 | tf_op jit(solution)/shard_map/ppermute | solution.py:34
  110.8 8.3 %collective-permute-start.22 = (s16[32,3712]{1,0:T(8,128)(2,1)S(1)}, s16[32,3712]{1,0:T(8,128)(2,1)S(1)}, u32[]{:S(2)}, u32[]{:S(2)}) collective-permute-start(s16[32,3712]{1,0:T(8,128)(2,1)S(1)} %get-tuple-element.99), channel_id=1, source_target_pairs={{0,48},{4,52},{8,56},{12,60},{16,0},{20,4},{24,8},{28,12},{32,16},... | collective-permute-start | bytes 712712 | tf_op jit(solution)/shard_map/ppermute | solution.py:34
  116.3 10.8 %collective-permute-start.23 = (s16[64,3712]{1,0:T(8,128)(2,1)S(1)}, s16[64,3712]{1,0:T(8,128)(2,1)S(1)}, u32[]{:S(2)}, u32[]{:S(2)}) collective-permute-start(s16[64,3712]{1,0:T(8,128)(2,1)S(1)} %get-tuple-element.98.refs_0_), channel_id=1, source_target_pairs={{0,4},{4,8},{8,12},{12,0},{16,20},{20,24},{24,28},{28,16},{32,36},... | collective-permute-start | bytes 1425416 | tf_op jit(solution)/shard_map/ppermute | solution.py:34
  116.7 10.4 %collective-permute-start.24 = (s16[64,3712]{1,0:T(8,128)(2,1)S(1)}, s16[64,3712]{1,0:T(8,128)(2,1)S(1)}, u32[]{:S(2)}, u32[]{:S(2)}) collective-permute-start(s16[64,3712]{1,0:T(8,128)(2,1)S(1)} %get-tuple-element.101), channel_id=1, source_target_pairs={{0,12},{4,0},{8,4},{12,8},{16,28},{20,16},{24,20},{28,24},{32,44},... | collective-permute-start | bytes 1425416 | tf_op jit(solution)/shard_map/ppermute | solution.py:34
  120.0 11.9 %collective-permute-start.25 = (s16[64,3712]{1,0:T(8,128)(2,1)S(1)}, s16[64,3712]{1,0:T(8,128)(2,1)S(1)}, u32[]{:S(2)}, u32[]{:S(2)}) collective-permute-start(s16[64,3712]{1,0:T(8,128)(2,1)S(1)} %get-tuple-element.100.refs_0_), channel_id=1, source_target_pairs={{0,16},{4,20},{8,24},{12,28},{16,32},{20,36},{24,40},{28,44},{32,4... | collective-permute-start | bytes 1425416 | tf_op jit(solution)/shard_map/ppermute | solution.py:34
  120.1 11.8 %collective-permute-start.26 = (s16[64,3712]{1,0:T(8,128)(2,1)S(1)}, s16[64,3712]{1,0:T(8,128)(2,1)S(1)}, u32[]{:S(2)}, u32[]{:S(2)}) collective-permute-start(s16[64,3712]{1,0:T(8,128)(2,1)S(1)} %get-tuple-element.103), channel_id=1, source_target_pairs={{0,48},{4,52},{8,56},{12,60},{16,0},{20,4},{24,8},{28,12},{32,16},... | collective-permute-start | bytes 1425416 | tf_op jit(solution)/shard_map/ppermute | solution.py:34
  127.9 7.2 %collective-permute-start.27 = (s16[16,3840]{1,0:T(8,128)(2,1)S(1)}, s16[16,3840]{1,0:T(8,128)(2,1)S(1)}, u32[]{:S(2)}, u32[]{:S(2)}) collective-permute-start(s16[16,3840]{1,0:T(8,128)(2,1)S(1)} %get-tuple-element.102.refs_0_), channel_id=1, source_target_pairs={{0,64},{4,68},{8,72},{12,76},{16,80},{20,84},{24,88},{28,92},{32,9... | collective-permute-start | bytes 368648 | tf_op jit(solution)/shard_map/ppermute | solution.py:34
  128.0 8.6 %collective-permute-start.28 = (s16[16,3840]{1,0:T(8,128)(2,1)S(1)}, s16[16,3840]{1,0:T(8,128)(2,1)S(1)}, u32[]{:S(2)}, u32[]{:S(2)}) collective-permute-start(s16[16,3840]{1,0:T(8,128)(2,1)S(1)} %get-tuple-element.106), channel_id=1, source_target_pairs={{0,2},{1,3},{2,0},{3,1},{4,6},{5,7},{6,4},{7,5},{8,10},{9,11},{10,... | collective-permute-start | bytes 368648 | tf_op jit(solution)/shard_map/ppermute | solution.py:38
  130.4 6.2 %collective-permute-start.29 = (s16[16,3840]{1,0:T(8,128)(2,1)S(1)}, s16[16,3840]{1,0:T(8,128)(2,1)S(1)}, u32[]{:S(2)}, u32[]{:S(2)}) collective-permute-start(s16[16,3840]{1,0:T(8,128)(2,1)S(1)} %get-tuple-element.107), channel_id=1, source_target_pairs={{0,66},{1,67},{2,64},{3,65},{4,70},{5,71},{6,68},{7,69},{8,74},{9,... | collective-permute-start | bytes 368648 | tf_op jit(solution)/shard_map/ppermute | solution.py:427
  132.7 5.4 %collective-permute-start.30 = (s16[16,3840]{1,0:T(8,128)(2,1)S(1)}, s16[16,3840]{1,0:T(8,128)(2,1)S(1)}, u32[]{:S(2)}, u32[]{:S(2)}) collective-permute-start(s16[16,3840]{1,0:T(8,128)(2,1)S(1)} %get-tuple-element.104.refs_0_), channel_id=1, source_target_pairs={{0,64},{4,68},{8,72},{12,76},{16,80},{20,84},{24,88},{28,92},{32,9... | collective-permute-start | bytes 368648 | tf_op jit(solution)/shard_map/ppermute | solution.py:34
  132.8 8.2 %collective-permute-start.31 = (s16[16,3840]{1,0:T(8,128)(2,1)S(1)}, s16[16,3840]{1,0:T(8,128)(2,1)S(1)}, u32[]{:S(2)}, u32[]{:S(2)}) collective-permute-start(s16[16,3840]{1,0:T(8,128)(2,1)S(1)} %get-tuple-element.110), channel_id=1, source_target_pairs={{0,2},{1,3},{2,0},{3,1},{4,6},{5,7},{6,4},{7,5},{8,10},{9,11},{10,... | collective-permute-start | bytes 368648 | tf_op jit(solution)/shard_map/ppermute | solution.py:38
  135.1 9.9 %collective-permute-start.32 = (s16[16,3840]{1,0:T(8,128)(2,1)S(1)}, s16[16,3840]{1,0:T(8,128)(2,1)S(1)}, u32[]{:S(2)}, u32[]{:S(2)}) collective-permute-start(s16[16,3840]{1,0:T(8,128)(2,1)S(1)} %get-tuple-element.111), channel_id=1, source_target_pairs={{0,66},{1,67},{2,64},{3,65},{4,70},{5,71},{6,68},{7,69},{8,74},{9,... | collective-permute-start | bytes 368648 | tf_op jit(solution)/shard_map/ppermute | solution.py:427
  (2 other events, 6.4 us)

commit v6 on v5

--- a/solution.py
+++ b/solution.py
@@ -14,6 +14,7 @@
 VMEM_LIMIT = 12 * 1024 * 1024
 BEGIN_LIMIT = 36 * 1024 * 1024
 TILE = 896
+WIDTH_TILES = 28
 
 
 def shift(dz, dx, dy):
@@ -48,24 +49,16 @@
 
 
 def finish(out_ref, code_ref):
-    rows = out_ref.shape[0]
-    codes = code_ref[...].astype(jnp.int32).astype(jnp.int16)
-    if rows == 16:
-        width = out_ref.shape[1] - 256
-        out_ref[:, width:width + 128] = codes[:16]
-        out_ref[:, width + 128:] = codes[16:]
-        return
-    width = out_ref.shape[1] - 128
-    out_ref[:32, width:] = codes
-    if rows > 32:
-        out_ref[32:, width:] = jnp.zeros((rows - 32, 128), jnp.int16)
+    out_ref[out_ref.shape[0] - 32:, :] = code_ref[...].astype(jnp.int32).astype(jnp.int16)
 
 
 def encode(value, t, out_ref, code_ref):
-    count = TILE // 128
-    out_ref[:, columns_of(t)], code = quantised(value)
+    count, rows = TILE // 128, value.shape[0]
+    coded, code = quantised(value)
     for i in range(count):
-        code_ref[pl.ds(t * count + i, 1), :] = code[:, i * 128:(i + 1) * 128]
+        at = t * count + i
+        out_ref[pl.ds(pl.multiple_of(at * rows, 16), rows), :] = coded[:, i * 128:(i + 1) * 128]
+        code_ref[pl.ds(at, 1), :] = code[:, i * 128:(i + 1) * 128]
 
 
 def columns_of(t):
@@ -147,16 +140,17 @@
         finish(ref, code_ref)
 
 
-def far_kernel(rows, pos, w0, w1, a, p0, q0, p1, q1, left, *code_refs):
+def far_kernel(pos, w0, w1, a, p0, q0, p1, q1, left, *code_refs):
     clear(*code_refs)
     for kind, w, p, q in ((0, w0, p0, q0), (1, w1, p1, q1)):
-        rows(pos, kind, a, left, 0, 64)
+        opposite_rows(pos, kind, a, left, 0, 128)
+        free_rows(pos, kind, a, left, 64, 192)
 
         @each_tile(w.shape[1], 2)
         def _(t):
             sums = dot(left[...], w[:, columns_of(t)])
-            encode(sums[:64], t, p, code_refs[2 * kind])
-            encode(sums[64:], t, q, code_refs[2 * kind + 1])
+            encode(sums[:128], t, p, code_refs[2 * kind])
+            encode(sums[128:], t, q, code_refs[2 * kind + 1])
 
         finish(p, code_refs[2 * kind])
         finish(q, code_refs[2 * kind + 1])
@@ -175,8 +169,8 @@
             sums = dot(left[...], w[:, columns_of(t)])
             for z in range(2):
                 parts = [
-                    decode(got[4 * kind + at + 1 - z], factor_refs[4 * kind + at + 1 - z], t, slice(start, start + 64))
-                    for at, start in ((0, 64), (2, 0))
+                    decode(got[4 * kind + at + 1 - z], factor_refs[4 * kind + at + 1 - z], t, 64, 64)
+                    for at in (0, 2)
                 ]
                 value = sums[z * 128:z * 128 + 128] + mixed(*parts)
                 own[z * 128:z * 128 + 128, columns_of(t)] = value
@@ -187,47 +181,57 @@
 
 
 def read_factors(ref, factor_ref):
-    if ref.shape[0] == 16:
-        width = ref.shape[1] - 256
-        codes = jnp.concatenate([ref[:, width:width + 128], ref[:, width + 128:]], axis=0)
-    else:
-        codes = ref[:32, ref.shape[1] - 128:]
-    factor_ref[...] = jnp.exp2(codes.astype(jnp.int32).astype(jnp.float32) * (1.0 / STEPS)) * (1.0 / LEVELS)
-
-
-def decode(ref, factor_ref, t, rows=slice(None)):
-    count = TILE // 128
-    scale = jnp.concatenate([factor_ref[pl.ds(t * count + i, 1), :] for i in range(count)], axis=1)
-    return ref[rows, columns_of(t)].astype(jnp.int32).astype(jnp.float32) * scale
-
-
-def pass_on_kernel(pos, w0, w1, near, far, *refs):
-    outs, left, factor_refs, code_refs = refs[8:12], refs[12], refs[13:21], refs[21:]
-    clear(*code_refs)
-    for kind, w in ((0, w0), (1, w1)):
-        got, scale = refs[4 * kind:4 * kind + 4], factor_refs[4 * kind:4 * kind + 4]
+    codes = ref[ref.shape[0] - 32:, :].astype(jnp.int32).astype(jnp.float32)
+    factor_ref[...] = jnp.exp2(codes * (1.0 / STEPS)) * (1.0 / LEVELS)
+
+
+def decode(ref, factor_ref, t, start=0, size=None):
+    count, rows = TILE // 128, (ref.shape[0] - 32) // WIDTH_TILES
+    parts = []
+    for i in range(count):
+        at = t * count + i
+        part = ref[pl.ds(pl.multiple_of(at * rows + start, 16), size or rows), :]
+        parts.append(part.astype(jnp.int32).astype(jnp.float32) * factor_ref[pl.ds(at, 1), :])
+    return jnp.concatenate(parts, axis=1)
+
+
+def later_kernel(pos, w0, w1, near, far, *refs):
+    got, outs, left, factor_refs = refs[:4], refs[4:6], refs[6], refs[7:]
+    for ref, factor in zip(got, factor_refs):
+        read_factors(ref, factor)
+    for kind, w, out in ((0, w0, outs[0]), (1, w1, outs[1])):
         copy_rows((near, far), left, 0, kind, (pos[1 + kind] + 1) % 4, 0)
         copy_rows((near, far), left, 128, kind, (pos[1 + kind] + 3) % 4, 1)
-        for ref, factor in zip(got, scale):
-            read_factors(ref, factor)
 
         @each_tile(w.shape[1], 2)
         def _(t):
             sums = dot(left[...], w[:, columns_of(t)])
             for way in range(2):
-                n, f = (decode(got[2 * part + way], scale[2 * part + way], t, slice(0, 64)) for part in range(2))
-                value = sums[way * 128:way * 128 + 128] + mixed(n, f)
-                encode(value, t, outs[2 * kind + way], code_refs[2 * kind + way])
-
-        for way in range(2):
-            finish(outs[2 * kind + way], code_refs[2 * kind + way])
+                n = decode(got[2 * kind + way], factor_refs[2 * kind + way], t, 0, 64)
+                out[way * 128:way * 128 + 128, columns_of(t)] = sums[way * 128:way * 128 + 128] + mixed(n, jnp.zeros_like(n))
+
+
+def pass_on_kernel(pos, later, p, q, *refs):
+    outs, factor_refs, code_refs = refs[:2], refs[2:4], refs[4:]
+    clear(*code_refs)
+    for ref, factor in zip((p, q), factor_refs):
+        read_factors(ref, factor)
+
+    @each_tile(later.shape[1], 2)
+    def _(t):
+        for way, ref in enumerate((p, q)):
+            f = decode(ref, factor_refs[way], t, 0, 64)
+            value = later[way * 128:way * 128 + 128, columns_of(t)] + mixed(jnp.zeros_like(f), f)
+            encode(value, t, outs[way], code_refs[way])
+
+    for way in range(2):
+        finish(outs[way], code_refs[way])
 
 
 def stage_one(refs, factor_refs, second, t):
     own, *got = refs
-    here = pl.ds(pl.multiple_of(second * 32, 32), 32)
     return [
-        own[pl.ds(pl.multiple_of(z * 128 + second * 32, 32), 32), columns_of(t)] + decode(got[z], factor_refs[z], t, here)
+        own[pl.ds(pl.multiple_of(z * 128 + second * 32, 32), 32), columns_of(t)] + decode(got[z], factor_refs[z], t, second * 32, 32)
         for z in range(2)
     ]
 
@@ -362,7 +366,7 @@
     near = both_cores(placed, send_col(placed, 1))
 
     def sent(rows):
-        return jax.ShapeDtypeStruct((rows, width + max(128, 4096 // rows)), jnp.int16)
+        return jax.ShapeDtypeStruct((WIDTH_TILES * rows + 32, 128), jnp.int16)
 
     def floats(rows):
         return jax.ShapeDtypeStruct((rows, width), jnp.float32)
@@ -393,18 +397,13 @@
     over, _ = lax.optimization_barrier((over, call.last))
     far = both_cores(over, send_col(over, 1))
 
-    def far_part(rows, after):
-        return call(
-            functools.partial(far_kernel, rows), weights + [far], [sent(64)] * 4, left_rows(128) + scales(4), after
-        )
-
-    f = exchange_both(far_part(opposite_rows, ()), n)
-    i = exchange_both(far_part(free_rows, n), f)
+    f = exchange_both(call(far_kernel, weights + [far], [sent(128)] * 4, left_rows(256) + scales(4)), n)
+    later = call(later_kernel, weights + [near, far, *n], [kept(256)] * 2, left_rows(256) + scales(4))
+    d = []
+    for k in range(2):
+        p, q = call(pass_on_kernel, [later[k], *f[2 * k:2 * k + 2]], [sent(128)] * 2, scales(4))
+        d += [send(p, FORWARD[k]), send(q, BACKWARD[k])]
     operands = [v for k in range(2) for v in (*n[2 * k:2 * k + 2], *f[2 * k:2 * k + 2])]
-    d = exchange_both(
-        call(pass_on_kernel, weights + [near, far] + operands, [sent(128)] * 4, left_rows(256) + scales(12)), i
-    )
-    operands = [v for k in range(2) for v in (*n[2 * k:2 * k + 2], *i[2 * k:2 * k + 2])]
     own = call(own_kernel, weights + [near, far] + operands, [kept(256)] * 2, left_rows(256) + scales(8))
 
     def stage_one_of(kind):

time: 149 us -> 147 us (0.987)
  starting transfers between devices: 48.9 us -> 45.1 us
    ppermute x26 -> x22, starting transfers between devices: 32.7 us -> 27.5 us  [send(): return lax.ppermute(value, 'row', pairs)]
    ppermute x2, starting transfers between devices: 2.94 us -> 5.47 us  [per_device(): b, c = (send_col(b, 2), lax.ppermute(c, ('row', 'col'), DIAGONAL))]
    ppermute x26 -> x22, waiting for transfers between devices: 37.7 us -> 39.7 us  [send(): return lax.ppermute(value, 'row', pairs)]
    pallas_call x13 -> x14, Pallas kernels: 31.5 us -> 32.4 us  [__call__(): pl.pallas_call(lambda *refs: kernel(position(), *refs[skipped:]), in_spec...]
  transfers between devices with their start and end apart: 34 -> 30, of which waited for: 12 -> 12; matrix products, arithmetic and copies ran while one was open for 0% -> 0% of each run, Pallas kernels for 21% -> 22%
where the time goes in v6:
time: 147 us; the launch traced here: 146 us
  waiting for transfers between devices  46.2 us (31%)
  starting transfers between devices  45.1 us (31%)
  Pallas kernels  35 us (24%)
  blocking collectives  18.6 us (13%)
    ppermute x22, waiting for transfers between devices, send(): return lax.ppermute(value, 'row', pairs)  39.7 us
    pallas_call x14, Pallas kernels, __call__(): pl.pallas_call(lambda *refs: kernel(position(), *refs[skipped:]), in_spec...  32.4 us
    ppermute x22, starting transfers between devices, send(): return lax.ppermute(value, 'row', pairs)  27.5 us
    all_to_all x1, blocking collectives, per_device(): lax.all_to_all(ordered, 'row', split_axis=1, concat_axis=0, tiled=True)  18.6 us
    ppermute x6, starting transfers between devices, send_col(): return lax.ppermute(value, 'col', [(c, c ^ step) for c in range(4)])  12.1 us
    ppermute x2, starting transfers between devices, per_device(): b, c = (send_col(b, 2), lax.ppermute(c, ('row', 'col'), DIAGONAL))  5.47 us
    ppermute x2, waiting for transfers between devices, per_device(): b, c = (send_col(b, 2), lax.ppermute(c, ('row', 'col'), DIAGONAL))  3.58 us
  transfers between devices with their start and end apart: 30, of which 12 were waited for; matrix products, arithmetic and copies ran while one was open for 0% of the time, Pallas kernels for 22%

profile of v6, /device:TPU:1, one launch (start us, length us, event | category | flops | bytes accessed | tf_op | source)
XLA Modules:
  0.0 146.4 jit_solution(15835336489719865143)
XLA Ops:
  0.0 2.6 %arrange.1 = (bf16[8,28672]{1,0:T(8,128)(2,1)}, bf16[7,7168]{1,0:T(8,128)(2,1)S(1)}) custom-call(s32[224]{0:T(256)} %order.1, bf16[8,28672]{1,0:T(8,128)(2,1)} %values.1, s32[8,224]{1,0:T(8,128)} %flags.1, s32[7,56]{1,0:T(8,128)} %tile_flags.1), custom_call_target="tpu_custom_call" | custom-call | tf_op jit(solution)/shard_map/arrange/pallas_call | solution.py:348
  2.6 18.6 %all_to_all.19 = bf16[8,32,896]{2,0,1:T(8,128)(2,1)S(1)} all-to-all(bf16[8,32,896]{2,0,1:T(8,128)(2,1)} %bitcast.40), channel_id=1, replica_groups=mesh['row'=32,'col'=4] {'row'}, dimensions={1} | all-to-all | bytes 917504 | tf_op jit(solution)/shard_map/all_to_all | solution.py:359
  21.2 2.6 %collective-permute-start = (bf16[256,896]{1,0:T(8,128)(2,1)S(1)}, bf16[256,896]{1,0:T(8,128)(2,1)S(1)}, u32[]{:S(2)}, u32[]{:S(2)}) collective-permute-start(bf16[256,896]{1,0:T(8,128)(2,1)S(1)} %bitcast.37), channel_id=1, source_target_pairs={{0,1},{1,0},{2,3},{3,2},{4,5},{5,4},{6,7},{7,6},{8,9},{9,8},{10,11... | collective-permute-start | bytes 1376264 | tf_op jit(solution)/shard_map/ppermute | solution.py:39
  23.8 3.3 %collective-permute-start.1 = (bf16[256,896]{1,0:T(8,128)(2,1)S(1)}, bf16[256,896]{1,0:T(8,128)(2,1)S(1)}, u32[]{:S(2)}, u32[]{:S(2)}) collective-permute-start(bf16[256,896]{1,0:T(8,128)(2,1)S(1)} %bitcast.38), channel_id=1, source_target_pairs={{0,2},{1,3},{2,0},{3,1},{4,6},{5,7},{6,4},{7,5},{8,10},{9,11},{10,... | collective-permute-start | bytes 1376264 | tf_op jit(solution)/shard_map/ppermute | solution.py:39
  27.3 9.0 %begin_kernel.1 = (s16[3616,128]{1,0:T(8,128)(2,1)S(1)}, s16[3616,128]{1,0:T(8,128)(2,1)S(1)}, s16[3616,128]{1,0:T(8,128)(2,1)S(1)}, s16[3616,128]{1,0:T(8,128)(...) custom-call(bf16[256,896]{1,0:T(8,128)(2,1)S(1)} %bitcast.39, bf16[896,7168]{1,0:T(8,128)(2,1)} %refs_1_.1, ...), custom_call_target="tpu_custom_call" | custom-call | flops 1000 | bytes 1000 | tf_op jit(solution)/shard_map/begin_kernel/pallas_call | solution.py:322
  36.7 2.3 %collective-permute-start.4 = (s16[3616,128]{1,0:T(8,128)(2,1)S(1)}, s16[3616,128]{1,0:T(8,128)(2,1)S(1)}, u32[]{:S(2)}, u32[]{:S(2)}) collective-permute-start(s16[3616,128]{1,0:T(8,128)(2,1)S(1)} %get-tuple-element.57), channel_id=1, source_target_pairs={{0,48},{4,52},{8,56},{12,60},{16,0},{20,4},{24,8},{28,12},{32,16},... | collective-permute-start | bytes 2777096 | tf_op jit(solution)/shard_map/ppermute | solution.py:35
  40.1 2.5 %collective-permute-start.6 = (s16[3616,128]{1,0:T(8,128)(2,1)S(1)}, s16[3616,128]{1,0:T(8,128)(2,1)S(1)}, u32[]{:S(2)}, u32[]{:S(2)}) collective-permute-start(s16[3616,128]{1,0:T(8,128)(2,1)S(1)} %get-tuple-element.59), channel_id=1, source_target_pairs={{0,12},{4,0},{8,4},{12,8},{16,28},{20,16},{24,20},{28,24},{32,44},... | collective-permute-start | bytes 2777096 | tf_op jit(solution)/shard_map/ppermute | solution.py:35
  42.8 5.9 %far_kernel.1 = (s16[3616,128]{1,0:T(8,128)(2,1)S(1)}, s16[3616,128]{1,0:T(8,128)(2,1)S(1)}, s16[3616,128]{1,0:T(8,128)(2,1)S(1)}, s16[3616,128]{1,0:T(8,128)(2,1)S(1)}) custom-call(s16[3616,128]{1,0:T(8,128)(2,1)S(1)} %get-tuple-element.52.refs_0_, bf16[896,3584]{1,0:T(8,128)(2,1)S(1)} %get-tuple-element.53.refs_1_, ...), custom_call_target="tpu_custom_call" | custom-call | flops 1000 | bytes 1000 | tf_op jit(solution)/shard_map/far_kernel/pallas_call | solution.py:322
  48.7 10.7 %collective-permute-done.3.refs_5_ = s16[3616,128]{1,0:T(8,128)(2,1)S(1)} collective-permute-done((s16[3616,128]{1,0:T(8,128)(2,1)S(1)}, s16[3616,128]{1,0:T(8,128)(2,1)S(1)}, u32[]{:S(2)}, u32[]{:S(2)}) %collective-permute-start.3) | collective-permute-done | bytes 925728 | tf_op jit(solution)/shard_map/ppermute | solution.py:35
  59.4 2.7 %collective-permute-start.8 = (s16[3616,128]{1,0:T(8,128)(2,1)S(1)}, s16[3616,128]{1,0:T(8,128)(2,1)S(1)}, u32[]{:S(2)}, u32[]{:S(2)}) collective-permute-start(s16[3616,128]{1,0:T(8,128)(2,1)S(1)} %get-tuple-element.63), channel_id=1, source_target_pairs={{0,48},{4,52},{8,56},{12,60},{16,0},{20,4},{24,8},{28,12},{32,16},... | collective-permute-start | bytes 2777096 | tf_op jit(solution)/shard_map/ppermute | solution.py:35
  63.3 2.7 %collective-permute-start.10 = (s16[3616,128]{1,0:T(8,128)(2,1)S(1)}, s16[3616,128]{1,0:T(8,128)(2,1)S(1)}, u32[]{:S(2)}, u32[]{:S(2)}) collective-permute-start(s16[3616,128]{1,0:T(8,128)(2,1)S(1)} %get-tuple-element.69), channel_id=1, source_target_pairs={{0,12},{4,0},{8,4},{12,8},{16,28},{20,16},{24,20},{28,24},{32,44},... | collective-permute-start | bytes 2777096 | tf_op jit(solution)/shard_map/ppermute | solution.py:35
  66.0 5.1 %later_kernel.1 = (f32[256,3584]{1,0:T(8,128)S(1)}, f32[256,3584]{1,0:T(8,128)S(1)}) custom-call(s16[3616,128]{1,0:T(8,128)(2,1)S(1)} %get-tuple-element.62.refs_0_, bf16[896,3584]{1,0:T(8,128)(2,1)S(1)} %get-tuple-element.53.refs_1_, bf16[896,3584]{1,0:T(8,128)(2,1)S(1)} %get-tuple-element.54.refs_2_, bf16[512,896]{1,0:T(8,128)(2,1)S(1)} %bitcast.35, ...), custom_call_target="tpu_custom_call" | custom-call | flops 1000 | bytes 1000 | tf_op jit(solution)/shard_map/later_kernel/pallas_call | solution.py:322
  71.0 10.5 %collective-permute-done.7.refs_2_.refs_7_ = s16[3616,128]{1,0:T(8,128)(2,1)S(1)} collective-permute-done((s16[3616,128]{1,0:T(8,128)(2,1)S(1)}, s16[3616,128]{1,0:T(8,128)(2,1)S(1)}, u32[]{:S(2)}, u32[]{:S(2)}) %collective-permute-start.7) | collective-permute-done | bytes 925728 | tf_op jit(solution)/shard_map/ppermute | solution.py:35
  81.6 1.2 pass_on_kernel.2
  83.1 2.5 %collective-permute-start.12 = (s16[3616,128]{1,0:T(8,128)(2,1)S(1)}, s16[3616,128]{1,0:T(8,128)(2,1)S(1)}, u32[]{:S(2)}, u32[]{:S(2)}) collective-permute-start(s16[3616,128]{1,0:T(8,128)(2,1)S(1)} %get-tuple-element.72), channel_id=1, source_target_pairs={{0,48},{4,52},{8,56},{12,60},{16,0},{20,4},{24,8},{28,12},{32,16},... | collective-permute-start | bytes 2777096 | tf_op jit(solution)/shard_map/ppermute | solution.py:35
  85.8 1.2 pass_on_kernel.3
  87.2 2.5 %collective-permute-start.14 = (s16[3616,128]{1,0:T(8,128)(2,1)S(1)}, s16[3616,128]{1,0:T(8,128)(2,1)S(1)}, u32[]{:S(2)}, u32[]{:S(2)}) collective-permute-start(s16[3616,128]{1,0:T(8,128)(2,1)S(1)} %get-tuple-element.75), channel_id=1, source_target_pairs={{0,12},{4,0},{8,4},{12,8},{16,28},{20,16},{24,20},{28,24},{32,44},... | collective-permute-start | bytes 2777096 | tf_op jit(solution)/shard_map/ppermute | solution.py:35
  89.7 5.1 %own_kernel.1 = (f32[256,3584]{1,0:T(8,128)S(1)}, f32[256,3584]{1,0:T(8,128)S(1)}) custom-call(s16[3616,128]{1,0:T(8,128)(2,1)S(1)} %get-tuple-element.70.refs_0_, bf16[896,3584]{1,0:T(8,128)(2,1)S(1)} %get-tuple-element.53.refs_1_, bf16[896,3584]{1,0:T(8,128)(2,1)S(1)} %get-tuple-element.54.refs_2_, bf16[512,896]{1,0:T(8,128)(2,1)S(1)} %bitcast.36, ...), custom_call_target="tpu_custom_call" | custom-call | flops 1000 | bytes 1000 | tf_op jit(solution)/shard_map/own_kernel/pallas_call | solution.py:322
  94.9 9.2 %collective-permute-done.11.refs_2_ = s16[3616,128]{1,0:T(8,128)(2,1)S(1)} collective-permute-done((s16[3616,128]{1,0:T(8,128)(2,1)S(1)}, s16[3616,128]{1,0:T(8,128)(2,1)S(1)}, u32[]{:S(2)}, u32[]{:S(2)}) %collective-permute-start.11) | collective-permute-done | bytes 925728 | tf_op jit(solution)/shard_map/ppermute | solution.py:35
  104.8 2.5 %collective-permute-start.16 = (s16[928,128]{1,0:T(8,128)(2,1)S(1)}, s16[928,128]{1,0:T(8,128)(2,1)S(1)}, u32[]{:S(2)}, u32[]{:S(2)}) collective-permute-start(s16[928,128]{1,0:T(8,128)(2,1)S(1)} %get-tuple-element.77), channel_id=1, source_target_pairs={{0,12},{4,0},{8,4},{12,8},{16,28},{20,16},{24,20},{28,24},{32,44},... | collective-permute-start | bytes 712712 | tf_op jit(solution)/shard_map/ppermute | solution.py:35
  108.5 2.7 %collective-permute-start.18 = (s16[928,128]{1,0:T(8,128)(2,1)S(1)}, s16[928,128]{1,0:T(8,128)(2,1)S(1)}, u32[]{:S(2)}, u32[]{:S(2)}) collective-permute-start(s16[928,128]{1,0:T(8,128)(2,1)S(1)} %get-tuple-element.79), channel_id=1, source_target_pairs={{0,48},{4,52},{8,56},{12,60},{16,0},{20,4},{24,8},{28,12},{32,16},... | collective-permute-start | bytes 712712 | tf_op jit(solution)/shard_map/ppermute | solution.py:35
  111.2 2.6 %collective-permute-done.15.refs_4_ = s16[928,128]{1,0:T(8,128)(2,1)S(1)} collective-permute-done((s16[928,128]{1,0:T(8,128)(2,1)S(1)}, s16[928,128]{1,0:T(8,128)(2,1)S(1)}, u32[]{:S(2)}, u32[]{:S(2)}) %collective-permute-start.15) | collective-permute-done | bytes 237600 | tf_op jit(solution)/shard_map/ppermute | solution.py:35
  114.8 2.7 %collective-permute-start.20 = (s16[1824,128]{1,0:T(8,128)(2,1)S(1)}, s16[1824,128]{1,0:T(8,128)(2,1)S(1)}, u32[]{:S(2)}, u32[]{:S(2)}) collective-permute-start(s16[1824,128]{1,0:T(8,128)(2,1)S(1)} %get-tuple-element.81), channel_id=1, source_target_pairs={{0,12},{4,0},{8,4},{12,8},{16,28},{20,16},{24,20},{28,24},{32,44},... | collective-permute-start | bytes 1400840 | tf_op jit(solution)/shard_map/ppermute | solution.py:35
  118.6 2.7 %collective-permute-start.22 = (s16[1824,128]{1,0:T(8,128)(2,1)S(1)}, s16[1824,128]{1,0:T(8,128)(2,1)S(1)}, u32[]{:S(2)}, u32[]{:S(2)}) collective-permute-start(s16[1824,128]{1,0:T(8,128)(2,1)S(1)} %get-tuple-element.83), channel_id=1, source_target_pairs={{0,48},{4,52},{8,56},{12,60},{16,0},{20,4},{24,8},{28,12},{32,16},... | collective-permute-start | bytes 1400840 | tf_op jit(solution)/shard_map/ppermute | solution.py:35
  121.3 3.5 %collective-permute-done.19.refs_4_ = s16[1824,128]{1,0:T(8,128)(2,1)S(1)} collective-permute-done((s16[1824,128]{1,0:T(8,128)(2,1)S(1)}, s16[1824,128]{1,0:T(8,128)(2,1)S(1)}, u32[]{:S(2)}, u32[]{:S(2)}) %collective-permute-start.19) | collective-permute-done | bytes 466976 | tf_op jit(solution)/shard_map/ppermute | solution.py:35
  126.7 2.8 %collective-permute-start.25 = (s16[480,128]{1,0:T(8,128)(2,1)S(1)}, s16[480,128]{1,0:T(8,128)(2,1)S(1)}, u32[]{:S(2)}, u32[]{:S(2)}) collective-permute-start(s16[480,128]{1,0:T(8,128)(2,1)S(1)} %get-tuple-element.87), channel_id=1, source_target_pairs={{0,66},{1,67},{2,64},{3,65},{4,70},{5,71},{6,68},{7,69},{8,74},{9,... | collective-permute-start | bytes 368648 | tf_op jit(solution)/shard_map/ppermute | solution.py:426
  130.4 1.2 collective-permute-start.27
  131.6 2.7 %collective-permute-start.28 = (s16[480,128]{1,0:T(8,128)(2,1)S(1)}, s16[480,128]{1,0:T(8,128)(2,1)S(1)}, u32[]{:S(2)}, u32[]{:S(2)}) collective-permute-start(s16[480,128]{1,0:T(8,128)(2,1)S(1)} %get-tuple-element.91), channel_id=1, source_target_pairs={{0,66},{1,67},{2,64},{3,65},{4,70},{5,71},{6,68},{7,69},{8,74},{9,... | collective-permute-start | bytes 368648 | tf_op jit(solution)/shard_map/ppermute | solution.py:426
  134.4 1.2 collective-permute-done.26.refs_2_
  135.6 1.8 %collective-permute-done.27.refs_3_ = s16[480,128]{1,0:T(8,128)(2,1)S(1)} collective-permute-done((s16[480,128]{1,0:T(8,128)(2,1)S(1)}, s16[480,128]{1,0:T(8,128)(2,1)S(1)}, u32[]{:S(2)}, u32[]{:S(2)}) %collective-permute-start.27) | collective-permute-done | bytes 122912 | tf_op jit(solution)/shard_map/ppermute | solution.py:39
  137.4 3.6 %collective-permute-done.28.refs_4_ = s16[480,128]{1,0:T(8,128)(2,1)S(1)} collective-permute-done((s16[480,128]{1,0:T(8,128)(2,1)S(1)}, s16[480,128]{1,0:T(8,128)(2,1)S(1)}, u32[]{:S(2)}, u32[]{:S(2)}) %collective-permute-start.28) | collective-permute-done | bytes 122912 | tf_op jit(solution)/shard_map/ppermute | solution.py:426
  141.2 3.2 %collective-permute-start.29 = (bf16[8,14336]{1,0:T(8,128)(2,1)S(1)}, bf16[8,14336]{1,0:T(8,128)(2,1)S(1)}, u32[]{:S(2)}, u32[]{:S(2)}) collective-permute-start(bf16[8,14336]{1,0:T(8,128)(2,1)S(1)} %dynamic-slice_bitcast_fusion), channel_id=1, source_target_pairs={{0,1},{1,0},{2,3},{3,2},{4,5},{5,4},{6,7},{7,6},{8,9},{9,8},{10,11... | collective-permute-start | bytes 688136 | tf_op jit(solution)/shard_map/ppermute | solution.py:39
  (53 shorter events, 12.9 us)
Async XLA Ops:
  21.2 5.9 %collective-permute-start = (bf16[256,896]{1,0:T(8,128)(2,1)S(1)}, bf16[256,896]{1,0:T(8,128)(2,1)S(1)}, u32[]{:S(2)}, u32[]{:S(2)}) collective-permute-start(bf16[256,896]{1,0:T(8,128)(2,1)S(1)} %bitcast.37), channel_id=1, source_target_pairs={{0,1},{1,0},{2,3},{3,2},{4,5},{5,4},{6,7},{7,6},{8,9},{9,8},{10,11... | collective-permute-start | bytes 1376264 | tf_op jit(solution)/shard_map/ppermute | solution.py:39
  23.8 15.3 %collective-permute-start.1 = (bf16[256,896]{1,0:T(8,128)(2,1)S(1)}, bf16[256,896]{1,0:T(8,128)(2,1)S(1)}, u32[]{:S(2)}, u32[]{:S(2)}) collective-permute-start(bf16[256,896]{1,0:T(8,128)(2,1)S(1)} %bitcast.38), channel_id=1, source_target_pairs={{0,2},{1,3},{2,0},{3,1},{4,6},{5,7},{6,4},{7,5},{8,10},{9,11},{10,... | collective-permute-start | bytes 1376264 | tf_op jit(solution)/shard_map/ppermute | solution.py:39
  36.3 23.1 %collective-permute-start.3 = (s16[3616,128]{1,0:T(8,128)(2,1)S(1)}, s16[3616,128]{1,0:T(8,128)(2,1)S(1)}, u32[]{:S(2)}, u32[]{:S(2)}) collective-permute-start(s16[3616,128]{1,0:T(8,128)(2,1)S(1)} %get-tuple-element.52.refs_0_), channel_id=1, source_target_pairs={{0,16},{4,20},{8,24},{12,28},{16,32},{20,36},{24,40},{28,44},{32,4... | collective-permute-start | bytes 2777096 | tf_op jit(solution)/shard_map/ppermute | solution.py:35
  36.7 22.7 %collective-permute-start.4 = (s16[3616,128]{1,0:T(8,128)(2,1)S(1)}, s16[3616,128]{1,0:T(8,128)(2,1)S(1)}, u32[]{:S(2)}, u32[]{:S(2)}) collective-permute-start(s16[3616,128]{1,0:T(8,128)(2,1)S(1)} %get-tuple-element.57), channel_id=1, source_target_pairs={{0,48},{4,52},{8,56},{12,60},{16,0},{20,4},{24,8},{28,12},{32,16},... | collective-permute-start | bytes 2777096 | tf_op jit(solution)/shard_map/ppermute | solution.py:35
  39.1 3.5 %collective-permute-start.2 = (bf16[256,896]{1,0:T(8,128)(2,1)S(1)}, bf16[256,896]{1,0:T(8,128)(2,1)S(1)}, u32[]{:S(2)}, u32[]{:S(2)}) collective-permute-start(bf16[256,896]{1,0:T(8,128)(2,1)S(1)} %collective-permute-done.1), channel_id=1, source_target_pairs={{0,1},{1,0},{2,3},{3,2},{4,5},{5,4},{6,7},{7,6},{8,9},{9,8},{10,11... | collective-permute-start | bytes 1376264 | tf_op jit(solution)/shard_map/ppermute | solution.py:39
  39.9 23.4 %collective-permute-start.5 = (s16[3616,128]{1,0:T(8,128)(2,1)S(1)}, s16[3616,128]{1,0:T(8,128)(2,1)S(1)}, u32[]{:S(2)}, u32[]{:S(2)}) collective-permute-start(s16[3616,128]{1,0:T(8,128)(2,1)S(1)} %get-tuple-element.58), channel_id=1, source_target_pairs={{0,4},{4,8},{8,12},{12,0},{16,20},{20,24},{24,28},{28,16},{32,36},... | collective-permute-start | bytes 2777096 | tf_op jit(solution)/shard_map/ppermute | solution.py:35
  40.1 23.2 %collective-permute-start.6 = (s16[3616,128]{1,0:T(8,128)(2,1)S(1)}, s16[3616,128]{1,0:T(8,128)(2,1)S(1)}, u32[]{:S(2)}, u32[]{:S(2)}) collective-permute-start(s16[3616,128]{1,0:T(8,128)(2,1)S(1)} %get-tuple-element.59), channel_id=1, source_target_pairs={{0,12},{4,0},{8,4},{12,8},{16,28},{20,16},{24,20},{28,24},{32,44},... | collective-permute-start | bytes 2777096 | tf_op jit(solution)/shard_map/ppermute | solution.py:35
  59.4 22.1 %collective-permute-start.7 = (s16[3616,128]{1,0:T(8,128)(2,1)S(1)}, s16[3616,128]{1,0:T(8,128)(2,1)S(1)}, u32[]{:S(2)}, u32[]{:S(2)}) collective-permute-start(s16[3616,128]{1,0:T(8,128)(2,1)S(1)} %get-tuple-element.62.refs_0_), channel_id=1, source_target_pairs={{0,16},{4,20},{8,24},{12,28},{16,32},{20,36},{24,40},{28,44},{32,4... | collective-permute-start | bytes 2777096 | tf_op jit(solution)/shard_map/ppermute | solution.py:35
  59.4 22.1 %collective-permute-start.8 = (s16[3616,128]{1,0:T(8,128)(2,1)S(1)}, s16[3616,128]{1,0:T(8,128)(2,1)S(1)}, u32[]{:S(2)}, u32[]{:S(2)}) collective-permute-start(s16[3616,128]{1,0:T(8,128)(2,1)S(1)} %get-tuple-element.63), channel_id=1, source_target_pairs={{0,48},{4,52},{8,56},{12,60},{16,0},{20,4},{24,8},{28,12},{32,16},... | collective-permute-start | bytes 2777096 | tf_op jit(solution)/shard_map/ppermute | solution.py:35
  63.3 22.5 %collective-permute-start.9 = (s16[3616,128]{1,0:T(8,128)(2,1)S(1)}, s16[3616,128]{1,0:T(8,128)(2,1)S(1)}, u32[]{:S(2)}, u32[]{:S(2)}) collective-permute-start(s16[3616,128]{1,0:T(8,128)(2,1)S(1)} %get-tuple-element.68), channel_id=1, source_target_pairs={{0,4},{4,8},{8,12},{12,0},{16,20},{20,24},{24,28},{28,16},{32,36},... | collective-permute-start | bytes 2777096 | tf_op jit(solution)/shard_map/ppermute | solution.py:35
  63.3 22.5 %collective-permute-start.10 = (s16[3616,128]{1,0:T(8,128)(2,1)S(1)}, s16[3616,128]{1,0:T(8,128)(2,1)S(1)}, u32[]{:S(2)}, u32[]{:S(2)}) collective-permute-start(s16[3616,128]{1,0:T(8,128)(2,1)S(1)} %get-tuple-element.69), channel_id=1, source_target_pairs={{0,12},{4,0},{8,4},{12,8},{16,28},{20,16},{24,20},{28,24},{32,44},... | collective-permute-start | bytes 2777096 | tf_op jit(solution)/shard_map/ppermute | solution.py:35
  82.8 21.3 %collective-permute-start.11 = (s16[3616,128]{1,0:T(8,128)(2,1)S(1)}, s16[3616,128]{1,0:T(8,128)(2,1)S(1)}, u32[]{:S(2)}, u32[]{:S(2)}) collective-permute-start(s16[3616,128]{1,0:T(8,128)(2,1)S(1)} %get-tuple-element.64.refs_0_), channel_id=1, source_target_pairs={{0,16},{4,20},{8,24},{12,28},{16,32},{20,36},{24,40},{28,44},{32,4... | collective-permute-start | bytes 2777096 | tf_op jit(solution)/shard_map/ppermute | solution.py:35
  83.1 21.0 %collective-permute-start.12 = (s16[3616,128]{1,0:T(8,128)(2,1)S(1)}, s16[3616,128]{1,0:T(8,128)(2,1)S(1)}, u32[]{:S(2)}, u32[]{:S(2)}) collective-permute-start(s16[3616,128]{1,0:T(8,128)(2,1)S(1)} %get-tuple-element.72), channel_id=1, source_target_pairs={{0,48},{4,52},{8,56},{12,60},{16,0},{20,4},{24,8},{28,12},{32,16},... | collective-permute-start | bytes 2777096 | tf_op jit(solution)/shard_map/ppermute | solution.py:35
  87.0 20.9 %collective-permute-start.13 = (s16[3616,128]{1,0:T(8,128)(2,1)S(1)}, s16[3616,128]{1,0:T(8,128)(2,1)S(1)}, u32[]{:S(2)}, u32[]{:S(2)}) collective-permute-start(s16[3616,128]{1,0:T(8,128)(2,1)S(1)} %get-tuple-element.70.refs_0_), channel_id=1, source_target_pairs={{0,4},{4,8},{8,12},{12,0},{16,20},{20,24},{24,28},{28,16},{32,36},... | collective-permute-start | bytes 2777096 | tf_op jit(solution)/shard_map/ppermute | solution.py:35
  87.2 20.7 %collective-permute-start.14 = (s16[3616,128]{1,0:T(8,128)(2,1)S(1)}, s16[3616,128]{1,0:T(8,128)(2,1)S(1)}, u32[]{:S(2)}, u32[]{:S(2)}) collective-permute-start(s16[3616,128]{1,0:T(8,128)(2,1)S(1)} %get-tuple-element.75), channel_id=1, source_target_pairs={{0,12},{4,0},{8,4},{12,8},{16,28},{20,16},{24,20},{28,24},{32,44},... | collective-permute-start | bytes 2777096 | tf_op jit(solution)/shard_map/ppermute | solution.py:35
  104.6 9.1 %collective-permute-start.15 = (s16[928,128]{1,0:T(8,128)(2,1)S(1)}, s16[928,128]{1,0:T(8,128)(2,1)S(1)}, u32[]{:S(2)}, u32[]{:S(2)}) collective-permute-start(s16[928,128]{1,0:T(8,128)(2,1)S(1)} %get-tuple-element.73.refs_0_), channel_id=1, source_target_pairs={{0,4},{4,8},{8,12},{12,0},{16,20},{20,24},{24,28},{28,16},{32,36},... | collective-permute-start | bytes 712712 | tf_op jit(solution)/shard_map/ppermute | solution.py:35
  104.8 8.9 %collective-permute-start.16 = (s16[928,128]{1,0:T(8,128)(2,1)S(1)}, s16[928,128]{1,0:T(8,128)(2,1)S(1)}, u32[]{:S(2)}, u32[]{:S(2)}) collective-permute-start(s16[928,128]{1,0:T(8,128)(2,1)S(1)} %get-tuple-element.77), channel_id=1, source_target_pairs={{0,12},{4,0},{8,4},{12,8},{16,28},{20,16},{24,20},{28,24},{32,44},... | collective-permute-start | bytes 712712 | tf_op jit(solution)/shard_map/ppermute | solution.py:35
  108.4 9.1 %collective-permute-start.17 = (s16[928,128]{1,0:T(8,128)(2,1)S(1)}, s16[928,128]{1,0:T(8,128)(2,1)S(1)}, u32[]{:S(2)}, u32[]{:S(2)}) collective-permute-start(s16[928,128]{1,0:T(8,128)(2,1)S(1)} %get-tuple-element.76.refs_0_), channel_id=1, source_target_pairs={{0,16},{4,20},{8,24},{12,28},{16,32},{20,36},{24,40},{28,44},{32,4... | collective-permute-start | bytes 712712 | tf_op jit(solution)/shard_map/ppermute | solution.py:35
  108.5 9.0 %collective-permute-start.18 = (s16[928,128]{1,0:T(8,128)(2,1)S(1)}, s16[928,128]{1,0:T(8,128)(2,1)S(1)}, u32[]{:S(2)}, u32[]{:S(2)}) collective-permute-start(s16[928,128]{1,0:T(8,128)(2,1)S(1)} %get-tuple-element.79), channel_id=1, source_target_pairs={{0,48},{4,52},{8,56},{12,60},{16,0},{20,4},{24,8},{28,12},{32,16},... | collective-permute-start | bytes 712712 | tf_op jit(solution)/shard_map/ppermute | solution.py:35
  114.7 10.0 %collective-permute-start.19 = (s16[1824,128]{1,0:T(8,128)(2,1)S(1)}, s16[1824,128]{1,0:T(8,128)(2,1)S(1)}, u32[]{:S(2)}, u32[]{:S(2)}) collective-permute-start(s16[1824,128]{1,0:T(8,128)(2,1)S(1)} %get-tuple-element.78.refs_0_), channel_id=1, source_target_pairs={{0,4},{4,8},{8,12},{12,0},{16,20},{20,24},{24,28},{28,16},{32,36},... | collective-permute-start | bytes 1400840 | tf_op jit(solution)/shard_map/ppermute | solution.py:35
  114.8 9.9 %collective-permute-start.20 = (s16[1824,128]{1,0:T(8,128)(2,1)S(1)}, s16[1824,128]{1,0:T(8,128)(2,1)S(1)}, u32[]{:S(2)}, u32[]{:S(2)}) collective-permute-start(s16[1824,128]{1,0:T(8,128)(2,1)S(1)} %get-tuple-element.81), channel_id=1, source_target_pairs={{0,12},{4,0},{8,4},{12,8},{16,28},{20,16},{24,20},{28,24},{32,44},... | collective-permute-start | bytes 1400840 | tf_op jit(solution)/shard_map/ppermute | solution.py:35
  118.5 11.0 %collective-permute-start.21 = (s16[1824,128]{1,0:T(8,128)(2,1)S(1)}, s16[1824,128]{1,0:T(8,128)(2,1)S(1)}, u32[]{:S(2)}, u32[]{:S(2)}) collective-permute-start(s16[1824,128]{1,0:T(8,128)(2,1)S(1)} %get-tuple-element.80.refs_0_), channel_id=1, source_target_pairs={{0,16},{4,20},{8,24},{12,28},{16,32},{20,36},{24,40},{28,44},{32,4... | collective-permute-start | bytes 1400840 | tf_op jit(solution)/shard_map/ppermute | solution.py:35
  118.6 10.9 %collective-permute-start.22 = (s16[1824,128]{1,0:T(8,128)(2,1)S(1)}, s16[1824,128]{1,0:T(8,128)(2,1)S(1)}, u32[]{:S(2)}, u32[]{:S(2)}) collective-permute-start(s16[1824,128]{1,0:T(8,128)(2,1)S(1)} %get-tuple-element.83), channel_id=1, source_target_pairs={{0,48},{4,52},{8,56},{12,60},{16,0},{20,4},{24,8},{28,12},{32,16},... | collective-permute-start | bytes 1400840 | tf_op jit(solution)/shard_map/ppermute | solution.py:35
  125.5 6.0 %collective-permute-start.23 = (s16[480,128]{1,0:T(8,128)(2,1)S(1)}, s16[480,128]{1,0:T(8,128)(2,1)S(1)}, u32[]{:S(2)}, u32[]{:S(2)}) collective-permute-start(s16[480,128]{1,0:T(8,128)(2,1)S(1)} %get-tuple-element.82.refs_0_), channel_id=1, source_target_pairs={{0,64},{4,68},{8,72},{12,76},{16,80},{20,84},{24,88},{28,92},{32,9... | collective-permute-start | bytes 368648 | tf_op jit(solution)/shard_map/ppermute | solution.py:35
  125.6 8.6 %collective-permute-start.24 = (s16[480,128]{1,0:T(8,128)(2,1)S(1)}, s16[480,128]{1,0:T(8,128)(2,1)S(1)}, u32[]{:S(2)}, u32[]{:S(2)}) collective-permute-start(s16[480,128]{1,0:T(8,128)(2,1)S(1)} %get-tuple-element.86), channel_id=1, source_target_pairs={{0,2},{1,3},{2,0},{3,1},{4,6},{5,7},{6,4},{7,5},{8,10},{9,11},{10,... | collective-permute-start | bytes 368648 | tf_op jit(solution)/shard_map/ppermute | solution.py:39
  126.7 7.6 %collective-permute-start.25 = (s16[480,128]{1,0:T(8,128)(2,1)S(1)}, s16[480,128]{1,0:T(8,128)(2,1)S(1)}, u32[]{:S(2)}, u32[]{:S(2)}) collective-permute-start(s16[480,128]{1,0:T(8,128)(2,1)S(1)} %get-tuple-element.87), channel_id=1, source_target_pairs={{0,66},{1,67},{2,64},{3,65},{4,70},{5,71},{6,68},{7,69},{8,74},{9,... | collective-permute-start | bytes 368648 | tf_op jit(solution)/shard_map/ppermute | solution.py:426
  130.3 5.3 %collective-permute-start.26 = (s16[480,128]{1,0:T(8,128)(2,1)S(1)}, s16[480,128]{1,0:T(8,128)(2,1)S(1)}, u32[]{:S(2)}, u32[]{:S(2)}) collective-permute-start(s16[480,128]{1,0:T(8,128)(2,1)S(1)} %get-tuple-element.84.refs_0_), channel_id=1, source_target_pairs={{0,64},{4,68},{8,72},{12,76},{16,80},{20,84},{24,88},{28,92},{32,9... | collective-permute-start | bytes 368648 | tf_op jit(solution)/shard_map/ppermute | solution.py:35
  130.4 7.0 %collective-permute-start.27 = (s16[480,128]{1,0:T(8,128)(2,1)S(1)}, s16[480,128]{1,0:T(8,128)(2,1)S(1)}, u32[]{:S(2)}, u32[]{:S(2)}) collective-permute-start(s16[480,128]{1,0:T(8,128)(2,1)S(1)} %get-tuple-element.90), channel_id=1, source_target_pairs={{0,2},{1,3},{2,0},{3,1},{4,6},{5,7},{6,4},{7,5},{8,10},{9,11},{10,... | collective-permute-start | bytes 368648 | tf_op jit(solution)/shard_map/ppermute | solution.py:39
  131.6 9.4 %collective-permute-start.28 = (s16[480,128]{1,0:T(8,128)(2,1)S(1)}, s16[480,128]{1,0:T(8,128)(2,1)S(1)}, u32[]{:S(2)}, u32[]{:S(2)}) collective-permute-start(s16[480,128]{1,0:T(8,128)(2,1)S(1)} %get-tuple-element.91), channel_id=1, source_target_pairs={{0,66},{1,67},{2,64},{3,65},{4,70},{5,71},{6,68},{7,69},{8,74},{9,... | collective-permute-start | bytes 368648 | tf_op jit(solution)/shard_map/ppermute | solution.py:426
  141.2 4.3 %collective-permute-start.29 = (bf16[8,14336]{1,0:T(8,128)(2,1)S(1)}, bf16[8,14336]{1,0:T(8,128)(2,1)S(1)}, u32[]{:S(2)}, u32[]{:S(2)}) collective-permute-start(bf16[8,14336]{1,0:T(8,128)(2,1)S(1)} %dynamic-slice_bitcast_fusion), channel_id=1, source_target_pairs={{0,1},{1,0},{2,3},{3,2},{4,5},{5,4},{6,7},{7,6},{8,9},{9,8},{10,11... | collective-permute-start | bytes 688136 | tf_op jit(solution)/shard_map/ppermute | solution.py:39

commit v7 on v6

--- a/solution.py
+++ b/solution.py
@@ -14,6 +14,7 @@
 VMEM_LIMIT = 12 * 1024 * 1024
 BEGIN_LIMIT = 36 * 1024 * 1024
 TILE = 896
+FIRST_TILE = 896
 WIDTH_TILES = 28
 
 
@@ -53,7 +54,7 @@
 
 
 def encode(value, t, out_ref, code_ref):
-    count, rows = TILE // 128, value.shape[0]
+    count, rows = value.shape[1] // 128, value.shape[0]
     coded, code = quantised(value)
     for i in range(count):
         at = t * count + i
@@ -78,10 +79,7 @@
             at += 16
 
 
-def arrange_kernel(order, values, flags, tile_flags, out, flags_out, kept):
-    for l in range(tile_flags.shape[1]):
-        wide = jnp.broadcast_to(tile_flags[:, l:l + 1].astype(jnp.float32), (tile_flags.shape[0], 128))
-        flags_out[:, l * 128:(l + 1) * 128] = wide.astype(jnp.bfloat16)
+def arrange_kernel(order, values, flags, out, kept):
     tiles = flags.shape[1]
     for t in range(tiles):
         at = slice(t * 128, (t + 1) * 128)
@@ -110,17 +108,19 @@
     copy_rows((a,), left, at_q, kind, (pos[1 + kind] + 3) % 4, 0)
 
 
-def begin_kernel(pos, b, m, a, p0, q0, p1, q1, w0, w1, left, sems, *code_refs):
-    tiles = w0.shape[1] // TILE
+def begin_kernel(pos, b, m, a, p0, q0, p1, q1, w0, w1, left, wide, sems, *code_refs):
+    tiles = w0.shape[1] // FIRST_TILE
 
     def copy(kind, t):
         w = (w0, w1)[kind]
-        at = pl.ds(kind * tiles * TILE + t * TILE, TILE)
-        return pltpu.make_async_copy(b.at[:, at], w.at[:, pl.ds(t * TILE, TILE)], sems.at[kind * tiles + t])
+        at = pl.ds(kind * tiles * FIRST_TILE + t * FIRST_TILE, FIRST_TILE)
+        return pltpu.make_async_copy(b.at[:, at], w.at[:, pl.ds(t * FIRST_TILE, FIRST_TILE)], sems.at[kind * tiles + t])
 
     for t in range(tiles):
         for kind in range(2):
             copy(kind, t).start()
+    for l in range(m.shape[1]):
+        wide[:, l * 128:(l + 1) * 128] = jnp.broadcast_to(m[:, l:l + 1].astype(jnp.float32), (m.shape[0], 128))
     clear(*code_refs)
     for kind in range(2):
         opposite_rows(pos, kind, a, left.at[kind], 0, 128)
@@ -128,8 +128,8 @@
     for t in range(tiles):
         for kind, w, p, q in ((0, w0, p0, q0), (1, w1, p1, q1)):
             copy(kind, t).wait()
-            at = slice(t * TILE, (t + 1) * TILE)
-            flags = m[:, (kind * tiles + t) * TILE:(kind * tiles + t + 1) * TILE]
+            at = slice(t * FIRST_TILE, (t + 1) * FIRST_TILE)
+            flags = wide[:, (kind * tiles + t) * FIRST_TILE:(kind * tiles + t + 1) * FIRST_TILE].astype(jnp.bfloat16)
             for k in range(w.shape[0] // 128):
                 rows = slice(k * 128, (k + 1) * 128)
                 w[rows, at] = w[rows, at] * flags[k:k + 1, :]
@@ -345,17 +345,14 @@
     col = lax.axis_index("col")
     core, z_hi = col % 2, col // 2
 
-    ordered, flags = pl.pallas_call(
+    ordered = pl.pallas_call(
         arrange_kernel,
-        in_specs=[pl.BlockSpec(memory_space=pltpu.SMEM)] + [pl.BlockSpec(memory_space=pltpu.VMEM)] * 3,
-        out_specs=[pl.BlockSpec(memory_space=pltpu.VMEM)] * 2,
-        out_shape=[
-            jax.ShapeDtypeStruct((pair_count, full_width), jnp.bfloat16),
-            pltpu.VMEM((integral_mask.shape[0], columns), jnp.bfloat16),
-        ],
+        in_specs=[pl.BlockSpec(memory_space=pltpu.SMEM)] + [pl.BlockSpec(memory_space=pltpu.VMEM)] * 2,
+        out_specs=pl.BlockSpec(memory_space=pltpu.VMEM),
+        out_shape=jax.ShapeDtypeStruct((pair_count, full_width), jnp.bfloat16),
         scratch_shapes=[pltpu.VMEM((pair_count, full_width), jnp.bfloat16)],
         name="arrange",
-    )(tile_order, amplitudes, amplitude_mask, integral_mask)
+    )(tile_order, amplitudes, amplitude_mask)
     placed = lax.all_to_all(ordered, "row", split_axis=1, concat_axis=0, tiled=True)
 
     def both_cores(mine, other):
@@ -389,8 +386,9 @@
         return sends
 
     results = call(
-        begin_kernel, [flags, near], [sent(128)] * 4 + [pltpu.VMEM((depth, width), jnp.bfloat16)] * 2,
-        left_rows(2, 256) + [pltpu.SemaphoreType.DMA((columns // TILE,))] + scales(4), in_hbm=[integrals],
+        begin_kernel, [integral_mask, near], [sent(128)] * 4 + [pltpu.VMEM((depth, width), jnp.bfloat16)] * 2,
+        left_rows(2, 256) + [pltpu.VMEM((integral_mask.shape[0], columns), jnp.float32)]
+        + [pltpu.SemaphoreType.DMA((columns // FIRST_TILE,))] + scales(4), in_hbm=[integrals],
         limit=BEGIN_LIMIT,
     )
     n, weights = exchange_both(results[:4]), list(results[4:])

time: 147 us -> 147 us (level)
  no operation moved by 1% of the time
where the time goes in v7:
time: 147 us; the launch traced here: 146 us
  waiting for transfers between devices  46 us (31%)
  starting transfers between devices  45.2 us (31%)
  Pallas kernels  35 us (24%)
  blocking collectives  18.6 us (13%)
    ppermute x22, waiting for transfers between devices, send(): return lax.ppermute(value, 'row', pairs)  39.5 us
    pallas_call x14, Pallas kernels, __call__(): pl.pallas_call(lambda *refs: kernel(position(), *refs[skipped:]), in_spec...  32.5 us
    ppermute x22, starting transfers between devices, send(): return lax.ppermute(value, 'row', pairs)  27.6 us
    all_to_all x1, blocking collectives, per_device(): lax.all_to_all(ordered, 'row', split_axis=1, concat_axis=0, tiled=True)  18.6 us
    ppermute x6, starting transfers between devices, send_col(): return lax.ppermute(value, 'col', [(c, c ^ step) for c in range(4)])  12.3 us
    ppermute x2, starting transfers between devices, per_device(): b, c = (send_col(b, 2), lax.ppermute(c, ('row', 'col'), DIAGONAL))  5.35 us
    ppermute x2, waiting for transfers between devices, per_device(): b, c = (send_col(b, 2), lax.ppermute(c, ('row', 'col'), DIAGONAL))  3.54 us
    ppermute x6, waiting for transfers between devices, send_col(): return lax.ppermute(value, 'col', [(c, c ^ step) for c in range(4)])  2.95 us
  transfers between devices with their start and end apart: 30, of which 12 were waited for; matrix products, arithmetic and copies ran while one was open for 0% of the time, Pallas kernels for 22%

profile of v7, /device:TPU:1, one launch (start us, length us, event | category | flops | bytes accessed | tf_op | source)
XLA Modules:
  0.0 146.4 jit_solution(319461758237115237)
XLA Ops:
  0.0 2.5 %arrange.1 = bf16[8,28672]{1,0:T(8,128)(2,1)} custom-call(s32[224]{0:T(256)} %order.1, bf16[8,28672]{1,0:T(8,128)(2,1)} %values.1, s32[8,224]{1,0:T(8,128)} %flags.1), custom_call_target="tpu_custom_call" | custom-call | tf_op jit(solution)/shard_map/arrange/pallas_call | solution.py:348
  2.5 18.6 %all_to_all.19 = bf16[8,32,896]{2,0,1:T(8,128)(2,1)S(1)} all-to-all(bf16[8,32,896]{2,0,1:T(8,128)(2,1)} %bitcast.40), channel_id=1, replica_groups=mesh['row'=32,'col'=4] {'row'}, dimensions={1} | all-to-all | bytes 917504 | tf_op jit(solution)/shard_map/all_to_all | solution.py:356
  21.1 2.6 %collective-permute-start = (bf16[256,896]{1,0:T(8,128)(2,1)S(1)}, bf16[256,896]{1,0:T(8,128)(2,1)S(1)}, u32[]{:S(2)}, u32[]{:S(2)}) collective-permute-start(bf16[256,896]{1,0:T(8,128)(2,1)S(1)} %bitcast.37), channel_id=1, source_target_pairs={{0,1},{1,0},{2,3},{3,2},{4,5},{5,4},{6,7},{7,6},{8,9},{9,8},{10,11... | collective-permute-start | bytes 1376264 | tf_op jit(solution)/shard_map/ppermute | solution.py:40
  23.7 3.3 %collective-permute-start.1 = (bf16[256,896]{1,0:T(8,128)(2,1)S(1)}, bf16[256,896]{1,0:T(8,128)(2,1)S(1)}, u32[]{:S(2)}, u32[]{:S(2)}) collective-permute-start(bf16[256,896]{1,0:T(8,128)(2,1)S(1)} %bitcast.38), channel_id=1, source_target_pairs={{0,2},{1,3},{2,0},{3,1},{4,6},{5,7},{6,4},{7,5},{8,10},{9,11},{10,... | collective-permute-start | bytes 1376264 | tf_op jit(solution)/shard_map/ppermute | solution.py:40
  27.3 9.1 %begin_kernel.1 = (s16[3616,128]{1,0:T(8,128)(2,1)S(1)}, s16[3616,128]{1,0:T(8,128)(2,1)S(1)}, s16[3616,128]{1,0:T(8,128)(2,1)S(1)}, s16[3616,128]{1,0:T(8,128)(...) custom-call(bf16[256,896]{1,0:T(8,128)(2,1)S(1)} %bitcast.39, bf16[896,7168]{1,0:T(8,128)(2,1)} %refs_1_.1, ...), custom_call_target="tpu_custom_call" | custom-call | flops 1000 | bytes 1000 | tf_op jit(solution)/shard_map/begin_kernel/pallas_call | solution.py:322
  36.8 2.3 %collective-permute-start.4 = (s16[3616,128]{1,0:T(8,128)(2,1)S(1)}, s16[3616,128]{1,0:T(8,128)(2,1)S(1)}, u32[]{:S(2)}, u32[]{:S(2)}) collective-permute-start(s16[3616,128]{1,0:T(8,128)(2,1)S(1)} %get-tuple-element.53), channel_id=1, source_target_pairs={{0,48},{4,52},{8,56},{12,60},{16,0},{20,4},{24,8},{28,12},{32,16},... | collective-permute-start | bytes 2777096 | tf_op jit(solution)/shard_map/ppermute | solution.py:36
  40.2 2.5 %collective-permute-start.6 = (s16[3616,128]{1,0:T(8,128)(2,1)S(1)}, s16[3616,128]{1,0:T(8,128)(2,1)S(1)}, u32[]{:S(2)}, u32[]{:S(2)}) collective-permute-start(s16[3616,128]{1,0:T(8,128)(2,1)S(1)} %get-tuple-element.55), channel_id=1, source_target_pairs={{0,12},{4,0},{8,4},{12,8},{16,28},{20,16},{24,20},{28,24},{32,44},... | collective-permute-start | bytes 2777096 | tf_op jit(solution)/shard_map/ppermute | solution.py:36
  42.9 5.9 %far_kernel.1 = (s16[3616,128]{1,0:T(8,128)(2,1)S(1)}, s16[3616,128]{1,0:T(8,128)(2,1)S(1)}, s16[3616,128]{1,0:T(8,128)(2,1)S(1)}, s16[3616,128]{1,0:T(8,128)(2,1)S(1)}) custom-call(s16[3616,128]{1,0:T(8,128)(2,1)S(1)} %get-tuple-element.48.refs_0_, bf16[896,3584]{1,0:T(8,128)(2,1)S(1)} %get-tuple-element.49.refs_1_, ...), custom_call_target="tpu_custom_call" | custom-call | flops 1000 | bytes 1000 | tf_op jit(solution)/shard_map/far_kernel/pallas_call | solution.py:322
  48.8 10.7 %collective-permute-done.3.refs_5_ = s16[3616,128]{1,0:T(8,128)(2,1)S(1)} collective-permute-done((s16[3616,128]{1,0:T(8,128)(2,1)S(1)}, s16[3616,128]{1,0:T(8,128)(2,1)S(1)}, u32[]{:S(2)}, u32[]{:S(2)}) %collective-permute-start.3) | collective-permute-done | bytes 925728 | tf_op jit(solution)/shard_map/ppermute | solution.py:36
  59.5 2.7 %collective-permute-start.8 = (s16[3616,128]{1,0:T(8,128)(2,1)S(1)}, s16[3616,128]{1,0:T(8,128)(2,1)S(1)}, u32[]{:S(2)}, u32[]{:S(2)}) collective-permute-start(s16[3616,128]{1,0:T(8,128)(2,1)S(1)} %get-tuple-element.59), channel_id=1, source_target_pairs={{0,48},{4,52},{8,56},{12,60},{16,0},{20,4},{24,8},{28,12},{32,16},... | collective-permute-start | bytes 2777096 | tf_op jit(solution)/shard_map/ppermute | solution.py:36
  62.2 1.2 collective-permute-done.5.refs_7_.refs_9_
  63.3 2.7 %collective-permute-start.10 = (s16[3616,128]{1,0:T(8,128)(2,1)S(1)}, s16[3616,128]{1,0:T(8,128)(2,1)S(1)}, u32[]{:S(2)}, u32[]{:S(2)}) collective-permute-start(s16[3616,128]{1,0:T(8,128)(2,1)S(1)} %get-tuple-element.65), channel_id=1, source_target_pairs={{0,12},{4,0},{8,4},{12,8},{16,28},{20,16},{24,20},{28,24},{32,44},... | collective-permute-start | bytes 2777096 | tf_op jit(solution)/shard_map/ppermute | solution.py:36
  66.0 5.1 %later_kernel.1 = (f32[256,3584]{1,0:T(8,128)S(1)}, f32[256,3584]{1,0:T(8,128)S(1)}) custom-call(s16[3616,128]{1,0:T(8,128)(2,1)S(1)} %get-tuple-element.58.refs_0_, bf16[896,3584]{1,0:T(8,128)(2,1)S(1)} %get-tuple-element.49.refs_1_, bf16[896,3584]{1,0:T(8,128)(2,1)S(1)} %get-tuple-element.50.refs_2_, bf16[512,896]{1,0:T(8,128)(2,1)S(1)} %bitcast.35, ...), custom_call_target="tpu_custom_call" | custom-call | flops 1000 | bytes 1000 | tf_op jit(solution)/shard_map/later_kernel/pallas_call | solution.py:322
  71.1 10.5 %collective-permute-done.7.refs_2_.refs_7_ = s16[3616,128]{1,0:T(8,128)(2,1)S(1)} collective-permute-done((s16[3616,128]{1,0:T(8,128)(2,1)S(1)}, s16[3616,128]{1,0:T(8,128)(2,1)S(1)}, u32[]{:S(2)}, u32[]{:S(2)}) %collective-permute-start.7) | collective-permute-done | bytes 925728 | tf_op jit(solution)/shard_map/ppermute | solution.py:36
  81.6 1.2 pass_on_kernel.2
  83.1 2.5 %collective-permute-start.12 = (s16[3616,128]{1,0:T(8,128)(2,1)S(1)}, s16[3616,128]{1,0:T(8,128)(2,1)S(1)}, u32[]{:S(2)}, u32[]{:S(2)}) collective-permute-start(s16[3616,128]{1,0:T(8,128)(2,1)S(1)} %get-tuple-element.68), channel_id=1, source_target_pairs={{0,48},{4,52},{8,56},{12,60},{16,0},{20,4},{24,8},{28,12},{32,16},... | collective-permute-start | bytes 2777096 | tf_op jit(solution)/shard_map/ppermute | solution.py:36
  85.8 1.2 pass_on_kernel.3
  87.3 2.5 %collective-permute-start.14 = (s16[3616,128]{1,0:T(8,128)(2,1)S(1)}, s16[3616,128]{1,0:T(8,128)(2,1)S(1)}, u32[]{:S(2)}, u32[]{:S(2)}) collective-permute-start(s16[3616,128]{1,0:T(8,128)(2,1)S(1)} %get-tuple-element.71), channel_id=1, source_target_pairs={{0,12},{4,0},{8,4},{12,8},{16,28},{20,16},{24,20},{28,24},{32,44},... | collective-permute-start | bytes 2777096 | tf_op jit(solution)/shard_map/ppermute | solution.py:36
  89.8 5.1 %own_kernel.1 = (f32[256,3584]{1,0:T(8,128)S(1)}, f32[256,3584]{1,0:T(8,128)S(1)}) custom-call(s16[3616,128]{1,0:T(8,128)(2,1)S(1)} %get-tuple-element.66.refs_0_, bf16[896,3584]{1,0:T(8,128)(2,1)S(1)} %get-tuple-element.49.refs_1_, bf16[896,3584]{1,0:T(8,128)(2,1)S(1)} %get-tuple-element.50.refs_2_, bf16[512,896]{1,0:T(8,128)(2,1)S(1)} %bitcast.36, ...), custom_call_target="tpu_custom_call" | custom-call | flops 1000 | bytes 1000 | tf_op jit(solution)/shard_map/own_kernel/pallas_call | solution.py:322
  94.9 9.2 %collective-permute-done.11.refs_2_ = s16[3616,128]{1,0:T(8,128)(2,1)S(1)} collective-permute-done((s16[3616,128]{1,0:T(8,128)(2,1)S(1)}, s16[3616,128]{1,0:T(8,128)(2,1)S(1)}, u32[]{:S(2)}, u32[]{:S(2)}) %collective-permute-start.11) | collective-permute-done | bytes 925728 | tf_op jit(solution)/shard_map/ppermute | solution.py:36
  104.8 2.5 %collective-permute-start.16 = (s16[928,128]{1,0:T(8,128)(2,1)S(1)}, s16[928,128]{1,0:T(8,128)(2,1)S(1)}, u32[]{:S(2)}, u32[]{:S(2)}) collective-permute-start(s16[928,128]{1,0:T(8,128)(2,1)S(1)} %get-tuple-element.73), channel_id=1, source_target_pairs={{0,12},{4,0},{8,4},{12,8},{16,28},{20,16},{24,20},{28,24},{32,44},... | collective-permute-start | bytes 712712 | tf_op jit(solution)/shard_map/ppermute | solution.py:36
  108.6 2.7 %collective-permute-start.18 = (s16[928,128]{1,0:T(8,128)(2,1)S(1)}, s16[928,128]{1,0:T(8,128)(2,1)S(1)}, u32[]{:S(2)}, u32[]{:S(2)}) collective-permute-start(s16[928,128]{1,0:T(8,128)(2,1)S(1)} %get-tuple-element.75), channel_id=1, source_target_pairs={{0,48},{4,52},{8,56},{12,60},{16,0},{20,4},{24,8},{28,12},{32,16},... | collective-permute-start | bytes 712712 | tf_op jit(solution)/shard_map/ppermute | solution.py:36
  111.2 2.5 %collective-permute-done.15.refs_4_ = s16[928,128]{1,0:T(8,128)(2,1)S(1)} collective-permute-done((s16[928,128]{1,0:T(8,128)(2,1)S(1)}, s16[928,128]{1,0:T(8,128)(2,1)S(1)}, u32[]{:S(2)}, u32[]{:S(2)}) %collective-permute-start.15) | collective-permute-done | bytes 237600 | tf_op jit(solution)/shard_map/ppermute | solution.py:36
  114.8 2.7 %collective-permute-start.20 = (s16[1824,128]{1,0:T(8,128)(2,1)S(1)}, s16[1824,128]{1,0:T(8,128)(2,1)S(1)}, u32[]{:S(2)}, u32[]{:S(2)}) collective-permute-start(s16[1824,128]{1,0:T(8,128)(2,1)S(1)} %get-tuple-element.77), channel_id=1, source_target_pairs={{0,12},{4,0},{8,4},{12,8},{16,28},{20,16},{24,20},{28,24},{32,44},... | collective-permute-start | bytes 1400840 | tf_op jit(solution)/shard_map/ppermute | solution.py:36
  118.6 2.7 %collective-permute-start.22 = (s16[1824,128]{1,0:T(8,128)(2,1)S(1)}, s16[1824,128]{1,0:T(8,128)(2,1)S(1)}, u32[]{:S(2)}, u32[]{:S(2)}) collective-permute-start(s16[1824,128]{1,0:T(8,128)(2,1)S(1)} %get-tuple-element.79), channel_id=1, source_target_pairs={{0,48},{4,52},{8,56},{12,60},{16,0},{20,4},{24,8},{28,12},{32,16},... | collective-permute-start | bytes 1400840 | tf_op jit(solution)/shard_map/ppermute | solution.py:36
  121.3 3.4 %collective-permute-done.19.refs_4_ = s16[1824,128]{1,0:T(8,128)(2,1)S(1)} collective-permute-done((s16[1824,128]{1,0:T(8,128)(2,1)S(1)}, s16[1824,128]{1,0:T(8,128)(2,1)S(1)}, u32[]{:S(2)}, u32[]{:S(2)}) %collective-permute-start.19) | collective-permute-done | bytes 466976 | tf_op jit(solution)/shard_map/ppermute | solution.py:36
  126.7 2.7 %collective-permute-start.25 = (s16[480,128]{1,0:T(8,128)(2,1)S(1)}, s16[480,128]{1,0:T(8,128)(2,1)S(1)}, u32[]{:S(2)}, u32[]{:S(2)}) collective-permute-start(s16[480,128]{1,0:T(8,128)(2,1)S(1)} %get-tuple-element.83), channel_id=1, source_target_pairs={{0,66},{1,67},{2,64},{3,65},{4,70},{5,71},{6,68},{7,69},{8,74},{9,... | collective-permute-start | bytes 368648 | tf_op jit(solution)/shard_map/ppermute | solution.py:424
  130.3 1.2 collective-permute-start.27
  131.5 2.7 %collective-permute-start.28 = (s16[480,128]{1,0:T(8,128)(2,1)S(1)}, s16[480,128]{1,0:T(8,128)(2,1)S(1)}, u32[]{:S(2)}, u32[]{:S(2)}) collective-permute-start(s16[480,128]{1,0:T(8,128)(2,1)S(1)} %get-tuple-element.87), channel_id=1, source_target_pairs={{0,66},{1,67},{2,64},{3,65},{4,70},{5,71},{6,68},{7,69},{8,74},{9,... | collective-permute-start | bytes 368648 | tf_op jit(solution)/shard_map/ppermute | solution.py:424
  135.5 1.8 %collective-permute-done.27.refs_3_ = s16[480,128]{1,0:T(8,128)(2,1)S(1)} collective-permute-done((s16[480,128]{1,0:T(8,128)(2,1)S(1)}, s16[480,128]{1,0:T(8,128)(2,1)S(1)}, u32[]{:S(2)}, u32[]{:S(2)}) %collective-permute-start.27) | collective-permute-done | bytes 122912 | tf_op jit(solution)/shard_map/ppermute | solution.py:40
  137.3 3.5 %collective-permute-done.28.refs_4_ = s16[480,128]{1,0:T(8,128)(2,1)S(1)} collective-permute-done((s16[480,128]{1,0:T(8,128)(2,1)S(1)}, s16[480,128]{1,0:T(8,128)(2,1)S(1)}, u32[]{:S(2)}, u32[]{:S(2)}) %collective-permute-start.28) | collective-permute-done | bytes 122912 | tf_op jit(solution)/shard_map/ppermute | solution.py:424
  141.1 3.3 %collective-permute-start.29 = (bf16[8,14336]{1,0:T(8,128)(2,1)S(1)}, bf16[8,14336]{1,0:T(8,128)(2,1)S(1)}, u32[]{:S(2)}, u32[]{:S(2)}) collective-permute-start(bf16[8,14336]{1,0:T(8,128)(2,1)S(1)} %dynamic-slice_bitcast_fusion), channel_id=1, source_target_pairs={{0,1},{1,0},{2,3},{3,2},{4,5},{5,4},{6,7},{7,6},{8,9},{9,8},{10,11... | collective-permute-start | bytes 688136 | tf_op jit(solution)/shard_map/ppermute | solution.py:40
  (55 shorter events, 13.2 us)
Async XLA Ops:
  0.0 27.3 %copy-start = (s32[7,56]{1,0:T(8,128)S(1)}, s32[7,56]{1,0:T(8,128)}, u32[]{:S(2)}) copy-start(s32[7,56]{1,0:T(8,128)} %refs_2_.1) | copy-start | bytes 4708
  21.1 5.9 %collective-permute-start = (bf16[256,896]{1,0:T(8,128)(2,1)S(1)}, bf16[256,896]{1,0:T(8,128)(2,1)S(1)}, u32[]{:S(2)}, u32[]{:S(2)}) collective-permute-start(bf16[256,896]{1,0:T(8,128)(2,1)S(1)} %bitcast.37), channel_id=1, source_target_pairs={{0,1},{1,0},{2,3},{3,2},{4,5},{5,4},{6,7},{7,6},{8,9},{9,8},{10,11... | collective-permute-start | bytes 1376264 | tf_op jit(solution)/shard_map/ppermute | solution.py:40
  23.7 15.4 %collective-permute-start.1 = (bf16[256,896]{1,0:T(8,128)(2,1)S(1)}, bf16[256,896]{1,0:T(8,128)(2,1)S(1)}, u32[]{:S(2)}, u32[]{:S(2)}) collective-permute-start(bf16[256,896]{1,0:T(8,128)(2,1)S(1)} %bitcast.38), channel_id=1, source_target_pairs={{0,2},{1,3},{2,0},{3,1},{4,6},{5,7},{6,4},{7,5},{8,10},{9,11},{10,... | collective-permute-start | bytes 1376264 | tf_op jit(solution)/shard_map/ppermute | solution.py:40
  36.4 23.1 %collective-permute-start.3 = (s16[3616,128]{1,0:T(8,128)(2,1)S(1)}, s16[3616,128]{1,0:T(8,128)(2,1)S(1)}, u32[]{:S(2)}, u32[]{:S(2)}) collective-permute-start(s16[3616,128]{1,0:T(8,128)(2,1)S(1)} %get-tuple-element.48.refs_0_), channel_id=1, source_target_pairs={{0,16},{4,20},{8,24},{12,28},{16,32},{20,36},{24,40},{28,44},{32,4... | collective-permute-start | bytes 2777096 | tf_op jit(solution)/shard_map/ppermute | solution.py:36
  36.8 22.7 %collective-permute-start.4 = (s16[3616,128]{1,0:T(8,128)(2,1)S(1)}, s16[3616,128]{1,0:T(8,128)(2,1)S(1)}, u32[]{:S(2)}, u32[]{:S(2)}) collective-permute-start(s16[3616,128]{1,0:T(8,128)(2,1)S(1)} %get-tuple-element.53), channel_id=1, source_target_pairs={{0,48},{4,52},{8,56},{12,60},{16,0},{20,4},{24,8},{28,12},{32,16},... | collective-permute-start | bytes 2777096 | tf_op jit(solution)/shard_map/ppermute | solution.py:36
  39.1 3.5 %collective-permute-start.2 = (bf16[256,896]{1,0:T(8,128)(2,1)S(1)}, bf16[256,896]{1,0:T(8,128)(2,1)S(1)}, u32[]{:S(2)}, u32[]{:S(2)}) collective-permute-start(bf16[256,896]{1,0:T(8,128)(2,1)S(1)} %collective-permute-done.1), channel_id=1, source_target_pairs={{0,1},{1,0},{2,3},{3,2},{4,5},{5,4},{6,7},{7,6},{8,9},{9,8},{10,11... | collective-permute-start | bytes 1376264 | tf_op jit(solution)/shard_map/ppermute | solution.py:40
  40.0 23.4 %collective-permute-start.5 = (s16[3616,128]{1,0:T(8,128)(2,1)S(1)}, s16[3616,128]{1,0:T(8,128)(2,1)S(1)}, u32[]{:S(2)}, u32[]{:S(2)}) collective-permute-start(s16[3616,128]{1,0:T(8,128)(2,1)S(1)} %get-tuple-element.54), channel_id=1, source_target_pairs={{0,4},{4,8},{8,12},{12,0},{16,20},{20,24},{24,28},{28,16},{32,36},... | collective-permute-start | bytes 2777096 | tf_op jit(solution)/shard_map/ppermute | solution.py:36
  40.2 23.2 %collective-permute-start.6 = (s16[3616,128]{1,0:T(8,128)(2,1)S(1)}, s16[3616,128]{1,0:T(8,128)(2,1)S(1)}, u32[]{:S(2)}, u32[]{:S(2)}) collective-permute-start(s16[3616,128]{1,0:T(8,128)(2,1)S(1)} %get-tuple-element.55), channel_id=1, source_target_pairs={{0,12},{4,0},{8,4},{12,8},{16,28},{20,16},{24,20},{28,24},{32,44},... | collective-permute-start | bytes 2777096 | tf_op jit(solution)/shard_map/ppermute | solution.py:36
  59.5 22.1 %collective-permute-start.7 = (s16[3616,128]{1,0:T(8,128)(2,1)S(1)}, s16[3616,128]{1,0:T(8,128)(2,1)S(1)}, u32[]{:S(2)}, u32[]{:S(2)}) collective-permute-start(s16[3616,128]{1,0:T(8,128)(2,1)S(1)} %get-tuple-element.58.refs_0_), channel_id=1, source_target_pairs={{0,16},{4,20},{8,24},{12,28},{16,32},{20,36},{24,40},{28,44},{32,4... | collective-permute-start | bytes 2777096 | tf_op jit(solution)/shard_map/ppermute | solution.py:36
  59.5 22.1 %collective-permute-start.8 = (s16[3616,128]{1,0:T(8,128)(2,1)S(1)}, s16[3616,128]{1,0:T(8,128)(2,1)S(1)}, u32[]{:S(2)}, u32[]{:S(2)}) collective-permute-start(s16[3616,128]{1,0:T(8,128)(2,1)S(1)} %get-tuple-element.59), channel_id=1, source_target_pairs={{0,48},{4,52},{8,56},{12,60},{16,0},{20,4},{24,8},{28,12},{32,16},... | collective-permute-start | bytes 2777096 | tf_op jit(solution)/shard_map/ppermute | solution.py:36
  63.3 22.5 %collective-permute-start.9 = (s16[3616,128]{1,0:T(8,128)(2,1)S(1)}, s16[3616,128]{1,0:T(8,128)(2,1)S(1)}, u32[]{:S(2)}, u32[]{:S(2)}) collective-permute-start(s16[3616,128]{1,0:T(8,128)(2,1)S(1)} %get-tuple-element.64), channel_id=1, source_target_pairs={{0,4},{4,8},{8,12},{12,0},{16,20},{20,24},{24,28},{28,16},{32,36},... | collective-permute-start | bytes 2777096 | tf_op jit(solution)/shard_map/ppermute | solution.py:36
  63.3 22.5 %collective-permute-start.10 = (s16[3616,128]{1,0:T(8,128)(2,1)S(1)}, s16[3616,128]{1,0:T(8,128)(2,1)S(1)}, u32[]{:S(2)}, u32[]{:S(2)}) collective-permute-start(s16[3616,128]{1,0:T(8,128)(2,1)S(1)} %get-tuple-element.65), channel_id=1, source_target_pairs={{0,12},{4,0},{8,4},{12,8},{16,28},{20,16},{24,20},{28,24},{32,44},... | collective-permute-start | bytes 2777096 | tf_op jit(solution)/shard_map/ppermute | solution.py:36
  82.8 21.3 %collective-permute-start.11 = (s16[3616,128]{1,0:T(8,128)(2,1)S(1)}, s16[3616,128]{1,0:T(8,128)(2,1)S(1)}, u32[]{:S(2)}, u32[]{:S(2)}) collective-permute-start(s16[3616,128]{1,0:T(8,128)(2,1)S(1)} %get-tuple-element.60.refs_0_), channel_id=1, source_target_pairs={{0,16},{4,20},{8,24},{12,28},{16,32},{20,36},{24,40},{28,44},{32,4... | collective-permute-start | bytes 2777096 | tf_op jit(solution)/shard_map/ppermute | solution.py:36
  83.1 21.0 %collective-permute-start.12 = (s16[3616,128]{1,0:T(8,128)(2,1)S(1)}, s16[3616,128]{1,0:T(8,128)(2,1)S(1)}, u32[]{:S(2)}, u32[]{:S(2)}) collective-permute-start(s16[3616,128]{1,0:T(8,128)(2,1)S(1)} %get-tuple-element.68), channel_id=1, source_target_pairs={{0,48},{4,52},{8,56},{12,60},{16,0},{20,4},{24,8},{28,12},{32,16},... | collective-permute-start | bytes 2777096 | tf_op jit(solution)/shard_map/ppermute | solution.py:36
  87.0 20.9 %collective-permute-start.13 = (s16[3616,128]{1,0:T(8,128)(2,1)S(1)}, s16[3616,128]{1,0:T(8,128)(2,1)S(1)}, u32[]{:S(2)}, u32[]{:S(2)}) collective-permute-start(s16[3616,128]{1,0:T(8,128)(2,1)S(1)} %get-tuple-element.66.refs_0_), channel_id=1, source_target_pairs={{0,4},{4,8},{8,12},{12,0},{16,20},{20,24},{24,28},{28,16},{32,36},... | collective-permute-start | bytes 2777096 | tf_op jit(solution)/shard_map/ppermute | solution.py:36
  87.3 20.7 %collective-permute-start.14 = (s16[3616,128]{1,0:T(8,128)(2,1)S(1)}, s16[3616,128]{1,0:T(8,128)(2,1)S(1)}, u32[]{:S(2)}, u32[]{:S(2)}) collective-permute-start(s16[3616,128]{1,0:T(8,128)(2,1)S(1)} %get-tuple-element.71), channel_id=1, source_target_pairs={{0,12},{4,0},{8,4},{12,8},{16,28},{20,16},{24,20},{28,24},{32,44},... | collective-permute-start | bytes 2777096 | tf_op jit(solution)/shard_map/ppermute | solution.py:36
  104.6 9.1 %collective-permute-start.15 = (s16[928,128]{1,0:T(8,128)(2,1)S(1)}, s16[928,128]{1,0:T(8,128)(2,1)S(1)}, u32[]{:S(2)}, u32[]{:S(2)}) collective-permute-start(s16[928,128]{1,0:T(8,128)(2,1)S(1)} %get-tuple-element.69.refs_0_), channel_id=1, source_target_pairs={{0,4},{4,8},{8,12},{12,0},{16,20},{20,24},{24,28},{28,16},{32,36},... | collective-permute-start | bytes 712712 | tf_op jit(solution)/shard_map/ppermute | solution.py:36
  104.8 8.9 %collective-permute-start.16 = (s16[928,128]{1,0:T(8,128)(2,1)S(1)}, s16[928,128]{1,0:T(8,128)(2,1)S(1)}, u32[]{:S(2)}, u32[]{:S(2)}) collective-permute-start(s16[928,128]{1,0:T(8,128)(2,1)S(1)} %get-tuple-element.73), channel_id=1, source_target_pairs={{0,12},{4,0},{8,4},{12,8},{16,28},{20,16},{24,20},{28,24},{32,44},... | collective-permute-start | bytes 712712 | tf_op jit(solution)/shard_map/ppermute | solution.py:36
  108.5 9.1 %collective-permute-start.17 = (s16[928,128]{1,0:T(8,128)(2,1)S(1)}, s16[928,128]{1,0:T(8,128)(2,1)S(1)}, u32[]{:S(2)}, u32[]{:S(2)}) collective-permute-start(s16[928,128]{1,0:T(8,128)(2,1)S(1)} %get-tuple-element.72.refs_0_), channel_id=1, source_target_pairs={{0,16},{4,20},{8,24},{12,28},{16,32},{20,36},{24,40},{28,44},{32,4... | collective-permute-start | bytes 712712 | tf_op jit(solution)/shard_map/ppermute | solution.py:36
  108.6 9.0 %collective-permute-start.18 = (s16[928,128]{1,0:T(8,128)(2,1)S(1)}, s16[928,128]{1,0:T(8,128)(2,1)S(1)}, u32[]{:S(2)}, u32[]{:S(2)}) collective-permute-start(s16[928,128]{1,0:T(8,128)(2,1)S(1)} %get-tuple-element.75), channel_id=1, source_target_pairs={{0,48},{4,52},{8,56},{12,60},{16,0},{20,4},{24,8},{28,12},{32,16},... | collective-permute-start | bytes 712712 | tf_op jit(solution)/shard_map/ppermute | solution.py:36
  114.7 9.9 %collective-permute-start.19 = (s16[1824,128]{1,0:T(8,128)(2,1)S(1)}, s16[1824,128]{1,0:T(8,128)(2,1)S(1)}, u32[]{:S(2)}, u32[]{:S(2)}) collective-permute-start(s16[1824,128]{1,0:T(8,128)(2,1)S(1)} %get-tuple-element.74.refs_0_), channel_id=1, source_target_pairs={{0,4},{4,8},{8,12},{12,0},{16,20},{20,24},{24,28},{28,16},{32,36},... | collective-permute-start | bytes 1400840 | tf_op jit(solution)/shard_map/ppermute | solution.py:36
  114.8 9.8 %collective-permute-start.20 = (s16[1824,128]{1,0:T(8,128)(2,1)S(1)}, s16[1824,128]{1,0:T(8,128)(2,1)S(1)}, u32[]{:S(2)}, u32[]{:S(2)}) collective-permute-start(s16[1824,128]{1,0:T(8,128)(2,1)S(1)} %get-tuple-element.77), channel_id=1, source_target_pairs={{0,12},{4,0},{8,4},{12,8},{16,28},{20,16},{24,20},{28,24},{32,44},... | collective-permute-start | bytes 1400840 | tf_op jit(solution)/shard_map/ppermute | solution.py:36
  118.5 10.9 %collective-permute-start.21 = (s16[1824,128]{1,0:T(8,128)(2,1)S(1)}, s16[1824,128]{1,0:T(8,128)(2,1)S(1)}, u32[]{:S(2)}, u32[]{:S(2)}) collective-permute-start(s16[1824,128]{1,0:T(8,128)(2,1)S(1)} %get-tuple-element.76.refs_0_), channel_id=1, source_target_pairs={{0,16},{4,20},{8,24},{12,28},{16,32},{20,36},{24,40},{28,44},{32,4... | collective-permute-start | bytes 1400840 | tf_op jit(solution)/shard_map/ppermute | solution.py:36
  118.6 10.8 %collective-permute-start.22 = (s16[1824,128]{1,0:T(8,128)(2,1)S(1)}, s16[1824,128]{1,0:T(8,128)(2,1)S(1)}, u32[]{:S(2)}, u32[]{:S(2)}) collective-permute-start(s16[1824,128]{1,0:T(8,128)(2,1)S(1)} %get-tuple-element.79), channel_id=1, source_target_pairs={{0,48},{4,52},{8,56},{12,60},{16,0},{20,4},{24,8},{28,12},{32,16},... | collective-permute-start | bytes 1400840 | tf_op jit(solution)/shard_map/ppermute | solution.py:36
  125.5 6.0 %collective-permute-start.23 = (s16[480,128]{1,0:T(8,128)(2,1)S(1)}, s16[480,128]{1,0:T(8,128)(2,1)S(1)}, u32[]{:S(2)}, u32[]{:S(2)}) collective-permute-start(s16[480,128]{1,0:T(8,128)(2,1)S(1)} %get-tuple-element.78.refs_0_), channel_id=1, source_target_pairs={{0,64},{4,68},{8,72},{12,76},{16,80},{20,84},{24,88},{28,92},{32,9... | collective-permute-start | bytes 368648 | tf_op jit(solution)/shard_map/ppermute | solution.py:36
  125.7 8.5 %collective-permute-start.24 = (s16[480,128]{1,0:T(8,128)(2,1)S(1)}, s16[480,128]{1,0:T(8,128)(2,1)S(1)}, u32[]{:S(2)}, u32[]{:S(2)}) collective-permute-start(s16[480,128]{1,0:T(8,128)(2,1)S(1)} %get-tuple-element.82), channel_id=1, source_target_pairs={{0,2},{1,3},{2,0},{3,1},{4,6},{5,7},{6,4},{7,5},{8,10},{9,11},{10,... | collective-permute-start | bytes 368648 | tf_op jit(solution)/shard_map/ppermute | solution.py:40
  126.7 7.5 %collective-permute-start.25 = (s16[480,128]{1,0:T(8,128)(2,1)S(1)}, s16[480,128]{1,0:T(8,128)(2,1)S(1)}, u32[]{:S(2)}, u32[]{:S(2)}) collective-permute-start(s16[480,128]{1,0:T(8,128)(2,1)S(1)} %get-tuple-element.83), channel_id=1, source_target_pairs={{0,66},{1,67},{2,64},{3,65},{4,70},{5,71},{6,68},{7,69},{8,74},{9,... | collective-permute-start | bytes 368648 | tf_op jit(solution)/shard_map/ppermute | solution.py:424
  130.2 5.3 %collective-permute-start.26 = (s16[480,128]{1,0:T(8,128)(2,1)S(1)}, s16[480,128]{1,0:T(8,128)(2,1)S(1)}, u32[]{:S(2)}, u32[]{:S(2)}) collective-permute-start(s16[480,128]{1,0:T(8,128)(2,1)S(1)} %get-tuple-element.80.refs_0_), channel_id=1, source_target_pairs={{0,64},{4,68},{8,72},{12,76},{16,80},{20,84},{24,88},{28,92},{32,9... | collective-permute-start | bytes 368648 | tf_op jit(solution)/shard_map/ppermute | solution.py:36
  130.3 7.0 %collective-permute-start.27 = (s16[480,128]{1,0:T(8,128)(2,1)S(1)}, s16[480,128]{1,0:T(8,128)(2,1)S(1)}, u32[]{:S(2)}, u32[]{:S(2)}) collective-permute-start(s16[480,128]{1,0:T(8,128)(2,1)S(1)} %get-tuple-element.86), channel_id=1, source_target_pairs={{0,2},{1,3},{2,0},{3,1},{4,6},{5,7},{6,4},{7,5},{8,10},{9,11},{10,... | collective-permute-start | bytes 368648 | tf_op jit(solution)/shard_map/ppermute | solution.py:40
  131.5 9.3 %collective-permute-start.28 = (s16[480,128]{1,0:T(8,128)(2,1)S(1)}, s16[480,128]{1,0:T(8,128)(2,1)S(1)}, u32[]{:S(2)}, u32[]{:S(2)}) collective-permute-start(s16[480,128]{1,0:T(8,128)(2,1)S(1)} %get-tuple-element.87), channel_id=1, source_target_pairs={{0,66},{1,67},{2,64},{3,65},{4,70},{5,71},{6,68},{7,69},{8,74},{9,... | collective-permute-start | bytes 368648 | tf_op jit(solution)/shard_map/ppermute | solution.py:424
  141.1 4.4 %collective-permute-start.29 = (bf16[8,14336]{1,0:T(8,128)(2,1)S(1)}, bf16[8,14336]{1,0:T(8,128)(2,1)S(1)}, u32[]{:S(2)}, u32[]{:S(2)}) collective-permute-start(bf16[8,14336]{1,0:T(8,128)(2,1)S(1)} %dynamic-slice_bitcast_fusion), channel_id=1, source_target_pairs={{0,1},{1,0},{2,3},{3,2},{4,5},{5,4},{6,7},{7,6},{8,9},{9,8},{10,11... | collective-permute-start | bytes 688136 | tf_op jit(solution)/shard_map/ppermute | solution.py:40

commit v8 on v7

--- a/solution.py
+++ b/solution.py
@@ -300,6 +300,16 @@
         at = columns_of(t)
         near[:, at] = (rest[:, at] + decode(a, f0, t)).astype(jnp.bfloat16)
         far[:, at] = (decode(b, f1, t) + decode(c, f2, t)).astype(jnp.bfloat16)
+
+
+def assemble_kernel(mine, other, out):
+    col = lax.axis_index("col")
+    columns = mine.shape[1] // 2
+    for far in range(2):
+        for step, ref in enumerate((mine, other)):
+            block = (col + 2 * far) % 4 if step == 0 else (col + 1 - 2 * (col % 2) + 2 * far) % 4
+            at = pl.multiple_of(block * columns, 128)
+            out[:, pl.ds(at, columns)] = ref[:, far * columns:(far + 1) * columns]
 
 
 COST = pl.CostEstimate(flops=1000, bytes_accessed=1000, transcendentals=0)
@@ -430,12 +440,14 @@
     summed = jnp.concatenate(outs, axis=1).reshape(2, 8, 2 * columns)
     mine = lax.dynamic_index_in_dim(summed, core, 0, keepdims=False)
     other = send_col(lax.dynamic_index_in_dim(summed, 1 - core, 0, keepdims=False), 1)
-    even, odd = jnp.where(core == 0, mine, other), jnp.where(core == 0, other, mine)
-    near_pair = [even[:, :columns], odd[:, :columns]]
-    far_pair = [even[:, columns:], odd[:, columns:]]
-    first = [jnp.where(z_hi == 0, u, v) for u, v in zip(near_pair, far_pair)]
-    last = [jnp.where(z_hi == 0, v, u) for u, v in zip(near_pair, far_pair)]
-    return jnp.concatenate(first + last, axis=1)
+    return pl.pallas_call(
+        assemble_kernel,
+        in_specs=[pl.BlockSpec(memory_space=pltpu.VMEM)] * 2,
+        out_specs=pl.BlockSpec(memory_space=pltpu.VMEM),
+        out_shape=jax.ShapeDtypeStruct((pair_count, full_width), jnp.bfloat16),
+        compiler_params=pltpu.CompilerParams(vmem_limit_bytes=VMEM_LIMIT),
+        name="assemble",
+    )(mine, other)
 
 
 def solution(mesh):

time: 147 us -> 148 us (level)
  starting transfers between devices: 45.2 us -> 47.2 us
    ppermute x6, starting transfers between devices: 12.3 us -> 16.7 us  [send_col(): return lax.ppermute(value, 'col', [(c, c ^ step) for c in range(4)])]
    ppermute x2, starting transfers between devices: 5.35 us -> 3.44 us  [per_device(): b, c = (send_col(b, 2), lax.ppermute(c, ('row', 'col'), DIAGONAL))]
  transfers between devices with their start and end apart: 30 -> 30, of which waited for: 12 -> 11; matrix products, arithmetic and copies ran while one was open for 0% -> 0% of each run, Pallas kernels for 22% -> 22%
where the time goes in v8:
time: 148 us
  starting transfers between devices  47.2 us (32%)
  waiting for transfers between devices  45.4 us (31%)
  Pallas kernels  35.8 us (24%)
  blocking collectives  18.6 us (13%)
    ppermute x22, waiting for transfers between devices, send(): return lax.ppermute(value, 'row', pairs)  38.6 us
    pallas_call x14, Pallas kernels, __call__(): pl.pallas_call(lambda *refs: kernel(position(), *refs[skipped:]), in_spec...  32.5 us
    ppermute x22, starting transfers between devices, send(): return lax.ppermute(value, 'row', pairs)  27.1 us
    all_to_all x1, blocking collectives, per_device(): lax.all_to_all(ordered, 'row', split_axis=1, concat_axis=0, tiled=True)  18.6 us
    ppermute x6, starting transfers between devices, send_col(): return lax.ppermute(value, 'col', [(c, c ^ step) for c in range(4)])  16.7 us
    ppermute x6, waiting for transfers between devices, send_col(): return lax.ppermute(value, 'col', [(c, c ^ step) for c in range(4)])  4 us
    ppermute x2, starting transfers between devices, per_device(): b, c = (send_col(b, 2), lax.ppermute(c, ('row', 'col'), DIAGONAL))  3.44 us
  transfers between devices with their start and end apart: 30, of which 11 were waited for; matrix products, arithmetic and copies ran while one was open for 0% of the time, Pallas kernels for 22%

profile of v8, /device:TPU:1, one launch (start us, length us, event | category | flops | bytes accessed | tf_op | source)
XLA Modules:
  0.0 147.7 jit_solution(14107161688029249945)
XLA Ops:
  0.0 2.5 %arrange.1 = bf16[8,28672]{1,0:T(8,128)(2,1)} custom-call(s32[224]{0:T(256)} %order.1, bf16[8,28672]{1,0:T(8,128)(2,1)} %values.1, s32[8,224]{1,0:T(8,128)} %flags.1), custom_call_target="tpu_custom_call" | custom-call | tf_op jit(solution)/shard_map/arrange/pallas_call | solution.py:358
  2.5 18.6 %all_to_all.19 = bf16[8,32,896]{2,0,1:T(8,128)(2,1)S(1)} all-to-all(bf16[8,32,896]{2,0,1:T(8,128)(2,1)} %bitcast.39), channel_id=1, replica_groups=mesh['row'=32,'col'=4] {'row'}, dimensions={1} | all-to-all | bytes 917504 | tf_op jit(solution)/shard_map/all_to_all | solution.py:366
  21.1 2.6 %collective-permute-start = (bf16[256,896]{1,0:T(8,128)(2,1)S(1)}, bf16[256,896]{1,0:T(8,128)(2,1)S(1)}, u32[]{:S(2)}, u32[]{:S(2)}) collective-permute-start(bf16[256,896]{1,0:T(8,128)(2,1)S(1)} %bitcast.36), channel_id=1, source_target_pairs={{0,1},{1,0},{2,3},{3,2},{4,5},{5,4},{6,7},{7,6},{8,9},{9,8},{10,11... | collective-permute-start | bytes 1376264 | tf_op jit(solution)/shard_map/ppermute | solution.py:40
  23.7 3.3 %collective-permute-start.1 = (bf16[256,896]{1,0:T(8,128)(2,1)S(1)}, bf16[256,896]{1,0:T(8,128)(2,1)S(1)}, u32[]{:S(2)}, u32[]{:S(2)}) collective-permute-start(bf16[256,896]{1,0:T(8,128)(2,1)S(1)} %bitcast.37), channel_id=1, source_target_pairs={{0,2},{1,3},{2,0},{3,1},{4,6},{5,7},{6,4},{7,5},{8,10},{9,11},{10,... | collective-permute-start | bytes 1376264 | tf_op jit(solution)/shard_map/ppermute | solution.py:40
  27.3 9.1 %begin_kernel.1 = (s16[3616,128]{1,0:T(8,128)(2,1)S(1)}, s16[3616,128]{1,0:T(8,128)(2,1)S(1)}, s16[3616,128]{1,0:T(8,128)(2,1)S(1)}, s16[3616,128]{1,0:T(8,128)(...) custom-call(bf16[256,896]{1,0:T(8,128)(2,1)S(1)} %bitcast.38, bf16[896,7168]{1,0:T(8,128)(2,1)} %refs_1_.1, ...), custom_call_target="tpu_custom_call" | custom-call | flops 1000 | bytes 1000 | tf_op jit(solution)/shard_map/begin_kernel/pallas_call | solution.py:332
  36.8 2.3 %collective-permute-start.4 = (s16[3616,128]{1,0:T(8,128)(2,1)S(1)}, s16[3616,128]{1,0:T(8,128)(2,1)S(1)}, u32[]{:S(2)}, u32[]{:S(2)}) collective-permute-start(s16[3616,128]{1,0:T(8,128)(2,1)S(1)} %get-tuple-element.53), channel_id=1, source_target_pairs={{0,48},{4,52},{8,56},{12,60},{16,0},{20,4},{24,8},{28,12},{32,16},... | collective-permute-start | bytes 2777096 | tf_op jit(solution)/shard_map/ppermute | solution.py:36
  40.2 2.5 %collective-permute-start.6 = (s16[3616,128]{1,0:T(8,128)(2,1)S(1)}, s16[3616,128]{1,0:T(8,128)(2,1)S(1)}, u32[]{:S(2)}, u32[]{:S(2)}) collective-permute-start(s16[3616,128]{1,0:T(8,128)(2,1)S(1)} %get-tuple-element.55), channel_id=1, source_target_pairs={{0,12},{4,0},{8,4},{12,8},{16,28},{20,16},{24,20},{28,24},{32,44},... | collective-permute-start | bytes 2777096 | tf_op jit(solution)/shard_map/ppermute | solution.py:36
  42.9 5.9 %far_kernel.1 = (s16[3616,128]{1,0:T(8,128)(2,1)S(1)}, s16[3616,128]{1,0:T(8,128)(2,1)S(1)}, s16[3616,128]{1,0:T(8,128)(2,1)S(1)}, s16[3616,128]{1,0:T(8,128)(2,1)S(1)}) custom-call(s16[3616,128]{1,0:T(8,128)(2,1)S(1)} %get-tuple-element.48.refs_0_, bf16[896,3584]{1,0:T(8,128)(2,1)S(1)} %get-tuple-element.49.refs_1_, ...), custom_call_target="tpu_custom_call" | custom-call | flops 1000 | bytes 1000 | tf_op jit(solution)/shard_map/far_kernel/pallas_call | solution.py:332
  48.8 10.7 %collective-permute-done.3.refs_5_ = s16[3616,128]{1,0:T(8,128)(2,1)S(1)} collective-permute-done((s16[3616,128]{1,0:T(8,128)(2,1)S(1)}, s16[3616,128]{1,0:T(8,128)(2,1)S(1)}, u32[]{:S(2)}, u32[]{:S(2)}) %collective-permute-start.3) | collective-permute-done | bytes 925728 | tf_op jit(solution)/shard_map/ppermute | solution.py:36
  59.5 2.7 %collective-permute-start.8 = (s16[3616,128]{1,0:T(8,128)(2,1)S(1)}, s16[3616,128]{1,0:T(8,128)(2,1)S(1)}, u32[]{:S(2)}, u32[]{:S(2)}) collective-permute-start(s16[3616,128]{1,0:T(8,128)(2,1)S(1)} %get-tuple-element.59), channel_id=1, source_target_pairs={{0,48},{4,52},{8,56},{12,60},{16,0},{20,4},{24,8},{28,12},{32,16},... | collective-permute-start | bytes 2777096 | tf_op jit(solution)/shard_map/ppermute | solution.py:36
  63.3 2.4 %collective-permute-start.10 = (s16[3616,128]{1,0:T(8,128)(2,1)S(1)}, s16[3616,128]{1,0:T(8,128)(2,1)S(1)}, u32[]{:S(2)}, u32[]{:S(2)}) collective-permute-start(s16[3616,128]{1,0:T(8,128)(2,1)S(1)} %get-tuple-element.65), channel_id=1, source_target_pairs={{0,12},{4,0},{8,4},{12,8},{16,28},{20,16},{24,20},{28,24},{32,44},... | collective-permute-start | bytes 2777096 | tf_op jit(solution)/shard_map/ppermute | solution.py:36
  65.7 5.1 %later_kernel.1 = (f32[256,3584]{1,0:T(8,128)S(1)}, f32[256,3584]{1,0:T(8,128)S(1)}) custom-call(s16[3616,128]{1,0:T(8,128)(2,1)S(1)} %get-tuple-element.58.refs_0_, bf16[896,3584]{1,0:T(8,128)(2,1)S(1)} %get-tuple-element.49.refs_1_, bf16[896,3584]{1,0:T(8,128)(2,1)S(1)} %get-tuple-element.50.refs_2_, bf16[512,896]{1,0:T(8,128)(2,1)S(1)} %bitcast.34, ...), custom_call_target="tpu_custom_call" | custom-call | flops 1000 | bytes 1000 | tf_op jit(solution)/shard_map/later_kernel/pallas_call | solution.py:332
  70.8 10.8 %collective-permute-done.7.refs_2_.refs_7_ = s16[3616,128]{1,0:T(8,128)(2,1)S(1)} collective-permute-done((s16[3616,128]{1,0:T(8,128)(2,1)S(1)}, s16[3616,128]{1,0:T(8,128)(2,1)S(1)}, u32[]{:S(2)}, u32[]{:S(2)}) %collective-permute-start.7) | collective-permute-done | bytes 925728 | tf_op jit(solution)/shard_map/ppermute | solution.py:36
  83.1 2.5 %collective-permute-start.12 = (s16[3616,128]{1,0:T(8,128)(2,1)S(1)}, s16[3616,128]{1,0:T(8,128)(2,1)S(1)}, u32[]{:S(2)}, u32[]{:S(2)}) collective-permute-start(s16[3616,128]{1,0:T(8,128)(2,1)S(1)} %get-tuple-element.68), channel_id=1, source_target_pairs={{0,48},{4,52},{8,56},{12,60},{16,0},{20,4},{24,8},{28,12},{32,16},... | collective-permute-start | bytes 2777096 | tf_op jit(solution)/shard_map/ppermute | solution.py:36
  85.6 2.0 %collective-permute-done.9.refs_2_.refs_11_ = s16[3616,128]{1,0:T(8,128)(2,1)S(1)} collective-permute-done((s16[3616,128]{1,0:T(8,128)(2,1)S(1)}, s16[3616,128]{1,0:T(8,128)(2,1)S(1)}, u32[]{:S(2)}, u32[]{:S(2)}) %collective-permute-start.9) | collective-permute-done | bytes 925728 | tf_op jit(solution)/shard_map/ppermute | solution.py:36
  88.8 2.7 %collective-permute-start.14 = (s16[3616,128]{1,0:T(8,128)(2,1)S(1)}, s16[3616,128]{1,0:T(8,128)(2,1)S(1)}, u32[]{:S(2)}, u32[]{:S(2)}) collective-permute-start(s16[3616,128]{1,0:T(8,128)(2,1)S(1)} %get-tuple-element.71), channel_id=1, source_target_pairs={{0,12},{4,0},{8,4},{12,8},{16,28},{20,16},{24,20},{28,24},{32,44},... | collective-permute-start | bytes 2777096 | tf_op jit(solution)/shard_map/ppermute | solution.py:36
  91.5 5.1 %own_kernel.1 = (f32[256,3584]{1,0:T(8,128)S(1)}, f32[256,3584]{1,0:T(8,128)S(1)}) custom-call(s16[3616,128]{1,0:T(8,128)(2,1)S(1)} %get-tuple-element.66.refs_0_, bf16[896,3584]{1,0:T(8,128)(2,1)S(1)} %get-tuple-element.49.refs_1_, bf16[896,3584]{1,0:T(8,128)(2,1)S(1)} %get-tuple-element.50.refs_2_, bf16[512,896]{1,0:T(8,128)(2,1)S(1)} %bitcast.35, ...), custom_call_target="tpu_custom_call" | custom-call | flops 1000 | bytes 1000 | tf_op jit(solution)/shard_map/own_kernel/pallas_call | solution.py:332
  96.6 7.5 %collective-permute-done.11.refs_2_ = s16[3616,128]{1,0:T(8,128)(2,1)S(1)} collective-permute-done((s16[3616,128]{1,0:T(8,128)(2,1)S(1)}, s16[3616,128]{1,0:T(8,128)(2,1)S(1)}, u32[]{:S(2)}, u32[]{:S(2)}) %collective-permute-start.11) | collective-permute-done | bytes 925728 | tf_op jit(solution)/shard_map/ppermute | solution.py:36
  104.8 2.5 %collective-permute-start.16 = (s16[928,128]{1,0:T(8,128)(2,1)S(1)}, s16[928,128]{1,0:T(8,128)(2,1)S(1)}, u32[]{:S(2)}, u32[]{:S(2)}) collective-permute-start(s16[928,128]{1,0:T(8,128)(2,1)S(1)} %get-tuple-element.73), channel_id=1, source_target_pairs={{0,12},{4,0},{8,4},{12,8},{16,28},{20,16},{24,20},{28,24},{32,44},... | collective-permute-start | bytes 712712 | tf_op jit(solution)/shard_map/ppermute | solution.py:36
  107.4 2.4 %collective-permute-done.13.refs_2_ = s16[3616,128]{1,0:T(8,128)(2,1)S(1)} collective-permute-done((s16[3616,128]{1,0:T(8,128)(2,1)S(1)}, s16[3616,128]{1,0:T(8,128)(2,1)S(1)}, u32[]{:S(2)}, u32[]{:S(2)}) %collective-permute-start.13) | collective-permute-done | bytes 925728 | tf_op jit(solution)/shard_map/ppermute | solution.py:36
  110.3 2.7 %collective-permute-start.18 = (s16[928,128]{1,0:T(8,128)(2,1)S(1)}, s16[928,128]{1,0:T(8,128)(2,1)S(1)}, u32[]{:S(2)}, u32[]{:S(2)}) collective-permute-start(s16[928,128]{1,0:T(8,128)(2,1)S(1)} %get-tuple-element.75), channel_id=1, source_target_pairs={{0,48},{4,52},{8,56},{12,60},{16,0},{20,4},{24,8},{28,12},{32,16},... | collective-permute-start | bytes 712712 | tf_op jit(solution)/shard_map/ppermute | solution.py:36
  113.0 1.8 %collective-permute-done.15.refs_4_ = s16[928,128]{1,0:T(8,128)(2,1)S(1)} collective-permute-done((s16[928,128]{1,0:T(8,128)(2,1)S(1)}, s16[928,128]{1,0:T(8,128)(2,1)S(1)}, u32[]{:S(2)}, u32[]{:S(2)}) %collective-permute-start.15) | collective-permute-done | bytes 237600 | tf_op jit(solution)/shard_map/ppermute | solution.py:36
  115.9 2.7 %collective-permute-start.20 = (s16[1824,128]{1,0:T(8,128)(2,1)S(1)}, s16[1824,128]{1,0:T(8,128)(2,1)S(1)}, u32[]{:S(2)}, u32[]{:S(2)}) collective-permute-start(s16[1824,128]{1,0:T(8,128)(2,1)S(1)} %get-tuple-element.77), channel_id=1, source_target_pairs={{0,12},{4,0},{8,4},{12,8},{16,28},{20,16},{24,20},{28,24},{32,44},... | collective-permute-start | bytes 1400840 | tf_op jit(solution)/shard_map/ppermute | solution.py:36
  119.6 2.7 %collective-permute-start.22 = (s16[1824,128]{1,0:T(8,128)(2,1)S(1)}, s16[1824,128]{1,0:T(8,128)(2,1)S(1)}, u32[]{:S(2)}, u32[]{:S(2)}) collective-permute-start(s16[1824,128]{1,0:T(8,128)(2,1)S(1)} %get-tuple-element.79), channel_id=1, source_target_pairs={{0,48},{4,52},{8,56},{12,60},{16,0},{20,4},{24,8},{28,12},{32,16},... | collective-permute-start | bytes 1400840 | tf_op jit(solution)/shard_map/ppermute | solution.py:36
  122.3 2.2 %collective-permute-done.19.refs_4_ = s16[1824,128]{1,0:T(8,128)(2,1)S(1)} collective-permute-done((s16[1824,128]{1,0:T(8,128)(2,1)S(1)}, s16[1824,128]{1,0:T(8,128)(2,1)S(1)}, u32[]{:S(2)}, u32[]{:S(2)}) %collective-permute-start.19) | collective-permute-done | bytes 466976 | tf_op jit(solution)/shard_map/ppermute | solution.py:36
  125.4 2.1 %collective-permute-start.24 = (s16[480,128]{1,0:T(8,128)(2,1)S(1)}, s16[480,128]{1,0:T(8,128)(2,1)S(1)}, u32[]{:S(2)}, u32[]{:S(2)}) collective-permute-start(s16[480,128]{1,0:T(8,128)(2,1)S(1)} %get-tuple-element.82), channel_id=1, source_target_pairs={{0,2},{1,3},{2,0},{3,1},{4,6},{5,7},{6,4},{7,5},{8,10},{9,11},{10,... | collective-permute-start | bytes 368648 | tf_op jit(solution)/shard_map/ppermute | solution.py:40
  127.6 1.7 %collective-permute-start.25 = (s16[480,128]{1,0:T(8,128)(2,1)S(1)}, s16[480,128]{1,0:T(8,128)(2,1)S(1)}, u32[]{:S(2)}, u32[]{:S(2)}) collective-permute-start(s16[480,128]{1,0:T(8,128)(2,1)S(1)} %get-tuple-element.83), channel_id=1, source_target_pairs={{0,66},{1,67},{2,64},{3,65},{4,70},{5,71},{6,68},{7,69},{8,74},{9,... | collective-permute-start | bytes 368648 | tf_op jit(solution)/shard_map/ppermute | solution.py:434
  130.2 2.1 %collective-permute-start.27 = (s16[480,128]{1,0:T(8,128)(2,1)S(1)}, s16[480,128]{1,0:T(8,128)(2,1)S(1)}, u32[]{:S(2)}, u32[]{:S(2)}) collective-permute-start(s16[480,128]{1,0:T(8,128)(2,1)S(1)} %get-tuple-element.86), channel_id=1, source_target_pairs={{0,2},{1,3},{2,0},{3,1},{4,6},{5,7},{6,4},{7,5},{8,10},{9,11},{10,... | collective-permute-start | bytes 368648 | tf_op jit(solution)/shard_map/ppermute | solution.py:40
  132.3 1.7 %collective-permute-start.28 = (s16[480,128]{1,0:T(8,128)(2,1)S(1)}, s16[480,128]{1,0:T(8,128)(2,1)S(1)}, u32[]{:S(2)}, u32[]{:S(2)}) collective-permute-start(s16[480,128]{1,0:T(8,128)(2,1)S(1)} %get-tuple-element.87), channel_id=1, source_target_pairs={{0,66},{1,67},{2,64},{3,65},{4,70},{5,71},{6,68},{7,69},{8,74},{9,... | collective-permute-start | bytes 368648 | tf_op jit(solution)/shard_map/ppermute | solution.py:434
  134.2 2.9 %collective-permute-done.27.refs_3_ = s16[480,128]{1,0:T(8,128)(2,1)S(1)} collective-permute-done((s16[480,128]{1,0:T(8,128)(2,1)S(1)}, s16[480,128]{1,0:T(8,128)(2,1)S(1)}, u32[]{:S(2)}, u32[]{:S(2)}) %collective-permute-start.27) | collective-permute-done | bytes 122912 | tf_op jit(solution)/shard_map/ppermute | solution.py:40
  137.1 2.8 %collective-permute-done.28.refs_4_ = s16[480,128]{1,0:T(8,128)(2,1)S(1)} collective-permute-done((s16[480,128]{1,0:T(8,128)(2,1)S(1)}, s16[480,128]{1,0:T(8,128)(2,1)S(1)}, u32[]{:S(2)}, u32[]{:S(2)}) %collective-permute-start.28) | collective-permute-done | bytes 122912 | tf_op jit(solution)/shard_map/ppermute | solution.py:434
  140.1 5.7 %collective-permute-start.29 = (bf16[8,14336]{1,0:T(8,128)(2,1)S(1)}, bf16[8,14336]{1,0:T(8,128)(2,1)S(1)}, u32[]{:S(2)}, u32[]{:S(2)}) collective-permute-start(bf16[8,14336]{1,0:T(8,128)(2,1)S(1)} %get-tuple-element.95), channel_id=1, source_target_pairs={{0,1},{1,0},{2,3},{3,2},{4,5},{5,4},{6,7},{7,6},{8,9},{9,8},{10,11... | collective-permute-start | bytes 688136 | tf_op jit(solution)/shard_map/ppermute | solution.py:40
  (53 shorter events, 13.4 us)
Async XLA Ops:
  0.0 27.3 %copy-start = (s32[7,56]{1,0:T(8,128)S(1)}, s32[7,56]{1,0:T(8,128)}, u32[]{:S(2)}) copy-start(s32[7,56]{1,0:T(8,128)} %refs_2_.1) | copy-start | bytes 4708
  21.1 5.9 %collective-permute-start = (bf16[256,896]{1,0:T(8,128)(2,1)S(1)}, bf16[256,896]{1,0:T(8,128)(2,1)S(1)}, u32[]{:S(2)}, u32[]{:S(2)}) collective-permute-start(bf16[256,896]{1,0:T(8,128)(2,1)S(1)} %bitcast.36), channel_id=1, source_target_pairs={{0,1},{1,0},{2,3},{3,2},{4,5},{5,4},{6,7},{7,6},{8,9},{9,8},{10,11... | collective-permute-start | bytes 1376264 | tf_op jit(solution)/shard_map/ppermute | solution.py:40
  23.7 15.4 %collective-permute-start.1 = (bf16[256,896]{1,0:T(8,128)(2,1)S(1)}, bf16[256,896]{1,0:T(8,128)(2,1)S(1)}, u32[]{:S(2)}, u32[]{:S(2)}) collective-permute-start(bf16[256,896]{1,0:T(8,128)(2,1)S(1)} %bitcast.37), channel_id=1, source_target_pairs={{0,2},{1,3},{2,0},{3,1},{4,6},{5,7},{6,4},{7,5},{8,10},{9,11},{10,... | collective-permute-start | bytes 1376264 | tf_op jit(solution)/shard_map/ppermute | solution.py:40
  36.4 23.1 %collective-permute-start.3 = (s16[3616,128]{1,0:T(8,128)(2,1)S(1)}, s16[3616,128]{1,0:T(8,128)(2,1)S(1)}, u32[]{:S(2)}, u32[]{:S(2)}) collective-permute-start(s16[3616,128]{1,0:T(8,128)(2,1)S(1)} %get-tuple-element.48.refs_0_), channel_id=1, source_target_pairs={{0,16},{4,20},{8,24},{12,28},{16,32},{20,36},{24,40},{28,44},{32,4... | collective-permute-start | bytes 2777096 | tf_op jit(solution)/shard_map/ppermute | solution.py:36
  36.8 22.7 %collective-permute-start.4 = (s16[3616,128]{1,0:T(8,128)(2,1)S(1)}, s16[3616,128]{1,0:T(8,128)(2,1)S(1)}, u32[]{:S(2)}, u32[]{:S(2)}) collective-permute-start(s16[3616,128]{1,0:T(8,128)(2,1)S(1)} %get-tuple-element.53), channel_id=1, source_target_pairs={{0,48},{4,52},{8,56},{12,60},{16,0},{20,4},{24,8},{28,12},{32,16},... | collective-permute-start | bytes 2777096 | tf_op jit(solution)/shard_map/ppermute | solution.py:36
  39.1 3.5 %collective-permute-start.2 = (bf16[256,896]{1,0:T(8,128)(2,1)S(1)}, bf16[256,896]{1,0:T(8,128)(2,1)S(1)}, u32[]{:S(2)}, u32[]{:S(2)}) collective-permute-start(bf16[256,896]{1,0:T(8,128)(2,1)S(1)} %collective-permute-done.1), channel_id=1, source_target_pairs={{0,1},{1,0},{2,3},{3,2},{4,5},{5,4},{6,7},{7,6},{8,9},{9,8},{10,11... | collective-permute-start | bytes 1376264 | tf_op jit(solution)/shard_map/ppermute | solution.py:40
  40.0 23.4 %collective-permute-start.5 = (s16[3616,128]{1,0:T(8,128)(2,1)S(1)}, s16[3616,128]{1,0:T(8,128)(2,1)S(1)}, u32[]{:S(2)}, u32[]{:S(2)}) collective-permute-start(s16[3616,128]{1,0:T(8,128)(2,1)S(1)} %get-tuple-element.54), channel_id=1, source_target_pairs={{0,4},{4,8},{8,12},{12,0},{16,20},{20,24},{24,28},{28,16},{32,36},... | collective-permute-start | bytes 2777096 | tf_op jit(solution)/shard_map/ppermute | solution.py:36
  40.2 23.2 %collective-permute-start.6 = (s16[3616,128]{1,0:T(8,128)(2,1)S(1)}, s16[3616,128]{1,0:T(8,128)(2,1)S(1)}, u32[]{:S(2)}, u32[]{:S(2)}) collective-permute-start(s16[3616,128]{1,0:T(8,128)(2,1)S(1)} %get-tuple-element.55), channel_id=1, source_target_pairs={{0,12},{4,0},{8,4},{12,8},{16,28},{20,16},{24,20},{28,24},{32,44},... | collective-permute-start | bytes 2777096 | tf_op jit(solution)/shard_map/ppermute | solution.py:36
  59.5 22.1 %collective-permute-start.7 = (s16[3616,128]{1,0:T(8,128)(2,1)S(1)}, s16[3616,128]{1,0:T(8,128)(2,1)S(1)}, u32[]{:S(2)}, u32[]{:S(2)}) collective-permute-start(s16[3616,128]{1,0:T(8,128)(2,1)S(1)} %get-tuple-element.58.refs_0_), channel_id=1, source_target_pairs={{0,16},{4,20},{8,24},{12,28},{16,32},{20,36},{24,40},{28,44},{32,4... | collective-permute-start | bytes 2777096 | tf_op jit(solution)/shard_map/ppermute | solution.py:36
  59.5 22.1 %collective-permute-start.8 = (s16[3616,128]{1,0:T(8,128)(2,1)S(1)}, s16[3616,128]{1,0:T(8,128)(2,1)S(1)}, u32[]{:S(2)}, u32[]{:S(2)}) collective-permute-start(s16[3616,128]{1,0:T(8,128)(2,1)S(1)} %get-tuple-element.59), channel_id=1, source_target_pairs={{0,48},{4,52},{8,56},{12,60},{16,0},{20,4},{24,8},{28,12},{32,16},... | collective-permute-start | bytes 2777096 | tf_op jit(solution)/shard_map/ppermute | solution.py:36
  63.3 22.2 %collective-permute-start.10 = (s16[3616,128]{1,0:T(8,128)(2,1)S(1)}, s16[3616,128]{1,0:T(8,128)(2,1)S(1)}, u32[]{:S(2)}, u32[]{:S(2)}) collective-permute-start(s16[3616,128]{1,0:T(8,128)(2,1)S(1)} %get-tuple-element.65), channel_id=1, source_target_pairs={{0,12},{4,0},{8,4},{12,8},{16,28},{20,16},{24,20},{28,24},{32,44},... | collective-permute-start | bytes 2777096 | tf_op jit(solution)/shard_map/ppermute | solution.py:36
  65.7 21.8 %collective-permute-start.9 = (s16[3616,128]{1,0:T(8,128)(2,1)S(1)}, s16[3616,128]{1,0:T(8,128)(2,1)S(1)}, u32[]{:S(2)}, u32[]{:S(2)}) collective-permute-start(s16[3616,128]{1,0:T(8,128)(2,1)S(1)} %get-tuple-element.64), channel_id=1, source_target_pairs={{0,4},{4,8},{8,12},{12,0},{16,20},{20,24},{24,28},{28,16},{32,36},... | collective-permute-start | bytes 2777096 | tf_op jit(solution)/shard_map/ppermute | solution.py:36
  82.8 21.3 %collective-permute-start.11 = (s16[3616,128]{1,0:T(8,128)(2,1)S(1)}, s16[3616,128]{1,0:T(8,128)(2,1)S(1)}, u32[]{:S(2)}, u32[]{:S(2)}) collective-permute-start(s16[3616,128]{1,0:T(8,128)(2,1)S(1)} %get-tuple-element.60.refs_0_), channel_id=1, source_target_pairs={{0,16},{4,20},{8,24},{12,28},{16,32},{20,36},{24,40},{28,44},{32,4... | collective-permute-start | bytes 2777096 | tf_op jit(solution)/shard_map/ppermute | solution.py:36
  83.1 21.0 %collective-permute-start.12 = (s16[3616,128]{1,0:T(8,128)(2,1)S(1)}, s16[3616,128]{1,0:T(8,128)(2,1)S(1)}, u32[]{:S(2)}, u32[]{:S(2)}) collective-permute-start(s16[3616,128]{1,0:T(8,128)(2,1)S(1)} %get-tuple-element.68), channel_id=1, source_target_pairs={{0,48},{4,52},{8,56},{12,60},{16,0},{20,4},{24,8},{28,12},{32,16},... | collective-permute-start | bytes 2777096 | tf_op jit(solution)/shard_map/ppermute | solution.py:36
  88.8 21.0 %collective-permute-start.13 = (s16[3616,128]{1,0:T(8,128)(2,1)S(1)}, s16[3616,128]{1,0:T(8,128)(2,1)S(1)}, u32[]{:S(2)}, u32[]{:S(2)}) collective-permute-start(s16[3616,128]{1,0:T(8,128)(2,1)S(1)} %get-tuple-element.66.refs_0_), channel_id=1, source_target_pairs={{0,4},{4,8},{8,12},{12,0},{16,20},{20,24},{24,28},{28,16},{32,36},... | collective-permute-start | bytes 2777096 | tf_op jit(solution)/shard_map/ppermute | solution.py:36
  88.8 20.9 %collective-permute-start.14 = (s16[3616,128]{1,0:T(8,128)(2,1)S(1)}, s16[3616,128]{1,0:T(8,128)(2,1)S(1)}, u32[]{:S(2)}, u32[]{:S(2)}) collective-permute-start(s16[3616,128]{1,0:T(8,128)(2,1)S(1)} %get-tuple-element.71), channel_id=1, source_target_pairs={{0,12},{4,0},{8,4},{12,8},{16,28},{20,16},{24,20},{28,24},{32,44},... | collective-permute-start | bytes 2777096 | tf_op jit(solution)/shard_map/ppermute | solution.py:36
  104.6 10.2 %collective-permute-start.15 = (s16[928,128]{1,0:T(8,128)(2,1)S(1)}, s16[928,128]{1,0:T(8,128)(2,1)S(1)}, u32[]{:S(2)}, u32[]{:S(2)}) collective-permute-start(s16[928,128]{1,0:T(8,128)(2,1)S(1)} %get-tuple-element.69.refs_0_), channel_id=1, source_target_pairs={{0,4},{4,8},{8,12},{12,0},{16,20},{20,24},{24,28},{28,16},{32,36},... | collective-permute-start | bytes 712712 | tf_op jit(solution)/shard_map/ppermute | solution.py:36
  104.8 10.0 %collective-permute-start.16 = (s16[928,128]{1,0:T(8,128)(2,1)S(1)}, s16[928,128]{1,0:T(8,128)(2,1)S(1)}, u32[]{:S(2)}, u32[]{:S(2)}) collective-permute-start(s16[928,128]{1,0:T(8,128)(2,1)S(1)} %get-tuple-element.73), channel_id=1, source_target_pairs={{0,12},{4,0},{8,4},{12,8},{16,28},{20,16},{24,20},{28,24},{32,44},... | collective-permute-start | bytes 712712 | tf_op jit(solution)/shard_map/ppermute | solution.py:36
  110.3 8.3 %collective-permute-start.17 = (s16[928,128]{1,0:T(8,128)(2,1)S(1)}, s16[928,128]{1,0:T(8,128)(2,1)S(1)}, u32[]{:S(2)}, u32[]{:S(2)}) collective-permute-start(s16[928,128]{1,0:T(8,128)(2,1)S(1)} %get-tuple-element.72.refs_0_), channel_id=1, source_target_pairs={{0,16},{4,20},{8,24},{12,28},{16,32},{20,36},{24,40},{28,44},{32,4... | collective-permute-start | bytes 712712 | tf_op jit(solution)/shard_map/ppermute | solution.py:36
  110.3 8.2 %collective-permute-start.18 = (s16[928,128]{1,0:T(8,128)(2,1)S(1)}, s16[928,128]{1,0:T(8,128)(2,1)S(1)}, u32[]{:S(2)}, u32[]{:S(2)}) collective-permute-start(s16[928,128]{1,0:T(8,128)(2,1)S(1)} %get-tuple-element.75), channel_id=1, source_target_pairs={{0,48},{4,52},{8,56},{12,60},{16,0},{20,4},{24,8},{28,12},{32,16},... | collective-permute-start | bytes 712712 | tf_op jit(solution)/shard_map/ppermute | solution.py:36
  115.8 8.7 %collective-permute-start.19 = (s16[1824,128]{1,0:T(8,128)(2,1)S(1)}, s16[1824,128]{1,0:T(8,128)(2,1)S(1)}, u32[]{:S(2)}, u32[]{:S(2)}) collective-permute-start(s16[1824,128]{1,0:T(8,128)(2,1)S(1)} %get-tuple-element.74.refs_0_), channel_id=1, source_target_pairs={{0,4},{4,8},{8,12},{12,0},{16,20},{20,24},{24,28},{28,16},{32,36},... | collective-permute-start | bytes 1400840 | tf_op jit(solution)/shard_map/ppermute | solution.py:36
  115.9 8.6 %collective-permute-start.20 = (s16[1824,128]{1,0:T(8,128)(2,1)S(1)}, s16[1824,128]{1,0:T(8,128)(2,1)S(1)}, u32[]{:S(2)}, u32[]{:S(2)}) collective-permute-start(s16[1824,128]{1,0:T(8,128)(2,1)S(1)} %get-tuple-element.77), channel_id=1, source_target_pairs={{0,12},{4,0},{8,4},{12,8},{16,28},{20,16},{24,20},{28,24},{32,44},... | collective-permute-start | bytes 1400840 | tf_op jit(solution)/shard_map/ppermute | solution.py:36
  119.5 9.7 %collective-permute-start.21 = (s16[1824,128]{1,0:T(8,128)(2,1)S(1)}, s16[1824,128]{1,0:T(8,128)(2,1)S(1)}, u32[]{:S(2)}, u32[]{:S(2)}) collective-permute-start(s16[1824,128]{1,0:T(8,128)(2,1)S(1)} %get-tuple-element.76.refs_0_), channel_id=1, source_target_pairs={{0,16},{4,20},{8,24},{12,28},{16,32},{20,36},{24,40},{28,44},{32,4... | collective-permute-start | bytes 1400840 | tf_op jit(solution)/shard_map/ppermute | solution.py:36
  119.6 9.7 %collective-permute-start.22 = (s16[1824,128]{1,0:T(8,128)(2,1)S(1)}, s16[1824,128]{1,0:T(8,128)(2,1)S(1)}, u32[]{:S(2)}, u32[]{:S(2)}) collective-permute-start(s16[1824,128]{1,0:T(8,128)(2,1)S(1)} %get-tuple-element.79), channel_id=1, source_target_pairs={{0,48},{4,52},{8,56},{12,60},{16,0},{20,4},{24,8},{28,12},{32,16},... | collective-permute-start | bytes 1400840 | tf_op jit(solution)/shard_map/ppermute | solution.py:36
  125.3 7.0 %collective-permute-start.23 = (s16[480,128]{1,0:T(8,128)(2,1)S(1)}, s16[480,128]{1,0:T(8,128)(2,1)S(1)}, u32[]{:S(2)}, u32[]{:S(2)}) collective-permute-start(s16[480,128]{1,0:T(8,128)(2,1)S(1)} %get-tuple-element.78.refs_0_), channel_id=1, source_target_pairs={{0,64},{4,68},{8,72},{12,76},{16,80},{20,84},{24,88},{28,92},{32,9... | collective-permute-start | bytes 368648 | tf_op jit(solution)/shard_map/ppermute | solution.py:36
  125.4 8.6 %collective-permute-start.24 = (s16[480,128]{1,0:T(8,128)(2,1)S(1)}, s16[480,128]{1,0:T(8,128)(2,1)S(1)}, u32[]{:S(2)}, u32[]{:S(2)}) collective-permute-start(s16[480,128]{1,0:T(8,128)(2,1)S(1)} %get-tuple-element.82), channel_id=1, source_target_pairs={{0,2},{1,3},{2,0},{3,1},{4,6},{5,7},{6,4},{7,5},{8,10},{9,11},{10,... | collective-permute-start | bytes 368648 | tf_op jit(solution)/shard_map/ppermute | solution.py:40
  127.6 6.5 %collective-permute-start.25 = (s16[480,128]{1,0:T(8,128)(2,1)S(1)}, s16[480,128]{1,0:T(8,128)(2,1)S(1)}, u32[]{:S(2)}, u32[]{:S(2)}) collective-permute-start(s16[480,128]{1,0:T(8,128)(2,1)S(1)} %get-tuple-element.83), channel_id=1, source_target_pairs={{0,66},{1,67},{2,64},{3,65},{4,70},{5,71},{6,68},{7,69},{8,74},{9,... | collective-permute-start | bytes 368648 | tf_op jit(solution)/shard_map/ppermute | solution.py:434
  130.1 4.1 %collective-permute-start.26 = (s16[480,128]{1,0:T(8,128)(2,1)S(1)}, s16[480,128]{1,0:T(8,128)(2,1)S(1)}, u32[]{:S(2)}, u32[]{:S(2)}) collective-permute-start(s16[480,128]{1,0:T(8,128)(2,1)S(1)} %get-tuple-element.80.refs_0_), channel_id=1, source_target_pairs={{0,64},{4,68},{8,72},{12,76},{16,80},{20,84},{24,88},{28,92},{32,9... | collective-permute-start | bytes 368648 | tf_op jit(solution)/shard_map/ppermute | solution.py:36
  130.2 6.9 %collective-permute-start.27 = (s16[480,128]{1,0:T(8,128)(2,1)S(1)}, s16[480,128]{1,0:T(8,128)(2,1)S(1)}, u32[]{:S(2)}, u32[]{:S(2)}) collective-permute-start(s16[480,128]{1,0:T(8,128)(2,1)S(1)} %get-tuple-element.86), channel_id=1, source_target_pairs={{0,2},{1,3},{2,0},{3,1},{4,6},{5,7},{6,4},{7,5},{8,10},{9,11},{10,... | collective-permute-start | bytes 368648 | tf_op jit(solution)/shard_map/ppermute | solution.py:40
  132.3 7.6 %collective-permute-start.28 = (s16[480,128]{1,0:T(8,128)(2,1)S(1)}, s16[480,128]{1,0:T(8,128)(2,1)S(1)}, u32[]{:S(2)}, u32[]{:S(2)}) collective-permute-start(s16[480,128]{1,0:T(8,128)(2,1)S(1)} %get-tuple-element.87), channel_id=1, source_target_pairs={{0,66},{1,67},{2,64},{3,65},{4,70},{5,71},{6,68},{7,69},{8,74},{9,... | collective-permute-start | bytes 368648 | tf_op jit(solution)/shard_map/ppermute | solution.py:434
  140.1 6.8 %collective-permute-start.29 = (bf16[8,14336]{1,0:T(8,128)(2,1)S(1)}, bf16[8,14336]{1,0:T(8,128)(2,1)S(1)}, u32[]{:S(2)}, u32[]{:S(2)}) collective-permute-start(bf16[8,14336]{1,0:T(8,128)(2,1)S(1)} %get-tuple-element.95), channel_id=1, source_target_pairs={{0,1},{1,0},{2,3},{3,2},{4,5},{5,4},{6,7},{7,6},{8,9},{9,8},{10,11... | collective-permute-start | bytes 688136 | tf_op jit(solution)/shard_map/ppermute | solution.py:40
